TPU v7x, 32 devices: a whole 2x2x4 slice. The times are simulated.
32 devices in a mesh: gx: 4 (over z), gy: 4 (over x, core), gz: 2 (over y).
Axes of the slice: x: 2, y: 2, z: 4, core: 2. Of those that a mesh axis runs over, the one named last changes fastest.
Arguments:
- populations: float32 [19, 16, 128, 512], P(None, 'gx', 'gy', 'gz'), may hold values from 0.02 to 0.09
- stretch: float32 [6, 16, 128, 512], P(None, 'gx', 'gy', 'gz'), may hold values from -2.5 to 2.5
- mass: float32 [16, 128, 512], P('gx', 'gy', 'gz'), may hold values from 0 to 1
- flags: int32 [16, 128, 512], P('gx', 'gy', 'gz'), may hold values from 0 to 2
- conv_source: int32 [32768], P(('gx', 'gy', 'gz')), may hold values from 0 to 32767, as said below
- conv_kind: int32 [32768], P(('gx', 'gy', 'gz')), may hold values from 0 to 1
- conv_direction: int32 [32768], P(('gx', 'gy', 'gz')), may hold values from 1 to 18
Outputs:
- new_populations: float32 [19, 16, 128, 512], P(None, 'gx', 'gy', 'gz')
- new_stretch: float32 [6, 16, 128, 512], P(None, 'gx', 'gy', 'gz')
- new_mass: float32 [16, 128, 512], P('gx', 'gy', 'gz')
Inputs may be any that keep to these rules, and one draw needn't show every extreme that they name: `conv_source`: the 1024 sources of one brick are distinct cells of that brick. Every brick lists, for each direction i = 1..18, a conversion with direction i whose source lies on the brick's boundary so that its neighbour x + c_i lies in another brick.
All inputs are finite; a program needn't handle non-finite values.
Results may differ from a plain program's by a relative error of at most 0.0003.
Values sent between devices are 32-bit elements; how exact they have to be, the bound alone decides.
No kernel may reach another device: no remote copies, remote signals or barrier semaphores. Data moves between devices by JAX's collectives and lax.ppermute only.
A program may use at most 64 MiB of HBM per device.

v0:
```python
import jax
import jax.numpy as jnp
from jax import lax
from jax.experimental import pallas as pl
from jax.experimental.pallas import tpu as pltpu
from jax.sharding import PartitionSpec as P

velocity_set = (
    (0, 0, 0),
    (1, 0, 0),
    (-1, 0, 0),
    (0, 1, 0),
    (0, -1, 0),
    (0, 0, 1),
    (0, 0, -1),
    (1, 1, 0),
    (-1, -1, 0),
    (1, -1, 0),
    (-1, 1, 0),
    (1, 0, 1),
    (-1, 0, -1),
    (1, 0, -1),
    (-1, 0, 1),
    (0, 1, 1),
    (0, -1, -1),
    (0, 1, -1),
    (0, -1, 1),
)
opposite_of = (0, 2, 1, 4, 3, 6, 5, 8, 7, 10, 9, 12, 11, 14, 13, 16, 15, 18, 17)
lattice_weights = (1.0 / 3.0,) + (1.0 / 18.0,) * 6 + (1.0 / 36.0,) * 12
symmetric_slot = ((0, 3, 4), (3, 1, 5), (4, 5, 2))
tensor_pairs = ((0, 0), (1, 1), (2, 2), (0, 1), (0, 2), (1, 2))
relax_time = 0.8
polymer_time = 8.0
polymer_coeff = 0.05


def moving(axis, sign):
    return tuple(index for index in range(19) if velocity_set[index][axis] == sign)


x_up, x_down = (moving(0, 1), moving(0, -1))
y_up, y_down = (moving(1, 1), moving(1, -1))
z_up, z_down = (moving(2, 1), moving(2, -1))
pairs = tuple(range(1, 19, 2))
gas_slot = 5
speed_slot = 6
edge_slot = 9
sides = 9
lanes = 128
tall = 8


def iota(shape, dim):
    return lax.broadcasted_iota(jnp.int32, shape, dim)


def wide(tile, width):
    return jnp.concatenate([tile] * (width // tile.shape[1]), axis=1)


def rows_of(load, chunk, chunks, step, edge):
    low = chunk * tall
    if step == 0:
        return load(low, low + tall)
    if step == 1 and chunk > 0:
        return load(low - 1, low + tall - 1)
    if step == -1 and chunk < chunks - 1:
        return load(low + 1, low + tall + 1)
    rows = load(low, low + tall)
    at = iota(rows.shape, 0)
    if step == 1:
        return jnp.where(at == 0, edge(), pltpu.roll(rows, 1, 0))
    return jnp.where(at == tall - 1, edge(), pltpu.roll(rows, tall - 1, 0))


def columns_of(rows, halo, lane, step):
    width = rows.shape[1]
    at = iota(rows.shape, 1)
    if step == 1:
        edge = wide(pltpu.roll(halo, (lanes - lane) % lanes, 1), width)
        return jnp.where(at == 0, edge, pltpu.roll(rows, 1, 1))
    edge = wide(pltpu.roll(halo, lanes - 1 - lane, 1), width)
    return jnp.where(at == width - 1, edge, pltpu.roll(rows, width - 1, 1))


def packed(high, low):
    at = iota(high[0].shape, 1)
    tile = jnp.zeros_like(high[0])
    for slot, part in enumerate(high):
        tile = jnp.where(at == slot, pltpu.roll(part, slot + 1, 1), tile)
    for place, part in enumerate(low):
        slot = len(high) + place
        tile = jnp.where(at == slot, pltpu.roll(part, slot, 1), tile)
    return tile


def along(index, vector):
    total = None
    for comp in range(3):
        sign = velocity_set[index][comp]
        if sign != 0:
            term = vector[comp] if sign > 0 else -vector[comp]
            total = term if total is None else total + term
    return total


def conversions(source, kind, heading, code, *, columns):
    count = source.shape[1]
    value = (heading[...] + 32 * kind[...]).astype(jnp.float32)
    row, column = (source[...] // columns, source[...] % columns)
    by_row = jnp.where(iota((code.shape[0], count), 0) == row, value, 0.0).astype(jnp.bfloat16)
    by_column = jnp.where(iota((columns, count), 0) == column, 1.0, 0.0).astype(jnp.bfloat16)
    code[...] = lax.dot_general(
        by_row, by_column, (((1,), (1,)), ((), ())), preferred_element_type=jnp.float32
    )


def odd(axis):
    return lax.rem(lax.axis_index(axis), 2) == 1


def select(chosen, first, second):
    return jnp.where(chosen, first[...], second[...])


def swap_rows(first, second, x, planes, high, low, flip):
    for slot, (top, bottom) in enumerate(zip(high, low)):
        by = top.shape[0]
        up, down = (top[by - 1 : by, :], bottom[0:1, :])
        at = slot * planes + x
        first[at : at + 1, :] = jnp.where(flip, down, up)
        second[at : at + 1, :] = jnp.where(flip, up, down)


def swapped_rows(first, second, slots, low_rows, high_rows, shift):
    flip = odd("gy")
    planes = low_rows.shape[0] - 2 * shift
    for x in range(planes):
        for place, slot in enumerate(slots):
            at = slot * planes + x
            one, two = (first[at : at + 1, :], second[at : at + 1, :])
            low_rows[x + shift, place : place + 1, :] = jnp.where(flip, one, two)
            high_rows[x + shift, place : place + 1, :] = jnp.where(flip, two, one)


def column_rows(tiles, count):
    return jnp.concatenate(tiles, axis=0).T[0:count, :]


def row_columns(rows):
    rest = jnp.zeros((lanes - rows.shape[0], rows.shape[1]), jnp.float32)
    return jnp.concatenate([rows, rest], axis=0).T


def first_faces(
    stretch_in,
    flags_in,
    stretch,
    flags,
    columns,
    y_first,
    y_second,
    x_first,
    x_second,
    sems,
):
    bx, by, bz = flags.shape
    flip_x, flip_y = (odd("gx"), odd("gy"))
    copies = [
        pltpu.make_async_copy(stretch_in, stretch, sems.at[0]),
        pltpu.make_async_copy(flags_in, flags, sems.at[1]),
    ]
    for copy in copies:
        copy.start()
    for copy in copies:
        copy.wait()
    tiles = []
    for x in range(bx):
        along_y = [stretch.at[symmetric_slot[comp][1], x] for comp in range(3)]
        swap_rows(y_first, y_second, x, bx, along_y, along_y, flip_y)
        fields = [stretch.at[symmetric_slot[comp][2], x] for comp in range(3)]
        tiles.append(
            packed(
                [field[:, bz - lanes : bz] for field in fields],
                [field[:, 0:lanes] for field in fields],
            )
        )
    columns[...] = column_rows(tiles, columns.shape[0])
    rest = y_first.shape[0] - 3 * bx
    y_first[3 * bx :, :] = jnp.zeros((rest, bz), jnp.float32)
    y_second[3 * bx :, :] = jnp.zeros((rest, bz), jnp.float32)
    for out, last in ((x_first, flip_x), (x_second, jnp.logical_not(flip_x))):
        for comp in range(3):
            slot = symmetric_slot[comp][0]
            out[comp] = jnp.where(last, stretch[slot, 0], stretch[slot, bx - 1])
        out[3] = jnp.where(jnp.where(last, flags[0], flags[bx - 1]) == 0, 1.0, 0.0)


def moments(pops_in, pops, flow, sems):
    bx, by = pops.shape[1:3]
    copies = [
        pltpu.make_async_copy(pops_in.at[:, x], pops.at[:, x], sems.at[x]) for x in range(bx)
    ]
    for copy in copies:
        copy.start()
    for x in range(bx):
        copies[x].wait()
        for chunk in range(by // tall):
            rows = pl.ds(chunk * tall, tall)
            part = [pops[index, x, rows, :] for index in range(19)]
            density = part[0]
            for index in range(1, 19):
                density = density + part[index]
            inverse = 1.0 / density
            for comp in range(3):
                total = None
                for index in pairs:
                    sign = velocity_set[index][comp]
                    if sign != 0:
                        term = part[index] - part[index + 1]
                        term = term if sign > 0 else -term
                        total = term if total is None else total + term
                flow[comp, x, rows, :] = total * inverse
            flow[3, x, rows, :] = density
            flow[4, x, rows, :] = inverse


def beside(ref, field, x, step, halo, slot):
    last = ref.shape[1] - 1
    if halo is None:
        return lambda low, high: ref[field, x + step, low:high, :]
    if isinstance(x, int):
        if 0 <= x + step <= last:
            return lambda low, high: ref[field, x + step, low:high, :]
        return lambda low, high: halo[slot, low:high, :]
    inside = jnp.clip(x + step, 0, last)
    beyond = x == (0 if step < 0 else last)
    return lambda low, high: jnp.where(
        beyond, halo[slot, low:high, :], ref[field, inside, low:high, :]
    )


def differences(
    ref, field, slots, x, chunk, chunks, below, above, y_below, y_above, z_halo, lane, side
):
    slot_x, slot_y, slot_z = slots
    low, high = (chunk * tall, chunk * tall + tall)

    def load(first, stop):
        return ref[field, x, first:stop, :]

    result = [None, None, None]
    if slot_x is not None:
        after = beside(ref, field, x, 1, above, slot_x)(low, high)
        before = beside(ref, field, x, -1, below, slot_x)(low, high)
        result[0] = after - before
    if slot_y is not None:
        after = rows_of(load, chunk, chunks, -1, lambda: y_above[x, slot_y : slot_y + 1, :])
        before = rows_of(load, chunk, chunks, 1, lambda: y_below[x, slot_y : slot_y + 1, :])
        result[1] = after - before
    if slot_z is not None:
        rows, halo = (load(low, high), z_halo[x, low:high, :])
        after = columns_of(rows, halo, lane + side + slot_z, -1)
        before = columns_of(rows, halo, lane + slot_z, 1)
        result[2] = after - before
    return result


def end_place(x, bx):
    return 0 if x == 0 else 1


def plane_of(inner, outer, field, x, bx):
    if 0 < x < bx - 1:
        return inner.at[field, x - 1]
    return outer.at[field, end_place(x, bx)]


def collide_plane(x, place, pops, stretch, flow, halos, post, shift):
    by = pops.shape[2]
    chunks = by // tall
    factor = 1.0 - 0.5 / relax_time
    rate = 1.0 / relax_time
    for chunk in range(chunks):
        rows = pl.ds(chunk * tall, tall)
        terms = [[], [], []]
        for field in range(6):
            slots = [None, None, None]
            for comp in range(3):
                for axis in range(3):
                    if symmetric_slot[comp][axis] == field:
                        slots[axis] = comp
            found = differences(stretch, field, slots, x, chunk, chunks, *halos)
            for axis in range(3):
                if slots[axis] is not None:
                    terms[slots[axis]].append(found[axis])
        force = [0.5 * polymer_coeff * (part[0] + part[1] + part[2]) for part in terms]
        density, half = (flow[3, x, rows, :], 0.5 * flow[4, x, rows, :])
        moved = [flow[comp, x, rows, :] + half * force[comp] for comp in range(3)]
        for comp in range(3):
            shift[comp, place, rows, :] = moved[comp]
        squared = moved[0] * moved[0] + moved[1] * moved[1] + moved[2] * moved[2]
        work = moved[0] * force[0] + moved[1] * force[1] + moved[2] * force[2]
        weight = rate * density
        common = weight - 1.5 * weight * squared - 3.0 * factor * work
        odd = [3.0 * weight * moved[comp] + 3.0 * factor * force[comp] for comp in range(3)]
        even = [4.5 * weight * moved[comp] + 9.0 * factor * force[comp] for comp in range(3)]
        keep = 1.0 - rate
        post[0, place, rows, :] = keep * pops[0, x, rows, :] + lattice_weights[0] * common
        for index in pairs:
            both = common + along(index, moved) * along(index, even)
            differ = along(index, odd)
            scale = lattice_weights[index]
            post[index, place, rows, :] = keep * pops[index, x, rows, :] + scale * (both + differ)
            post[index + 1, place, rows, :] = keep * pops[index + 1, x, rows, :] + scale * (
                both - differ
            )


def collide_inner(
    pops,
    stretch,
    flow,
    y_first,
    y_second,
    z_rows,
    post,
    shift,
    y_below,
    y_above,
    z_halo,
):
    swapped_rows(y_first, y_second, range(3), y_below, y_above, 0)
    z_halo[...] = row_columns(z_rows[...]).reshape(z_halo.shape)
    halos = (None, None, y_below, y_above, z_halo, 0, 3)

    def plane(x, carry):
        collide_plane(x, x - 1, pops, stretch, flow, halos, post, shift)
        return carry

    lax.fori_loop(1, pops.shape[1] - 1, plane, 0)


def collide_outer(
    pops,
    stretch,
    flags,
    flow,
    x_first,
    x_second,
    y_first,
    y_second,
    z_rows,
    inner,
    post,
    shift,
    columns,
    ahead,
    behind,
    up_first,
    up_second,
    below,
    above,
    y_below,
    y_above,
    z_halo,
    gas,
):
    bx, by, bz = flags.shape
    halos = (below, above, y_below, y_above, z_halo, 0, 3)
    flip_x, flip_y = (odd("gx"), odd("gy"))
    below[...] = select(flip_x, x_first, x_second)
    above[...] = select(flip_x, x_second, x_first)
    swapped_rows(y_first, y_second, range(3), y_below, y_above, 0)
    z_halo[...] = row_columns(z_rows[...]).reshape(z_halo.shape)
    for x in (0, bx - 1):
        collide_plane(x, end_place(x, bx), pops, stretch, flow, halos, post, shift)

    tiles = []
    for x in range(bx):
        gas[x] = jnp.where(flags[x] == 0, 1.0, 0.0)
        rest = [gas.at[x]] + [flow.at[comp, x] for comp in range(3)]

        def fields(indices):
            return [plane_of(inner, post, index, x, bx) for index in indices] + rest

        swap_rows(up_first, up_second, x, bx, fields(y_up), fields(y_down), flip_y)
        tiles.append(
            packed(
                [field[:, bz - lanes : bz] for field in fields(z_up)],
                [field[:, 0:lanes] for field in fields(z_down)],
            )
        )
    columns[...] = column_rows(tiles, columns.shape[0])
    rest = up_first.shape[0] - sides * bx
    up_first[sides * bx :, :] = jnp.zeros((rest, bz), jnp.float32)
    up_second[sides * bx :, :] = jnp.zeros((rest, bz), jnp.float32)
    for slot in range(5):
        up, down = (post[x_up[slot], 1], post[x_down[slot], 0])
        ahead[slot] = jnp.where(flip_x, down, up)
        behind[slot] = jnp.where(flip_x, up, down)
    for comp in range(3):
        up, down = (flow[comp, bx - 1], flow[comp, 0])
        ahead[5 + comp] = jnp.where(flip_x, down, up)
        behind[5 + comp] = jnp.where(flip_x, up, down)


def restretch(
    stretch,
    flow,
    x_first,
    x_second,
    y_first,
    y_second,
    z_rows,
    inner,
    outer,
    inner_slanted,
    outer_slanted,
    late,
    updated,
    fresh,
    below,
    above,
    y_below,
    y_above,
    z_halo,
    sems,
):
    bx, by, bz = stretch.shape[1:]
    moves = [
        (inner, fresh.at[0:first_slanted, 1 : bx - 1]),
        (inner_slanted, fresh.at[first_slanted:, 1 : bx - 1]),
    ]
    for place, x in enumerate((0, bx - 1)):
        moves.append((outer_slanted.at[:, place], fresh.at[first_slanted:, x]))
        order = (x_up, x_down)[place]
        start = 0
        for index in order + (first_slanted,):
            if index > start:
                run = slice(start, index)
                moves.append((outer.at[run, place], fresh.at[run, x]))
            if index in order:
                moves.append((late.at[order.index(index), place], fresh.at[index, x]))
            start = index + 1
    copies = [
        pltpu.make_async_copy(source, target, sems.at[place])
        for place, (source, target) in enumerate(moves)
    ]
    for copy in copies:
        copy.start()
    chunks = by // tall
    flip_x = odd("gx")
    below[...] = select(flip_x, x_first, x_second)
    above[...] = select(flip_x, x_second, x_first)
    swapped_rows(y_first, y_second, range(speed_slot, sides), y_below, y_above, 0)
    z_halo[...] = row_columns(z_rows[...]).reshape(z_halo.shape)

    def plane(x, carry):
        for chunk in range(chunks):
            rows = pl.ds(chunk * tall, tall)
            grad = [
                differences(
                    flow,
                    comp,
                    (5 + comp, comp, comp),
                    x,
                    chunk,
                    chunks,
                    below,
                    above,
                    y_below,
                    y_above,
                    z_halo,
                    speed_slot,
                    sides,
                )
                for comp in range(3)
            ]
            part = [stretch[slot, x, rows, :] for slot in range(6)]
            full = [part[slot] + 1.0 if slot < 3 else part[slot] for slot in range(6)]

            def product(row, col):
                total = grad[row][0] * full[symmetric_slot[0][col]]
                for inner in (1, 2):
                    total = total + grad[row][inner] * full[symmetric_slot[inner][col]]
                return total

            for slot, (row, col) in enumerate(tensor_pairs):
                old = (1.0 - 1.0 / polymer_time) * part[slot]
                if row == col:
                    updated[slot, x, rows, :] = old + product(row, col)
                else:
                    updated[slot, x, rows, :] = old + 0.5 * (product(row, col) + product(col, row))
        return carry

    lax.fori_loop(0, bx, plane, 0)
    for copy in copies:
        copy.wait()


up_edges = ((0, y_up.index(7)), (0, gas_slot), (1, y_down.index(9)), (1, gas_slot))
down_edges = ((0, y_up.index(10)), (0, gas_slot), (1, y_down.index(8)), (1, gas_slot))


def forward_edges(y_first, y_second, z_rows, first_out, second_out, corner, *, bx):
    halves = y_first.shape[1] // lanes
    flip_x, flip_y = (odd("gx"), odd("gy"))
    for half in range(halves):
        cut = slice(half * lanes, half * lanes + lanes)
        for place in range(4):
            found = []
            for x, edges in ((bx - 1, up_edges), (0, down_edges)):
                side, slot = edges[place]
                row = slot * bx + x
                one = y_first[row : row + 1, cut]
                two = y_second[row : row + 1, cut]
                found.append(jnp.where(flip_y, one, two) if side == 0 else jnp.where(flip_y, two, one))
            at = half * 4 + place
            first_out[at : at + 1, :] = jnp.where(flip_x, found[1], found[0])
            second_out[at : at + 1, :] = jnp.where(flip_x, found[0], found[1])
    first_out[4 * halves :, :] = z_rows[...]
    second_out[4 * halves :, :] = z_rows[...]
    corner[...] = z_rows[...]


def own_halos(flags, y_first, y_second, z_rows, gas, low_rows, high_rows, columns):
    bx, by = flags.shape[:2]
    tile = row_columns(z_rows[...])
    swapped_rows(y_first, y_second, range(speed_slot), low_rows, high_rows, 1)
    for x in range(bx):
        gas[x + 1] = jnp.where(flags[x] == 0, 1.0, 0.0)
        columns[x + 1] = tile[x * by : x * by + by, :]


def own_corners(corner_first, corner_second, low_rows, high_rows):
    bx = low_rows.shape[0] - 2
    flip = odd("gy")
    corner_below = row_columns(select(flip, corner_first, corner_second))
    corner_above = row_columns(select(flip, corner_second, corner_first))
    by = corner_below.shape[0] // bx
    for x in range(bx):
        end = x * by + by - 1
        low_rows[x + 1, edge_slot : edge_slot + 1, 0:lanes] = corner_below[end : end + 1, :]
        high_rows[x + 1, edge_slot : edge_slot + 1, 0:lanes] = corner_above[
            x * by : x * by + 1, :
        ]


def pass_on(x, chunk, indices, source, leaving_of, speed, halos, fresh, place, total, change):
    gas, low_rows, high_rows, columns = halos
    by = gas.shape[1]
    chunks = by // tall
    rows = pl.ds(chunk * tall, tall)
    rest = 1.0 - 1.5 * (speed[0] * speed[0] + speed[1] * speed[1] + speed[2] * speed[2])
    equals = {}

    def moved(load, index, slot, lane):
        step_x, step_y, step_z = velocity_set[index]
        plane = x + 1 - step_x
        edges = low_rows if step_y == 1 else high_rows
        found = rows_of(load, chunk, chunks, step_y, lambda: edges[plane, slot : slot + 1, :])
        if step_z == 0:
            return found
        halo = rows_of(
            lambda low, high: columns[plane, low:high, :],
            chunk,
            chunks,
            step_y,
            lambda: edges[plane, edge_slot : edge_slot + 1, 0:lanes],
        )
        return columns_of(found, halo, lane, step_z)

    for index in indices:
        step_x, step_y, step_z = velocity_set[index]
        first = min(index, opposite_of[index])
        if first not in equals:
            proj = along(first, speed)
            equals[first] = 2.0 * lattice_weights[first] * (rest + 4.5 * proj * proj)
        slot, lane, gas_lane = (None, None, None)
        if step_y != 0:
            slot = (y_up if step_y == 1 else y_down).index(index)
        if step_z == 1:
            lane, gas_lane = (z_up.index(index), gas_slot)
        elif step_z == -1:
            lane, gas_lane = (sides + z_down.index(index), sides + gas_slot)
        field = source(index)
        marks = gas.at[x + 1 - step_x]
        arriving = moved(lambda low, high: field[low:high, :], index, slot, lane)
        from_gas = moved(lambda low, high: marks[low:high, :], index, gas_slot, gas_lane)
        leaving = leaving_of(opposite_of[index])[rows, :]
        open_side = from_gas > 0.5
        value = jnp.where(open_side, equals[first] - leaving, arriving)
        fresh(index)[place, rows, :] = value
        total = total + value
        change = change + jnp.where(open_side, 0.0, arriving - leaving)
    return total, change


def settle(x, rows, mass, flags, code, total, change):
    read = mass[x, rows, :] + jnp.where(flags[x, rows, :] == 1, change, 0.0)
    mark = code[x, rows, :]
    liquid = mark >= 32.0
    converts = mark > 0.0
    level = jnp.where(liquid, total, 0.0)
    excess = jnp.where(converts, read - level, 0.0)
    heading = jnp.where(liquid, mark - 32.0, mark)
    return jnp.where(converts, level, read), excess, heading


slanted = tuple(index for index in range(19) if velocity_set[index][1] * velocity_set[index][2])
first_slanted = slanted[0]


def from_inside(x, bx):
    found = [index for index in range(1, 19) if 0 <= x - velocity_set[index][0] < bx]
    return [index for index in found if index not in slanted]


def from_beyond(x, bx):
    return [index for index in range(1, 19) if not 0 <= x - velocity_set[index][0] < bx]


def stream_early(
    inner_post,
    outer_post,
    inner_shift,
    outer_shift,
    flags,
    y_first,
    y_second,
    z_rows,
    inner,
    outer,
    totals,
    changes,
    gas,
    low_rows,
    high_rows,
    columns,
):
    bx, by, bz = flags.shape
    halos = (gas, low_rows, high_rows, columns)
    own_halos(flags, y_first, y_second, z_rows, *halos)

    for x in range(bx):
        inside = 0 < x < bx - 1
        place = x - 1 if inside else end_place(x, bx)
        fresh = inner if inside else outer
        for chunk in range(by // tall):
            rows = pl.ds(chunk * tall, tall)
            total = plane_of(inner_post, outer_post, 0, x, bx)[rows, :]
            fresh[0, place, rows, :] = total
            total, change = pass_on(
                x,
                chunk,
                from_inside(x, bx),
                lambda index: plane_of(
                    inner_post, outer_post, index, x - velocity_set[index][0], bx
                ),
                lambda index: plane_of(inner_post, outer_post, index, x, bx),
                [plane_of(inner_shift, outer_shift, comp, x, bx)[rows, :] for comp in range(3)],
                halos,
                lambda index: fresh.at[index],
                place,
                total,
                jnp.zeros((tall, bz), jnp.float32),
            )
            totals[x, rows, :] = total
            changes[x, rows, :] = change


def stream_slanted(
    inner_post,
    outer_post,
    inner_shift,
    outer_shift,
    mass,
    flags,
    code,
    y_first,
    y_second,
    z_rows,
    corner_first,
    corner_second,
    totals,
    changes,
    inner,
    outer,
    settled,
    excess,
    heading,
    end_totals,
    end_changes,
    gas,
    low_rows,
    high_rows,
    columns,
):
    bx, by, bz = flags.shape
    halos = (gas, low_rows, high_rows, columns)
    own_halos(flags, y_first, y_second, z_rows, *halos)
    own_corners(corner_first, corner_second, low_rows, high_rows)

    for x in range(bx):
        inside = 0 < x < bx - 1
        place = x - 1 if inside else end_place(x, bx)
        fresh = inner if inside else outer
        for chunk in range(by // tall):
            rows = pl.ds(chunk * tall, tall)
            total, change = pass_on(
                x,
                chunk,
                slanted,
                lambda index: plane_of(inner_post, outer_post, index, x, bx),
                lambda index: plane_of(inner_post, outer_post, index, x, bx),
                [plane_of(inner_shift, outer_shift, comp, x, bx)[rows, :] for comp in range(3)],
                halos,
                lambda index: fresh.at[index - first_slanted],
                place,
                totals[x, rows, :],
                changes[x, rows, :],
            )
            if inside:
                now = settle(x, rows, mass, flags, code, total, change)
                settled[place, rows, :], excess[place, rows, :], heading[place, rows, :] = now
            else:
                end_totals[place, rows, :] = total
                end_changes[place, rows, :] = change


def stream_late(
    post,
    shift,
    mass,
    flags,
    code,
    totals,
    changes,
    gas_first,
    gas_second,
    x_first,
    x_second,
    edges_first,
    edges_second,
    inner_excess,
    inner_heading,
    late,
    settled,
    spread,
    line_first,
    line_second,
    out_z,
    gas,
    low_rows,
    high_rows,
    columns,
    below,
    above,
    excess,
    heading,
):
    bx, by, bz = flags.shape
    halves = bz // lanes
    flip_x = odd("gx")
    halos = (gas, low_rows, high_rows, columns)

    for slot in range(5):
        below[slot] = jnp.where(flip_x, x_first[slot], x_second[slot])
        above[slot] = jnp.where(flip_x, x_second[slot], x_first[slot])
    gas[0] = jnp.where(flip_x, gas_first[3], gas_second[3])
    gas[bx + 1] = jnp.where(flip_x, gas_second[3], gas_first[3])
    edges_below = select(flip_x, edges_first, edges_second)
    edges_above = select(flip_x, edges_second, edges_first)
    for found, at, x, edges in (
        (edges_below, 0, bx - 1, up_edges),
        (edges_above, bx + 1, 0, down_edges),
    ):
        for place, (side, slot) in enumerate(edges):
            line = jnp.concatenate(
                [found[half * 4 + place : half * 4 + place + 1, :] for half in range(halves)],
                axis=1,
            )
            (low_rows, high_rows)[side][at, slot : slot + 1, :] = line
        columns[at] = row_columns(found[4 * halves :, :])[x * by : x * by + by, :]
    for place, x in enumerate((0, bx - 1)):
        halo, order = ((below, x_up), (above, x_down))[place]
        for chunk in range(by // tall):
            rows = pl.ds(chunk * tall, tall)
            total, change = pass_on(
                x,
                chunk,
                from_beyond(x, bx),
                lambda index: halo.at[order.index(index)],
                lambda index: post.at[index, place],
                [shift[comp, place, rows, :] for comp in range(3)],
                halos,
                lambda index: late.at[order.index(index)],
                place,
                totals[place, rows, :],
                changes[place, rows, :],
            )
            now = settle(x, rows, mass, flags, code, total, change)
            settled[place, rows, :], excess[x, rows, :], heading[x, rows, :] = now
    for x in range(1, bx - 1):
        excess[x] = inner_excess[x - 1]
        heading[x] = inner_heading[x - 1]

    row_at, lane_at = (iota((by, bz), 0), iota((by, bz), 1))
    line_at = iota((1, bz), 1)
    tile_lane, line_lane = (iota((by, lanes), 1), iota((1, lanes), 1))

    def rows_up(rows):
        return jnp.where(row_at == 0, 0.0, pltpu.roll(rows, 1, 0))

    def rows_down(rows):
        return jnp.where(row_at == by - 1, 0.0, pltpu.roll(rows, by - 1, 0))

    def over(rows, at, step):
        if step == 1:
            return jnp.where(at == 0, 0.0, pltpu.roll(rows, 1, 1))
        return jnp.where(at == bz - 1, 0.0, pltpu.roll(rows, bz - 1, 1))

    def summed(parts):
        total = parts[0]
        for part in parts[1:]:
            total = total + part
        return total

    tile = jnp.zeros((by, lanes), jnp.float32)
    line_up = jnp.zeros((1, lanes), jnp.float32)
    line_down = jnp.zeros((1, lanes), jnp.float32)
    flip_y = odd("gy")
    line_first[...] = jnp.zeros(line_first.shape, jnp.float32)
    line_second[...] = jnp.zeros(line_second.shape, jnp.float32)
    for target in range(bx + 2):
        groups = {}
        for index in range(1, 19):
            step_x, step_y, step_z = velocity_set[index]
            x = target - 1 - step_x
            if 0 <= x < bx:
                part = jnp.where(heading[x] == float(index), excess[x], 0.0)
                groups.setdefault((step_y, step_z), []).append(part)
        groups = {key: summed(parts) for key, parts in groups.items()}
        total = jnp.zeros((by, bz), jnp.float32)
        line = {1: jnp.zeros((1, bz), jnp.float32), -1: jnp.zeros((1, bz), jnp.float32)}
        for step_z in (0, 1, -1):
            group = jnp.zeros((by, bz), jnp.float32)
            ends = {}
            if (0, step_z) in groups:
                group = group + groups[(0, step_z)]
            if (1, step_z) in groups:
                group = group + rows_up(groups[(1, step_z)])
                ends[1] = groups[(1, step_z)][by - 1 : by, :]
            if (-1, step_z) in groups:
                group = group + rows_down(groups[(-1, step_z)])
                ends[-1] = groups[(-1, step_z)][0:1, :]
            if step_z == 0:
                total = total + group
                for side in ends:
                    line[side] = line[side] + ends[side]
                continue
            total = total + over(group, lane_at, step_z)
            for side in ends:
                line[side] = line[side] + over(ends[side], line_at, step_z)
            if step_z == 1:
                spot, cut, roll = (target, slice(bz - lanes, bz), target + 1)
            else:
                spot, cut, roll = (8 + target, slice(0, lanes), 8 + target)
            tile = jnp.where(tile_lane == spot, pltpu.roll(group[:, cut], roll, 1), tile)
            if 1 in ends:
                line_up = jnp.where(
                    line_lane == spot, pltpu.roll(ends[1][:, cut], roll, 1), line_up
                )
            if -1 in ends:
                line_down = jnp.where(
                    line_lane == spot, pltpu.roll(ends[-1][:, cut], roll, 1), line_down
                )
        spread[target] = total
        line_first[target : target + 1, :] = jnp.where(flip_y, line[-1], line[1])
        line_second[target : target + 1, :] = jnp.where(flip_y, line[1], line[-1])
    rest = jnp.zeros((lanes - by - 2, lanes), jnp.float32)
    out_z[...] = column_rows([tile, line_up, line_down, rest], 16)


def with_edges(total, target, tile, y_below, y_above):
    by, bz = total.shape
    row_at, lane_at = (iota((by, bz), 0), iota((by, bz), 1))
    total = total + jnp.where(lane_at == 0, tile[0:by, target : target + 1], 0.0)
    total = total + jnp.where(lane_at == bz - 1, tile[0:by, 8 + target : 9 + target], 0.0)
    total = total + jnp.where(row_at == 0, y_below[target : target + 1, :], 0.0)
    return total + jnp.where(row_at == by - 1, y_above[target : target + 1, :], 0.0)


def add_faces(spread, z_rows, y_first, y_second, first, second):
    last = spread.shape[0] - 1
    flip_x, flip_y = (odd("gx"), odd("gy"))
    tile = row_columns(z_rows[...])
    y_below, y_above = (select(flip_y, y_first, y_second), select(flip_y, y_second, y_first))
    up = with_edges(spread[last], last, tile, y_below, y_above)
    down = with_edges(spread[0], 0, tile, y_below, y_above)
    first[...] = jnp.where(flip_x, down, up)
    second[...] = jnp.where(flip_x, up, down)


def add_all(
    inner_settled,
    outer_settled,
    spread,
    z_rows,
    y_first,
    y_second,
    corner_first,
    corner_second,
    x_first,
    x_second,
    new_mass,
):
    bx, by, bz = new_mass.shape
    flip_x, flip_y = (odd("gx"), odd("gy"))
    tile = row_columns(z_rows[...])
    y_below, y_above = (select(flip_y, y_first, y_second), select(flip_y, y_second, y_first))
    at = iota((8, bz), 1)
    found = []
    for rows, side, corner in (
        (y_below, 0, select(flip_y, corner_first, corner_second)),
        (y_above, 1, select(flip_y, corner_second, corner_first)),
    ):
        edge = corner[:, by + side : by + side + 1]
        rows = rows + jnp.where(at == 0, edge[0:8, :], 0.0)
        found.append(rows + jnp.where(at == bz - 1, edge[8:16, :], 0.0))
    for x in range(bx):
        total = with_edges(spread[x + 1], x + 1, tile, *found)
        if x == 0:
            total = total + select(flip_x, x_first, x_second)
        if x == bx - 1:
            total = total + select(flip_x, x_second, x_first)
        if 0 < x < bx - 1:
            total = total + inner_settled[x - 1]
        else:
            total = total + outer_settled[0 if x == 0 else 1]
        new_mass[x] = total


def swapped(first, second, axis):
    devices = lax.axis_size(axis)
    ahead = [(i, (i + 1) % devices if i % 2 == 0 else i - 1) for i in range(devices)]
    behind = [(i, (i - 1) % devices if i % 2 == 0 else (i + 1) % devices) for i in range(devices)]
    return lax.ppermute(first, axis, ahead), lax.ppermute(second, axis, behind)


def both_ways(rows, lower):
    devices = lax.axis_size("gz")
    before = lax.ppermute(rows, "gz", [(i, (i + 1) % devices) for i in range(devices)])
    if devices == 2:
        return before
    after = lax.ppermute(rows, "gz", [(i, (i - 1) % devices) for i in range(devices)])
    return jnp.where(iota(rows.shape, 0) < lower, before, after)


remote = pl.BlockSpec(memory_space=pltpu.HBM)


def call(body, outs, specs=None, out_specs=None, scratch=(), cost=(0, 0)):
    extra = {} if specs is None else {"in_specs": specs}
    if out_specs is not None:
        extra["out_specs"] = out_specs
    return pl.pallas_call(
        body,
        out_shape=[
            shape
            if isinstance(shape, jax.ShapeDtypeStruct)
            else jax.ShapeDtypeStruct(shape, jnp.float32)
            for shape in outs
        ],
        scratch_shapes=[
            pltpu.VMEM(shape, jnp.float32) if isinstance(shape, tuple) else shape
            for shape in scratch
        ],
        compiler_params=pltpu.CompilerParams(vmem_limit_bytes=40 * 1024 * 1024),
        cost_estimate=pl.CostEstimate(flops=cost[0], bytes_accessed=cost[1], transcendentals=0),
        **extra,
    )


def shards(populations, stretch, mass, flags, conv_source, conv_kind, conv_direction):
    bx, by, bz = flags.shape
    cells = bx * by * bz
    box, face, tile = ((bx, by, bz), (by, bz), (bx, by, lanes))

    stretch, flags, z_out, y_one, y_two, x_one, x_two = call(
        first_faces,
        [
            (6, *box),
            jax.ShapeDtypeStruct(box, jnp.int32),
            (8, bx * by),
            (4 * bx, bz),
            (4 * bx, bz),
            (4, *face),
            (4, *face),
        ],
        specs=[remote] * 2,
        scratch=[pltpu.SemaphoreType.DMA((2,))],
        cost=(10 * cells, 60 * cells),
    )(*(pltpu.with_memory_space_constraint(array, pltpu.HBM) for array in (stretch, flags)))
    first_x = swapped(x_one, x_two, "gx")
    z_first = both_ways(z_out, 3)
    y_first = swapped(y_one, y_two, "gy")

    entries = conv_source.shape[0]
    (code,) = call(
        lambda *refs: conversions(*refs, columns=bz), [(bx * by, bz)], cost=(40 * cells, 4 * cells)
    )(*(array.reshape(1, entries) for array in (conv_source, conv_kind, conv_direction)))
    code = code.reshape(box)

    pops, flow = call(
        moments,
        [(19, *box), (5, *box)],
        specs=[remote],
        scratch=[pltpu.SemaphoreType.DMA((bx,))],
        cost=(60 * cells, 150 * cells),
    )(pltpu.with_memory_space_constraint(populations, pltpu.HBM))

    columns, rows = ((24, bx * by), (10 * bx, bz))
    sides_y = [(bx, 8, bz), (bx, 8, bz), tile]
    inside, ends = ((bx - 2, *face), (2, *face))
    inner_post, inner_shift = call(
        collide_inner,
        [(19, *inside), (3, *inside)],
        scratch=sides_y,
        cost=(150 * cells, 150 * cells),
    )(pops, stretch, flow, *y_first, z_first)
    outer_post, outer_shift, z_out, x_one, x_two, y_one, y_two = call(
        collide_outer,
        [(19, *ends), (3, *ends), columns, (8, *face), (8, *face), rows, rows],
        scratch=[(4, *face), (4, *face)] + sides_y + [box],
        cost=(150 * cells, 150 * cells),
    )(pops, stretch, flags, flow, *first_x, *y_first, z_first, inner_post)
    z_post = both_ways(z_out, sides)
    post_y = swapped(y_one, y_two, "gy")
    post_x = swapped(x_one, x_two, "gx")
    edges = (4 * (bz // lanes) + columns[0], lanes)
    x_one, x_two, corner = call(
        lambda *refs: forward_edges(*refs, bx=bx), [edges, edges, columns]
    )(*post_y, z_post)
    corners = swapped(corner, corner, "gy")
    edges_x = swapped(x_one, x_two, "gx")

    rims = [(bx + 2, *face), (bx + 2, 16, bz), (bx + 2, 16, bz), (bx + 2, by, lanes)]
    posts = (inner_post, outer_post, inner_shift, outer_shift)
    inner, outer, totals, changes = call(
        stream_early,
        [(first_slanted, *inside), (first_slanted, *ends), box, box],
        scratch=rims,
        cost=(350 * cells, 200 * cells),
    )(*posts, flags, *post_y, z_post)
    (
        inner_slanted,
        outer_slanted,
        inner_settled,
        inner_excess,
        inner_heading,
        totals,
        changes,
    ) = call(
        stream_slanted,
        [(4, *inside), (4, *ends), inside, inside, inside, ends, ends],
        scratch=rims,
        cost=(100 * cells, 60 * cells),
    )(*posts, mass, flags, code, *post_y, z_post, *corners, totals, changes)
    late, outer_settled, spread, y_one, y_two, z_out = call(
        stream_late,
        [(5, *ends), ends, (bx + 2, *face), (8, bz), (8, bz), (16, bx * by)],
        scratch=rims + [(5, *face), (5, *face), box, box],
        cost=(150 * cells, 100 * cells),
    )(
        outer_post,
        outer_shift,
        mass,
        flags,
        code,
        totals,
        changes,
        *first_x,
        *post_x,
        *edges_x,
        inner_excess,
        inner_heading,
    )
    z_last = both_ways(z_out, 8)
    last_y = swapped(y_one, y_two, "gy")
    last_corners = swapped(z_last, z_last, "gy")
    x_one, x_two = call(add_faces, [face, face])(spread, z_last, *last_y)
    last_x = swapped(x_one, x_two, "gx")
    new_stretch, fresh = call(
        restretch,
        [(6, *box), (19, *box)],
        out_specs=[pl.BlockSpec(), remote],
        scratch=[
            (8, *face),
            (8, *face),
            (bx, 8, bz),
            (bx, 8, bz),
            tile,
            pltpu.SemaphoreType.DMA((32,)),
        ],
        cost=(150 * cells, 80 * cells),
    )(
        stretch,
        flow,
        *post_x,
        *post_y,
        z_post,
        inner,
        outer,
        inner_slanted,
        outer_slanted,
        late,
    )
    (new_mass,) = call(add_all, [box])(
        inner_settled, outer_settled, spread, z_last, *last_y, *last_corners, *last_x
    )
    return (fresh, new_stretch, new_mass)


def solution(mesh):
    return jax.shard_map(
        shards,
        mesh=mesh,
        in_specs=(
            P(None, "gx", "gy", "gz"),
            P(None, "gx", "gy", "gz"),
            P("gx", "gy", "gz"),
            P("gx", "gy", "gz"),
            P(("gx", "gy", "gz")),
            P(("gx", "gy", "gz")),
            P(("gx", "gy", "gz")),
        ),
        out_specs=(P(None, "gx", "gy", "gz"), P(None, "gx", "gy", "gz"), P("gx", "gy", "gz")),
        check_vma=False,
    )
```

profile of v0, /device:TPU:0, one launch (start us, length us, event | category | flops | bytes accessed | tf_op | source)
XLA Modules:
  0.0 42.4 jit_solution(9285947013810138048)
XLA Ops:
  0.6 1.4 %shard_map.94 = (f32[6,4,32,256]{3,2,1,0:T(8,128)S(1)}, s32[4,32,256]{2,1,0:T(8,128)S(1)}, f32[8,128]{1,0:T(8,128)S(1)}, f32[16,256]{1,0:T(8,128)S(1)}, f32[16,2...) custom-call(f32[6,4,32,256]{3,2,1,0:T(8,128)} %stretch_in.1, s32[4,32,256]{2,1,0:T(8,128)} %flags_in.1), custom_call_target="tpu_custom_call" | custom-call | flops 327680 | bytes 1966080 | tf_op jit(solution)/shard_map/pallas_call | solution.py:992
  2.0 3.1 %collective-permute-start = (f32[4,32,256]{2,1,0:T(8,128)S(1)}, f32[4,32,256]{2,1,0:T(8,128)S(1)}, u32[]{:S(2)}, u32[]{:S(2)}) collective-permute-start(f32[4,32,256]{2,1,0:T(8,128)S(1)} %get-tuple-element.49), channel_id=1, source_target_pairs={{0,8},{8,0},{16,24},{24,16},{1,9},{9,1},{17,25},{25,17},{2,10},{10... | collective-permute-start | bytes 393224 | tf_op jit(solution)/shard_map/ppermute | solution.py:950
  5.1 2.5 %collective-permute-start.1 = (f32[4,32,256]{2,1,0:T(8,128)S(1)}, f32[4,32,256]{2,1,0:T(8,128)S(1)}, u32[]{:S(2)}, u32[]{:S(2)}) collective-permute-start(f32[4,32,256]{2,1,0:T(8,128)S(1)} %get-tuple-element.50), channel_id=1, source_target_pairs={{0,24},{8,16},{16,8},{24,0},{1,25},{9,17},{17,9},{25,1},{2,26},{10... | collective-permute-start | bytes 393224 | tf_op jit(solution)/shard_map/ppermute | solution.py:950
  7.6 0.0 collective-permute-start.2
  7.6 1.6 %collective-permute-start.3 = (f32[16,256]{1,0:T(8,128)S(1)}, f32[16,256]{1,0:T(8,128)S(1)}, u32[]{:S(2)}, u32[]{:S(2)}) collective-permute-start(f32[16,256]{1,0:T(8,128)S(1)} %get-tuple-element.52), channel_id=1, source_target_pairs={{0,6},{2,4},{4,2},{6,0},{1,7},{3,5},{5,3},{7,1},{8,14},{10,12},{12... | collective-permute-start | bytes 49160 | tf_op jit(solution)/shard_map/ppermute | solution.py:950
  9.2 1.5 %collective-permute-start.4 = (f32[8,128]{1,0:T(8,128)S(1)}, f32[8,128]{1,0:T(8,128)S(1)}, u32[]{:S(2)}, u32[]{:S(2)}) collective-permute-start(f32[8,128]{1,0:T(8,128)S(1)} %get-tuple-element.53), channel_id=1, source_target_pairs={{0,1},{1,0},{2,3},{3,2},{4,5},{5,4},{6,7},{7,6},{8,9},{9,8},{10,11... | collective-permute-start | bytes 12296 | tf_op jit(solution)/shard_map/ppermute | solution.py:955
  10.7 1.7 %shard_map.95 = (f32[19,4,32,256]{3,2,1,0:T(8,128)S(1)}, f32[5,4,32,256]{3,2,1,0:T(8,128)S(1)}) custom-call(f32[19,4,32,256]{3,2,1,0:T(8,128)} %pops_in.1), custom_call_target="tpu_custom_call" | custom-call | flops 1966080 | bytes 4915200 | tf_op jit(solution)/shard_map/pallas_call | solution.py:1017
  12.5 0.3 collective-permute-done.4.z_rows
  12.8 0.0 collective-permute-done.2.y_first
  12.8 0.0 collective-permute-done.3.y_second
  12.8 0.8 %shard_map.96 = (f32[19,2,32,256]{3,2,1,0:T(8,128)S(1)}, f32[3,2,32,256]{3,2,1,0:T(8,128)S(1)}) custom-call(f32[19,4,32,256]{3,2,1,0:T(8,128)S(1)} %get-tuple-element.47.pops, f32[6,4,32,256]{3,2,1,0:T(8,128)S(1)} %get-tuple-element.45.stretch, f32[5,4,32,256]{3,2,1,0:T(8,128)S(1)} %get-tuple-element.46.flow, f32[16,256]{1,0:T(8,128)S(1)} %collective-permute-done.2.y_first, ...), custom_call_target="tpu_custom_call" | custom-call | flops 4915200 | bytes 4915200 | tf_op jit(solution)/shard_map/pallas_call | solution.py:1028
  13.6 0.0 collective-permute-done.x_first.gas_first
  13.6 0.1 collective-permute-done.1.x_second.gas_second
  13.7 0.0 copy-start.1
  13.7 0.0 copy-start.2
  13.7 0.0 copy-start.3
  13.7 1.0 %shard_map.97 = (f32[19,2,32,256]{3,2,1,0:T(8,128)S(1)}, f32[3,2,32,256]{3,2,1,0:T(8,128)S(1)}, f32[24,128]{1,0:T(8,128)S(1)}, f32[8,32,256]{2,1,0:T(8,128)S(1)}...) custom-call(f32[19,4,32,256]{3,2,1,0:T(8,128)S(1)} %get-tuple-element.47.pops, ...), custom_call_target="tpu_custom_call" | custom-call | flops 4915200 | bytes 4915200 | tf_op jit(solution)/shard_map/pallas_call | solution.py:1034
  14.7 0.0 copy-start
  14.7 0.6 %collective-permute-start.5 = (f32[8,32,256]{2,1,0:T(8,128)S(1)}, f32[8,32,256]{2,1,0:T(8,128)S(1)}, u32[]{:S(2)}, u32[]{:S(2)}) collective-permute-start(f32[8,32,256]{2,1,0:T(8,128)S(1)} %get-tuple-element.55), channel_id=1, source_target_pairs={{0,8},{8,0},{16,24},{24,16},{1,9},{9,1},{17,25},{25,17},{2,10},{10... | collective-permute-start | bytes 786440 | tf_op jit(solution)/shard_map/ppermute | solution.py:950
  15.4 2.6 %collective-permute-start.6 = (f32[8,32,256]{2,1,0:T(8,128)S(1)}, f32[8,32,256]{2,1,0:T(8,128)S(1)}, u32[]{:S(2)}, u32[]{:S(2)}) collective-permute-start(f32[8,32,256]{2,1,0:T(8,128)S(1)} %get-tuple-element.56), channel_id=1, source_target_pairs={{0,24},{8,16},{16,8},{24,0},{1,25},{9,17},{17,9},{25,1},{2,26},{10... | collective-permute-start | bytes 786440 | tf_op jit(solution)/shard_map/ppermute | solution.py:950
  18.0 0.0 collective-permute-start.7
  18.0 1.6 %collective-permute-start.8 = (f32[40,256]{1,0:T(8,128)S(1)}, f32[40,256]{1,0:T(8,128)S(1)}, u32[]{:S(2)}, u32[]{:S(2)}) collective-permute-start(f32[40,256]{1,0:T(8,128)S(1)} %get-tuple-element.58), channel_id=1, source_target_pairs={{0,6},{2,4},{4,2},{6,0},{1,7},{3,5},{5,3},{7,1},{8,14},{10,12},{12... | collective-permute-start | bytes 122888 | tf_op jit(solution)/shard_map/ppermute | solution.py:950
  19.6 1.5 %collective-permute-start.9 = (f32[24,128]{1,0:T(8,128)S(1)}, f32[24,128]{1,0:T(8,128)S(1)}, u32[]{:S(2)}, u32[]{:S(2)}) collective-permute-start(f32[24,128]{1,0:T(8,128)S(1)} %get-tuple-element.59), channel_id=1, source_target_pairs={{0,1},{1,0},{2,3},{3,2},{4,5},{5,4},{6,7},{7,6},{8,9},{9,8},{10,11... | collective-permute-start | bytes 36872 | tf_op jit(solution)/shard_map/ppermute | solution.py:955
  21.1 2.2 %collective-permute-done.9.z_rows.refs_2_ = f32[24,128]{1,0:T(8,128)S(1)} collective-permute-done((f32[24,128]{1,0:T(8,128)S(1)}, f32[24,128]{1,0:T(8,128)S(1)}, u32[]{:S(2)}, u32[]{:S(2)}) %collective-permute-start.9) | collective-permute-done | bytes 12320 | tf_op jit(solution)/shard_map/ppermute | solution.py:955
  23.3 0.0 collective-permute-done.7.y_first.refs_0_
  23.3 0.0 collective-permute-done.8.y_second.refs_1_
  23.3 0.1 collective-permute-start.11
  23.4 0.1 collective-permute-start.12
  23.5 1.7 %collective-permute-start.13 = (f32[32,128]{1,0:T(8,128)S(1)}, f32[32,128]{1,0:T(8,128)S(1)}, u32[]{:S(2)}, u32[]{:S(2)}) collective-permute-start(f32[32,128]{1,0:T(8,128)S(1)} %get-tuple-element.73), channel_id=1, source_target_pairs={{0,24},{8,16},{16,8},{24,0},{1,25},{9,17},{17,9},{25,1},{2,26},{10... | collective-permute-start | bytes 49160 | tf_op jit(solution)/shard_map/ppermute | solution.py:950
  25.2 1.3 %collective-permute-done.11.corner_second = f32[24,128]{1,0:T(8,128)S(1)} collective-permute-done((f32[24,128]{1,0:T(8,128)S(1)}, f32[24,128]{1,0:T(8,128)S(1)}, u32[]{:S(2)}, u32[]{:S(2)}) %collective-permute-start.11) | collective-permute-done | bytes 12320 | tf_op jit(solution)/shard_map/ppermute | solution.py:950
  26.5 0.0 collective-permute-start.10
  26.5 0.0 copy-done.1
  26.5 0.0 copy-done.2
  26.5 0.0 copy-done.3
  26.5 0.3 shard_map.99
  26.9 0.9 %shard_map.98 = (f32[15,2,32,256]{3,2,1,0:T(8,128)S(1)}, f32[15,2,32,256]{3,2,1,0:T(8,128)S(1)}, f32[4,32,256]{2,1,0:T(8,128)S(1)}, f32[4,32,256]{2,1,0:T(8,128)S(1)}) custom-call(f32[19,2,32,256]{3,2,1,0:T(8,128)S(1)} %get-tuple-element.54.inner.inner_post, f32[19,2,32,256]{3,2,1,0:T(8,128)S(1)} %get-tuple-element.60.outer_post.post, ...), custom_call_target="tpu_custom_call" | custom-call | flops 11468800 | bytes 6553600 | tf_op jit(solution)/shard_map/pallas_call | solution.py:1052
  27.8 0.0 collective-permute-done.10.corner_first
  27.8 0.0 copy-done
  27.8 0.6 %shard_map.101 = (f32[4,2,32,256]{3,2,1,0:T(8,128)S(1)}, f32[4,2,32,256]{3,2,1,0:T(8,128)S(1)}, f32[2,32,256]{2,1,0:T(8,128)S(1)}, f32[2,32,256]{2,1,0:T(8,128)S...) custom-call(f32[19,2,32,256]{3,2,1,0:T(8,128)S(1)} %get-tuple-element.54.inner.inner_post, ...), custom_call_target="tpu_custom_call" | custom-call | flops 3276800 | bytes 1966080 | tf_op jit(solution)/shard_map/pallas_call | solution.py:1066
  28.4 1.1 %collective-permute-done.12.edges_first = f32[32,128]{1,0:T(8,128)S(1)} collective-permute-done((f32[32,128]{1,0:T(8,128)S(1)}, f32[32,128]{1,0:T(8,128)S(1)}, u32[]{:S(2)}, u32[]{:S(2)}) %collective-permute-start.12) | collective-permute-done | bytes 16416 | tf_op jit(solution)/shard_map/ppermute | solution.py:950
  29.6 0.0 collective-permute-done.13.edges_second
  29.6 0.0 collective-permute-done.5.x_first
  29.6 0.0 collective-permute-done.6.x_second
  29.6 0.8 %shard_map.102 = (f32[5,2,32,256]{3,2,1,0:T(8,128)S(1)}, f32[2,32,256]{2,1,0:T(8,128)S(1)}, f32[6,32,256]{2,1,0:T(8,128)S(1)}, f32[8,256]{1,0:T(8,128)S(1)}, f32...) custom-call(f32[19,2,32,256]{3,2,1,0:T(8,128)S(1)} %get-tuple-element.60.outer_post.post, ...), custom_call_target="tpu_custom_call" | custom-call | flops 4915200 | bytes 3276800 | tf_op jit(solution)/shard_map/pallas_call | solution.py:1072
  30.3 1.5 %collective-permute-start.14 = (f32[16,128]{1,0:T(8,128)S(1)}, f32[16,128]{1,0:T(8,128)S(1)}, u32[]{:S(2)}, u32[]{:S(2)}) collective-permute-start(f32[16,128]{1,0:T(8,128)S(1)} %get-tuple-element.82), channel_id=1, source_target_pairs={{0,1},{1,0},{2,3},{3,2},{4,5},{5,4},{6,7},{7,6},{8,9},{9,8},{10,11... | collective-permute-start | bytes 24584 | tf_op jit(solution)/shard_map/ppermute | solution.py:955
  31.8 0.0 collective-permute-start.15
  31.8 1.6 %collective-permute-start.16 = (f32[8,256]{1,0:T(8,128)S(1)}, f32[8,256]{1,0:T(8,128)S(1)}, u32[]{:S(2)}, u32[]{:S(2)}) collective-permute-start(f32[8,256]{1,0:T(8,128)S(1)} %get-tuple-element.84), channel_id=1, source_target_pairs={{0,6},{2,4},{4,2},{6,0},{1,7},{3,5},{5,3},{7,1},{8,14},{10,12},{12... | collective-permute-start | bytes 24584 | tf_op jit(solution)/shard_map/ppermute | solution.py:950
  33.4 0.6 %collective-permute-done.14.z_rows = f32[16,128]{1,0:T(8,128)S(1)} collective-permute-done((f32[16,128]{1,0:T(8,128)S(1)}, f32[16,128]{1,0:T(8,128)S(1)}, u32[]{:S(2)}, u32[]{:S(2)}) %collective-permute-start.14) | collective-permute-done | bytes 8224 | tf_op jit(solution)/shard_map/ppermute | solution.py:955
  34.0 0.0 collective-permute-done.15.y_first
  34.0 0.8 %collective-permute-done.16.y_second = f32[8,256]{1,0:T(8,128)S(1)} collective-permute-done((f32[8,256]{1,0:T(8,128)S(1)}, f32[8,256]{1,0:T(8,128)S(1)}, u32[]{:S(2)}, u32[]{:S(2)}) %collective-permute-start.16) | collective-permute-done | bytes 8224 | tf_op jit(solution)/shard_map/ppermute | solution.py:950
  34.9 0.2 shard_map.104
  35.1 0.8 %collective-permute-start.19 = (f32[32,256]{1,0:T(8,128)S(1)}, f32[32,256]{1,0:T(8,128)S(1)}, u32[]{:S(2)}, u32[]{:S(2)}) collective-permute-start(f32[32,256]{1,0:T(8,128)S(1)} %get-tuple-element.85), channel_id=1, source_target_pairs={{0,8},{8,0},{16,24},{24,16},{1,9},{9,1},{17,25},{25,17},{2,10},{10... | collective-permute-start | bytes 98312 | tf_op jit(solution)/shard_map/ppermute | solution.py:950
  35.9 1.4 %collective-permute-start.20 = (f32[32,256]{1,0:T(8,128)S(1)}, f32[32,256]{1,0:T(8,128)S(1)}, u32[]{:S(2)}, u32[]{:S(2)}) collective-permute-start(f32[32,256]{1,0:T(8,128)S(1)} %get-tuple-element.86), channel_id=1, source_target_pairs={{0,24},{8,16},{16,8},{24,0},{1,25},{9,17},{17,9},{25,1},{2,26},{10... | collective-permute-start | bytes 98312 | tf_op jit(solution)/shard_map/ppermute | solution.py:950
  37.3 1.0 %collective-permute-start.18 = (f32[16,128]{1,0:T(8,128)S(1)}, f32[16,128]{1,0:T(8,128)S(1)}, u32[]{:S(2)}, u32[]{:S(2)}) collective-permute-start(f32[16,128]{1,0:T(8,128)S(1)} %collective-permute-done.14.z_rows), channel_id=1, source_target_pairs={{0,6},{2,4},{4,2},{6,0},{1,7},{3,5},{5,3},{7,1},{8,14},{10,12},{12... | collective-permute-start | bytes 24584 | tf_op jit(solution)/shard_map/ppermute | solution.py:950
  38.3 0.6 %collective-permute-start.17 = (f32[16,128]{1,0:T(8,128)S(1)}, f32[16,128]{1,0:T(8,128)S(1)}, u32[]{:S(2)}, u32[]{:S(2)}) collective-permute-start(f32[16,128]{1,0:T(8,128)S(1)} %collective-permute-done.14.z_rows), channel_id=1, source_target_pairs={{0,2},{2,0},{4,6},{6,4},{1,3},{3,1},{5,7},{7,5},{8,10},{10,8},{12,... | collective-permute-start | bytes 24584 | tf_op jit(solution)/shard_map/ppermute | solution.py:950
  38.9 2.6 %shard_map.103 = (f32[6,4,32,256]{3,2,1,0:T(8,128)}, f32[19,4,32,256]{3,2,1,0:T(8,128)}) custom-call(f32[6,4,32,256]{3,2,1,0:T(8,128)S(1)} %get-tuple-element.45.stretch, f32[5,4,32,256]{3,2,1,0:T(8,128)S(1)} %get-tuple-element.46.flow, f32[8,32,256]{2,1,0:T(8,128)S(1)} %collective-permute-done.5.x_first, f32[8,32,256]{2,1,0:T(8,128)S(1)} %collective-permute-done.6.x_second, ...), custom_call_target="tpu_custom_call" | custom-call | flops 4915200 | bytes 2621440 | tf_op jit(solution)/shard_map/pallas_call | solution.py:1096
  41.5 0.0 collective-permute-done.18.corner_second
  41.5 0.0 collective-permute-done.17.corner_first
  41.5 0.0 collective-permute-done.19.x_first
  41.5 0.1 collective-permute-done.20.x_second
  41.6 0.9 %shard_map.105 = f32[4,32,256]{2,1,0:T(8,128)} custom-call(f32[2,32,256]{2,1,0:T(8,128)S(1)} %get-tuple-element.79.inner_settled, f32[2,32,256]{2,1,0:T(8,128)S(1)} %get-tuple-element.80.outer_settled, f32[6,32,256]{2,1,0:T(8,128)S(1)} %get-tuple-element.81.spread, f32[16,128]{1,0:T(8,128)S(1)} %collective-permute-done.14.z_rows, ...), custom_call_target="tpu_custom_call" | custom-call | tf_op jit(solution)/shard_map/pallas_call | solution.py:1121
  (1 shorter events, 0.0 us)
Async XLA Ops:
  2.0 11.5 %collective-permute-start = (f32[4,32,256]{2,1,0:T(8,128)S(1)}, f32[4,32,256]{2,1,0:T(8,128)S(1)}, u32[]{:S(2)}, u32[]{:S(2)}) collective-permute-start(f32[4,32,256]{2,1,0:T(8,128)S(1)} %get-tuple-element.49), channel_id=1, source_target_pairs={{0,8},{8,0},{16,24},{24,16},{1,9},{9,1},{17,25},{25,17},{2,10},{10... | collective-permute-start | bytes 393224 | tf_op jit(solution)/shard_map/ppermute | solution.py:950
  5.1 8.6 %collective-permute-start.1 = (f32[4,32,256]{2,1,0:T(8,128)S(1)}, f32[4,32,256]{2,1,0:T(8,128)S(1)}, u32[]{:S(2)}, u32[]{:S(2)}) collective-permute-start(f32[4,32,256]{2,1,0:T(8,128)S(1)} %get-tuple-element.50), channel_id=1, source_target_pairs={{0,24},{8,16},{16,8},{24,0},{1,25},{9,17},{17,9},{25,1},{2,26},{10... | collective-permute-start | bytes 393224 | tf_op jit(solution)/shard_map/ppermute | solution.py:950
  7.6 5.2 %collective-permute-start.2 = (f32[16,256]{1,0:T(8,128)S(1)}, f32[16,256]{1,0:T(8,128)S(1)}, u32[]{:S(2)}, u32[]{:S(2)}) collective-permute-start(f32[16,256]{1,0:T(8,128)S(1)} %get-tuple-element.51), channel_id=1, source_target_pairs={{0,2},{2,0},{4,6},{6,4},{1,3},{3,1},{5,7},{7,5},{8,10},{10,8},{12,... | collective-permute-start | bytes 49160 | tf_op jit(solution)/shard_map/ppermute | solution.py:950
  7.6 5.2 %collective-permute-start.3 = (f32[16,256]{1,0:T(8,128)S(1)}, f32[16,256]{1,0:T(8,128)S(1)}, u32[]{:S(2)}, u32[]{:S(2)}) collective-permute-start(f32[16,256]{1,0:T(8,128)S(1)} %get-tuple-element.52), channel_id=1, source_target_pairs={{0,6},{2,4},{4,2},{6,0},{1,7},{3,5},{5,3},{7,1},{8,14},{10,12},{12... | collective-permute-start | bytes 49160 | tf_op jit(solution)/shard_map/ppermute | solution.py:950
  9.2 3.6 %collective-permute-start.4 = (f32[8,128]{1,0:T(8,128)S(1)}, f32[8,128]{1,0:T(8,128)S(1)}, u32[]{:S(2)}, u32[]{:S(2)}) collective-permute-start(f32[8,128]{1,0:T(8,128)S(1)} %get-tuple-element.53), channel_id=1, source_target_pairs={{0,1},{1,0},{2,3},{3,2},{4,5},{5,4},{6,7},{7,6},{8,9},{9,8},{10,11... | collective-permute-start | bytes 12296 | tf_op jit(solution)/shard_map/ppermute | solution.py:955
  13.7 12.8 %copy-start.1 = (s32[1024]{0:T(1024)S(1)}, s32[1024]{0:T(1024)}, u32[]{:S(2)}) copy-start(s32[1024]{0:T(1024)} %param.11) | copy-start | bytes 12292
  13.7 12.8 %copy-start.2 = (s32[1024]{0:T(1024)S(1)}, s32[1024]{0:T(1024)}, u32[]{:S(2)}) copy-start(s32[1024]{0:T(1024)} %param.12) | copy-start | bytes 12292
  13.7 12.8 %copy-start.3 = (s32[1024]{0:T(1024)S(1)}, s32[1024]{0:T(1024)}, u32[]{:S(2)}) copy-start(s32[1024]{0:T(1024)} %param.13) | copy-start | bytes 12292
  14.7 13.1 %copy-start = (f32[4,32,256]{2,1,0:T(8,128)S(1)}, f32[4,32,256]{2,1,0:T(8,128)}, u32[]{:S(2)}) copy-start(f32[4,32,256]{2,1,0:T(8,128)} %mass.3) | copy-start | bytes 393220
  14.7 14.8 %collective-permute-start.5 = (f32[8,32,256]{2,1,0:T(8,128)S(1)}, f32[8,32,256]{2,1,0:T(8,128)S(1)}, u32[]{:S(2)}, u32[]{:S(2)}) collective-permute-start(f32[8,32,256]{2,1,0:T(8,128)S(1)} %get-tuple-element.55), channel_id=1, source_target_pairs={{0,8},{8,0},{16,24},{24,16},{1,9},{9,1},{17,25},{25,17},{2,10},{10... | collective-permute-start | bytes 786440 | tf_op jit(solution)/shard_map/ppermute | solution.py:950
  15.4 14.2 %collective-permute-start.6 = (f32[8,32,256]{2,1,0:T(8,128)S(1)}, f32[8,32,256]{2,1,0:T(8,128)S(1)}, u32[]{:S(2)}, u32[]{:S(2)}) collective-permute-start(f32[8,32,256]{2,1,0:T(8,128)S(1)} %get-tuple-element.56), channel_id=1, source_target_pairs={{0,24},{8,16},{16,8},{24,0},{1,25},{9,17},{17,9},{25,1},{2,26},{10... | collective-permute-start | bytes 786440 | tf_op jit(solution)/shard_map/ppermute | solution.py:950
  18.0 5.3 %collective-permute-start.7 = (f32[40,256]{1,0:T(8,128)S(1)}, f32[40,256]{1,0:T(8,128)S(1)}, u32[]{:S(2)}, u32[]{:S(2)}) collective-permute-start(f32[40,256]{1,0:T(8,128)S(1)} %get-tuple-element.57), channel_id=1, source_target_pairs={{0,2},{2,0},{4,6},{6,4},{1,3},{3,1},{5,7},{7,5},{8,10},{10,8},{12,... | collective-permute-start | bytes 122888 | tf_op jit(solution)/shard_map/ppermute | solution.py:950
  18.0 5.3 %collective-permute-start.8 = (f32[40,256]{1,0:T(8,128)S(1)}, f32[40,256]{1,0:T(8,128)S(1)}, u32[]{:S(2)}, u32[]{:S(2)}) collective-permute-start(f32[40,256]{1,0:T(8,128)S(1)} %get-tuple-element.58), channel_id=1, source_target_pairs={{0,6},{2,4},{4,2},{6,0},{1,7},{3,5},{5,3},{7,1},{8,14},{10,12},{12... | collective-permute-start | bytes 122888 | tf_op jit(solution)/shard_map/ppermute | solution.py:950
  19.6 3.7 %collective-permute-start.9 = (f32[24,128]{1,0:T(8,128)S(1)}, f32[24,128]{1,0:T(8,128)S(1)}, u32[]{:S(2)}, u32[]{:S(2)}) collective-permute-start(f32[24,128]{1,0:T(8,128)S(1)} %get-tuple-element.59), channel_id=1, source_target_pairs={{0,1},{1,0},{2,3},{3,2},{4,5},{5,4},{6,7},{7,6},{8,9},{9,8},{10,11... | collective-permute-start | bytes 36872 | tf_op jit(solution)/shard_map/ppermute | solution.py:955
  23.3 3.2 %collective-permute-start.11 = (f32[24,128]{1,0:T(8,128)S(1)}, f32[24,128]{1,0:T(8,128)S(1)}, u32[]{:S(2)}, u32[]{:S(2)}) collective-permute-start(f32[24,128]{1,0:T(8,128)S(1)} %get-tuple-element.65), channel_id=1, source_target_pairs={{0,6},{2,4},{4,2},{6,0},{1,7},{3,5},{5,3},{7,1},{8,14},{10,12},{12... | collective-permute-start | bytes 36872 | tf_op jit(solution)/shard_map/ppermute | solution.py:950
  23.4 6.1 %collective-permute-start.12 = (f32[32,128]{1,0:T(8,128)S(1)}, f32[32,128]{1,0:T(8,128)S(1)}, u32[]{:S(2)}, u32[]{:S(2)}) collective-permute-start(f32[32,128]{1,0:T(8,128)S(1)} %get-tuple-element.72), channel_id=1, source_target_pairs={{0,8},{8,0},{16,24},{24,16},{1,9},{9,1},{17,25},{25,17},{2,10},{10... | collective-permute-start | bytes 49160 | tf_op jit(solution)/shard_map/ppermute | solution.py:950
  23.5 6.1 %collective-permute-start.13 = (f32[32,128]{1,0:T(8,128)S(1)}, f32[32,128]{1,0:T(8,128)S(1)}, u32[]{:S(2)}, u32[]{:S(2)}) collective-permute-start(f32[32,128]{1,0:T(8,128)S(1)} %get-tuple-element.73), channel_id=1, source_target_pairs={{0,24},{8,16},{16,8},{24,0},{1,25},{9,17},{17,9},{25,1},{2,26},{10... | collective-permute-start | bytes 49160 | tf_op jit(solution)/shard_map/ppermute | solution.py:950
  26.5 1.3 %collective-permute-start.10 = (f32[24,128]{1,0:T(8,128)S(1)}, f32[24,128]{1,0:T(8,128)S(1)}, u32[]{:S(2)}, u32[]{:S(2)}) collective-permute-start(f32[24,128]{1,0:T(8,128)S(1)} %get-tuple-element.65), channel_id=1, source_target_pairs={{0,2},{2,0},{4,6},{6,4},{1,3},{3,1},{5,7},{7,5},{8,10},{10,8},{12,... | collective-permute-start | bytes 36872 | tf_op jit(solution)/shard_map/ppermute | solution.py:950
  30.3 3.7 %collective-permute-start.14 = (f32[16,128]{1,0:T(8,128)S(1)}, f32[16,128]{1,0:T(8,128)S(1)}, u32[]{:S(2)}, u32[]{:S(2)}) collective-permute-start(f32[16,128]{1,0:T(8,128)S(1)} %get-tuple-element.82), channel_id=1, source_target_pairs={{0,1},{1,0},{2,3},{3,2},{4,5},{5,4},{6,7},{7,6},{8,9},{9,8},{10,11... | collective-permute-start | bytes 24584 | tf_op jit(solution)/shard_map/ppermute | solution.py:955
  31.8 2.2 %collective-permute-start.15 = (f32[8,256]{1,0:T(8,128)S(1)}, f32[8,256]{1,0:T(8,128)S(1)}, u32[]{:S(2)}, u32[]{:S(2)}) collective-permute-start(f32[8,256]{1,0:T(8,128)S(1)} %get-tuple-element.83), channel_id=1, source_target_pairs={{0,2},{2,0},{4,6},{6,4},{1,3},{3,1},{5,7},{7,5},{8,10},{10,8},{12,... | collective-permute-start | bytes 24584 | tf_op jit(solution)/shard_map/ppermute | solution.py:950
  31.8 3.1 %collective-permute-start.16 = (f32[8,256]{1,0:T(8,128)S(1)}, f32[8,256]{1,0:T(8,128)S(1)}, u32[]{:S(2)}, u32[]{:S(2)}) collective-permute-start(f32[8,256]{1,0:T(8,128)S(1)} %get-tuple-element.84), channel_id=1, source_target_pairs={{0,6},{2,4},{4,2},{6,0},{1,7},{3,5},{5,3},{7,1},{8,14},{10,12},{12... | collective-permute-start | bytes 24584 | tf_op jit(solution)/shard_map/ppermute | solution.py:950
  35.1 6.4 %collective-permute-start.19 = (f32[32,256]{1,0:T(8,128)S(1)}, f32[32,256]{1,0:T(8,128)S(1)}, u32[]{:S(2)}, u32[]{:S(2)}) collective-permute-start(f32[32,256]{1,0:T(8,128)S(1)} %get-tuple-element.85), channel_id=1, source_target_pairs={{0,8},{8,0},{16,24},{24,16},{1,9},{9,1},{17,25},{25,17},{2,10},{10... | collective-permute-start | bytes 98312 | tf_op jit(solution)/shard_map/ppermute | solution.py:950
  35.9 5.7 %collective-permute-start.20 = (f32[32,256]{1,0:T(8,128)S(1)}, f32[32,256]{1,0:T(8,128)S(1)}, u32[]{:S(2)}, u32[]{:S(2)}) collective-permute-start(f32[32,256]{1,0:T(8,128)S(1)} %get-tuple-element.86), channel_id=1, source_target_pairs={{0,24},{8,16},{16,8},{24,0},{1,25},{9,17},{17,9},{25,1},{2,26},{10... | collective-permute-start | bytes 98312 | tf_op jit(solution)/shard_map/ppermute | solution.py:950
  37.3 4.2 %collective-permute-start.18 = (f32[16,128]{1,0:T(8,128)S(1)}, f32[16,128]{1,0:T(8,128)S(1)}, u32[]{:S(2)}, u32[]{:S(2)}) collective-permute-start(f32[16,128]{1,0:T(8,128)S(1)} %collective-permute-done.14.z_rows), channel_id=1, source_target_pairs={{0,6},{2,4},{4,2},{6,0},{1,7},{3,5},{5,3},{7,1},{8,14},{10,12},{12... | collective-permute-start | bytes 24584 | tf_op jit(solution)/shard_map/ppermute | solution.py:950
  38.3 3.2 %collective-permute-start.17 = (f32[16,128]{1,0:T(8,128)S(1)}, f32[16,128]{1,0:T(8,128)S(1)}, u32[]{:S(2)}, u32[]{:S(2)}) collective-permute-start(f32[16,128]{1,0:T(8,128)S(1)} %collective-permute-done.14.z_rows), channel_id=1, source_target_pairs={{0,2},{2,0},{4,6},{6,4},{1,3},{3,1},{5,7},{7,5},{8,10},{10,8},{12,... | collective-permute-start | bytes 24584 | tf_op jit(solution)/shard_map/ppermute | solution.py:950
where the time goes:
time: 42.6 us; the launch traced here: 42.4 us
  starting transfers between devices  23.8 us (56%)
  Pallas kernels  11.1 us (26%)
  waiting for transfers between devices  6.67 us (16%)
  between operations  0.8 us (2%)
    ppermute x9, starting transfers between devices, swapped(): lax.ppermute(second, axis, behind)  14.1 us
    ppermute x9, starting transfers between devices, swapped(): lax.ppermute(first, axis, ahead)  5.15 us
    ppermute x3, starting transfers between devices, both_ways(): lax.ppermute(rows, 'gz', [(i, (i + 1) % devices) for i in range(devices)])  4.51 us
    ppermute x3, waiting for transfers between devices, both_ways(): lax.ppermute(rows, 'gz', [(i, (i + 1) % devices) for i in range(devices)])  3.14 us
    pallas_call x1, Pallas kernels, shards(): call(restretch, [(6, *box), (19, *box)], out_specs=[pl.BlockSpec(), remot...  2.58 us
    ppermute x9, waiting for transfers between devices, swapped(): lax.ppermute(second, axis, behind)  2.38 us
    pallas_call x1, Pallas kernels, shards(): call(moments, [(19, *box), (5, *box)], specs=[remote], scratch=[pltpu.Sem...  1.74 us
    pallas_call x1, Pallas kernels, shards(): call(first_faces, [(6, *box), jax.ShapeDtypeStruct(box, jnp.int32), (8, b...  1.38 us
  transfers between devices with their start and end apart: 21, of which 8 were waited for; matrix products, arithmetic and copies ran while one was open for 0% of the time, Pallas kernels for 16%

commit v1 on v0

--- a/solution.py
+++ b/solution.py
@@ -322,9 +322,9 @@
     pops,
     stretch,
     flow,
+    z_rows,
     y_first,
     y_second,
-    z_rows,
     post,
     shift,
     y_below,
@@ -409,8 +409,8 @@
 def restretch(
     stretch,
     flow,
+    x_second,
     x_first,
-    x_second,
     y_first,
     y_second,
     z_rows,
@@ -504,7 +504,7 @@
 down_edges = ((0, y_up.index(10)), (0, gas_slot), (1, y_down.index(8)), (1, gas_slot))
 
 
-def forward_edges(y_first, y_second, z_rows, first_out, second_out, corner, *, bx):
+def forward_edges(z_rows, y_first, y_second, first_out, second_out, corner, *, bx):
     halves = y_first.shape[1] // lanes
     flip_x, flip_y = (odd("gx"), odd("gy"))
     for half in range(halves):
@@ -740,8 +740,8 @@
     changes,
     gas_first,
     gas_second,
+    x_second,
     x_first,
-    x_second,
     edges_first,
     edges_second,
     inner_excess,
@@ -913,8 +913,8 @@
     y_second,
     corner_first,
     corner_second,
+    x_second,
     x_first,
-    x_second,
     new_mass,
 ):
     bx, by, bz = new_mass.shape
@@ -1030,7 +1030,7 @@
         [(19, *inside), (3, *inside)],
         scratch=sides_y,
         cost=(150 * cells, 150 * cells),
-    )(pops, stretch, flow, *y_first, z_first)
+    )(pops, stretch, flow, z_first, *y_first)
     outer_post, outer_shift, z_out, x_one, x_two, y_one, y_two = call(
         collide_outer,
         [(19, *ends), (3, *ends), columns, (8, *face), (8, *face), rows, rows],
@@ -1043,7 +1043,7 @@
     edges = (4 * (bz // lanes) + columns[0], lanes)
     x_one, x_two, corner = call(
         lambda *refs: forward_edges(*refs, bx=bx), [edges, edges, columns]
-    )(*post_y, z_post)
+    )(z_post, *post_y)
     corners = swapped(corner, corner, "gy")
     edges_x = swapped(x_one, x_two, "gx")
 
@@ -1083,7 +1083,7 @@
         totals,
         changes,
         *first_x,
-        *post_x,
+        *post_x[::-1],
         *edges_x,
         inner_excess,
         inner_heading,
@@ -1109,7 +1109,7 @@
     )(
         stretch,
         flow,
-        *post_x,
+        *post_x[::-1],
         *post_y,
         z_post,
         inner,
@@ -1119,7 +1119,7 @@
         late,
     )
     (new_mass,) = call(add_all, [box])(
-        inner_settled, outer_settled, spread, z_last, *last_y, *last_corners, *last_x
+        inner_settled, outer_settled, spread, z_last, *last_y, *last_corners, *last_x[::-1]
     )
     return (fresh, new_stretch, new_mass)
 

time: 42.6 us -> 42.7 us (level)
    ppermute x9, waiting for transfers between devices: 2.38 us -> 1.58 us  [swapped(): lax.ppermute(second, axis, behind)]
  transfers between devices with their start and end apart: 21 -> 21, of which waited for: 8 -> 7; matrix products, arithmetic and copies ran while one was open for 0% -> 0% of each run, Pallas kernels for 16% -> 16%
where the time goes in v1:
time: 42.7 us; the launch traced here: 42.5 us
  starting transfers between devices  24 us (56%)
  Pallas kernels  11.1 us (26%)
  waiting for transfers between devices  6.62 us (16%)
  between operations  0.78 us (2%)
    ppermute x9, starting transfers between devices, swapped(): lax.ppermute(second, axis, behind)  14.3 us
    ppermute x9, starting transfers between devices, swapped(): lax.ppermute(first, axis, ahead)  5.49 us
    ppermute x3, starting transfers between devices, both_ways(): lax.ppermute(rows, 'gz', [(i, (i + 1) % devices) for i in range(devices)])  4.14 us
    ppermute x3, waiting for transfers between devices, both_ways(): lax.ppermute(rows, 'gz', [(i, (i + 1) % devices) for i in range(devices)])  3.5 us
    pallas_call x1, Pallas kernels, shards(): call(restretch, [(6, *box), (19, *box)], out_specs=[pl.BlockSpec(), remot...  2.58 us
    pallas_call x1, Pallas kernels, shards(): call(moments, [(19, *box), (5, *box)], specs=[remote], scratch=[pltpu.Sem...  1.74 us
    ppermute x9, waiting for transfers between devices, swapped(): lax.ppermute(second, axis, behind)  1.58 us
    ppermute x9, waiting for transfers between devices, swapped(): lax.ppermute(first, axis, ahead)  1.53 us
  transfers between devices with their start and end apart: 21, of which 7 were waited for; matrix products, arithmetic and copies ran while one was open for 0% of the time, Pallas kernels for 16%

profile of v1, /device:TPU:0, one launch (start us, length us, event | category | flops | bytes accessed | tf_op | source)
XLA Modules:
  0.0 42.5 jit_solution(13469705689511288477)
XLA Ops:
  0.6 1.4 %shard_map.94 = (f32[6,4,32,256]{3,2,1,0:T(8,128)S(1)}, s32[4,32,256]{2,1,0:T(8,128)S(1)}, f32[8,128]{1,0:T(8,128)S(1)}, f32[16,256]{1,0:T(8,128)S(1)}, f32[16,2...) custom-call(f32[6,4,32,256]{3,2,1,0:T(8,128)} %stretch_in.1, s32[4,32,256]{2,1,0:T(8,128)} %flags_in.1), custom_call_target="tpu_custom_call" | custom-call | flops 327680 | bytes 1966080 | tf_op jit(solution)/shard_map/pallas_call | solution.py:992
  2.0 3.1 %collective-permute-start = (f32[4,32,256]{2,1,0:T(8,128)S(1)}, f32[4,32,256]{2,1,0:T(8,128)S(1)}, u32[]{:S(2)}, u32[]{:S(2)}) collective-permute-start(f32[4,32,256]{2,1,0:T(8,128)S(1)} %get-tuple-element.49), channel_id=1, source_target_pairs={{0,8},{8,0},{16,24},{24,16},{1,9},{9,1},{17,25},{25,17},{2,10},{10... | collective-permute-start | bytes 393224 | tf_op jit(solution)/shard_map/ppermute | solution.py:950
  5.1 2.5 %collective-permute-start.1 = (f32[4,32,256]{2,1,0:T(8,128)S(1)}, f32[4,32,256]{2,1,0:T(8,128)S(1)}, u32[]{:S(2)}, u32[]{:S(2)}) collective-permute-start(f32[4,32,256]{2,1,0:T(8,128)S(1)} %get-tuple-element.50), channel_id=1, source_target_pairs={{0,24},{8,16},{16,8},{24,0},{1,25},{9,17},{17,9},{25,1},{2,26},{10... | collective-permute-start | bytes 393224 | tf_op jit(solution)/shard_map/ppermute | solution.py:950
  7.6 0.0 collective-permute-start.2
  7.6 1.6 %collective-permute-start.3 = (f32[16,256]{1,0:T(8,128)S(1)}, f32[16,256]{1,0:T(8,128)S(1)}, u32[]{:S(2)}, u32[]{:S(2)}) collective-permute-start(f32[16,256]{1,0:T(8,128)S(1)} %get-tuple-element.52), channel_id=1, source_target_pairs={{0,6},{2,4},{4,2},{6,0},{1,7},{3,5},{5,3},{7,1},{8,14},{10,12},{12... | collective-permute-start | bytes 49160 | tf_op jit(solution)/shard_map/ppermute | solution.py:950
  9.2 1.5 %collective-permute-start.4 = (f32[8,128]{1,0:T(8,128)S(1)}, f32[8,128]{1,0:T(8,128)S(1)}, u32[]{:S(2)}, u32[]{:S(2)}) collective-permute-start(f32[8,128]{1,0:T(8,128)S(1)} %get-tuple-element.53), channel_id=1, source_target_pairs={{0,1},{1,0},{2,3},{3,2},{4,5},{5,4},{6,7},{7,6},{8,9},{9,8},{10,11... | collective-permute-start | bytes 12296 | tf_op jit(solution)/shard_map/ppermute | solution.py:955
  10.7 1.7 %shard_map.95 = (f32[19,4,32,256]{3,2,1,0:T(8,128)S(1)}, f32[5,4,32,256]{3,2,1,0:T(8,128)S(1)}) custom-call(f32[19,4,32,256]{3,2,1,0:T(8,128)} %pops_in.1), custom_call_target="tpu_custom_call" | custom-call | flops 1966080 | bytes 4915200 | tf_op jit(solution)/shard_map/pallas_call | solution.py:1017
  12.5 0.3 collective-permute-done.4.z_rows
  12.8 0.0 collective-permute-done.2.y_first
  12.8 0.0 collective-permute-done.3.y_second
  12.8 0.8 %shard_map.96 = (f32[19,2,32,256]{3,2,1,0:T(8,128)S(1)}, f32[3,2,32,256]{3,2,1,0:T(8,128)S(1)}) custom-call(f32[19,4,32,256]{3,2,1,0:T(8,128)S(1)} %get-tuple-element.47.pops, f32[6,4,32,256]{3,2,1,0:T(8,128)S(1)} %get-tuple-element.45.stretch, f32[5,4,32,256]{3,2,1,0:T(8,128)S(1)} %get-tuple-element.46.flow, f32[8,128]{1,0:T(8,128)S(1)} %collective-permute-done.4.z_rows, ...), custom_call_target="tpu_custom_call" | custom-call | flops 4915200 | bytes 4915200 | tf_op jit(solution)/shard_map/pallas_call | solution.py:1028
  13.6 0.0 collective-permute-done.x_first.gas_first
  13.6 0.1 collective-permute-done.1.x_second.gas_second
  13.7 0.0 copy-start.1
  13.7 0.0 copy-start.2
  13.7 0.0 copy-start.3
  13.7 1.0 %shard_map.97 = (f32[19,2,32,256]{3,2,1,0:T(8,128)S(1)}, f32[3,2,32,256]{3,2,1,0:T(8,128)S(1)}, f32[24,128]{1,0:T(8,128)S(1)}, f32[8,32,256]{2,1,0:T(8,128)S(1)}...) custom-call(f32[19,4,32,256]{3,2,1,0:T(8,128)S(1)} %get-tuple-element.47.pops, ...), custom_call_target="tpu_custom_call" | custom-call | flops 4915200 | bytes 4915200 | tf_op jit(solution)/shard_map/pallas_call | solution.py:1034
  14.7 0.0 copy-start
  14.7 1.5 %collective-permute-start.5 = (f32[8,32,256]{2,1,0:T(8,128)S(1)}, f32[8,32,256]{2,1,0:T(8,128)S(1)}, u32[]{:S(2)}, u32[]{:S(2)}) collective-permute-start(f32[8,32,256]{2,1,0:T(8,128)S(1)} %get-tuple-element.55), channel_id=1, source_target_pairs={{0,24},{8,16},{16,8},{24,0},{1,25},{9,17},{17,9},{25,1},{2,26},{10... | collective-permute-start | bytes 786440 | tf_op jit(solution)/shard_map/ppermute | solution.py:950
  16.3 0.8 %collective-permute-start.6 = (f32[8,32,256]{2,1,0:T(8,128)S(1)}, f32[8,32,256]{2,1,0:T(8,128)S(1)}, u32[]{:S(2)}, u32[]{:S(2)}) collective-permute-start(f32[8,32,256]{2,1,0:T(8,128)S(1)} %get-tuple-element.56), channel_id=1, source_target_pairs={{0,8},{8,0},{16,24},{24,16},{1,9},{9,1},{17,25},{25,17},{2,10},{10... | collective-permute-start | bytes 786440 | tf_op jit(solution)/shard_map/ppermute | solution.py:950
  17.1 0.0 collective-permute-start.7
  17.1 1.6 %collective-permute-start.8 = (f32[40,256]{1,0:T(8,128)S(1)}, f32[40,256]{1,0:T(8,128)S(1)}, u32[]{:S(2)}, u32[]{:S(2)}) collective-permute-start(f32[40,256]{1,0:T(8,128)S(1)} %get-tuple-element.58), channel_id=1, source_target_pairs={{0,6},{2,4},{4,2},{6,0},{1,7},{3,5},{5,3},{7,1},{8,14},{10,12},{12... | collective-permute-start | bytes 122888 | tf_op jit(solution)/shard_map/ppermute | solution.py:950
  18.7 1.5 %collective-permute-start.9 = (f32[24,128]{1,0:T(8,128)S(1)}, f32[24,128]{1,0:T(8,128)S(1)}, u32[]{:S(2)}, u32[]{:S(2)}) collective-permute-start(f32[24,128]{1,0:T(8,128)S(1)} %get-tuple-element.59), channel_id=1, source_target_pairs={{0,1},{1,0},{2,3},{3,2},{4,5},{5,4},{6,7},{7,6},{8,9},{9,8},{10,11... | collective-permute-start | bytes 36872 | tf_op jit(solution)/shard_map/ppermute | solution.py:955
  20.2 2.2 %collective-permute-done.9.z_rows.refs_0_ = f32[24,128]{1,0:T(8,128)S(1)} collective-permute-done((f32[24,128]{1,0:T(8,128)S(1)}, f32[24,128]{1,0:T(8,128)S(1)}, u32[]{:S(2)}, u32[]{:S(2)}) %collective-permute-start.9) | collective-permute-done | bytes 12320 | tf_op jit(solution)/shard_map/ppermute | solution.py:955
  22.4 0.0 collective-permute-done.7.y_first.refs_1_
  22.4 0.0 collective-permute-done.8.y_second.refs_2_
  22.4 0.1 collective-permute-start.11
  22.5 1.3 %collective-permute-start.12 = (f32[32,128]{1,0:T(8,128)S(1)}, f32[32,128]{1,0:T(8,128)S(1)}, u32[]{:S(2)}, u32[]{:S(2)}) collective-permute-start(f32[32,128]{1,0:T(8,128)S(1)} %get-tuple-element.72), channel_id=1, source_target_pairs={{0,8},{8,0},{16,24},{24,16},{1,9},{9,1},{17,25},{25,17},{2,10},{10... | collective-permute-start | bytes 49160 | tf_op jit(solution)/shard_map/ppermute | solution.py:950
  23.8 2.3 %collective-permute-start.13 = (f32[32,128]{1,0:T(8,128)S(1)}, f32[32,128]{1,0:T(8,128)S(1)}, u32[]{:S(2)}, u32[]{:S(2)}) collective-permute-start(f32[32,128]{1,0:T(8,128)S(1)} %get-tuple-element.73), channel_id=1, source_target_pairs={{0,24},{8,16},{16,8},{24,0},{1,25},{9,17},{17,9},{25,1},{2,26},{10... | collective-permute-start | bytes 49160 | tf_op jit(solution)/shard_map/ppermute | solution.py:950
  26.1 0.0 collective-permute-done.11.corner_second
  26.1 0.0 collective-permute-start.10
  26.1 0.0 copy-done.1
  26.1 0.0 copy-done.2
  26.1 0.0 copy-done.3
  26.2 0.3 shard_map.99
  26.5 0.9 %shard_map.98 = (f32[15,2,32,256]{3,2,1,0:T(8,128)S(1)}, f32[15,2,32,256]{3,2,1,0:T(8,128)S(1)}, f32[4,32,256]{2,1,0:T(8,128)S(1)}, f32[4,32,256]{2,1,0:T(8,128)S(1)}) custom-call(f32[19,2,32,256]{3,2,1,0:T(8,128)S(1)} %get-tuple-element.54.inner.inner_post, f32[19,2,32,256]{3,2,1,0:T(8,128)S(1)} %get-tuple-element.60.outer_post.post, ...), custom_call_target="tpu_custom_call" | custom-call | flops 11468800 | bytes 6553600 | tf_op jit(solution)/shard_map/pallas_call | solution.py:1052
  27.4 0.0 collective-permute-done.10.corner_first
  27.4 0.0 copy-done
  27.5 0.6 %shard_map.101 = (f32[4,2,32,256]{3,2,1,0:T(8,128)S(1)}, f32[4,2,32,256]{3,2,1,0:T(8,128)S(1)}, f32[2,32,256]{2,1,0:T(8,128)S(1)}, f32[2,32,256]{2,1,0:T(8,128)S...) custom-call(f32[19,2,32,256]{3,2,1,0:T(8,128)S(1)} %get-tuple-element.54.inner.inner_post, ...), custom_call_target="tpu_custom_call" | custom-call | flops 3276800 | bytes 1966080 | tf_op jit(solution)/shard_map/pallas_call | solution.py:1066
  28.0 1.5 %collective-permute-done.12.edges_first = f32[32,128]{1,0:T(8,128)S(1)} collective-permute-done((f32[32,128]{1,0:T(8,128)S(1)}, f32[32,128]{1,0:T(8,128)S(1)}, u32[]{:S(2)}, u32[]{:S(2)}) %collective-permute-start.12) | collective-permute-done | bytes 16416 | tf_op jit(solution)/shard_map/ppermute | solution.py:950
  29.5 0.9 %collective-permute-done.13.edges_second = f32[32,128]{1,0:T(8,128)S(1)} collective-permute-done((f32[32,128]{1,0:T(8,128)S(1)}, f32[32,128]{1,0:T(8,128)S(1)}, u32[]{:S(2)}, u32[]{:S(2)}) %collective-permute-start.13) | collective-permute-done | bytes 16416 | tf_op jit(solution)/shard_map/ppermute | solution.py:950
  30.5 0.0 collective-permute-done.5.x_second
  30.5 0.0 collective-permute-done.6.x_first
  30.5 0.8 %shard_map.102 = (f32[5,2,32,256]{3,2,1,0:T(8,128)S(1)}, f32[2,32,256]{2,1,0:T(8,128)S(1)}, f32[6,32,256]{2,1,0:T(8,128)S(1)}, f32[8,256]{1,0:T(8,128)S(1)}, f32...) custom-call(f32[19,2,32,256]{3,2,1,0:T(8,128)S(1)} %get-tuple-element.60.outer_post.post, ...), custom_call_target="tpu_custom_call" | custom-call | flops 4915200 | bytes 3276800 | tf_op jit(solution)/shard_map/pallas_call | solution.py:1072
  31.2 1.1 %collective-permute-start.14 = (f32[16,128]{1,0:T(8,128)S(1)}, f32[16,128]{1,0:T(8,128)S(1)}, u32[]{:S(2)}, u32[]{:S(2)}) collective-permute-start(f32[16,128]{1,0:T(8,128)S(1)} %get-tuple-element.82), channel_id=1, source_target_pairs={{0,1},{1,0},{2,3},{3,2},{4,5},{5,4},{6,7},{7,6},{8,9},{9,8},{10,11... | collective-permute-start | bytes 24584 | tf_op jit(solution)/shard_map/ppermute | solution.py:955
  32.3 0.0 collective-permute-start.15
  32.4 1.6 %collective-permute-start.16 = (f32[8,256]{1,0:T(8,128)S(1)}, f32[8,256]{1,0:T(8,128)S(1)}, u32[]{:S(2)}, u32[]{:S(2)}) collective-permute-start(f32[8,256]{1,0:T(8,128)S(1)} %get-tuple-element.84), channel_id=1, source_target_pairs={{0,6},{2,4},{4,2},{6,0},{1,7},{3,5},{5,3},{7,1},{8,14},{10,12},{12... | collective-permute-start | bytes 24584 | tf_op jit(solution)/shard_map/ppermute | solution.py:950
  34.0 1.0 %collective-permute-done.14.z_rows = f32[16,128]{1,0:T(8,128)S(1)} collective-permute-done((f32[16,128]{1,0:T(8,128)S(1)}, f32[16,128]{1,0:T(8,128)S(1)}, u32[]{:S(2)}, u32[]{:S(2)}) %collective-permute-start.14) | collective-permute-done | bytes 8224 | tf_op jit(solution)/shard_map/ppermute | solution.py:955
  34.9 0.0 collective-permute-done.15.y_first
  34.9 0.5 %collective-permute-done.16.y_second = f32[8,256]{1,0:T(8,128)S(1)} collective-permute-done((f32[8,256]{1,0:T(8,128)S(1)}, f32[8,256]{1,0:T(8,128)S(1)}, u32[]{:S(2)}, u32[]{:S(2)}) %collective-permute-start.16) | collective-permute-done | bytes 8224 | tf_op jit(solution)/shard_map/ppermute | solution.py:950
  35.4 0.2 shard_map.104
  35.6 1.8 %collective-permute-start.19 = (f32[32,256]{1,0:T(8,128)S(1)}, f32[32,256]{1,0:T(8,128)S(1)}, u32[]{:S(2)}, u32[]{:S(2)}) collective-permute-start(f32[32,256]{1,0:T(8,128)S(1)} %get-tuple-element.85), channel_id=1, source_target_pairs={{0,24},{8,16},{16,8},{24,0},{1,25},{9,17},{17,9},{25,1},{2,26},{10... | collective-permute-start | bytes 98312 | tf_op jit(solution)/shard_map/ppermute | solution.py:950
  37.4 0.0 collective-permute-start.20
  37.4 1.3 %collective-permute-start.18 = (f32[16,128]{1,0:T(8,128)S(1)}, f32[16,128]{1,0:T(8,128)S(1)}, u32[]{:S(2)}, u32[]{:S(2)}) collective-permute-start(f32[16,128]{1,0:T(8,128)S(1)} %collective-permute-done.14.z_rows), channel_id=1, source_target_pairs={{0,6},{2,4},{4,2},{6,0},{1,7},{3,5},{5,3},{7,1},{8,14},{10,12},{12... | collective-permute-start | bytes 24584 | tf_op jit(solution)/shard_map/ppermute | solution.py:950
  38.7 0.3 collective-permute-start.17
  39.0 2.6 %shard_map.103 = (f32[6,4,32,256]{3,2,1,0:T(8,128)}, f32[19,4,32,256]{3,2,1,0:T(8,128)}) custom-call(f32[6,4,32,256]{3,2,1,0:T(8,128)S(1)} %get-tuple-element.45.stretch, f32[5,4,32,256]{3,2,1,0:T(8,128)S(1)} %get-tuple-element.46.flow, f32[8,32,256]{2,1,0:T(8,128)S(1)} %collective-permute-done.5.x_second, f32[8,32,256]{2,1,0:T(8,128)S(1)} %collective-permute-done.6.x_first, ...), custom_call_target="tpu_custom_call" | custom-call | flops 4915200 | bytes 2621440 | tf_op jit(solution)/shard_map/pallas_call | solution.py:1096
  41.6 0.0 collective-permute-done.18.corner_second
  41.6 0.0 collective-permute-done.17.corner_first
  41.6 0.0 collective-permute-done.19.x_second
  41.6 0.0 collective-permute-done.20.x_first
  41.7 0.9 %shard_map.105 = f32[4,32,256]{2,1,0:T(8,128)} custom-call(f32[2,32,256]{2,1,0:T(8,128)S(1)} %get-tuple-element.79.inner_settled, f32[2,32,256]{2,1,0:T(8,128)S(1)} %get-tuple-element.80.outer_settled, f32[6,32,256]{2,1,0:T(8,128)S(1)} %get-tuple-element.81.spread, f32[16,128]{1,0:T(8,128)S(1)} %collective-permute-done.14.z_rows, ...), custom_call_target="tpu_custom_call" | custom-call | tf_op jit(solution)/shard_map/pallas_call | solution.py:1121
  (1 shorter events, 0.0 us)
Async XLA Ops:
  2.0 11.5 %collective-permute-start = (f32[4,32,256]{2,1,0:T(8,128)S(1)}, f32[4,32,256]{2,1,0:T(8,128)S(1)}, u32[]{:S(2)}, u32[]{:S(2)}) collective-permute-start(f32[4,32,256]{2,1,0:T(8,128)S(1)} %get-tuple-element.49), channel_id=1, source_target_pairs={{0,8},{8,0},{16,24},{24,16},{1,9},{9,1},{17,25},{25,17},{2,10},{10... | collective-permute-start | bytes 393224 | tf_op jit(solution)/shard_map/ppermute | solution.py:950
  5.1 8.6 %collective-permute-start.1 = (f32[4,32,256]{2,1,0:T(8,128)S(1)}, f32[4,32,256]{2,1,0:T(8,128)S(1)}, u32[]{:S(2)}, u32[]{:S(2)}) collective-permute-start(f32[4,32,256]{2,1,0:T(8,128)S(1)} %get-tuple-element.50), channel_id=1, source_target_pairs={{0,24},{8,16},{16,8},{24,0},{1,25},{9,17},{17,9},{25,1},{2,26},{10... | collective-permute-start | bytes 393224 | tf_op jit(solution)/shard_map/ppermute | solution.py:950
  7.6 5.2 %collective-permute-start.2 = (f32[16,256]{1,0:T(8,128)S(1)}, f32[16,256]{1,0:T(8,128)S(1)}, u32[]{:S(2)}, u32[]{:S(2)}) collective-permute-start(f32[16,256]{1,0:T(8,128)S(1)} %get-tuple-element.51), channel_id=1, source_target_pairs={{0,2},{2,0},{4,6},{6,4},{1,3},{3,1},{5,7},{7,5},{8,10},{10,8},{12,... | collective-permute-start | bytes 49160 | tf_op jit(solution)/shard_map/ppermute | solution.py:950
  7.6 5.2 %collective-permute-start.3 = (f32[16,256]{1,0:T(8,128)S(1)}, f32[16,256]{1,0:T(8,128)S(1)}, u32[]{:S(2)}, u32[]{:S(2)}) collective-permute-start(f32[16,256]{1,0:T(8,128)S(1)} %get-tuple-element.52), channel_id=1, source_target_pairs={{0,6},{2,4},{4,2},{6,0},{1,7},{3,5},{5,3},{7,1},{8,14},{10,12},{12... | collective-permute-start | bytes 49160 | tf_op jit(solution)/shard_map/ppermute | solution.py:950
  9.2 3.6 %collective-permute-start.4 = (f32[8,128]{1,0:T(8,128)S(1)}, f32[8,128]{1,0:T(8,128)S(1)}, u32[]{:S(2)}, u32[]{:S(2)}) collective-permute-start(f32[8,128]{1,0:T(8,128)S(1)} %get-tuple-element.53), channel_id=1, source_target_pairs={{0,1},{1,0},{2,3},{3,2},{4,5},{5,4},{6,7},{7,6},{8,9},{9,8},{10,11... | collective-permute-start | bytes 12296 | tf_op jit(solution)/shard_map/ppermute | solution.py:955
  13.7 12.4 %copy-start.1 = (s32[1024]{0:T(1024)S(1)}, s32[1024]{0:T(1024)}, u32[]{:S(2)}) copy-start(s32[1024]{0:T(1024)} %param.11) | copy-start | bytes 12292
  13.7 12.4 %copy-start.2 = (s32[1024]{0:T(1024)S(1)}, s32[1024]{0:T(1024)}, u32[]{:S(2)}) copy-start(s32[1024]{0:T(1024)} %param.12) | copy-start | bytes 12292
  13.7 12.4 %copy-start.3 = (s32[1024]{0:T(1024)S(1)}, s32[1024]{0:T(1024)}, u32[]{:S(2)}) copy-start(s32[1024]{0:T(1024)} %param.13) | copy-start | bytes 12292
  14.7 12.7 %copy-start = (f32[4,32,256]{2,1,0:T(8,128)S(1)}, f32[4,32,256]{2,1,0:T(8,128)}, u32[]{:S(2)}) copy-start(f32[4,32,256]{2,1,0:T(8,128)} %mass.3) | copy-start | bytes 393220
  14.7 15.7 %collective-permute-start.5 = (f32[8,32,256]{2,1,0:T(8,128)S(1)}, f32[8,32,256]{2,1,0:T(8,128)S(1)}, u32[]{:S(2)}, u32[]{:S(2)}) collective-permute-start(f32[8,32,256]{2,1,0:T(8,128)S(1)} %get-tuple-element.55), channel_id=1, source_target_pairs={{0,24},{8,16},{16,8},{24,0},{1,25},{9,17},{17,9},{25,1},{2,26},{10... | collective-permute-start | bytes 786440 | tf_op jit(solution)/shard_map/ppermute | solution.py:950
  16.3 14.2 %collective-permute-start.6 = (f32[8,32,256]{2,1,0:T(8,128)S(1)}, f32[8,32,256]{2,1,0:T(8,128)S(1)}, u32[]{:S(2)}, u32[]{:S(2)}) collective-permute-start(f32[8,32,256]{2,1,0:T(8,128)S(1)} %get-tuple-element.56), channel_id=1, source_target_pairs={{0,8},{8,0},{16,24},{24,16},{1,9},{9,1},{17,25},{25,17},{2,10},{10... | collective-permute-start | bytes 786440 | tf_op jit(solution)/shard_map/ppermute | solution.py:950
  17.1 5.3 %collective-permute-start.7 = (f32[40,256]{1,0:T(8,128)S(1)}, f32[40,256]{1,0:T(8,128)S(1)}, u32[]{:S(2)}, u32[]{:S(2)}) collective-permute-start(f32[40,256]{1,0:T(8,128)S(1)} %get-tuple-element.57), channel_id=1, source_target_pairs={{0,2},{2,0},{4,6},{6,4},{1,3},{3,1},{5,7},{7,5},{8,10},{10,8},{12,... | collective-permute-start | bytes 122888 | tf_op jit(solution)/shard_map/ppermute | solution.py:950
  17.1 5.3 %collective-permute-start.8 = (f32[40,256]{1,0:T(8,128)S(1)}, f32[40,256]{1,0:T(8,128)S(1)}, u32[]{:S(2)}, u32[]{:S(2)}) collective-permute-start(f32[40,256]{1,0:T(8,128)S(1)} %get-tuple-element.58), channel_id=1, source_target_pairs={{0,6},{2,4},{4,2},{6,0},{1,7},{3,5},{5,3},{7,1},{8,14},{10,12},{12... | collective-permute-start | bytes 122888 | tf_op jit(solution)/shard_map/ppermute | solution.py:950
  18.7 3.7 %collective-permute-start.9 = (f32[24,128]{1,0:T(8,128)S(1)}, f32[24,128]{1,0:T(8,128)S(1)}, u32[]{:S(2)}, u32[]{:S(2)}) collective-permute-start(f32[24,128]{1,0:T(8,128)S(1)} %get-tuple-element.59), channel_id=1, source_target_pairs={{0,1},{1,0},{2,3},{3,2},{4,5},{5,4},{6,7},{7,6},{8,9},{9,8},{10,11... | collective-permute-start | bytes 36872 | tf_op jit(solution)/shard_map/ppermute | solution.py:955
  22.4 3.7 %collective-permute-start.11 = (f32[24,128]{1,0:T(8,128)S(1)}, f32[24,128]{1,0:T(8,128)S(1)}, u32[]{:S(2)}, u32[]{:S(2)}) collective-permute-start(f32[24,128]{1,0:T(8,128)S(1)} %get-tuple-element.65), channel_id=1, source_target_pairs={{0,6},{2,4},{4,2},{6,0},{1,7},{3,5},{5,3},{7,1},{8,14},{10,12},{12... | collective-permute-start | bytes 36872 | tf_op jit(solution)/shard_map/ppermute | solution.py:950
  22.5 7.0 %collective-permute-start.12 = (f32[32,128]{1,0:T(8,128)S(1)}, f32[32,128]{1,0:T(8,128)S(1)}, u32[]{:S(2)}, u32[]{:S(2)}) collective-permute-start(f32[32,128]{1,0:T(8,128)S(1)} %get-tuple-element.72), channel_id=1, source_target_pairs={{0,8},{8,0},{16,24},{24,16},{1,9},{9,1},{17,25},{25,17},{2,10},{10... | collective-permute-start | bytes 49160 | tf_op jit(solution)/shard_map/ppermute | solution.py:950
  23.8 6.7 %collective-permute-start.13 = (f32[32,128]{1,0:T(8,128)S(1)}, f32[32,128]{1,0:T(8,128)S(1)}, u32[]{:S(2)}, u32[]{:S(2)}) collective-permute-start(f32[32,128]{1,0:T(8,128)S(1)} %get-tuple-element.73), channel_id=1, source_target_pairs={{0,24},{8,16},{16,8},{24,0},{1,25},{9,17},{17,9},{25,1},{2,26},{10... | collective-permute-start | bytes 49160 | tf_op jit(solution)/shard_map/ppermute | solution.py:950
  26.1 1.3 %collective-permute-start.10 = (f32[24,128]{1,0:T(8,128)S(1)}, f32[24,128]{1,0:T(8,128)S(1)}, u32[]{:S(2)}, u32[]{:S(2)}) collective-permute-start(f32[24,128]{1,0:T(8,128)S(1)} %get-tuple-element.65), channel_id=1, source_target_pairs={{0,2},{2,0},{4,6},{6,4},{1,3},{3,1},{5,7},{7,5},{8,10},{10,8},{12,... | collective-permute-start | bytes 36872 | tf_op jit(solution)/shard_map/ppermute | solution.py:950
  31.2 3.7 %collective-permute-start.14 = (f32[16,128]{1,0:T(8,128)S(1)}, f32[16,128]{1,0:T(8,128)S(1)}, u32[]{:S(2)}, u32[]{:S(2)}) collective-permute-start(f32[16,128]{1,0:T(8,128)S(1)} %get-tuple-element.82), channel_id=1, source_target_pairs={{0,1},{1,0},{2,3},{3,2},{4,5},{5,4},{6,7},{7,6},{8,9},{9,8},{10,11... | collective-permute-start | bytes 24584 | tf_op jit(solution)/shard_map/ppermute | solution.py:955
  32.3 2.6 %collective-permute-start.15 = (f32[8,256]{1,0:T(8,128)S(1)}, f32[8,256]{1,0:T(8,128)S(1)}, u32[]{:S(2)}, u32[]{:S(2)}) collective-permute-start(f32[8,256]{1,0:T(8,128)S(1)} %get-tuple-element.83), channel_id=1, source_target_pairs={{0,2},{2,0},{4,6},{6,4},{1,3},{3,1},{5,7},{7,5},{8,10},{10,8},{12,... | collective-permute-start | bytes 24584 | tf_op jit(solution)/shard_map/ppermute | solution.py:950
  32.4 3.1 %collective-permute-start.16 = (f32[8,256]{1,0:T(8,128)S(1)}, f32[8,256]{1,0:T(8,128)S(1)}, u32[]{:S(2)}, u32[]{:S(2)}) collective-permute-start(f32[8,256]{1,0:T(8,128)S(1)} %get-tuple-element.84), channel_id=1, source_target_pairs={{0,6},{2,4},{4,2},{6,0},{1,7},{3,5},{5,3},{7,1},{8,14},{10,12},{12... | collective-permute-start | bytes 24584 | tf_op jit(solution)/shard_map/ppermute | solution.py:950
  35.6 6.0 %collective-permute-start.19 = (f32[32,256]{1,0:T(8,128)S(1)}, f32[32,256]{1,0:T(8,128)S(1)}, u32[]{:S(2)}, u32[]{:S(2)}) collective-permute-start(f32[32,256]{1,0:T(8,128)S(1)} %get-tuple-element.85), channel_id=1, source_target_pairs={{0,24},{8,16},{16,8},{24,0},{1,25},{9,17},{17,9},{25,1},{2,26},{10... | collective-permute-start | bytes 98312 | tf_op jit(solution)/shard_map/ppermute | solution.py:950
  37.4 4.3 %collective-permute-start.20 = (f32[32,256]{1,0:T(8,128)S(1)}, f32[32,256]{1,0:T(8,128)S(1)}, u32[]{:S(2)}, u32[]{:S(2)}) collective-permute-start(f32[32,256]{1,0:T(8,128)S(1)} %get-tuple-element.86), channel_id=1, source_target_pairs={{0,8},{8,0},{16,24},{24,16},{1,9},{9,1},{17,25},{25,17},{2,10},{10... | collective-permute-start | bytes 98312 | tf_op jit(solution)/shard_map/ppermute | solution.py:950
  37.4 4.2 %collective-permute-start.18 = (f32[16,128]{1,0:T(8,128)S(1)}, f32[16,128]{1,0:T(8,128)S(1)}, u32[]{:S(2)}, u32[]{:S(2)}) collective-permute-start(f32[16,128]{1,0:T(8,128)S(1)} %collective-permute-done.14.z_rows), channel_id=1, source_target_pairs={{0,6},{2,4},{4,2},{6,0},{1,7},{3,5},{5,3},{7,1},{8,14},{10,12},{12... | collective-permute-start | bytes 24584 | tf_op jit(solution)/shard_map/ppermute | solution.py:950
  38.7 2.9 %collective-permute-start.17 = (f32[16,128]{1,0:T(8,128)S(1)}, f32[16,128]{1,0:T(8,128)S(1)}, u32[]{:S(2)}, u32[]{:S(2)}) collective-permute-start(f32[16,128]{1,0:T(8,128)S(1)} %collective-permute-done.14.z_rows), channel_id=1, source_target_pairs={{0,2},{2,0},{4,6},{6,4},{1,3},{3,1},{5,7},{7,5},{8,10},{10,8},{12,... | collective-permute-start | bytes 24584 | tf_op jit(solution)/shard_map/ppermute | solution.py:950

commit v2 on v1

--- a/solution.py
+++ b/solution.py
@@ -406,21 +406,74 @@
         behind[5 + comp] = jnp.where(flip_x, up, down)
 
 
-def restretch(
+def restretch_plane(x, place, stretch, flow, halos, updated):
+    chunks = stretch.shape[2] // tall
+    for chunk in range(chunks):
+        rows = pl.ds(chunk * tall, tall)
+        grad = [
+            differences(
+                flow, comp, (comp, comp, comp), x, chunk, chunks, *halos, speed_slot, sides
+            )
+            for comp in range(3)
+        ]
+        part = [stretch[slot, x, rows, :] for slot in range(6)]
+        full = [part[slot] + 1.0 if slot < 3 else part[slot] for slot in range(6)]
+
+        def product(row, col):
+            total = grad[row][0] * full[symmetric_slot[0][col]]
+            for inner in (1, 2):
+                total = total + grad[row][inner] * full[symmetric_slot[inner][col]]
+            return total
+
+        for slot, (row, col) in enumerate(tensor_pairs):
+            old = (1.0 - 1.0 / polymer_time) * part[slot]
+            if row == col:
+                updated[slot, place, rows, :] = old + product(row, col)
+            else:
+                updated[slot, place, rows, :] = old + 0.5 * (product(row, col) + product(col, row))
+
+
+def restretch_inner(
     stretch,
     flow,
-    x_second,
-    x_first,
     y_first,
     y_second,
     z_rows,
-    inner,
-    outer,
-    inner_slanted,
-    outer_slanted,
-    late,
+    new_stretch,
+    mark,
     updated,
-    fresh,
+    y_below,
+    y_above,
+    z_halo,
+    sem,
+):
+    bx = stretch.shape[1]
+    swapped_rows(y_first, y_second, range(speed_slot, sides), y_below, y_above, 0)
+    z_halo[...] = row_columns(z_rows[...]).reshape(z_halo.shape)
+    halos = (None, None, y_below, y_above, z_halo)
+
+    def plane(x, carry):
+        restretch_plane(x, x - 1, stretch, flow, halos, updated)
+        return carry
+
+    lax.fori_loop(1, bx - 1, plane, 0)
+    copy = pltpu.make_async_copy(updated, new_stretch.at[:, 1 : bx - 1], sem)
+    copy.start()
+    mark[...] = jnp.zeros(mark.shape, jnp.float32)
+    copy.wait()
+
+
+def restretch_outer(
+    stretch,
+    flow,
+    x_first,
+    x_second,
+    y_first,
+    y_second,
+    z_rows,
+    inner_stretch,
+    new_stretch,
+    updated,
     below,
     above,
     y_below,
@@ -428,7 +481,27 @@
     z_halo,
     sems,
 ):
-    bx, by, bz = stretch.shape[1:]
+    bx = stretch.shape[1]
+    flip_x = odd("gx")
+    for comp in range(3):
+        below[comp] = jnp.where(flip_x, x_first[5 + comp], x_second[5 + comp])
+        above[comp] = jnp.where(flip_x, x_second[5 + comp], x_first[5 + comp])
+    swapped_rows(y_first, y_second, range(speed_slot, sides), y_below, y_above, 0)
+    z_halo[...] = row_columns(z_rows[...]).reshape(z_halo.shape)
+    halos = (below, above, y_below, y_above, z_halo)
+    copies = []
+    for place, x in enumerate((0, bx - 1)):
+        restretch_plane(x, place, stretch, flow, halos, updated)
+        copies.append(
+            pltpu.make_async_copy(updated.at[:, place], new_stretch.at[:, x], sems.at[place])
+        )
+        copies[-1].start()
+    for copy in copies:
+        copy.wait()
+
+
+def store(inner, outer, inner_slanted, outer_slanted, late, fresh, mark, sems):
+    bx = fresh.shape[1]
     moves = [
         (inner, fresh.at[0:first_slanted, 1 : bx - 1]),
         (inner_slanted, fresh.at[first_slanted:, 1 : bx - 1]),
@@ -450,52 +523,7 @@
     ]
     for copy in copies:
         copy.start()
-    chunks = by // tall
-    flip_x = odd("gx")
-    below[...] = select(flip_x, x_first, x_second)
-    above[...] = select(flip_x, x_second, x_first)
-    swapped_rows(y_first, y_second, range(speed_slot, sides), y_below, y_above, 0)
-    z_halo[...] = row_columns(z_rows[...]).reshape(z_halo.shape)
-
-    def plane(x, carry):
-        for chunk in range(chunks):
-            rows = pl.ds(chunk * tall, tall)
-            grad = [
-                differences(
-                    flow,
-                    comp,
-                    (5 + comp, comp, comp),
-                    x,
-                    chunk,
-                    chunks,
-                    below,
-                    above,
-                    y_below,
-                    y_above,
-                    z_halo,
-                    speed_slot,
-                    sides,
-                )
-                for comp in range(3)
-            ]
-            part = [stretch[slot, x, rows, :] for slot in range(6)]
-            full = [part[slot] + 1.0 if slot < 3 else part[slot] for slot in range(6)]
-
-            def product(row, col):
-                total = grad[row][0] * full[symmetric_slot[0][col]]
-                for inner in (1, 2):
-                    total = total + grad[row][inner] * full[symmetric_slot[inner][col]]
-                return total
-
-            for slot, (row, col) in enumerate(tensor_pairs):
-                old = (1.0 - 1.0 / polymer_time) * part[slot]
-                if row == col:
-                    updated[slot, x, rows, :] = old + product(row, col)
-                else:
-                    updated[slot, x, rows, :] = old + 0.5 * (product(row, col) + product(col, row))
-        return carry
-
-    lax.fori_loop(0, bx, plane, 0)
+    mark[...] = jnp.zeros(mark.shape, jnp.float32)
     for copy in copies:
         copy.wait()
 
@@ -740,12 +768,13 @@
     changes,
     gas_first,
     gas_second,
+    x_first,
     x_second,
-    x_first,
     edges_first,
     edges_second,
     inner_excess,
     inner_heading,
+    after,
     late,
     settled,
     spread,
@@ -893,7 +922,7 @@
     return total + jnp.where(row_at == by - 1, y_above[target : target + 1, :], 0.0)
 
 
-def add_faces(spread, z_rows, y_first, y_second, first, second):
+def add_faces(spread, z_rows, y_first, y_second, after, first, second):
     last = spread.shape[0] - 1
     flip_x, flip_y = (odd("gx"), odd("gy"))
     tile = row_columns(z_rows[...])
@@ -962,7 +991,7 @@
 remote = pl.BlockSpec(memory_space=pltpu.HBM)
 
 
-def call(body, outs, specs=None, out_specs=None, scratch=(), cost=(0, 0)):
+def call(body, outs, specs=None, out_specs=None, scratch=(), cost=(0, 0), aliases=None):
     extra = {} if specs is None else {"in_specs": specs}
     if out_specs is not None:
         extra["out_specs"] = out_specs
@@ -979,6 +1008,7 @@
             for shape in scratch
         ],
         compiler_params=pltpu.CompilerParams(vmem_limit_bytes=40 * 1024 * 1024),
+        input_output_aliases=aliases or {},
         cost_estimate=pl.CostEstimate(flops=cost[0], bytes_accessed=cost[1], transcendentals=0),
         **extra,
     )
@@ -1069,6 +1099,14 @@
         scratch=rims,
         cost=(100 * cells, 60 * cells),
     )(*posts, mass, flags, code, *post_y, z_post, *corners, totals, changes)
+    mark = (tall, lanes)
+    new_stretch, inner_done = call(
+        restretch_inner,
+        [(6, *box), mark],
+        out_specs=[remote, pl.BlockSpec()],
+        scratch=[(6, *inside)] + sides_y + [pltpu.SemaphoreType.DMA],
+        cost=(80 * cells, 40 * cells),
+    )(stretch, flow, *post_y, z_post)
     late, outer_settled, spread, y_one, y_two, z_out = call(
         stream_late,
         [(5, *ends), ends, (bx + 2, *face), (8, bz), (8, bz), (16, bx * by)],
@@ -1083,41 +1121,35 @@
         totals,
         changes,
         *first_x,
-        *post_x[::-1],
+        *post_x,
         *edges_x,
         inner_excess,
         inner_heading,
+        inner_done,
     )
     z_last = both_ways(z_out, 8)
     last_y = swapped(y_one, y_two, "gy")
     last_corners = swapped(z_last, z_last, "gy")
-    x_one, x_two = call(add_faces, [face, face])(spread, z_last, *last_y)
+    fresh, stored = call(
+        store,
+        [(19, *box), mark],
+        out_specs=[remote, pl.BlockSpec()],
+        scratch=[pltpu.SemaphoreType.DMA((32,))],
+        cost=(0, 160 * cells),
+    )(inner, outer, inner_slanted, outer_slanted, late)
+    x_one, x_two = call(add_faces, [face, face])(spread, z_last, *last_y, stored)
     last_x = swapped(x_one, x_two, "gx")
-    new_stretch, fresh = call(
-        restretch,
-        [(6, *box), (19, *box)],
-        out_specs=[pl.BlockSpec(), remote],
-        scratch=[
-            (8, *face),
-            (8, *face),
-            (bx, 8, bz),
-            (bx, 8, bz),
-            tile,
-            pltpu.SemaphoreType.DMA((32,)),
-        ],
-        cost=(150 * cells, 80 * cells),
-    )(
-        stretch,
-        flow,
-        *post_x[::-1],
-        *post_y,
-        z_post,
-        inner,
-        outer,
-        inner_slanted,
-        outer_slanted,
-        late,
-    )
+    (new_stretch,) = call(
+        restretch_outer,
+        [(6, *box)],
+        specs=[pl.BlockSpec()] * 7 + [remote],
+        out_specs=[remote],
+        scratch=[(6, *ends), (3, *face), (3, *face)]
+        + sides_y
+        + [pltpu.SemaphoreType.DMA((2,))],
+        cost=(80 * cells, 40 * cells),
+        aliases={7: 0},
+    )(stretch, flow, *post_x, *post_y, z_post, new_stretch)
     (new_mass,) = call(add_all, [box])(
         inner_settled, outer_settled, spread, z_last, *last_y, *last_corners, *last_x[::-1]
     )

time: 42.7 us -> 42.3 us (level)
  starting transfers between devices: 24 us -> 22.4 us
  Pallas kernels: 11.1 us -> 12.5 us
    ppermute x9, waiting for transfers between devices: 1.58 us -> 3.79 us  [swapped(): lax.ppermute(second, axis, behind)]
    ppermute x9, waiting for transfers between devices: 1.53 us -> 0.02 us  [swapped(): lax.ppermute(first, axis, ahead)]
    pallas_call x2 -> x4, Pallas kernels: 2.75 us -> 4.13 us  [the longest x1 1.7 us: shards(): call(store, [(19, *box), mark], out_specs=[remote, pl.BlockSpec()], scrat...]
    ppermute x9, starting transfers between devices: 5.49 us -> 4.3 us  [swapped(): lax.ppermute(first, axis, ahead)]
    ppermute x3, waiting for transfers between devices: 3.5 us -> 2.52 us  [both_ways(): lax.ppermute(rows, 'gz', [(i, (i + 1) % devices) for i in range(devices)])]
    ppermute x9, starting transfers between devices: 14.3 us -> 13.5 us  [swapped(): lax.ppermute(second, axis, behind)]
    ppermute x3, starting transfers between devices: 4.14 us -> 4.61 us  [both_ways(): lax.ppermute(rows, 'gz', [(i, (i + 1) % devices) for i in range(devices)])]
  transfers between devices with their start and end apart: 21 -> 21, of which waited for: 7 -> 7; matrix products, arithmetic and copies ran while one was open for 0% -> 0% of each run, Pallas kernels for 16% -> 20%
where the time goes in v2:
time: 42.3 us; the launch traced here: 42.1 us
  starting transfers between devices  22.4 us (53%)
  Pallas kernels  12.5 us (30%)
  waiting for transfers between devices  6.34 us (15%)
  between operations  0.83 us (2%)
    ppermute x9, starting transfers between devices, swapped(): lax.ppermute(second, axis, behind)  13.5 us
    ppermute x3, starting transfers between devices, both_ways(): lax.ppermute(rows, 'gz', [(i, (i + 1) % devices) for i in range(devices)])  4.61 us
    ppermute x9, starting transfers between devices, swapped(): lax.ppermute(first, axis, ahead)  4.3 us
    ppermute x9, waiting for transfers between devices, swapped(): lax.ppermute(second, axis, behind)  3.79 us
    ppermute x3, waiting for transfers between devices, both_ways(): lax.ppermute(rows, 'gz', [(i, (i + 1) % devices) for i in range(devices)])  2.52 us
    pallas_call x1, Pallas kernels, shards(): call(moments, [(19, *box), (5, *box)], specs=[remote], scratch=[pltpu.Sem...  1.74 us
    pallas_call x1, Pallas kernels, shards(): call(store, [(19, *box), mark], out_specs=[remote, pl.BlockSpec()], scrat...  1.7 us
    pallas_call x1, Pallas kernels, shards(): call(first_faces, [(6, *box), jax.ShapeDtypeStruct(box, jnp.int32), (8, b...  1.38 us
  transfers between devices with their start and end apart: 21, of which 7 were waited for; matrix products, arithmetic and copies ran while one was open for 0% of the time, Pallas kernels for 20%

profile of v2, /device:TPU:0, one launch (start us, length us, event | category | flops | bytes accessed | tf_op | source)
XLA Modules:
  0.0 42.1 jit_solution(15549676064010760835)
XLA Ops:
  0.6 1.4 %shard_map.95 = (f32[6,4,32,256]{3,2,1,0:T(8,128)S(1)}, s32[4,32,256]{2,1,0:T(8,128)S(1)}, f32[8,128]{1,0:T(8,128)S(1)}, f32[16,256]{1,0:T(8,128)S(1)}, f32[16,2...) custom-call(f32[6,4,32,256]{3,2,1,0:T(8,128)} %stretch_in.1, s32[4,32,256]{2,1,0:T(8,128)} %flags_in.1), custom_call_target="tpu_custom_call" | custom-call | flops 327680 | bytes 1966080 | tf_op jit(solution)/shard_map/pallas_call | solution.py:1022
  2.0 3.1 %collective-permute-start.3 = (f32[4,32,256]{2,1,0:T(8,128)S(1)}, f32[4,32,256]{2,1,0:T(8,128)S(1)}, u32[]{:S(2)}, u32[]{:S(2)}) collective-permute-start(f32[4,32,256]{2,1,0:T(8,128)S(1)} %get-tuple-element.55), channel_id=1, source_target_pairs={{0,8},{8,0},{16,24},{24,16},{1,9},{9,1},{17,25},{25,17},{2,10},{10... | collective-permute-start | bytes 393224 | tf_op jit(solution)/shard_map/ppermute | solution.py:979
  5.1 2.5 %collective-permute-start.4 = (f32[4,32,256]{2,1,0:T(8,128)S(1)}, f32[4,32,256]{2,1,0:T(8,128)S(1)}, u32[]{:S(2)}, u32[]{:S(2)}) collective-permute-start(f32[4,32,256]{2,1,0:T(8,128)S(1)} %get-tuple-element.56), channel_id=1, source_target_pairs={{0,24},{8,16},{16,8},{24,0},{1,25},{9,17},{17,9},{25,1},{2,26},{10... | collective-permute-start | bytes 393224 | tf_op jit(solution)/shard_map/ppermute | solution.py:979
  7.6 0.0 collective-permute-start.1
  7.6 1.6 %collective-permute-start.2 = (f32[16,256]{1,0:T(8,128)S(1)}, f32[16,256]{1,0:T(8,128)S(1)}, u32[]{:S(2)}, u32[]{:S(2)}) collective-permute-start(f32[16,256]{1,0:T(8,128)S(1)} %get-tuple-element.52), channel_id=1, source_target_pairs={{0,6},{2,4},{4,2},{6,0},{1,7},{3,5},{5,3},{7,1},{8,14},{10,12},{12... | collective-permute-start | bytes 49160 | tf_op jit(solution)/shard_map/ppermute | solution.py:979
  9.2 1.5 %collective-permute-start = (f32[8,128]{1,0:T(8,128)S(1)}, f32[8,128]{1,0:T(8,128)S(1)}, u32[]{:S(2)}, u32[]{:S(2)}) collective-permute-start(f32[8,128]{1,0:T(8,128)S(1)} %get-tuple-element.50), channel_id=1, source_target_pairs={{0,1},{1,0},{2,3},{3,2},{4,5},{5,4},{6,7},{7,6},{8,9},{9,8},{10,11... | collective-permute-start | bytes 12296 | tf_op jit(solution)/shard_map/ppermute | solution.py:984
  10.7 1.7 %shard_map.94 = (f32[19,4,32,256]{3,2,1,0:T(8,128)S(1)}, f32[5,4,32,256]{3,2,1,0:T(8,128)S(1)}) custom-call(f32[19,4,32,256]{3,2,1,0:T(8,128)} %pops_in.1), custom_call_target="tpu_custom_call" | custom-call | flops 1966080 | bytes 4915200 | tf_op jit(solution)/shard_map/pallas_call | solution.py:1047
  12.5 0.3 collective-permute-done.z_rows
  12.8 0.0 collective-permute-done.1.y_first
  12.8 0.0 collective-permute-done.2.y_second
  12.8 0.8 %shard_map.96 = (f32[19,2,32,256]{3,2,1,0:T(8,128)S(1)}, f32[3,2,32,256]{3,2,1,0:T(8,128)S(1)}) custom-call(f32[19,4,32,256]{3,2,1,0:T(8,128)S(1)} %get-tuple-element.47.pops, f32[6,4,32,256]{3,2,1,0:T(8,128)S(1)} %get-tuple-element.48.stretch, f32[5,4,32,256]{3,2,1,0:T(8,128)S(1)} %get-tuple-element.49.flow, f32[8,128]{1,0:T(8,128)S(1)} %collective-permute-done.z_rows, ...), custom_call_target="tpu_custom_call" | custom-call | flops 4915200 | bytes 4915200 | tf_op jit(solution)/shard_map/pallas_call | solution.py:1058
  13.6 0.0 collective-permute-done.3.x_first.gas_first
  13.6 0.1 collective-permute-done.4.x_second.gas_second
  13.7 0.0 copy-start.1
  13.7 0.0 copy-start.2
  13.7 0.0 copy-start.3
  13.7 1.0 %shard_map.97 = (f32[19,2,32,256]{3,2,1,0:T(8,128)S(1)}, f32[3,2,32,256]{3,2,1,0:T(8,128)S(1)}, f32[24,128]{1,0:T(8,128)S(1)}, f32[8,32,256]{2,1,0:T(8,128)S(1)}...) custom-call(f32[19,4,32,256]{3,2,1,0:T(8,128)S(1)} %get-tuple-element.47.pops, ...), custom_call_target="tpu_custom_call" | custom-call | flops 4915200 | bytes 4915200 | tf_op jit(solution)/shard_map/pallas_call | solution.py:1064
  14.7 0.0 copy-start
  14.7 0.6 %collective-permute-start.10 = (f32[8,32,256]{2,1,0:T(8,128)S(1)}, f32[8,32,256]{2,1,0:T(8,128)S(1)}, u32[]{:S(2)}, u32[]{:S(2)}) collective-permute-start(f32[8,32,256]{2,1,0:T(8,128)S(1)} %get-tuple-element.72), channel_id=1, source_target_pairs={{0,8},{8,0},{16,24},{24,16},{1,9},{9,1},{17,25},{25,17},{2,10},{10... | collective-permute-start | bytes 786440 | tf_op jit(solution)/shard_map/ppermute | solution.py:979
  15.4 2.6 %collective-permute-start.11 = (f32[8,32,256]{2,1,0:T(8,128)S(1)}, f32[8,32,256]{2,1,0:T(8,128)S(1)}, u32[]{:S(2)}, u32[]{:S(2)}) collective-permute-start(f32[8,32,256]{2,1,0:T(8,128)S(1)} %get-tuple-element.73), channel_id=1, source_target_pairs={{0,24},{8,16},{16,8},{24,0},{1,25},{9,17},{17,9},{25,1},{2,26},{10... | collective-permute-start | bytes 786440 | tf_op jit(solution)/shard_map/ppermute | solution.py:979
  18.0 0.0 collective-permute-start.5
  18.0 1.6 %collective-permute-start.6 = (f32[40,256]{1,0:T(8,128)S(1)}, f32[40,256]{1,0:T(8,128)S(1)}, u32[]{:S(2)}, u32[]{:S(2)}) collective-permute-start(f32[40,256]{1,0:T(8,128)S(1)} %get-tuple-element.61), channel_id=1, source_target_pairs={{0,6},{2,4},{4,2},{6,0},{1,7},{3,5},{5,3},{7,1},{8,14},{10,12},{12... | collective-permute-start | bytes 122888 | tf_op jit(solution)/shard_map/ppermute | solution.py:979
  19.6 1.5 %collective-permute-start.7 = (f32[24,128]{1,0:T(8,128)S(1)}, f32[24,128]{1,0:T(8,128)S(1)}, u32[]{:S(2)}, u32[]{:S(2)}) collective-permute-start(f32[24,128]{1,0:T(8,128)S(1)} %get-tuple-element.62), channel_id=1, source_target_pairs={{0,1},{1,0},{2,3},{3,2},{4,5},{5,4},{6,7},{7,6},{8,9},{9,8},{10,11... | collective-permute-start | bytes 36872 | tf_op jit(solution)/shard_map/ppermute | solution.py:984
  21.1 2.2 %collective-permute-done.7.z_rows.refs_0_ = f32[24,128]{1,0:T(8,128)S(1)} collective-permute-done((f32[24,128]{1,0:T(8,128)S(1)}, f32[24,128]{1,0:T(8,128)S(1)}, u32[]{:S(2)}, u32[]{:S(2)}) %collective-permute-start.7) | collective-permute-done | bytes 12320 | tf_op jit(solution)/shard_map/ppermute | solution.py:984
  23.3 0.0 collective-permute-done.5.y_first.refs_1_
  23.3 0.0 collective-permute-done.6.y_second.refs_2_
  23.3 0.1 collective-permute-start.9
  23.4 0.1 collective-permute-start.12
  23.5 1.7 %collective-permute-start.13 = (f32[32,128]{1,0:T(8,128)S(1)}, f32[32,128]{1,0:T(8,128)S(1)}, u32[]{:S(2)}, u32[]{:S(2)}) collective-permute-start(f32[32,128]{1,0:T(8,128)S(1)} %get-tuple-element.75), channel_id=1, source_target_pairs={{0,24},{8,16},{16,8},{24,0},{1,25},{9,17},{17,9},{25,1},{2,26},{10... | collective-permute-start | bytes 49160 | tf_op jit(solution)/shard_map/ppermute | solution.py:979
  25.2 1.3 %collective-permute-done.9.corner_second = f32[24,128]{1,0:T(8,128)S(1)} collective-permute-done((f32[24,128]{1,0:T(8,128)S(1)}, f32[24,128]{1,0:T(8,128)S(1)}, u32[]{:S(2)}, u32[]{:S(2)}) %collective-permute-start.9) | collective-permute-done | bytes 12320 | tf_op jit(solution)/shard_map/ppermute | solution.py:979
  26.5 0.0 collective-permute-start.8
  26.5 0.0 copy-done.1
  26.5 0.0 copy-done.2
  26.5 0.0 copy-done.3
  26.5 0.3 shard_map.99
  26.9 1.2 %shard_map.102 = (f32[6,4,32,256]{3,2,1,0:T(8,128)}, f32[8,128]{1,0:T(8,128)S(1)}) custom-call(f32[6,4,32,256]{3,2,1,0:T(8,128)S(1)} %get-tuple-element.48.stretch, f32[5,4,32,256]{3,2,1,0:T(8,128)S(1)} %get-tuple-element.49.flow, f32[40,256]{1,0:T(8,128)S(1)} %collective-permute-done.5.y_first.refs_1_, ...), custom_call_target="tpu_custom_call" | custom-call | flops 2621440 | bytes 1310720 | tf_op jit(solution)/shard_map/pallas_call | solution.py:1103
  28.1 0.9 %shard_map.98 = (f32[15,2,32,256]{3,2,1,0:T(8,128)S(1)}, f32[15,2,32,256]{3,2,1,0:T(8,128)S(1)}, f32[4,32,256]{2,1,0:T(8,128)S(1)}, f32[4,32,256]{2,1,0:T(8,128)S(1)}) custom-call(f32[19,2,32,256]{3,2,1,0:T(8,128)S(1)} %get-tuple-element.53.inner.inner_post, f32[19,2,32,256]{3,2,1,0:T(8,128)S(1)} %get-tuple-element.57.outer_post.post, ...), custom_call_target="tpu_custom_call" | custom-call | flops 11468800 | bytes 6553600 | tf_op jit(solution)/shard_map/pallas_call | solution.py:1082
  29.0 0.0 collective-permute-done.8.corner_first
  29.0 0.0 copy-done
  29.0 0.6 %shard_map.101 = (f32[4,2,32,256]{3,2,1,0:T(8,128)S(1)}, f32[4,2,32,256]{3,2,1,0:T(8,128)S(1)}, f32[2,32,256]{2,1,0:T(8,128)S(1)}, f32[2,32,256]{2,1,0:T(8,128)S...) custom-call(f32[19,2,32,256]{3,2,1,0:T(8,128)S(1)} %get-tuple-element.53.inner.inner_post, ...), custom_call_target="tpu_custom_call" | custom-call | flops 3276800 | bytes 1966080 | tf_op jit(solution)/shard_map/pallas_call | solution.py:1096
  29.6 0.0 collective-permute-done.12.edges_first
  29.6 0.0 collective-permute-done.13.edges_second
  29.6 0.0 collective-permute-done.10.x_first
  29.6 0.0 collective-permute-done.11.x_second
  29.7 0.8 %shard_map.103 = (f32[5,2,32,256]{3,2,1,0:T(8,128)S(1)}, f32[2,32,256]{2,1,0:T(8,128)S(1)}, f32[6,32,256]{2,1,0:T(8,128)S(1)}, f32[8,256]{1,0:T(8,128)S(1)}, f32...) custom-call(f32[19,2,32,256]{3,2,1,0:T(8,128)S(1)} %get-tuple-element.57.outer_post.post, ...), custom_call_target="tpu_custom_call" | custom-call | flops 4915200 | bytes 3276800 | tf_op jit(solution)/shard_map/pallas_call | solution.py:1110
  30.4 1.6 %collective-permute-start.14 = (f32[16,128]{1,0:T(8,128)S(1)}, f32[16,128]{1,0:T(8,128)S(1)}, u32[]{:S(2)}, u32[]{:S(2)}) collective-permute-start(f32[16,128]{1,0:T(8,128)S(1)} %get-tuple-element.85), channel_id=1, source_target_pairs={{0,1},{1,0},{2,3},{3,2},{4,5},{5,4},{6,7},{7,6},{8,9},{9,8},{10,11... | collective-permute-start | bytes 24584 | tf_op jit(solution)/shard_map/ppermute | solution.py:984
  32.0 0.2 collective-permute-start.15
  32.2 1.2 %collective-permute-start.16 = (f32[8,256]{1,0:T(8,128)S(1)}, f32[8,256]{1,0:T(8,128)S(1)}, u32[]{:S(2)}, u32[]{:S(2)}) collective-permute-start(f32[8,256]{1,0:T(8,128)S(1)} %get-tuple-element.87), channel_id=1, source_target_pairs={{0,6},{2,4},{4,2},{6,0},{1,7},{3,5},{5,3},{7,1},{8,14},{10,12},{12... | collective-permute-start | bytes 24584 | tf_op jit(solution)/shard_map/ppermute | solution.py:979
  33.4 1.7 %shard_map.104 = (f32[19,4,32,256]{3,2,1,0:T(8,128)}, f32[8,128]{1,0:T(8,128)S(1)}) custom-call(f32[15,2,32,256]{3,2,1,0:T(8,128)S(1)} %get-tuple-element.63.inner, f32[15,2,32,256]{3,2,1,0:T(8,128)S(1)} %get-tuple-element.64.outer, f32[4,2,32,256]{3,2,1,0:T(8,128)S(1)} %get-tuple-element.68.inner_slanted, ...), custom_call_target="tpu_custom_call" | custom-call | bytes 5242880 | tf_op jit(solution)/shard_map/pallas_call | solution.py:1133
  35.1 0.0 collective-permute-done.14.z_rows
  35.1 0.0 collective-permute-done.15.y_first
  35.1 0.1 collective-permute-done.16.y_second
  35.3 0.2 shard_map.106
  35.5 1.2 %collective-permute-start.19 = (f32[32,256]{1,0:T(8,128)S(1)}, f32[32,256]{1,0:T(8,128)S(1)}, u32[]{:S(2)}, u32[]{:S(2)}) collective-permute-start(f32[32,256]{1,0:T(8,128)S(1)} %get-tuple-element.89), channel_id=1, source_target_pairs={{0,24},{8,16},{16,8},{24,0},{1,25},{9,17},{17,9},{25,1},{2,26},{10... | collective-permute-start | bytes 98312 | tf_op jit(solution)/shard_map/ppermute | solution.py:979
  36.7 0.0 collective-permute-start.20
  36.7 1.0 %collective-permute-start.18 = (f32[16,128]{1,0:T(8,128)S(1)}, f32[16,128]{1,0:T(8,128)S(1)}, u32[]{:S(2)}, u32[]{:S(2)}) collective-permute-start(f32[16,128]{1,0:T(8,128)S(1)} %collective-permute-done.14.z_rows), channel_id=1, source_target_pairs={{0,6},{2,4},{4,2},{6,0},{1,7},{3,5},{5,3},{7,1},{8,14},{10,12},{12... | collective-permute-start | bytes 24584 | tf_op jit(solution)/shard_map/ppermute | solution.py:979
  37.7 0.3 collective-permute-start.17
  38.0 1.1 %shard_map.105 = f32[6,4,32,256]{3,2,1,0:T(8,128)} custom-call(f32[6,4,32,256]{3,2,1,0:T(8,128)S(1)} %get-tuple-element.48.stretch, f32[5,4,32,256]{3,2,1,0:T(8,128)S(1)} %get-tuple-element.49.flow, f32[8,32,256]{2,1,0:T(8,128)S(1)} %collective-permute-done.10.x_first, ...), custom_call_target="tpu_custom_call", output_to_operand_aliasing={{}: (7, {})} | custom-call | flops 2621440 | bytes 1310720 | tf_op jit(solution)/shard_map/pallas_call | solution.py:1142
  39.1 0.7 %collective-permute-done.18.corner_second = f32[16,128]{1,0:T(8,128)S(1)} collective-permute-done((f32[16,128]{1,0:T(8,128)S(1)}, f32[16,128]{1,0:T(8,128)S(1)}, u32[]{:S(2)}, u32[]{:S(2)}) %collective-permute-start.18) | collective-permute-done | bytes 8224 | tf_op jit(solution)/shard_map/ppermute | solution.py:979
  39.8 0.0 collective-permute-done.17.corner_first
  39.8 1.5 %collective-permute-done.19.x_second = f32[32,256]{1,0:T(8,128)S(1)} collective-permute-done((f32[32,256]{1,0:T(8,128)S(1)}, f32[32,256]{1,0:T(8,128)S(1)}, u32[]{:S(2)}, u32[]{:S(2)}) %collective-permute-start.19) | collective-permute-done | bytes 32800 | tf_op jit(solution)/shard_map/ppermute | solution.py:979
  41.3 0.0 collective-permute-done.20.x_first
  41.3 0.9 %shard_map.107 = f32[4,32,256]{2,1,0:T(8,128)} custom-call(f32[2,32,256]{2,1,0:T(8,128)S(1)} %get-tuple-element.82.inner_settled, f32[2,32,256]{2,1,0:T(8,128)S(1)} %get-tuple-element.83.outer_settled, f32[6,32,256]{2,1,0:T(8,128)S(1)} %get-tuple-element.84.spread, f32[16,128]{1,0:T(8,128)S(1)} %collective-permute-done.14.z_rows, ...), custom_call_target="tpu_custom_call" | custom-call | tf_op jit(solution)/shard_map/pallas_call | solution.py:1153
  (1 shorter events, 0.0 us)
Async XLA Ops:
  2.0 11.5 %collective-permute-start.3 = (f32[4,32,256]{2,1,0:T(8,128)S(1)}, f32[4,32,256]{2,1,0:T(8,128)S(1)}, u32[]{:S(2)}, u32[]{:S(2)}) collective-permute-start(f32[4,32,256]{2,1,0:T(8,128)S(1)} %get-tuple-element.55), channel_id=1, source_target_pairs={{0,8},{8,0},{16,24},{24,16},{1,9},{9,1},{17,25},{25,17},{2,10},{10... | collective-permute-start | bytes 393224 | tf_op jit(solution)/shard_map/ppermute | solution.py:979
  5.1 8.6 %collective-permute-start.4 = (f32[4,32,256]{2,1,0:T(8,128)S(1)}, f32[4,32,256]{2,1,0:T(8,128)S(1)}, u32[]{:S(2)}, u32[]{:S(2)}) collective-permute-start(f32[4,32,256]{2,1,0:T(8,128)S(1)} %get-tuple-element.56), channel_id=1, source_target_pairs={{0,24},{8,16},{16,8},{24,0},{1,25},{9,17},{17,9},{25,1},{2,26},{10... | collective-permute-start | bytes 393224 | tf_op jit(solution)/shard_map/ppermute | solution.py:979
  7.6 5.2 %collective-permute-start.1 = (f32[16,256]{1,0:T(8,128)S(1)}, f32[16,256]{1,0:T(8,128)S(1)}, u32[]{:S(2)}, u32[]{:S(2)}) collective-permute-start(f32[16,256]{1,0:T(8,128)S(1)} %get-tuple-element.51), channel_id=1, source_target_pairs={{0,2},{2,0},{4,6},{6,4},{1,3},{3,1},{5,7},{7,5},{8,10},{10,8},{12,... | collective-permute-start | bytes 49160 | tf_op jit(solution)/shard_map/ppermute | solution.py:979
  7.6 5.2 %collective-permute-start.2 = (f32[16,256]{1,0:T(8,128)S(1)}, f32[16,256]{1,0:T(8,128)S(1)}, u32[]{:S(2)}, u32[]{:S(2)}) collective-permute-start(f32[16,256]{1,0:T(8,128)S(1)} %get-tuple-element.52), channel_id=1, source_target_pairs={{0,6},{2,4},{4,2},{6,0},{1,7},{3,5},{5,3},{7,1},{8,14},{10,12},{12... | collective-permute-start | bytes 49160 | tf_op jit(solution)/shard_map/ppermute | solution.py:979
  9.2 3.6 %collective-permute-start = (f32[8,128]{1,0:T(8,128)S(1)}, f32[8,128]{1,0:T(8,128)S(1)}, u32[]{:S(2)}, u32[]{:S(2)}) collective-permute-start(f32[8,128]{1,0:T(8,128)S(1)} %get-tuple-element.50), channel_id=1, source_target_pairs={{0,1},{1,0},{2,3},{3,2},{4,5},{5,4},{6,7},{7,6},{8,9},{9,8},{10,11... | collective-permute-start | bytes 12296 | tf_op jit(solution)/shard_map/ppermute | solution.py:984
  13.7 12.8 %copy-start.1 = (s32[1024]{0:T(1024)S(1)}, s32[1024]{0:T(1024)}, u32[]{:S(2)}) copy-start(s32[1024]{0:T(1024)} %param.11) | copy-start | bytes 12292
  13.7 12.8 %copy-start.2 = (s32[1024]{0:T(1024)S(1)}, s32[1024]{0:T(1024)}, u32[]{:S(2)}) copy-start(s32[1024]{0:T(1024)} %param.12) | copy-start | bytes 12292
  13.7 12.8 %copy-start.3 = (s32[1024]{0:T(1024)S(1)}, s32[1024]{0:T(1024)}, u32[]{:S(2)}) copy-start(s32[1024]{0:T(1024)} %param.13) | copy-start | bytes 12292
  14.7 14.3 %copy-start = (f32[4,32,256]{2,1,0:T(8,128)S(1)}, f32[4,32,256]{2,1,0:T(8,128)}, u32[]{:S(2)}) copy-start(f32[4,32,256]{2,1,0:T(8,128)} %mass.3) | copy-start | bytes 393220
  14.7 14.9 %collective-permute-start.10 = (f32[8,32,256]{2,1,0:T(8,128)S(1)}, f32[8,32,256]{2,1,0:T(8,128)S(1)}, u32[]{:S(2)}, u32[]{:S(2)}) collective-permute-start(f32[8,32,256]{2,1,0:T(8,128)S(1)} %get-tuple-element.72), channel_id=1, source_target_pairs={{0,8},{8,0},{16,24},{24,16},{1,9},{9,1},{17,25},{25,17},{2,10},{10... | collective-permute-start | bytes 786440 | tf_op jit(solution)/shard_map/ppermute | solution.py:979
  15.4 14.3 %collective-permute-start.11 = (f32[8,32,256]{2,1,0:T(8,128)S(1)}, f32[8,32,256]{2,1,0:T(8,128)S(1)}, u32[]{:S(2)}, u32[]{:S(2)}) collective-permute-start(f32[8,32,256]{2,1,0:T(8,128)S(1)} %get-tuple-element.73), channel_id=1, source_target_pairs={{0,24},{8,16},{16,8},{24,0},{1,25},{9,17},{17,9},{25,1},{2,26},{10... | collective-permute-start | bytes 786440 | tf_op jit(solution)/shard_map/ppermute | solution.py:979
  18.0 5.3 %collective-permute-start.5 = (f32[40,256]{1,0:T(8,128)S(1)}, f32[40,256]{1,0:T(8,128)S(1)}, u32[]{:S(2)}, u32[]{:S(2)}) collective-permute-start(f32[40,256]{1,0:T(8,128)S(1)} %get-tuple-element.60), channel_id=1, source_target_pairs={{0,2},{2,0},{4,6},{6,4},{1,3},{3,1},{5,7},{7,5},{8,10},{10,8},{12,... | collective-permute-start | bytes 122888 | tf_op jit(solution)/shard_map/ppermute | solution.py:979
  18.0 5.3 %collective-permute-start.6 = (f32[40,256]{1,0:T(8,128)S(1)}, f32[40,256]{1,0:T(8,128)S(1)}, u32[]{:S(2)}, u32[]{:S(2)}) collective-permute-start(f32[40,256]{1,0:T(8,128)S(1)} %get-tuple-element.61), channel_id=1, source_target_pairs={{0,6},{2,4},{4,2},{6,0},{1,7},{3,5},{5,3},{7,1},{8,14},{10,12},{12... | collective-permute-start | bytes 122888 | tf_op jit(solution)/shard_map/ppermute | solution.py:979
  19.6 3.7 %collective-permute-start.7 = (f32[24,128]{1,0:T(8,128)S(1)}, f32[24,128]{1,0:T(8,128)S(1)}, u32[]{:S(2)}, u32[]{:S(2)}) collective-permute-start(f32[24,128]{1,0:T(8,128)S(1)} %get-tuple-element.62), channel_id=1, source_target_pairs={{0,1},{1,0},{2,3},{3,2},{4,5},{5,4},{6,7},{7,6},{8,9},{9,8},{10,11... | collective-permute-start | bytes 36872 | tf_op jit(solution)/shard_map/ppermute | solution.py:984
  23.3 3.2 %collective-permute-start.9 = (f32[24,128]{1,0:T(8,128)S(1)}, f32[24,128]{1,0:T(8,128)S(1)}, u32[]{:S(2)}, u32[]{:S(2)}) collective-permute-start(f32[24,128]{1,0:T(8,128)S(1)} %get-tuple-element.65), channel_id=1, source_target_pairs={{0,6},{2,4},{4,2},{6,0},{1,7},{3,5},{5,3},{7,1},{8,14},{10,12},{12... | collective-permute-start | bytes 36872 | tf_op jit(solution)/shard_map/ppermute | solution.py:979
  23.4 6.2 %collective-permute-start.12 = (f32[32,128]{1,0:T(8,128)S(1)}, f32[32,128]{1,0:T(8,128)S(1)}, u32[]{:S(2)}, u32[]{:S(2)}) collective-permute-start(f32[32,128]{1,0:T(8,128)S(1)} %get-tuple-element.74), channel_id=1, source_target_pairs={{0,8},{8,0},{16,24},{24,16},{1,9},{9,1},{17,25},{25,17},{2,10},{10... | collective-permute-start | bytes 49160 | tf_op jit(solution)/shard_map/ppermute | solution.py:979
  23.5 6.1 %collective-permute-start.13 = (f32[32,128]{1,0:T(8,128)S(1)}, f32[32,128]{1,0:T(8,128)S(1)}, u32[]{:S(2)}, u32[]{:S(2)}) collective-permute-start(f32[32,128]{1,0:T(8,128)S(1)} %get-tuple-element.75), channel_id=1, source_target_pairs={{0,24},{8,16},{16,8},{24,0},{1,25},{9,17},{17,9},{25,1},{2,26},{10... | collective-permute-start | bytes 49160 | tf_op jit(solution)/shard_map/ppermute | solution.py:979
  26.5 2.5 %collective-permute-start.8 = (f32[24,128]{1,0:T(8,128)S(1)}, f32[24,128]{1,0:T(8,128)S(1)}, u32[]{:S(2)}, u32[]{:S(2)}) collective-permute-start(f32[24,128]{1,0:T(8,128)S(1)} %get-tuple-element.65), channel_id=1, source_target_pairs={{0,2},{2,0},{4,6},{6,4},{1,3},{3,1},{5,7},{7,5},{8,10},{10,8},{12,... | collective-permute-start | bytes 36872 | tf_op jit(solution)/shard_map/ppermute | solution.py:979
  30.4 4.7 %collective-permute-start.14 = (f32[16,128]{1,0:T(8,128)S(1)}, f32[16,128]{1,0:T(8,128)S(1)}, u32[]{:S(2)}, u32[]{:S(2)}) collective-permute-start(f32[16,128]{1,0:T(8,128)S(1)} %get-tuple-element.85), channel_id=1, source_target_pairs={{0,1},{1,0},{2,3},{3,2},{4,5},{5,4},{6,7},{7,6},{8,9},{9,8},{10,11... | collective-permute-start | bytes 24584 | tf_op jit(solution)/shard_map/ppermute | solution.py:984
  32.0 3.1 %collective-permute-start.15 = (f32[8,256]{1,0:T(8,128)S(1)}, f32[8,256]{1,0:T(8,128)S(1)}, u32[]{:S(2)}, u32[]{:S(2)}) collective-permute-start(f32[8,256]{1,0:T(8,128)S(1)} %get-tuple-element.86), channel_id=1, source_target_pairs={{0,2},{2,0},{4,6},{6,4},{1,3},{3,1},{5,7},{7,5},{8,10},{10,8},{12,... | collective-permute-start | bytes 24584 | tf_op jit(solution)/shard_map/ppermute | solution.py:979
  32.2 3.1 %collective-permute-start.16 = (f32[8,256]{1,0:T(8,128)S(1)}, f32[8,256]{1,0:T(8,128)S(1)}, u32[]{:S(2)}, u32[]{:S(2)}) collective-permute-start(f32[8,256]{1,0:T(8,128)S(1)} %get-tuple-element.87), channel_id=1, source_target_pairs={{0,6},{2,4},{4,2},{6,0},{1,7},{3,5},{5,3},{7,1},{8,14},{10,12},{12... | collective-permute-start | bytes 24584 | tf_op jit(solution)/shard_map/ppermute | solution.py:979
  35.5 5.8 %collective-permute-start.19 = (f32[32,256]{1,0:T(8,128)S(1)}, f32[32,256]{1,0:T(8,128)S(1)}, u32[]{:S(2)}, u32[]{:S(2)}) collective-permute-start(f32[32,256]{1,0:T(8,128)S(1)} %get-tuple-element.89), channel_id=1, source_target_pairs={{0,24},{8,16},{16,8},{24,0},{1,25},{9,17},{17,9},{25,1},{2,26},{10... | collective-permute-start | bytes 98312 | tf_op jit(solution)/shard_map/ppermute | solution.py:979
  36.7 4.6 %collective-permute-start.20 = (f32[32,256]{1,0:T(8,128)S(1)}, f32[32,256]{1,0:T(8,128)S(1)}, u32[]{:S(2)}, u32[]{:S(2)}) collective-permute-start(f32[32,256]{1,0:T(8,128)S(1)} %get-tuple-element.90), channel_id=1, source_target_pairs={{0,8},{8,0},{16,24},{24,16},{1,9},{9,1},{17,25},{25,17},{2,10},{10... | collective-permute-start | bytes 98312 | tf_op jit(solution)/shard_map/ppermute | solution.py:979
  36.7 3.1 %collective-permute-start.18 = (f32[16,128]{1,0:T(8,128)S(1)}, f32[16,128]{1,0:T(8,128)S(1)}, u32[]{:S(2)}, u32[]{:S(2)}) collective-permute-start(f32[16,128]{1,0:T(8,128)S(1)} %collective-permute-done.14.z_rows), channel_id=1, source_target_pairs={{0,6},{2,4},{4,2},{6,0},{1,7},{3,5},{5,3},{7,1},{8,14},{10,12},{12... | collective-permute-start | bytes 24584 | tf_op jit(solution)/shard_map/ppermute | solution.py:979
  37.7 2.1 %collective-permute-start.17 = (f32[16,128]{1,0:T(8,128)S(1)}, f32[16,128]{1,0:T(8,128)S(1)}, u32[]{:S(2)}, u32[]{:S(2)}) collective-permute-start(f32[16,128]{1,0:T(8,128)S(1)} %collective-permute-done.14.z_rows), channel_id=1, source_target_pairs={{0,2},{2,0},{4,6},{6,4},{1,3},{3,1},{5,7},{7,5},{8,10},{10,8},{12,... | collective-permute-start | bytes 24584 | tf_op jit(solution)/shard_map/ppermute | solution.py:979

commit v3 on v2

--- a/solution.py
+++ b/solution.py
@@ -105,7 +105,7 @@
     return total
 
 
-def conversions(source, kind, heading, code, *, columns):
+def conversions(source, kind, heading, code, mark, *, columns):
     count = source.shape[1]
     value = (heading[...] + 32 * kind[...]).astype(jnp.float32)
     row, column = (source[...] // columns, source[...] % columns)
@@ -114,6 +114,7 @@
     code[...] = lax.dot_general(
         by_row, by_column, (((1,), (1,)), ((), ())), preferred_element_type=jnp.float32
     )
+    mark[...] = jnp.zeros(mark.shape, jnp.float32)
 
 
 def odd(axis):
@@ -472,7 +473,9 @@
     y_second,
     z_rows,
     inner_stretch,
+    after,
     new_stretch,
+    mark,
     updated,
     below,
     above,
@@ -496,11 +499,12 @@
             pltpu.make_async_copy(updated.at[:, place], new_stretch.at[:, x], sems.at[place])
         )
         copies[-1].start()
+    mark[...] = jnp.zeros(mark.shape, jnp.float32)
     for copy in copies:
         copy.wait()
 
 
-def store(inner, outer, inner_slanted, outer_slanted, late, fresh, mark, sems):
+def store(inner, outer, inner_slanted, outer_slanted, late, fresh, sems):
     bx = fresh.shape[1]
     moves = [
         (inner, fresh.at[0:first_slanted, 1 : bx - 1]),
@@ -523,7 +527,6 @@
     ]
     for copy in copies:
         copy.start()
-    mark[...] = jnp.zeros(mark.shape, jnp.float32)
     for copy in copies:
         copy.wait()
 
@@ -532,7 +535,7 @@
 down_edges = ((0, y_up.index(10)), (0, gas_slot), (1, y_down.index(8)), (1, gas_slot))
 
 
-def forward_edges(z_rows, y_first, y_second, first_out, second_out, corner, *, bx):
+def forward_edges(z_rows, y_first, y_second, after, first_out, second_out, corner, *, bx):
     halves = y_first.shape[1] // lanes
     flip_x, flip_y = (odd("gx"), odd("gy"))
     for half in range(halves):
@@ -989,6 +992,7 @@
 
 
 remote = pl.BlockSpec(memory_space=pltpu.HBM)
+anywhere = pl.BlockSpec(memory_space=pl.ANY)
 
 
 def call(body, outs, specs=None, out_specs=None, scratch=(), cost=(0, 0), aliases=None):
@@ -1039,8 +1043,11 @@
     y_first = swapped(y_one, y_two, "gy")
 
     entries = conv_source.shape[0]
-    (code,) = call(
-        lambda *refs: conversions(*refs, columns=bz), [(bx * by, bz)], cost=(40 * cells, 4 * cells)
+    mark = (tall, lanes)
+    code, code_done = call(
+        lambda *refs: conversions(*refs, columns=bz),
+        [(bx * by, bz), mark],
+        cost=(40 * cells, 4 * cells),
     )(*(array.reshape(1, entries) for array in (conv_source, conv_kind, conv_direction)))
     code = code.reshape(box)
 
@@ -1073,7 +1080,7 @@
     edges = (4 * (bz // lanes) + columns[0], lanes)
     x_one, x_two, corner = call(
         lambda *refs: forward_edges(*refs, bx=bx), [edges, edges, columns]
-    )(z_post, *post_y)
+    )(z_post, *post_y, code_done)
     corners = swapped(corner, corner, "gy")
     edges_x = swapped(x_one, x_two, "gx")
 
@@ -1099,7 +1106,6 @@
         scratch=rims,
         cost=(100 * cells, 60 * cells),
     )(*posts, mass, flags, code, *post_y, z_post, *corners, totals, changes)
-    mark = (tall, lanes)
     new_stretch, inner_done = call(
         restretch_inner,
         [(6, *box), mark],
@@ -1130,26 +1136,26 @@
     z_last = both_ways(z_out, 8)
     last_y = swapped(y_one, y_two, "gy")
     last_corners = swapped(z_last, z_last, "gy")
-    fresh, stored = call(
-        store,
-        [(19, *box), mark],
+    new_stretch, outer_done = call(
+        restretch_outer,
+        [(6, *box), mark],
+        specs=[pl.BlockSpec()] * 7 + [remote, anywhere],
         out_specs=[remote, pl.BlockSpec()],
-        scratch=[pltpu.SemaphoreType.DMA((32,))],
-        cost=(0, 160 * cells),
-    )(inner, outer, inner_slanted, outer_slanted, late)
-    x_one, x_two = call(add_faces, [face, face])(spread, z_last, *last_y, stored)
-    last_x = swapped(x_one, x_two, "gx")
-    (new_stretch,) = call(
-        restretch_outer,
-        [(6, *box)],
-        specs=[pl.BlockSpec()] * 7 + [remote],
-        out_specs=[remote],
         scratch=[(6, *ends), (3, *face), (3, *face)]
         + sides_y
         + [pltpu.SemaphoreType.DMA((2,))],
         cost=(80 * cells, 40 * cells),
         aliases={7: 0},
-    )(stretch, flow, *post_x, *post_y, z_post, new_stretch)
+    )(stretch, flow, *post_x, *post_y, z_post, new_stretch, outer_settled)
+    x_one, x_two = call(add_faces, [face, face])(spread, z_last, *last_y, outer_done)
+    last_x = swapped(x_one, x_two, "gx")
+    (fresh,) = call(
+        store,
+        [(19, *box)],
+        out_specs=[remote],
+        scratch=[pltpu.SemaphoreType.DMA((32,))],
+        cost=(0, 160 * cells),
+    )(inner, outer, inner_slanted, outer_slanted, late)
     (new_mass,) = call(add_all, [box])(
         inner_settled, outer_settled, spread, z_last, *last_y, *last_corners, *last_x[::-1]
     )

time: 42.3 us -> 42.2 us (level)
  waiting for transfers between devices: 6.34 us -> 5.71 us
  starting transfers between devices: 22.4 us -> 23 us
    ppermute x9, waiting for transfers between devices: 3.79 us -> 2.89 us  [swapped(): lax.ppermute(second, axis, behind)]
    ppermute x9, starting transfers between devices: 13.5 us -> 14.4 us  [swapped(): lax.ppermute(second, axis, behind)]
    ppermute x9, waiting for transfers between devices: 0.02 us -> 0.65 us  [swapped(): lax.ppermute(first, axis, ahead)]
  transfers between devices with their start and end apart: 21 -> 21, of which waited for: 7 -> 9; matrix products, arithmetic and copies ran while one was open for 0% -> 0% of each run, Pallas kernels for 20% -> 20%
where the time goes in v3:
time: 42.2 us; the launch traced here: 42 us
  starting transfers between devices  23 us (55%)
  Pallas kernels  12.5 us (30%)
  waiting for transfers between devices  5.71 us (14%)
  between operations  0.79 us (2%)
    ppermute x9, starting transfers between devices, swapped(): lax.ppermute(second, axis, behind)  14.4 us
    ppermute x3, starting transfers between devices, both_ways(): lax.ppermute(rows, 'gz', [(i, (i + 1) % devices) for i in range(devices)])  4.51 us
    ppermute x9, starting transfers between devices, swapped(): lax.ppermute(first, axis, ahead)  4.04 us
    ppermute x9, waiting for transfers between devices, swapped(): lax.ppermute(second, axis, behind)  2.89 us
    ppermute x3, waiting for transfers between devices, both_ways(): lax.ppermute(rows, 'gz', [(i, (i + 1) % devices) for i in range(devices)])  2.18 us
    pallas_call x1, Pallas kernels, shards(): call(moments, [(19, *box), (5, *box)], specs=[remote], scratch=[pltpu.Sem...  1.74 us
    pallas_call x1, Pallas kernels, shards(): call(store, [(19, *box)], out_specs=[remote], scratch=[pltpu.SemaphoreTyp...  1.7 us
    pallas_call x1, Pallas kernels, shards(): call(first_faces, [(6, *box), jax.ShapeDtypeStruct(box, jnp.int32), (8, b...  1.38 us
  transfers between devices with their start and end apart: 21, of which 9 were waited for; matrix products, arithmetic and copies ran while one was open for 0% of the time, Pallas kernels for 20%

profile of v3, /device:TPU:0, one launch (start us, length us, event | category | flops | bytes accessed | tf_op | source)
XLA Modules:
  0.0 42.0 jit_solution(4501261986905117326)
XLA Ops:
  0.6 1.4 %shard_map.95 = (f32[6,4,32,256]{3,2,1,0:T(8,128)S(1)}, s32[4,32,256]{2,1,0:T(8,128)S(1)}, f32[8,128]{1,0:T(8,128)S(1)}, f32[16,256]{1,0:T(8,128)S(1)}, f32[16,2...) custom-call(f32[6,4,32,256]{3,2,1,0:T(8,128)} %stretch_in.1, s32[4,32,256]{2,1,0:T(8,128)} %flags_in.1), custom_call_target="tpu_custom_call" | custom-call | flops 327680 | bytes 1966080 | tf_op jit(solution)/shard_map/pallas_call | solution.py:1026
  2.0 3.1 %collective-permute-start.3 = (f32[4,32,256]{2,1,0:T(8,128)S(1)}, f32[4,32,256]{2,1,0:T(8,128)S(1)}, u32[]{:S(2)}, u32[]{:S(2)}) collective-permute-start(f32[4,32,256]{2,1,0:T(8,128)S(1)} %get-tuple-element.57), channel_id=1, source_target_pairs={{0,8},{8,0},{16,24},{24,16},{1,9},{9,1},{17,25},{25,17},{2,10},{10... | collective-permute-start | bytes 393224 | tf_op jit(solution)/shard_map/ppermute | solution.py:982
  5.1 2.5 %collective-permute-start.4 = (f32[4,32,256]{2,1,0:T(8,128)S(1)}, f32[4,32,256]{2,1,0:T(8,128)S(1)}, u32[]{:S(2)}, u32[]{:S(2)}) collective-permute-start(f32[4,32,256]{2,1,0:T(8,128)S(1)} %get-tuple-element.58), channel_id=1, source_target_pairs={{0,24},{8,16},{16,8},{24,0},{1,25},{9,17},{17,9},{25,1},{2,26},{10... | collective-permute-start | bytes 393224 | tf_op jit(solution)/shard_map/ppermute | solution.py:982
  7.6 0.0 collective-permute-start.1
  7.6 1.6 %collective-permute-start.2 = (f32[16,256]{1,0:T(8,128)S(1)}, f32[16,256]{1,0:T(8,128)S(1)}, u32[]{:S(2)}, u32[]{:S(2)}) collective-permute-start(f32[16,256]{1,0:T(8,128)S(1)} %get-tuple-element.54), channel_id=1, source_target_pairs={{0,6},{2,4},{4,2},{6,0},{1,7},{3,5},{5,3},{7,1},{8,14},{10,12},{12... | collective-permute-start | bytes 49160 | tf_op jit(solution)/shard_map/ppermute | solution.py:982
  9.2 1.5 %collective-permute-start = (f32[8,128]{1,0:T(8,128)S(1)}, f32[8,128]{1,0:T(8,128)S(1)}, u32[]{:S(2)}, u32[]{:S(2)}) collective-permute-start(f32[8,128]{1,0:T(8,128)S(1)} %get-tuple-element.52), channel_id=1, source_target_pairs={{0,1},{1,0},{2,3},{3,2},{4,5},{5,4},{6,7},{7,6},{8,9},{9,8},{10,11... | collective-permute-start | bytes 12296 | tf_op jit(solution)/shard_map/ppermute | solution.py:987
  10.7 1.7 %shard_map.94 = (f32[19,4,32,256]{3,2,1,0:T(8,128)S(1)}, f32[5,4,32,256]{3,2,1,0:T(8,128)S(1)}) custom-call(f32[19,4,32,256]{3,2,1,0:T(8,128)} %pops_in.1), custom_call_target="tpu_custom_call" | custom-call | flops 1966080 | bytes 4915200 | tf_op jit(solution)/shard_map/pallas_call | solution.py:1054
  12.5 0.3 collective-permute-done.z_rows
  12.8 0.0 collective-permute-done.1.y_first
  12.8 0.0 collective-permute-done.2.y_second
  12.8 0.8 %shard_map.96 = (f32[19,2,32,256]{3,2,1,0:T(8,128)S(1)}, f32[3,2,32,256]{3,2,1,0:T(8,128)S(1)}) custom-call(f32[19,4,32,256]{3,2,1,0:T(8,128)S(1)} %get-tuple-element.49.pops, f32[6,4,32,256]{3,2,1,0:T(8,128)S(1)} %get-tuple-element.50.stretch, f32[5,4,32,256]{3,2,1,0:T(8,128)S(1)} %get-tuple-element.51.flow, f32[8,128]{1,0:T(8,128)S(1)} %collective-permute-done.z_rows, ...), custom_call_target="tpu_custom_call" | custom-call | flops 4915200 | bytes 4915200 | tf_op jit(solution)/shard_map/pallas_call | solution.py:1065
  13.6 0.0 collective-permute-done.3.x_first.gas_first
  13.6 0.1 collective-permute-done.4.x_second.gas_second
  13.7 0.0 copy-start.1
  13.7 0.0 copy-start.2
  13.7 0.0 copy-start.3
  13.7 1.0 %shard_map.97 = (f32[19,2,32,256]{3,2,1,0:T(8,128)S(1)}, f32[3,2,32,256]{3,2,1,0:T(8,128)S(1)}, f32[24,128]{1,0:T(8,128)S(1)}, f32[8,32,256]{2,1,0:T(8,128)S(1)}...) custom-call(f32[19,4,32,256]{3,2,1,0:T(8,128)S(1)} %get-tuple-element.49.pops, ...), custom_call_target="tpu_custom_call" | custom-call | flops 4915200 | bytes 4915200 | tf_op jit(solution)/shard_map/pallas_call | solution.py:1071
  14.7 0.0 copy-start
  14.7 0.6 %collective-permute-start.10 = (f32[8,32,256]{2,1,0:T(8,128)S(1)}, f32[8,32,256]{2,1,0:T(8,128)S(1)}, u32[]{:S(2)}, u32[]{:S(2)}) collective-permute-start(f32[8,32,256]{2,1,0:T(8,128)S(1)} %get-tuple-element.76), channel_id=1, source_target_pairs={{0,8},{8,0},{16,24},{24,16},{1,9},{9,1},{17,25},{25,17},{2,10},{10... | collective-permute-start | bytes 786440 | tf_op jit(solution)/shard_map/ppermute | solution.py:982
  15.4 2.6 %collective-permute-start.11 = (f32[8,32,256]{2,1,0:T(8,128)S(1)}, f32[8,32,256]{2,1,0:T(8,128)S(1)}, u32[]{:S(2)}, u32[]{:S(2)}) collective-permute-start(f32[8,32,256]{2,1,0:T(8,128)S(1)} %get-tuple-element.77), channel_id=1, source_target_pairs={{0,24},{8,16},{16,8},{24,0},{1,25},{9,17},{17,9},{25,1},{2,26},{10... | collective-permute-start | bytes 786440 | tf_op jit(solution)/shard_map/ppermute | solution.py:982
  18.0 0.0 collective-permute-start.5
  18.0 1.6 %collective-permute-start.6 = (f32[40,256]{1,0:T(8,128)S(1)}, f32[40,256]{1,0:T(8,128)S(1)}, u32[]{:S(2)}, u32[]{:S(2)}) collective-permute-start(f32[40,256]{1,0:T(8,128)S(1)} %get-tuple-element.63), channel_id=1, source_target_pairs={{0,6},{2,4},{4,2},{6,0},{1,7},{3,5},{5,3},{7,1},{8,14},{10,12},{12... | collective-permute-start | bytes 122888 | tf_op jit(solution)/shard_map/ppermute | solution.py:982
  19.6 1.5 %collective-permute-start.7 = (f32[24,128]{1,0:T(8,128)S(1)}, f32[24,128]{1,0:T(8,128)S(1)}, u32[]{:S(2)}, u32[]{:S(2)}) collective-permute-start(f32[24,128]{1,0:T(8,128)S(1)} %get-tuple-element.64), channel_id=1, source_target_pairs={{0,1},{1,0},{2,3},{3,2},{4,5},{5,4},{6,7},{7,6},{8,9},{9,8},{10,11... | collective-permute-start | bytes 36872 | tf_op jit(solution)/shard_map/ppermute | solution.py:987
  21.1 0.0 copy-done.1
  21.1 0.0 copy-done.2
  21.1 0.0 copy-done.3
  21.1 0.3 shard_map.99
  21.4 1.8 %collective-permute-done.7.z_rows.refs_0_ = f32[24,128]{1,0:T(8,128)S(1)} collective-permute-done((f32[24,128]{1,0:T(8,128)S(1)}, f32[24,128]{1,0:T(8,128)S(1)}, u32[]{:S(2)}, u32[]{:S(2)}) %collective-permute-start.7) | collective-permute-done | bytes 12320 | tf_op jit(solution)/shard_map/ppermute | solution.py:987
  23.3 0.0 collective-permute-done.5.y_first.refs_1_
  23.3 0.0 collective-permute-done.6.y_second.refs_2_
  23.3 0.1 collective-permute-start.8
  23.4 0.1 collective-permute-start.12
  23.5 1.7 %collective-permute-start.13 = (f32[32,128]{1,0:T(8,128)S(1)}, f32[32,128]{1,0:T(8,128)S(1)}, u32[]{:S(2)}, u32[]{:S(2)}) collective-permute-start(f32[32,128]{1,0:T(8,128)S(1)} %get-tuple-element.79), channel_id=1, source_target_pairs={{0,24},{8,16},{16,8},{24,0},{1,25},{9,17},{17,9},{25,1},{2,26},{10... | collective-permute-start | bytes 49160 | tf_op jit(solution)/shard_map/ppermute | solution.py:982
  25.2 0.0 collective-permute-done.8.corner_first
  25.2 0.0 collective-permute-start.9
  25.2 1.2 %shard_map.102 = (f32[6,4,32,256]{3,2,1,0:T(8,128)}, f32[8,128]{1,0:T(8,128)S(1)}) custom-call(f32[6,4,32,256]{3,2,1,0:T(8,128)S(1)} %get-tuple-element.50.stretch, f32[5,4,32,256]{3,2,1,0:T(8,128)S(1)} %get-tuple-element.51.flow, f32[40,256]{1,0:T(8,128)S(1)} %collective-permute-done.5.y_first.refs_1_, ...), custom_call_target="tpu_custom_call" | custom-call | flops 2621440 | bytes 1310720 | tf_op jit(solution)/shard_map/pallas_call | solution.py:1109
  26.4 0.9 %shard_map.98 = (f32[15,2,32,256]{3,2,1,0:T(8,128)S(1)}, f32[15,2,32,256]{3,2,1,0:T(8,128)S(1)}, f32[4,32,256]{2,1,0:T(8,128)S(1)}, f32[4,32,256]{2,1,0:T(8,128)S(1)}) custom-call(f32[19,2,32,256]{3,2,1,0:T(8,128)S(1)} %get-tuple-element.55.inner.inner_post, f32[19,2,32,256]{3,2,1,0:T(8,128)S(1)} %get-tuple-element.59.outer_post.post, ...), custom_call_target="tpu_custom_call" | custom-call | flops 11468800 | bytes 6553600 | tf_op jit(solution)/shard_map/pallas_call | solution.py:1089
  27.4 1.0 %collective-permute-done.9.corner_second = f32[24,128]{1,0:T(8,128)S(1)} collective-permute-done((f32[24,128]{1,0:T(8,128)S(1)}, f32[24,128]{1,0:T(8,128)S(1)}, u32[]{:S(2)}, u32[]{:S(2)}) %collective-permute-start.9) | collective-permute-done | bytes 12320 | tf_op jit(solution)/shard_map/ppermute | solution.py:982
  28.4 0.0 copy-done
  28.4 0.6 %shard_map.101 = (f32[4,2,32,256]{3,2,1,0:T(8,128)S(1)}, f32[4,2,32,256]{3,2,1,0:T(8,128)S(1)}, f32[2,32,256]{2,1,0:T(8,128)S(1)}, f32[2,32,256]{2,1,0:T(8,128)S...) custom-call(f32[19,2,32,256]{3,2,1,0:T(8,128)S(1)} %get-tuple-element.55.inner.inner_post, ...), custom_call_target="tpu_custom_call" | custom-call | flops 3276800 | bytes 1966080 | tf_op jit(solution)/shard_map/pallas_call | solution.py:1103
  29.0 0.6 %collective-permute-done.12.edges_first = f32[32,128]{1,0:T(8,128)S(1)} collective-permute-done((f32[32,128]{1,0:T(8,128)S(1)}, f32[32,128]{1,0:T(8,128)S(1)}, u32[]{:S(2)}, u32[]{:S(2)}) %collective-permute-start.12) | collective-permute-done | bytes 16416 | tf_op jit(solution)/shard_map/ppermute | solution.py:982
  29.5 0.0 collective-permute-done.13.edges_second
  29.5 0.0 collective-permute-done.10.x_first
  29.6 0.0 collective-permute-done.11.x_second
  29.6 0.8 %shard_map.103 = (f32[5,2,32,256]{3,2,1,0:T(8,128)S(1)}, f32[2,32,256]{2,1,0:T(8,128)S(1)}, f32[6,32,256]{2,1,0:T(8,128)S(1)}, f32[8,256]{1,0:T(8,128)S(1)}, f32...) custom-call(f32[19,2,32,256]{3,2,1,0:T(8,128)S(1)} %get-tuple-element.59.outer_post.post, ...), custom_call_target="tpu_custom_call" | custom-call | flops 4915200 | bytes 3276800 | tf_op jit(solution)/shard_map/pallas_call | solution.py:1116
  30.3 1.5 %collective-permute-start.14 = (f32[16,128]{1,0:T(8,128)S(1)}, f32[16,128]{1,0:T(8,128)S(1)}, u32[]{:S(2)}, u32[]{:S(2)}) collective-permute-start(f32[16,128]{1,0:T(8,128)S(1)} %get-tuple-element.89), channel_id=1, source_target_pairs={{0,1},{1,0},{2,3},{3,2},{4,5},{5,4},{6,7},{7,6},{8,9},{9,8},{10,11... | collective-permute-start | bytes 24584 | tf_op jit(solution)/shard_map/ppermute | solution.py:987
  31.8 0.0 collective-permute-start.15
  31.8 1.6 %collective-permute-start.16 = (f32[8,256]{1,0:T(8,128)S(1)}, f32[8,256]{1,0:T(8,128)S(1)}, u32[]{:S(2)}, u32[]{:S(2)}) collective-permute-start(f32[8,256]{1,0:T(8,128)S(1)} %get-tuple-element.91), channel_id=1, source_target_pairs={{0,6},{2,4},{4,2},{6,0},{1,7},{3,5},{5,3},{7,1},{8,14},{10,12},{12... | collective-permute-start | bytes 24584 | tf_op jit(solution)/shard_map/ppermute | solution.py:982
  33.4 1.1 %shard_map.105 = (f32[6,4,32,256]{3,2,1,0:T(8,128)}, f32[8,128]{1,0:T(8,128)S(1)}) custom-call(f32[6,4,32,256]{3,2,1,0:T(8,128)S(1)} %get-tuple-element.50.stretch, f32[5,4,32,256]{3,2,1,0:T(8,128)S(1)} %get-tuple-element.51.flow, f32[8,32,256]{2,1,0:T(8,128)S(1)} %collective-permute-done.10.x_first, ...), custom_call_target="tpu_custom_call", output_to_operand_aliasing={{0}: (7, {})} | custom-call | flops 2621440 | bytes 1310720 | tf_op jit(solution)/shard_map/pallas_call | solution.py:1139
  34.5 0.0 collective-permute-done.14.z_rows
  34.5 0.0 collective-permute-done.15.y_first
  34.5 0.4 collective-permute-done.16.y_second
  34.9 0.2 shard_map.106
  35.1 1.8 %collective-permute-start.19 = (f32[32,256]{1,0:T(8,128)S(1)}, f32[32,256]{1,0:T(8,128)S(1)}, u32[]{:S(2)}, u32[]{:S(2)}) collective-permute-start(f32[32,256]{1,0:T(8,128)S(1)} %get-tuple-element.93), channel_id=1, source_target_pairs={{0,24},{8,16},{16,8},{24,0},{1,25},{9,17},{17,9},{25,1},{2,26},{10... | collective-permute-start | bytes 98312 | tf_op jit(solution)/shard_map/ppermute | solution.py:982
  36.9 0.1 collective-permute-start.20
  37.0 0.0 collective-permute-start.17
  37.0 0.9 %collective-permute-start.18 = (f32[16,128]{1,0:T(8,128)S(1)}, f32[16,128]{1,0:T(8,128)S(1)}, u32[]{:S(2)}, u32[]{:S(2)}) collective-permute-start(f32[16,128]{1,0:T(8,128)S(1)} %collective-permute-done.14.z_rows), channel_id=1, source_target_pairs={{0,6},{2,4},{4,2},{6,0},{1,7},{3,5},{5,3},{7,1},{8,14},{10,12},{12... | collective-permute-start | bytes 24584 | tf_op jit(solution)/shard_map/ppermute | solution.py:982
  38.0 1.7 %shard_map.104 = f32[19,4,32,256]{3,2,1,0:T(8,128)} custom-call(f32[15,2,32,256]{3,2,1,0:T(8,128)S(1)} %get-tuple-element.65.inner, f32[15,2,32,256]{3,2,1,0:T(8,128)S(1)} %get-tuple-element.66.outer, f32[4,2,32,256]{3,2,1,0:T(8,128)S(1)} %get-tuple-element.72.inner_slanted, f32[4,2,32,256]{3,2,1,0:T(8,128)S(1)} %get-tuple-element.73.outer_slanted, ...), custom_call_target="tpu_custom_call" | custom-call | bytes 5242880 | tf_op jit(solution)/shard_map/pallas_call | solution.py:1152
  39.7 0.0 collective-permute-done.17.corner_first
  39.7 0.4 %collective-permute-done.18.corner_second = f32[16,128]{1,0:T(8,128)S(1)} collective-permute-done((f32[16,128]{1,0:T(8,128)S(1)}, f32[16,128]{1,0:T(8,128)S(1)}, u32[]{:S(2)}, u32[]{:S(2)}) %collective-permute-start.18) | collective-permute-done | bytes 8224 | tf_op jit(solution)/shard_map/ppermute | solution.py:982
  40.1 1.0 %collective-permute-done.19.x_second = f32[32,256]{1,0:T(8,128)S(1)} collective-permute-done((f32[32,256]{1,0:T(8,128)S(1)}, f32[32,256]{1,0:T(8,128)S(1)}, u32[]{:S(2)}, u32[]{:S(2)}) %collective-permute-start.19) | collective-permute-done | bytes 32800 | tf_op jit(solution)/shard_map/ppermute | solution.py:982
  41.1 0.1 collective-permute-done.20.x_first
  41.1 0.9 %shard_map.107 = f32[4,32,256]{2,1,0:T(8,128)} custom-call(f32[2,32,256]{2,1,0:T(8,128)S(1)} %get-tuple-element.87.inner_settled, f32[2,32,256]{2,1,0:T(8,128)S(1)} %get-tuple-element.85.after.outer_settled, f32[6,32,256]{2,1,0:T(8,128)S(1)} %get-tuple-element.88.spread, f32[16,128]{1,0:T(8,128)S(1)} %collective-permute-done.14.z_rows, ...), custom_call_target="tpu_custom_call" | custom-call | tf_op jit(solution)/shard_map/pallas_call | solution.py:1159
  (1 shorter events, 0.0 us)
Async XLA Ops:
  2.0 11.6 %collective-permute-start.3 = (f32[4,32,256]{2,1,0:T(8,128)S(1)}, f32[4,32,256]{2,1,0:T(8,128)S(1)}, u32[]{:S(2)}, u32[]{:S(2)}) collective-permute-start(f32[4,32,256]{2,1,0:T(8,128)S(1)} %get-tuple-element.57), channel_id=1, source_target_pairs={{0,8},{8,0},{16,24},{24,16},{1,9},{9,1},{17,25},{25,17},{2,10},{10... | collective-permute-start | bytes 393224 | tf_op jit(solution)/shard_map/ppermute | solution.py:982
  5.1 8.6 %collective-permute-start.4 = (f32[4,32,256]{2,1,0:T(8,128)S(1)}, f32[4,32,256]{2,1,0:T(8,128)S(1)}, u32[]{:S(2)}, u32[]{:S(2)}) collective-permute-start(f32[4,32,256]{2,1,0:T(8,128)S(1)} %get-tuple-element.58), channel_id=1, source_target_pairs={{0,24},{8,16},{16,8},{24,0},{1,25},{9,17},{17,9},{25,1},{2,26},{10... | collective-permute-start | bytes 393224 | tf_op jit(solution)/shard_map/ppermute | solution.py:982
  7.6 5.2 %collective-permute-start.1 = (f32[16,256]{1,0:T(8,128)S(1)}, f32[16,256]{1,0:T(8,128)S(1)}, u32[]{:S(2)}, u32[]{:S(2)}) collective-permute-start(f32[16,256]{1,0:T(8,128)S(1)} %get-tuple-element.53), channel_id=1, source_target_pairs={{0,2},{2,0},{4,6},{6,4},{1,3},{3,1},{5,7},{7,5},{8,10},{10,8},{12,... | collective-permute-start | bytes 49160 | tf_op jit(solution)/shard_map/ppermute | solution.py:982
  7.6 5.2 %collective-permute-start.2 = (f32[16,256]{1,0:T(8,128)S(1)}, f32[16,256]{1,0:T(8,128)S(1)}, u32[]{:S(2)}, u32[]{:S(2)}) collective-permute-start(f32[16,256]{1,0:T(8,128)S(1)} %get-tuple-element.54), channel_id=1, source_target_pairs={{0,6},{2,4},{4,2},{6,0},{1,7},{3,5},{5,3},{7,1},{8,14},{10,12},{12... | collective-permute-start | bytes 49160 | tf_op jit(solution)/shard_map/ppermute | solution.py:982
  9.2 3.6 %collective-permute-start = (f32[8,128]{1,0:T(8,128)S(1)}, f32[8,128]{1,0:T(8,128)S(1)}, u32[]{:S(2)}, u32[]{:S(2)}) collective-permute-start(f32[8,128]{1,0:T(8,128)S(1)} %get-tuple-element.52), channel_id=1, source_target_pairs={{0,1},{1,0},{2,3},{3,2},{4,5},{5,4},{6,7},{7,6},{8,9},{9,8},{10,11... | collective-permute-start | bytes 12296 | tf_op jit(solution)/shard_map/ppermute | solution.py:987
  13.7 7.4 %copy-start.1 = (s32[1024]{0:T(1024)S(1)}, s32[1024]{0:T(1024)}, u32[]{:S(2)}) copy-start(s32[1024]{0:T(1024)} %param.11) | copy-start | bytes 12292
  13.7 7.4 %copy-start.2 = (s32[1024]{0:T(1024)S(1)}, s32[1024]{0:T(1024)}, u32[]{:S(2)}) copy-start(s32[1024]{0:T(1024)} %param.12) | copy-start | bytes 12292
  13.7 7.4 %copy-start.3 = (s32[1024]{0:T(1024)S(1)}, s32[1024]{0:T(1024)}, u32[]{:S(2)}) copy-start(s32[1024]{0:T(1024)} %param.13) | copy-start | bytes 12292
  14.7 13.7 %copy-start = (f32[4,32,256]{2,1,0:T(8,128)S(1)}, f32[4,32,256]{2,1,0:T(8,128)}, u32[]{:S(2)}) copy-start(f32[4,32,256]{2,1,0:T(8,128)} %mass.3) | copy-start | bytes 393220
  14.7 14.8 %collective-permute-start.10 = (f32[8,32,256]{2,1,0:T(8,128)S(1)}, f32[8,32,256]{2,1,0:T(8,128)S(1)}, u32[]{:S(2)}, u32[]{:S(2)}) collective-permute-start(f32[8,32,256]{2,1,0:T(8,128)S(1)} %get-tuple-element.76), channel_id=1, source_target_pairs={{0,8},{8,0},{16,24},{24,16},{1,9},{9,1},{17,25},{25,17},{2,10},{10... | collective-permute-start | bytes 786440 | tf_op jit(solution)/shard_map/ppermute | solution.py:982
  15.4 14.2 %collective-permute-start.11 = (f32[8,32,256]{2,1,0:T(8,128)S(1)}, f32[8,32,256]{2,1,0:T(8,128)S(1)}, u32[]{:S(2)}, u32[]{:S(2)}) collective-permute-start(f32[8,32,256]{2,1,0:T(8,128)S(1)} %get-tuple-element.77), channel_id=1, source_target_pairs={{0,24},{8,16},{16,8},{24,0},{1,25},{9,17},{17,9},{25,1},{2,26},{10... | collective-permute-start | bytes 786440 | tf_op jit(solution)/shard_map/ppermute | solution.py:982
  18.0 5.3 %collective-permute-start.5 = (f32[40,256]{1,0:T(8,128)S(1)}, f32[40,256]{1,0:T(8,128)S(1)}, u32[]{:S(2)}, u32[]{:S(2)}) collective-permute-start(f32[40,256]{1,0:T(8,128)S(1)} %get-tuple-element.62), channel_id=1, source_target_pairs={{0,2},{2,0},{4,6},{6,4},{1,3},{3,1},{5,7},{7,5},{8,10},{10,8},{12,... | collective-permute-start | bytes 122888 | tf_op jit(solution)/shard_map/ppermute | solution.py:982
  18.0 5.3 %collective-permute-start.6 = (f32[40,256]{1,0:T(8,128)S(1)}, f32[40,256]{1,0:T(8,128)S(1)}, u32[]{:S(2)}, u32[]{:S(2)}) collective-permute-start(f32[40,256]{1,0:T(8,128)S(1)} %get-tuple-element.63), channel_id=1, source_target_pairs={{0,6},{2,4},{4,2},{6,0},{1,7},{3,5},{5,3},{7,1},{8,14},{10,12},{12... | collective-permute-start | bytes 122888 | tf_op jit(solution)/shard_map/ppermute | solution.py:982
  19.6 3.7 %collective-permute-start.7 = (f32[24,128]{1,0:T(8,128)S(1)}, f32[24,128]{1,0:T(8,128)S(1)}, u32[]{:S(2)}, u32[]{:S(2)}) collective-permute-start(f32[24,128]{1,0:T(8,128)S(1)} %get-tuple-element.64), channel_id=1, source_target_pairs={{0,1},{1,0},{2,3},{3,2},{4,5},{5,4},{6,7},{7,6},{8,9},{9,8},{10,11... | collective-permute-start | bytes 36872 | tf_op jit(solution)/shard_map/ppermute | solution.py:987
  23.3 1.9 %collective-permute-start.8 = (f32[24,128]{1,0:T(8,128)S(1)}, f32[24,128]{1,0:T(8,128)S(1)}, u32[]{:S(2)}, u32[]{:S(2)}) collective-permute-start(f32[24,128]{1,0:T(8,128)S(1)} %get-tuple-element.69), channel_id=1, source_target_pairs={{0,2},{2,0},{4,6},{6,4},{1,3},{3,1},{5,7},{7,5},{8,10},{10,8},{12,... | collective-permute-start | bytes 36872 | tf_op jit(solution)/shard_map/ppermute | solution.py:982
  23.4 6.1 %collective-permute-start.12 = (f32[32,128]{1,0:T(8,128)S(1)}, f32[32,128]{1,0:T(8,128)S(1)}, u32[]{:S(2)}, u32[]{:S(2)}) collective-permute-start(f32[32,128]{1,0:T(8,128)S(1)} %get-tuple-element.78), channel_id=1, source_target_pairs={{0,8},{8,0},{16,24},{24,16},{1,9},{9,1},{17,25},{25,17},{2,10},{10... | collective-permute-start | bytes 49160 | tf_op jit(solution)/shard_map/ppermute | solution.py:982
  23.5 6.1 %collective-permute-start.13 = (f32[32,128]{1,0:T(8,128)S(1)}, f32[32,128]{1,0:T(8,128)S(1)}, u32[]{:S(2)}, u32[]{:S(2)}) collective-permute-start(f32[32,128]{1,0:T(8,128)S(1)} %get-tuple-element.79), channel_id=1, source_target_pairs={{0,24},{8,16},{16,8},{24,0},{1,25},{9,17},{17,9},{25,1},{2,26},{10... | collective-permute-start | bytes 49160 | tf_op jit(solution)/shard_map/ppermute | solution.py:982
  25.2 3.2 %collective-permute-start.9 = (f32[24,128]{1,0:T(8,128)S(1)}, f32[24,128]{1,0:T(8,128)S(1)}, u32[]{:S(2)}, u32[]{:S(2)}) collective-permute-start(f32[24,128]{1,0:T(8,128)S(1)} %get-tuple-element.69), channel_id=1, source_target_pairs={{0,6},{2,4},{4,2},{6,0},{1,7},{3,5},{5,3},{7,1},{8,14},{10,12},{12... | collective-permute-start | bytes 36872 | tf_op jit(solution)/shard_map/ppermute | solution.py:982
  30.3 4.2 %collective-permute-start.14 = (f32[16,128]{1,0:T(8,128)S(1)}, f32[16,128]{1,0:T(8,128)S(1)}, u32[]{:S(2)}, u32[]{:S(2)}) collective-permute-start(f32[16,128]{1,0:T(8,128)S(1)} %get-tuple-element.89), channel_id=1, source_target_pairs={{0,1},{1,0},{2,3},{3,2},{4,5},{5,4},{6,7},{7,6},{8,9},{9,8},{10,11... | collective-permute-start | bytes 24584 | tf_op jit(solution)/shard_map/ppermute | solution.py:987
  31.8 2.7 %collective-permute-start.15 = (f32[8,256]{1,0:T(8,128)S(1)}, f32[8,256]{1,0:T(8,128)S(1)}, u32[]{:S(2)}, u32[]{:S(2)}) collective-permute-start(f32[8,256]{1,0:T(8,128)S(1)} %get-tuple-element.90), channel_id=1, source_target_pairs={{0,2},{2,0},{4,6},{6,4},{1,3},{3,1},{5,7},{7,5},{8,10},{10,8},{12,... | collective-permute-start | bytes 24584 | tf_op jit(solution)/shard_map/ppermute | solution.py:982
  31.8 3.1 %collective-permute-start.16 = (f32[8,256]{1,0:T(8,128)S(1)}, f32[8,256]{1,0:T(8,128)S(1)}, u32[]{:S(2)}, u32[]{:S(2)}) collective-permute-start(f32[8,256]{1,0:T(8,128)S(1)} %get-tuple-element.91), channel_id=1, source_target_pairs={{0,6},{2,4},{4,2},{6,0},{1,7},{3,5},{5,3},{7,1},{8,14},{10,12},{12... | collective-permute-start | bytes 24584 | tf_op jit(solution)/shard_map/ppermute | solution.py:982
  35.1 6.0 %collective-permute-start.19 = (f32[32,256]{1,0:T(8,128)S(1)}, f32[32,256]{1,0:T(8,128)S(1)}, u32[]{:S(2)}, u32[]{:S(2)}) collective-permute-start(f32[32,256]{1,0:T(8,128)S(1)} %get-tuple-element.93), channel_id=1, source_target_pairs={{0,24},{8,16},{16,8},{24,0},{1,25},{9,17},{17,9},{25,1},{2,26},{10... | collective-permute-start | bytes 98312 | tf_op jit(solution)/shard_map/ppermute | solution.py:982
  36.9 4.3 %collective-permute-start.20 = (f32[32,256]{1,0:T(8,128)S(1)}, f32[32,256]{1,0:T(8,128)S(1)}, u32[]{:S(2)}, u32[]{:S(2)}) collective-permute-start(f32[32,256]{1,0:T(8,128)S(1)} %get-tuple-element.94), channel_id=1, source_target_pairs={{0,8},{8,0},{16,24},{24,16},{1,9},{9,1},{17,25},{25,17},{2,10},{10... | collective-permute-start | bytes 98312 | tf_op jit(solution)/shard_map/ppermute | solution.py:982
  37.0 2.7 %collective-permute-start.17 = (f32[16,128]{1,0:T(8,128)S(1)}, f32[16,128]{1,0:T(8,128)S(1)}, u32[]{:S(2)}, u32[]{:S(2)}) collective-permute-start(f32[16,128]{1,0:T(8,128)S(1)} %collective-permute-done.14.z_rows), channel_id=1, source_target_pairs={{0,2},{2,0},{4,6},{6,4},{1,3},{3,1},{5,7},{7,5},{8,10},{10,8},{12,... | collective-permute-start | bytes 24584 | tf_op jit(solution)/shard_map/ppermute | solution.py:982
  37.0 3.1 %collective-permute-start.18 = (f32[16,128]{1,0:T(8,128)S(1)}, f32[16,128]{1,0:T(8,128)S(1)}, u32[]{:S(2)}, u32[]{:S(2)}) collective-permute-start(f32[16,128]{1,0:T(8,128)S(1)} %collective-permute-done.14.z_rows), channel_id=1, source_target_pairs={{0,6},{2,4},{4,2},{6,0},{1,7},{3,5},{5,3},{7,1},{8,14},{10,12},{12... | collective-permute-start | bytes 24584 | tf_op jit(solution)/shard_map/ppermute | solution.py:982

commit v4 on v3

--- a/solution.py
+++ b/solution.py
@@ -168,14 +168,26 @@
 ):
     bx, by, bz = flags.shape
     flip_x, flip_y = (odd("gx"), odd("gy"))
-    copies = [
-        pltpu.make_async_copy(stretch_in, stretch, sems.at[0]),
-        pltpu.make_async_copy(flags_in, flags, sems.at[1]),
-    ]
-    for copy in copies:
-        copy.start()
-    for copy in copies:
-        copy.wait()
+    order = (0, bx - 1) + tuple(range(1, bx - 1))
+    copies = {}
+    for x in order:
+        copies[x] = (
+            pltpu.make_async_copy(stretch_in.at[:, x], stretch.at[:, x], sems.at[0, x]),
+            pltpu.make_async_copy(flags_in.at[x], flags.at[x], sems.at[1, x]),
+        )
+        for copy in copies[x]:
+            copy.start()
+    for x in order[0:2]:
+        for copy in copies[x]:
+            copy.wait()
+    for out, last in ((x_first, flip_x), (x_second, jnp.logical_not(flip_x))):
+        for comp in range(3):
+            slot = symmetric_slot[comp][0]
+            out[comp] = jnp.where(last, stretch[slot, 0], stretch[slot, bx - 1])
+        out[3] = jnp.where(jnp.where(last, flags[0], flags[bx - 1]) == 0, 1.0, 0.0)
+    for x in order[2:]:
+        for copy in copies[x]:
+            copy.wait()
     tiles = []
     for x in range(bx):
         along_y = [stretch.at[symmetric_slot[comp][1], x] for comp in range(3)]
@@ -191,11 +203,6 @@
     rest = y_first.shape[0] - 3 * bx
     y_first[3 * bx :, :] = jnp.zeros((rest, bz), jnp.float32)
     y_second[3 * bx :, :] = jnp.zeros((rest, bz), jnp.float32)
-    for out, last in ((x_first, flip_x), (x_second, jnp.logical_not(flip_x))):
-        for comp in range(3):
-            slot = symmetric_slot[comp][0]
-            out[comp] = jnp.where(last, stretch[slot, 0], stretch[slot, bx - 1])
-        out[3] = jnp.where(jnp.where(last, flags[0], flags[bx - 1]) == 0, 1.0, 0.0)
 
 
 def moments(pops_in, pops, flow, sems):
@@ -936,43 +943,44 @@
     second[...] = jnp.where(flip_x, up, down)
 
 
-def add_all(
-    inner_settled,
-    outer_settled,
-    spread,
-    z_rows,
-    y_first,
-    y_second,
-    corner_first,
-    corner_second,
-    x_second,
-    x_first,
-    new_mass,
-):
+def add_sides(inner_settled, outer_settled, spread, z_rows, y_first, y_second, summed):
+    bx = summed.shape[0]
+    flip = odd("gy")
+    tile = row_columns(z_rows[...])
+    sides_y = (select(flip, y_first, y_second), select(flip, y_second, y_first))
+    for x in range(bx):
+        inside = 0 < x < bx - 1
+        own = inner_settled[x - 1] if inside else outer_settled[end_place(x, bx)]
+        summed[x] = own + with_edges(spread[x + 1], x + 1, tile, *sides_y)
+
+
+def add_last(summed, corner_first, corner_second, x_second, x_first, new_mass, total, sems):
     bx, by, bz = new_mass.shape
     flip_x, flip_y = (odd("gx"), odd("gy"))
-    tile = row_columns(z_rows[...])
-    y_below, y_above = (select(flip_y, y_first, y_second), select(flip_y, y_second, y_first))
     at = iota((8, bz), 1)
-    found = []
-    for rows, side, corner in (
-        (y_below, 0, select(flip_y, corner_first, corner_second)),
-        (y_above, 1, select(flip_y, corner_second, corner_first)),
+    edges = []
+    for side, corner in (
+        (0, select(flip_y, corner_first, corner_second)),
+        (1, select(flip_y, corner_second, corner_first)),
     ):
         edge = corner[:, by + side : by + side + 1]
-        rows = rows + jnp.where(at == 0, edge[0:8, :], 0.0)
-        found.append(rows + jnp.where(at == bz - 1, edge[8:16, :], 0.0))
+        edges.append(
+            jnp.where(at == 0, edge[0:8, :], 0.0) + jnp.where(at == bz - 1, edge[8:16, :], 0.0)
+        )
+    copies = []
     for x in range(bx):
-        total = with_edges(spread[x + 1], x + 1, tile, *found)
+        now = summed[x]
         if x == 0:
-            total = total + select(flip_x, x_first, x_second)
+            now = now + select(flip_x, x_first, x_second)
         if x == bx - 1:
-            total = total + select(flip_x, x_second, x_first)
-        if 0 < x < bx - 1:
-            total = total + inner_settled[x - 1]
-        else:
-            total = total + outer_settled[0 if x == 0 else 1]
-        new_mass[x] = total
+            now = now + select(flip_x, x_second, x_first)
+        total[x] = now
+        for row, edge in ((0, edges[0]), (by - 1, edges[1])):
+            total[x, row : row + 1, :] = now[row : row + 1, :] + edge[x + 1 : x + 2, :]
+        copies.append(pltpu.make_async_copy(total.at[x], new_mass.at[x], sems.at[x]))
+        copies[-1].start()
+    for copy in copies:
+        copy.wait()
 
 
 def swapped(first, second, axis):
@@ -1035,7 +1043,7 @@
             (4, *face),
         ],
         specs=[remote] * 2,
-        scratch=[pltpu.SemaphoreType.DMA((2,))],
+        scratch=[pltpu.SemaphoreType.DMA((2, bx))],
         cost=(10 * cells, 60 * cells),
     )(*(pltpu.with_memory_space_constraint(array, pltpu.HBM) for array in (stretch, flags)))
     first_x = swapped(x_one, x_two, "gx")
@@ -1156,9 +1164,15 @@
         scratch=[pltpu.SemaphoreType.DMA((32,))],
         cost=(0, 160 * cells),
     )(inner, outer, inner_slanted, outer_slanted, late)
-    (new_mass,) = call(add_all, [box])(
-        inner_settled, outer_settled, spread, z_last, *last_y, *last_corners, *last_x[::-1]
+    (summed,) = call(add_sides, [box], cost=(10 * cells, 12 * cells))(
+        inner_settled, outer_settled, spread, z_last, *last_y
     )
+    (new_mass,) = call(
+        add_last,
+        [box],
+        out_specs=[remote],
+        scratch=[box, pltpu.SemaphoreType.DMA((bx,))],
+    )(summed, *last_corners, *last_x[::-1])
     return (fresh, new_stretch, new_mass)
 
 

time: 42.2 us -> 42.3 us (level)
    pallas_call x1 -> x2, Pallas kernels: 0.86 us -> 0.97 us  [the longest x1 0.77 us: shards(): call(add_last, [box], out_specs=[remote], scratch=[box, pltpu.SemaphoreTy...]
where the time goes in v4:
time: 42.3 us; the launch traced here: 42.1 us
  starting transfers between devices  23 us (54%)
  Pallas kernels  12.8 us (30%)
  waiting for transfers between devices  5.51 us (13%)
  between operations  0.8 us (2%)
    ppermute x9, starting transfers between devices, swapped(): lax.ppermute(second, axis, behind)  14.4 us
    ppermute x3, starting transfers between devices, both_ways(): lax.ppermute(rows, 'gz', [(i, (i + 1) % devices) for i in range(devices)])  4.51 us
    ppermute x9, starting transfers between devices, swapped(): lax.ppermute(first, axis, ahead)  4.04 us
    ppermute x9, waiting for transfers between devices, swapped(): lax.ppermute(second, axis, behind)  2.68 us
    ppermute x3, waiting for transfers between devices, both_ways(): lax.ppermute(rows, 'gz', [(i, (i + 1) % devices) for i in range(devices)])  2.18 us
    pallas_call x1, Pallas kernels, shards(): call(moments, [(19, *box), (5, *box)], specs=[remote], scratch=[pltpu.Sem...  1.74 us
    pallas_call x1, Pallas kernels, shards(): call(store, [(19, *box)], out_specs=[remote], scratch=[pltpu.SemaphoreTyp...  1.7 us
    pallas_call x1, Pallas kernels, shards(): call(first_faces, [(6, *box), jax.ShapeDtypeStruct(box, jnp.int32), (8, b...  1.55 us
  transfers between devices with their start and end apart: 21, of which 9 were waited for; matrix products, arithmetic and copies ran while one was open for 0% of the time, Pallas kernels for 20%

profile of v4, /device:TPU:0, one launch (start us, length us, event | category | flops | bytes accessed | tf_op | source)
XLA Modules:
  0.0 42.1 jit_solution(14449596153928208178)
XLA Ops:
  0.6 1.6 %shard_map.95 = (f32[6,4,32,256]{3,2,1,0:T(8,128)S(1)}, s32[4,32,256]{2,1,0:T(8,128)S(1)}, f32[8,128]{1,0:T(8,128)S(1)}, f32[16,256]{1,0:T(8,128)S(1)}, f32[16,2...) custom-call(f32[6,4,32,256]{3,2,1,0:T(8,128)} %stretch_in.1, s32[4,32,256]{2,1,0:T(8,128)} %flags_in.1), custom_call_target="tpu_custom_call" | custom-call | flops 327680 | bytes 1966080 | tf_op jit(solution)/shard_map/pallas_call | solution.py:1034
  2.2 3.1 %collective-permute-start.3 = (f32[4,32,256]{2,1,0:T(8,128)S(1)}, f32[4,32,256]{2,1,0:T(8,128)S(1)}, u32[]{:S(2)}, u32[]{:S(2)}) collective-permute-start(f32[4,32,256]{2,1,0:T(8,128)S(1)} %get-tuple-element.57), channel_id=1, source_target_pairs={{0,8},{8,0},{16,24},{24,16},{1,9},{9,1},{17,25},{25,17},{2,10},{10... | collective-permute-start | bytes 393224 | tf_op jit(solution)/shard_map/ppermute | solution.py:990
  5.3 2.5 %collective-permute-start.4 = (f32[4,32,256]{2,1,0:T(8,128)S(1)}, f32[4,32,256]{2,1,0:T(8,128)S(1)}, u32[]{:S(2)}, u32[]{:S(2)}) collective-permute-start(f32[4,32,256]{2,1,0:T(8,128)S(1)} %get-tuple-element.58), channel_id=1, source_target_pairs={{0,24},{8,16},{16,8},{24,0},{1,25},{9,17},{17,9},{25,1},{2,26},{10... | collective-permute-start | bytes 393224 | tf_op jit(solution)/shard_map/ppermute | solution.py:990
  7.8 0.0 collective-permute-start.1
  7.8 1.6 %collective-permute-start.2 = (f32[16,256]{1,0:T(8,128)S(1)}, f32[16,256]{1,0:T(8,128)S(1)}, u32[]{:S(2)}, u32[]{:S(2)}) collective-permute-start(f32[16,256]{1,0:T(8,128)S(1)} %get-tuple-element.54), channel_id=1, source_target_pairs={{0,6},{2,4},{4,2},{6,0},{1,7},{3,5},{5,3},{7,1},{8,14},{10,12},{12... | collective-permute-start | bytes 49160 | tf_op jit(solution)/shard_map/ppermute | solution.py:990
  9.4 1.5 %collective-permute-start = (f32[8,128]{1,0:T(8,128)S(1)}, f32[8,128]{1,0:T(8,128)S(1)}, u32[]{:S(2)}, u32[]{:S(2)}) collective-permute-start(f32[8,128]{1,0:T(8,128)S(1)} %get-tuple-element.52), channel_id=1, source_target_pairs={{0,1},{1,0},{2,3},{3,2},{4,5},{5,4},{6,7},{7,6},{8,9},{9,8},{10,11... | collective-permute-start | bytes 12296 | tf_op jit(solution)/shard_map/ppermute | solution.py:995
  10.9 1.7 %shard_map.94 = (f32[19,4,32,256]{3,2,1,0:T(8,128)S(1)}, f32[5,4,32,256]{3,2,1,0:T(8,128)S(1)}) custom-call(f32[19,4,32,256]{3,2,1,0:T(8,128)} %pops_in.1), custom_call_target="tpu_custom_call" | custom-call | flops 1966080 | bytes 4915200 | tf_op jit(solution)/shard_map/pallas_call | solution.py:1062
  12.6 0.3 collective-permute-done.z_rows
  13.0 0.0 collective-permute-done.1.y_first
  13.0 0.0 collective-permute-done.2.y_second
  13.0 0.8 %shard_map.96 = (f32[19,2,32,256]{3,2,1,0:T(8,128)S(1)}, f32[3,2,32,256]{3,2,1,0:T(8,128)S(1)}) custom-call(f32[19,4,32,256]{3,2,1,0:T(8,128)S(1)} %get-tuple-element.49.pops, f32[6,4,32,256]{3,2,1,0:T(8,128)S(1)} %get-tuple-element.50.stretch, f32[5,4,32,256]{3,2,1,0:T(8,128)S(1)} %get-tuple-element.51.flow, f32[8,128]{1,0:T(8,128)S(1)} %collective-permute-done.z_rows, ...), custom_call_target="tpu_custom_call" | custom-call | flops 4915200 | bytes 4915200 | tf_op jit(solution)/shard_map/pallas_call | solution.py:1073
  13.7 0.0 collective-permute-done.3.x_first.gas_first
  13.7 0.1 collective-permute-done.4.x_second.gas_second
  13.9 0.0 copy-start.1
  13.9 0.0 copy-start.2
  13.9 0.0 copy-start.3
  13.9 1.0 %shard_map.97 = (f32[19,2,32,256]{3,2,1,0:T(8,128)S(1)}, f32[3,2,32,256]{3,2,1,0:T(8,128)S(1)}, f32[24,128]{1,0:T(8,128)S(1)}, f32[8,32,256]{2,1,0:T(8,128)S(1)}...) custom-call(f32[19,4,32,256]{3,2,1,0:T(8,128)S(1)} %get-tuple-element.49.pops, ...), custom_call_target="tpu_custom_call" | custom-call | flops 4915200 | bytes 4915200 | tf_op jit(solution)/shard_map/pallas_call | solution.py:1079
  14.9 0.0 copy-start
  14.9 0.6 %collective-permute-start.10 = (f32[8,32,256]{2,1,0:T(8,128)S(1)}, f32[8,32,256]{2,1,0:T(8,128)S(1)}, u32[]{:S(2)}, u32[]{:S(2)}) collective-permute-start(f32[8,32,256]{2,1,0:T(8,128)S(1)} %get-tuple-element.76), channel_id=1, source_target_pairs={{0,8},{8,0},{16,24},{24,16},{1,9},{9,1},{17,25},{25,17},{2,10},{10... | collective-permute-start | bytes 786440 | tf_op jit(solution)/shard_map/ppermute | solution.py:990
  15.5 2.6 %collective-permute-start.11 = (f32[8,32,256]{2,1,0:T(8,128)S(1)}, f32[8,32,256]{2,1,0:T(8,128)S(1)}, u32[]{:S(2)}, u32[]{:S(2)}) collective-permute-start(f32[8,32,256]{2,1,0:T(8,128)S(1)} %get-tuple-element.77), channel_id=1, source_target_pairs={{0,24},{8,16},{16,8},{24,0},{1,25},{9,17},{17,9},{25,1},{2,26},{10... | collective-permute-start | bytes 786440 | tf_op jit(solution)/shard_map/ppermute | solution.py:990
  18.2 0.0 collective-permute-start.5
  18.2 1.6 %collective-permute-start.6 = (f32[40,256]{1,0:T(8,128)S(1)}, f32[40,256]{1,0:T(8,128)S(1)}, u32[]{:S(2)}, u32[]{:S(2)}) collective-permute-start(f32[40,256]{1,0:T(8,128)S(1)} %get-tuple-element.63), channel_id=1, source_target_pairs={{0,6},{2,4},{4,2},{6,0},{1,7},{3,5},{5,3},{7,1},{8,14},{10,12},{12... | collective-permute-start | bytes 122888 | tf_op jit(solution)/shard_map/ppermute | solution.py:990
  19.8 1.5 %collective-permute-start.7 = (f32[24,128]{1,0:T(8,128)S(1)}, f32[24,128]{1,0:T(8,128)S(1)}, u32[]{:S(2)}, u32[]{:S(2)}) collective-permute-start(f32[24,128]{1,0:T(8,128)S(1)} %get-tuple-element.64), channel_id=1, source_target_pairs={{0,1},{1,0},{2,3},{3,2},{4,5},{5,4},{6,7},{7,6},{8,9},{9,8},{10,11... | collective-permute-start | bytes 36872 | tf_op jit(solution)/shard_map/ppermute | solution.py:995
  21.3 0.0 copy-done.1
  21.3 0.0 copy-done.2
  21.3 0.0 copy-done.3
  21.3 0.3 shard_map.99
  21.6 1.8 %collective-permute-done.7.z_rows.refs_0_ = f32[24,128]{1,0:T(8,128)S(1)} collective-permute-done((f32[24,128]{1,0:T(8,128)S(1)}, f32[24,128]{1,0:T(8,128)S(1)}, u32[]{:S(2)}, u32[]{:S(2)}) %collective-permute-start.7) | collective-permute-done | bytes 12320 | tf_op jit(solution)/shard_map/ppermute | solution.py:995
  23.5 0.0 collective-permute-done.5.y_first.refs_1_
  23.5 0.0 collective-permute-done.6.y_second.refs_2_
  23.5 0.1 collective-permute-start.8
  23.6 0.1 collective-permute-start.12
  23.7 1.7 %collective-permute-start.13 = (f32[32,128]{1,0:T(8,128)S(1)}, f32[32,128]{1,0:T(8,128)S(1)}, u32[]{:S(2)}, u32[]{:S(2)}) collective-permute-start(f32[32,128]{1,0:T(8,128)S(1)} %get-tuple-element.79), channel_id=1, source_target_pairs={{0,24},{8,16},{16,8},{24,0},{1,25},{9,17},{17,9},{25,1},{2,26},{10... | collective-permute-start | bytes 49160 | tf_op jit(solution)/shard_map/ppermute | solution.py:990
  25.4 0.0 collective-permute-done.8.corner_first
  25.4 0.0 collective-permute-start.9
  25.4 1.2 %shard_map.102 = (f32[6,4,32,256]{3,2,1,0:T(8,128)}, f32[8,128]{1,0:T(8,128)S(1)}) custom-call(f32[6,4,32,256]{3,2,1,0:T(8,128)S(1)} %get-tuple-element.50.stretch, f32[5,4,32,256]{3,2,1,0:T(8,128)S(1)} %get-tuple-element.51.flow, f32[40,256]{1,0:T(8,128)S(1)} %collective-permute-done.5.y_first.refs_1_, ...), custom_call_target="tpu_custom_call" | custom-call | flops 2621440 | bytes 1310720 | tf_op jit(solution)/shard_map/pallas_call | solution.py:1117
  26.6 0.9 %shard_map.98 = (f32[15,2,32,256]{3,2,1,0:T(8,128)S(1)}, f32[15,2,32,256]{3,2,1,0:T(8,128)S(1)}, f32[4,32,256]{2,1,0:T(8,128)S(1)}, f32[4,32,256]{2,1,0:T(8,128)S(1)}) custom-call(f32[19,2,32,256]{3,2,1,0:T(8,128)S(1)} %get-tuple-element.55.inner.inner_post, f32[19,2,32,256]{3,2,1,0:T(8,128)S(1)} %get-tuple-element.59.outer_post.post, ...), custom_call_target="tpu_custom_call" | custom-call | flops 11468800 | bytes 6553600 | tf_op jit(solution)/shard_map/pallas_call | solution.py:1097
  27.6 1.0 %collective-permute-done.9.corner_second = f32[24,128]{1,0:T(8,128)S(1)} collective-permute-done((f32[24,128]{1,0:T(8,128)S(1)}, f32[24,128]{1,0:T(8,128)S(1)}, u32[]{:S(2)}, u32[]{:S(2)}) %collective-permute-start.9) | collective-permute-done | bytes 12320 | tf_op jit(solution)/shard_map/ppermute | solution.py:990
  28.6 0.0 copy-done
  28.6 0.6 %shard_map.101 = (f32[4,2,32,256]{3,2,1,0:T(8,128)S(1)}, f32[4,2,32,256]{3,2,1,0:T(8,128)S(1)}, f32[2,32,256]{2,1,0:T(8,128)S(1)}, f32[2,32,256]{2,1,0:T(8,128)S...) custom-call(f32[19,2,32,256]{3,2,1,0:T(8,128)S(1)} %get-tuple-element.55.inner.inner_post, ...), custom_call_target="tpu_custom_call" | custom-call | flops 3276800 | bytes 1966080 | tf_op jit(solution)/shard_map/pallas_call | solution.py:1111
  29.2 0.6 %collective-permute-done.12.edges_first = f32[32,128]{1,0:T(8,128)S(1)} collective-permute-done((f32[32,128]{1,0:T(8,128)S(1)}, f32[32,128]{1,0:T(8,128)S(1)}, u32[]{:S(2)}, u32[]{:S(2)}) %collective-permute-start.12) | collective-permute-done | bytes 16416 | tf_op jit(solution)/shard_map/ppermute | solution.py:990
  29.7 0.0 collective-permute-done.13.edges_second
  29.7 0.0 collective-permute-done.10.x_first
  29.7 0.0 collective-permute-done.11.x_second
  29.7 0.8 %shard_map.103 = (f32[5,2,32,256]{3,2,1,0:T(8,128)S(1)}, f32[2,32,256]{2,1,0:T(8,128)S(1)}, f32[6,32,256]{2,1,0:T(8,128)S(1)}, f32[8,256]{1,0:T(8,128)S(1)}, f32...) custom-call(f32[19,2,32,256]{3,2,1,0:T(8,128)S(1)} %get-tuple-element.59.outer_post.post, ...), custom_call_target="tpu_custom_call" | custom-call | flops 4915200 | bytes 3276800 | tf_op jit(solution)/shard_map/pallas_call | solution.py:1124
  30.5 1.5 %collective-permute-start.14 = (f32[16,128]{1,0:T(8,128)S(1)}, f32[16,128]{1,0:T(8,128)S(1)}, u32[]{:S(2)}, u32[]{:S(2)}) collective-permute-start(f32[16,128]{1,0:T(8,128)S(1)} %get-tuple-element.89), channel_id=1, source_target_pairs={{0,1},{1,0},{2,3},{3,2},{4,5},{5,4},{6,7},{7,6},{8,9},{9,8},{10,11... | collective-permute-start | bytes 24584 | tf_op jit(solution)/shard_map/ppermute | solution.py:995
  32.0 0.0 collective-permute-start.15
  32.0 1.6 %collective-permute-start.16 = (f32[8,256]{1,0:T(8,128)S(1)}, f32[8,256]{1,0:T(8,128)S(1)}, u32[]{:S(2)}, u32[]{:S(2)}) collective-permute-start(f32[8,256]{1,0:T(8,128)S(1)} %get-tuple-element.91), channel_id=1, source_target_pairs={{0,6},{2,4},{4,2},{6,0},{1,7},{3,5},{5,3},{7,1},{8,14},{10,12},{12... | collective-permute-start | bytes 24584 | tf_op jit(solution)/shard_map/ppermute | solution.py:990
  33.6 1.1 %shard_map.105 = (f32[6,4,32,256]{3,2,1,0:T(8,128)}, f32[8,128]{1,0:T(8,128)S(1)}) custom-call(f32[6,4,32,256]{3,2,1,0:T(8,128)S(1)} %get-tuple-element.50.stretch, f32[5,4,32,256]{3,2,1,0:T(8,128)S(1)} %get-tuple-element.51.flow, f32[8,32,256]{2,1,0:T(8,128)S(1)} %collective-permute-done.10.x_first, ...), custom_call_target="tpu_custom_call", output_to_operand_aliasing={{0}: (7, {})} | custom-call | flops 2621440 | bytes 1310720 | tf_op jit(solution)/shard_map/pallas_call | solution.py:1147
  34.7 0.0 collective-permute-done.14.z_rows
  34.7 0.0 collective-permute-done.15.y_first
  34.7 0.4 collective-permute-done.16.y_second
  35.1 0.2 shard_map.107
  35.2 1.8 %collective-permute-start.19 = (f32[32,256]{1,0:T(8,128)S(1)}, f32[32,256]{1,0:T(8,128)S(1)}, u32[]{:S(2)}, u32[]{:S(2)}) collective-permute-start(f32[32,256]{1,0:T(8,128)S(1)} %get-tuple-element.93), channel_id=1, source_target_pairs={{0,24},{8,16},{16,8},{24,0},{1,25},{9,17},{17,9},{25,1},{2,26},{10... | collective-permute-start | bytes 98312 | tf_op jit(solution)/shard_map/ppermute | solution.py:990
  37.1 0.1 collective-permute-start.20
  37.2 0.0 collective-permute-start.17
  37.2 0.9 %collective-permute-start.18 = (f32[16,128]{1,0:T(8,128)S(1)}, f32[16,128]{1,0:T(8,128)S(1)}, u32[]{:S(2)}, u32[]{:S(2)}) collective-permute-start(f32[16,128]{1,0:T(8,128)S(1)} %collective-permute-done.14.z_rows), channel_id=1, source_target_pairs={{0,6},{2,4},{4,2},{6,0},{1,7},{3,5},{5,3},{7,1},{8,14},{10,12},{12... | collective-permute-start | bytes 24584 | tf_op jit(solution)/shard_map/ppermute | solution.py:990
  38.2 1.7 %shard_map.104 = f32[19,4,32,256]{3,2,1,0:T(8,128)} custom-call(f32[15,2,32,256]{3,2,1,0:T(8,128)S(1)} %get-tuple-element.65.inner, f32[15,2,32,256]{3,2,1,0:T(8,128)S(1)} %get-tuple-element.66.outer, f32[4,2,32,256]{3,2,1,0:T(8,128)S(1)} %get-tuple-element.72.inner_slanted, f32[4,2,32,256]{3,2,1,0:T(8,128)S(1)} %get-tuple-element.73.outer_slanted, ...), custom_call_target="tpu_custom_call" | custom-call | bytes 5242880 | tf_op jit(solution)/shard_map/pallas_call | solution.py:1160
  39.9 0.2 shard_map.106.summed
  40.1 0.0 collective-permute-done.17.corner_first
  40.1 0.2 collective-permute-done.18.corner_second
  40.3 1.0 %collective-permute-done.19.x_second = f32[32,256]{1,0:T(8,128)S(1)} collective-permute-done((f32[32,256]{1,0:T(8,128)S(1)}, f32[32,256]{1,0:T(8,128)S(1)}, u32[]{:S(2)}, u32[]{:S(2)}) %collective-permute-start.19) | collective-permute-done | bytes 32800 | tf_op jit(solution)/shard_map/ppermute | solution.py:990
  41.3 0.1 collective-permute-done.20.x_first
  41.3 0.8 %shard_map.108 = f32[4,32,256]{2,1,0:T(8,128)} custom-call(f32[4,32,256]{2,1,0:T(8,128)S(1)} %shard_map.106.summed, f32[16,128]{1,0:T(8,128)S(1)} %collective-permute-done.17.corner_first, f32[16,128]{1,0:T(8,128)S(1)} %collective-permute-done.18.corner_second, f32[32,256]{1,0:T(8,128)S(1)} %collective-permute-done.19.x_second, ...), custom_call_target="tpu_custom_call" | custom-call | tf_op jit(solution)/shard_map/pallas_call | solution.py:1170
  (1 shorter events, 0.0 us)
Async XLA Ops:
  2.2 11.6 %collective-permute-start.3 = (f32[4,32,256]{2,1,0:T(8,128)S(1)}, f32[4,32,256]{2,1,0:T(8,128)S(1)}, u32[]{:S(2)}, u32[]{:S(2)}) collective-permute-start(f32[4,32,256]{2,1,0:T(8,128)S(1)} %get-tuple-element.57), channel_id=1, source_target_pairs={{0,8},{8,0},{16,24},{24,16},{1,9},{9,1},{17,25},{25,17},{2,10},{10... | collective-permute-start | bytes 393224 | tf_op jit(solution)/shard_map/ppermute | solution.py:990
  5.3 8.6 %collective-permute-start.4 = (f32[4,32,256]{2,1,0:T(8,128)S(1)}, f32[4,32,256]{2,1,0:T(8,128)S(1)}, u32[]{:S(2)}, u32[]{:S(2)}) collective-permute-start(f32[4,32,256]{2,1,0:T(8,128)S(1)} %get-tuple-element.58), channel_id=1, source_target_pairs={{0,24},{8,16},{16,8},{24,0},{1,25},{9,17},{17,9},{25,1},{2,26},{10... | collective-permute-start | bytes 393224 | tf_op jit(solution)/shard_map/ppermute | solution.py:990
  7.8 5.2 %collective-permute-start.1 = (f32[16,256]{1,0:T(8,128)S(1)}, f32[16,256]{1,0:T(8,128)S(1)}, u32[]{:S(2)}, u32[]{:S(2)}) collective-permute-start(f32[16,256]{1,0:T(8,128)S(1)} %get-tuple-element.53), channel_id=1, source_target_pairs={{0,2},{2,0},{4,6},{6,4},{1,3},{3,1},{5,7},{7,5},{8,10},{10,8},{12,... | collective-permute-start | bytes 49160 | tf_op jit(solution)/shard_map/ppermute | solution.py:990
  7.8 5.2 %collective-permute-start.2 = (f32[16,256]{1,0:T(8,128)S(1)}, f32[16,256]{1,0:T(8,128)S(1)}, u32[]{:S(2)}, u32[]{:S(2)}) collective-permute-start(f32[16,256]{1,0:T(8,128)S(1)} %get-tuple-element.54), channel_id=1, source_target_pairs={{0,6},{2,4},{4,2},{6,0},{1,7},{3,5},{5,3},{7,1},{8,14},{10,12},{12... | collective-permute-start | bytes 49160 | tf_op jit(solution)/shard_map/ppermute | solution.py:990
  9.4 3.6 %collective-permute-start = (f32[8,128]{1,0:T(8,128)S(1)}, f32[8,128]{1,0:T(8,128)S(1)}, u32[]{:S(2)}, u32[]{:S(2)}) collective-permute-start(f32[8,128]{1,0:T(8,128)S(1)} %get-tuple-element.52), channel_id=1, source_target_pairs={{0,1},{1,0},{2,3},{3,2},{4,5},{5,4},{6,7},{7,6},{8,9},{9,8},{10,11... | collective-permute-start | bytes 12296 | tf_op jit(solution)/shard_map/ppermute | solution.py:995
  13.9 7.4 %copy-start.1 = (s32[1024]{0:T(1024)S(1)}, s32[1024]{0:T(1024)}, u32[]{:S(2)}) copy-start(s32[1024]{0:T(1024)} %param.11) | copy-start | bytes 12292
  13.9 7.4 %copy-start.2 = (s32[1024]{0:T(1024)S(1)}, s32[1024]{0:T(1024)}, u32[]{:S(2)}) copy-start(s32[1024]{0:T(1024)} %param.12) | copy-start | bytes 12292
  13.9 7.4 %copy-start.3 = (s32[1024]{0:T(1024)S(1)}, s32[1024]{0:T(1024)}, u32[]{:S(2)}) copy-start(s32[1024]{0:T(1024)} %param.13) | copy-start | bytes 12292
  14.9 13.7 %copy-start = (f32[4,32,256]{2,1,0:T(8,128)S(1)}, f32[4,32,256]{2,1,0:T(8,128)}, u32[]{:S(2)}) copy-start(f32[4,32,256]{2,1,0:T(8,128)} %mass.3) | copy-start | bytes 393220
  14.9 14.8 %collective-permute-start.10 = (f32[8,32,256]{2,1,0:T(8,128)S(1)}, f32[8,32,256]{2,1,0:T(8,128)S(1)}, u32[]{:S(2)}, u32[]{:S(2)}) collective-permute-start(f32[8,32,256]{2,1,0:T(8,128)S(1)} %get-tuple-element.76), channel_id=1, source_target_pairs={{0,8},{8,0},{16,24},{24,16},{1,9},{9,1},{17,25},{25,17},{2,10},{10... | collective-permute-start | bytes 786440 | tf_op jit(solution)/shard_map/ppermute | solution.py:990
  15.5 14.2 %collective-permute-start.11 = (f32[8,32,256]{2,1,0:T(8,128)S(1)}, f32[8,32,256]{2,1,0:T(8,128)S(1)}, u32[]{:S(2)}, u32[]{:S(2)}) collective-permute-start(f32[8,32,256]{2,1,0:T(8,128)S(1)} %get-tuple-element.77), channel_id=1, source_target_pairs={{0,24},{8,16},{16,8},{24,0},{1,25},{9,17},{17,9},{25,1},{2,26},{10... | collective-permute-start | bytes 786440 | tf_op jit(solution)/shard_map/ppermute | solution.py:990
  18.2 5.3 %collective-permute-start.5 = (f32[40,256]{1,0:T(8,128)S(1)}, f32[40,256]{1,0:T(8,128)S(1)}, u32[]{:S(2)}, u32[]{:S(2)}) collective-permute-start(f32[40,256]{1,0:T(8,128)S(1)} %get-tuple-element.62), channel_id=1, source_target_pairs={{0,2},{2,0},{4,6},{6,4},{1,3},{3,1},{5,7},{7,5},{8,10},{10,8},{12,... | collective-permute-start | bytes 122888 | tf_op jit(solution)/shard_map/ppermute | solution.py:990
  18.2 5.3 %collective-permute-start.6 = (f32[40,256]{1,0:T(8,128)S(1)}, f32[40,256]{1,0:T(8,128)S(1)}, u32[]{:S(2)}, u32[]{:S(2)}) collective-permute-start(f32[40,256]{1,0:T(8,128)S(1)} %get-tuple-element.63), channel_id=1, source_target_pairs={{0,6},{2,4},{4,2},{6,0},{1,7},{3,5},{5,3},{7,1},{8,14},{10,12},{12... | collective-permute-start | bytes 122888 | tf_op jit(solution)/shard_map/ppermute | solution.py:990
  19.8 3.7 %collective-permute-start.7 = (f32[24,128]{1,0:T(8,128)S(1)}, f32[24,128]{1,0:T(8,128)S(1)}, u32[]{:S(2)}, u32[]{:S(2)}) collective-permute-start(f32[24,128]{1,0:T(8,128)S(1)} %get-tuple-element.64), channel_id=1, source_target_pairs={{0,1},{1,0},{2,3},{3,2},{4,5},{5,4},{6,7},{7,6},{8,9},{9,8},{10,11... | collective-permute-start | bytes 36872 | tf_op jit(solution)/shard_map/ppermute | solution.py:995
  23.5 1.9 %collective-permute-start.8 = (f32[24,128]{1,0:T(8,128)S(1)}, f32[24,128]{1,0:T(8,128)S(1)}, u32[]{:S(2)}, u32[]{:S(2)}) collective-permute-start(f32[24,128]{1,0:T(8,128)S(1)} %get-tuple-element.69), channel_id=1, source_target_pairs={{0,2},{2,0},{4,6},{6,4},{1,3},{3,1},{5,7},{7,5},{8,10},{10,8},{12,... | collective-permute-start | bytes 36872 | tf_op jit(solution)/shard_map/ppermute | solution.py:990
  23.6 6.1 %collective-permute-start.12 = (f32[32,128]{1,0:T(8,128)S(1)}, f32[32,128]{1,0:T(8,128)S(1)}, u32[]{:S(2)}, u32[]{:S(2)}) collective-permute-start(f32[32,128]{1,0:T(8,128)S(1)} %get-tuple-element.78), channel_id=1, source_target_pairs={{0,8},{8,0},{16,24},{24,16},{1,9},{9,1},{17,25},{25,17},{2,10},{10... | collective-permute-start | bytes 49160 | tf_op jit(solution)/shard_map/ppermute | solution.py:990
  23.7 6.1 %collective-permute-start.13 = (f32[32,128]{1,0:T(8,128)S(1)}, f32[32,128]{1,0:T(8,128)S(1)}, u32[]{:S(2)}, u32[]{:S(2)}) collective-permute-start(f32[32,128]{1,0:T(8,128)S(1)} %get-tuple-element.79), channel_id=1, source_target_pairs={{0,24},{8,16},{16,8},{24,0},{1,25},{9,17},{17,9},{25,1},{2,26},{10... | collective-permute-start | bytes 49160 | tf_op jit(solution)/shard_map/ppermute | solution.py:990
  25.4 3.2 %collective-permute-start.9 = (f32[24,128]{1,0:T(8,128)S(1)}, f32[24,128]{1,0:T(8,128)S(1)}, u32[]{:S(2)}, u32[]{:S(2)}) collective-permute-start(f32[24,128]{1,0:T(8,128)S(1)} %get-tuple-element.69), channel_id=1, source_target_pairs={{0,6},{2,4},{4,2},{6,0},{1,7},{3,5},{5,3},{7,1},{8,14},{10,12},{12... | collective-permute-start | bytes 36872 | tf_op jit(solution)/shard_map/ppermute | solution.py:990
  30.5 4.2 %collective-permute-start.14 = (f32[16,128]{1,0:T(8,128)S(1)}, f32[16,128]{1,0:T(8,128)S(1)}, u32[]{:S(2)}, u32[]{:S(2)}) collective-permute-start(f32[16,128]{1,0:T(8,128)S(1)} %get-tuple-element.89), channel_id=1, source_target_pairs={{0,1},{1,0},{2,3},{3,2},{4,5},{5,4},{6,7},{7,6},{8,9},{9,8},{10,11... | collective-permute-start | bytes 24584 | tf_op jit(solution)/shard_map/ppermute | solution.py:995
  32.0 2.7 %collective-permute-start.15 = (f32[8,256]{1,0:T(8,128)S(1)}, f32[8,256]{1,0:T(8,128)S(1)}, u32[]{:S(2)}, u32[]{:S(2)}) collective-permute-start(f32[8,256]{1,0:T(8,128)S(1)} %get-tuple-element.90), channel_id=1, source_target_pairs={{0,2},{2,0},{4,6},{6,4},{1,3},{3,1},{5,7},{7,5},{8,10},{10,8},{12,... | collective-permute-start | bytes 24584 | tf_op jit(solution)/shard_map/ppermute | solution.py:990
  32.0 3.1 %collective-permute-start.16 = (f32[8,256]{1,0:T(8,128)S(1)}, f32[8,256]{1,0:T(8,128)S(1)}, u32[]{:S(2)}, u32[]{:S(2)}) collective-permute-start(f32[8,256]{1,0:T(8,128)S(1)} %get-tuple-element.91), channel_id=1, source_target_pairs={{0,6},{2,4},{4,2},{6,0},{1,7},{3,5},{5,3},{7,1},{8,14},{10,12},{12... | collective-permute-start | bytes 24584 | tf_op jit(solution)/shard_map/ppermute | solution.py:990
  35.2 6.0 %collective-permute-start.19 = (f32[32,256]{1,0:T(8,128)S(1)}, f32[32,256]{1,0:T(8,128)S(1)}, u32[]{:S(2)}, u32[]{:S(2)}) collective-permute-start(f32[32,256]{1,0:T(8,128)S(1)} %get-tuple-element.93), channel_id=1, source_target_pairs={{0,24},{8,16},{16,8},{24,0},{1,25},{9,17},{17,9},{25,1},{2,26},{10... | collective-permute-start | bytes 98312 | tf_op jit(solution)/shard_map/ppermute | solution.py:990
  37.1 4.3 %collective-permute-start.20 = (f32[32,256]{1,0:T(8,128)S(1)}, f32[32,256]{1,0:T(8,128)S(1)}, u32[]{:S(2)}, u32[]{:S(2)}) collective-permute-start(f32[32,256]{1,0:T(8,128)S(1)} %get-tuple-element.94), channel_id=1, source_target_pairs={{0,8},{8,0},{16,24},{24,16},{1,9},{9,1},{17,25},{25,17},{2,10},{10... | collective-permute-start | bytes 98312 | tf_op jit(solution)/shard_map/ppermute | solution.py:990
  37.2 2.9 %collective-permute-start.17 = (f32[16,128]{1,0:T(8,128)S(1)}, f32[16,128]{1,0:T(8,128)S(1)}, u32[]{:S(2)}, u32[]{:S(2)}) collective-permute-start(f32[16,128]{1,0:T(8,128)S(1)} %collective-permute-done.14.z_rows), channel_id=1, source_target_pairs={{0,2},{2,0},{4,6},{6,4},{1,3},{3,1},{5,7},{7,5},{8,10},{10,8},{12,... | collective-permute-start | bytes 24584 | tf_op jit(solution)/shard_map/ppermute | solution.py:990
  37.2 3.1 %collective-permute-start.18 = (f32[16,128]{1,0:T(8,128)S(1)}, f32[16,128]{1,0:T(8,128)S(1)}, u32[]{:S(2)}, u32[]{:S(2)}) collective-permute-start(f32[16,128]{1,0:T(8,128)S(1)} %collective-permute-done.14.z_rows), channel_id=1, source_target_pairs={{0,6},{2,4},{4,2},{6,0},{1,7},{3,5},{5,3},{7,1},{8,14},{10,12},{12... | collective-permute-start | bytes 24584 | tf_op jit(solution)/shard_map/ppermute | solution.py:990

commit v5 on v2

--- a/solution.py
+++ b/solution.py
@@ -400,10 +400,6 @@
         up, down = (post[x_up[slot], 1], post[x_down[slot], 0])
         ahead[slot] = jnp.where(flip_x, down, up)
         behind[slot] = jnp.where(flip_x, up, down)
-    for comp in range(3):
-        up, down = (flow[comp, bx - 1], flow[comp, 0])
-        ahead[5 + comp] = jnp.where(flip_x, down, up)
-        behind[5 + comp] = jnp.where(flip_x, up, down)
 
 
 def restretch_plane(x, place, stretch, flow, halos, updated):
@@ -473,6 +469,7 @@
     z_rows,
     inner_stretch,
     new_stretch,
+    mark,
     updated,
     below,
     above,
@@ -484,8 +481,8 @@
     bx = stretch.shape[1]
     flip_x = odd("gx")
     for comp in range(3):
-        below[comp] = jnp.where(flip_x, x_first[5 + comp], x_second[5 + comp])
-        above[comp] = jnp.where(flip_x, x_second[5 + comp], x_first[5 + comp])
+        below[comp] = jnp.where(flip_x, x_first[comp], x_second[comp])
+        above[comp] = jnp.where(flip_x, x_second[comp], x_first[comp])
     swapped_rows(y_first, y_second, range(speed_slot, sides), y_below, y_above, 0)
     z_halo[...] = row_columns(z_rows[...]).reshape(z_halo.shape)
     halos = (below, above, y_below, y_above, z_halo)
@@ -496,11 +493,12 @@
             pltpu.make_async_copy(updated.at[:, place], new_stretch.at[:, x], sems.at[place])
         )
         copies[-1].start()
+    mark[...] = jnp.zeros(mark.shape, jnp.float32)
     for copy in copies:
         copy.wait()
 
 
-def store(inner, outer, inner_slanted, outer_slanted, late, fresh, mark, sems):
+def store(inner, outer, inner_slanted, outer_slanted, late, fresh, sems):
     bx = fresh.shape[1]
     moves = [
         (inner, fresh.at[0:first_slanted, 1 : bx - 1]),
@@ -523,7 +521,6 @@
     ]
     for copy in copies:
         copy.start()
-    mark[...] = jnp.zeros(mark.shape, jnp.float32)
     for copy in copies:
         copy.wait()
 
@@ -774,8 +771,11 @@
     edges_second,
     inner_excess,
     inner_heading,
+    flow,
     after,
     late,
+    v_first,
+    v_second,
     settled,
     spread,
     line_first,
@@ -795,6 +795,10 @@
     flip_x = odd("gx")
     halos = (gas, low_rows, high_rows, columns)
 
+    for comp in range(3):
+        up, down = (flow[comp, bx - 1], flow[comp, 0])
+        v_first[comp] = jnp.where(flip_x, down, up)
+        v_second[comp] = jnp.where(flip_x, up, down)
     for slot in range(5):
         below[slot] = jnp.where(flip_x, x_first[slot], x_second[slot])
         above[slot] = jnp.where(flip_x, x_second[slot], x_first[slot])
@@ -922,7 +926,7 @@
     return total + jnp.where(row_at == by - 1, y_above[target : target + 1, :], 0.0)
 
 
-def add_faces(spread, z_rows, y_first, y_second, after, first, second):
+def add_faces(spread, z_rows, y_first, y_second, first, second):
     last = spread.shape[0] - 1
     flip_x, flip_y = (odd("gx"), odd("gy"))
     tile = row_columns(z_rows[...])
@@ -944,6 +948,7 @@
     corner_second,
     x_second,
     x_first,
+    after,
     new_mass,
 ):
     bx, by, bz = new_mass.shape
@@ -989,6 +994,7 @@
 
 
 remote = pl.BlockSpec(memory_space=pltpu.HBM)
+anywhere = pl.BlockSpec(memory_space=pl.ANY)
 
 
 def call(body, outs, specs=None, out_specs=None, scratch=(), cost=(0, 0), aliases=None):
@@ -1039,8 +1045,11 @@
     y_first = swapped(y_one, y_two, "gy")
 
     entries = conv_source.shape[0]
+    mark = (tall, lanes)
     (code,) = call(
-        lambda *refs: conversions(*refs, columns=bz), [(bx * by, bz)], cost=(40 * cells, 4 * cells)
+        lambda *refs: conversions(*refs, columns=bz),
+        [(bx * by, bz)],
+        cost=(40 * cells, 4 * cells),
     )(*(array.reshape(1, entries) for array in (conv_source, conv_kind, conv_direction)))
     code = code.reshape(box)
 
@@ -1063,7 +1072,7 @@
     )(pops, stretch, flow, z_first, *y_first)
     outer_post, outer_shift, z_out, x_one, x_two, y_one, y_two = call(
         collide_outer,
-        [(19, *ends), (3, *ends), columns, (8, *face), (8, *face), rows, rows],
+        [(19, *ends), (3, *ends), columns, (5, *face), (5, *face), rows, rows],
         scratch=[(4, *face), (4, *face)] + sides_y + [box],
         cost=(150 * cells, 150 * cells),
     )(pops, stretch, flags, flow, *first_x, *y_first, z_first, inner_post)
@@ -1072,7 +1081,7 @@
     post_x = swapped(x_one, x_two, "gx")
     edges = (4 * (bz // lanes) + columns[0], lanes)
     x_one, x_two, corner = call(
-        lambda *refs: forward_edges(*refs, bx=bx), [edges, edges, columns]
+        lambda *refs: forward_edges(*refs, bx=bx), [edges, edges, columns], cost=(4 * 10**9, 0)
     )(z_post, *post_y)
     corners = swapped(corner, corner, "gy")
     edges_x = swapped(x_one, x_two, "gx")
@@ -1099,7 +1108,6 @@
         scratch=rims,
         cost=(100 * cells, 60 * cells),
     )(*posts, mass, flags, code, *post_y, z_post, *corners, totals, changes)
-    mark = (tall, lanes)
     new_stretch, inner_done = call(
         restretch_inner,
         [(6, *box), mark],
@@ -1107,9 +1115,18 @@
         scratch=[(6, *inside)] + sides_y + [pltpu.SemaphoreType.DMA],
         cost=(80 * cells, 40 * cells),
     )(stretch, flow, *post_y, z_post)
-    late, outer_settled, spread, y_one, y_two, z_out = call(
+    late, v_one, v_two, outer_settled, spread, y_one, y_two, z_out = call(
         stream_late,
-        [(5, *ends), ends, (bx + 2, *face), (8, bz), (8, bz), (16, bx * by)],
+        [
+            (5, *ends),
+            (3, *face),
+            (3, *face),
+            ends,
+            (bx + 2, *face),
+            (8, bz),
+            (8, bz),
+            (16, bx * by),
+        ],
         scratch=rims + [(5, *face), (5, *face), box, box],
         cost=(150 * cells, 100 * cells),
     )(
@@ -1125,33 +1142,35 @@
         *edges_x,
         inner_excess,
         inner_heading,
+        flow,
         inner_done,
     )
     z_last = both_ways(z_out, 8)
     last_y = swapped(y_one, y_two, "gy")
     last_corners = swapped(z_last, z_last, "gy")
-    fresh, stored = call(
+    flow_x = swapped(v_one, v_two, "gx")
+    x_one, x_two = call(add_faces, [face, face], cost=(4 * 10**9, 0))(spread, z_last, *last_y)
+    last_x = swapped(x_one, x_two, "gx")
+    (fresh,) = call(
         store,
-        [(19, *box), mark],
-        out_specs=[remote, pl.BlockSpec()],
+        [(19, *box)],
+        out_specs=[remote],
         scratch=[pltpu.SemaphoreType.DMA((32,))],
         cost=(0, 160 * cells),
     )(inner, outer, inner_slanted, outer_slanted, late)
-    x_one, x_two = call(add_faces, [face, face])(spread, z_last, *last_y, stored)
-    last_x = swapped(x_one, x_two, "gx")
-    (new_stretch,) = call(
+    new_stretch, outer_done = call(
         restretch_outer,
-        [(6, *box)],
+        [(6, *box), mark],
         specs=[pl.BlockSpec()] * 7 + [remote],
-        out_specs=[remote],
+        out_specs=[remote, pl.BlockSpec()],
         scratch=[(6, *ends), (3, *face), (3, *face)]
         + sides_y
         + [pltpu.SemaphoreType.DMA((2,))],
         cost=(80 * cells, 40 * cells),
         aliases={7: 0},
-    )(stretch, flow, *post_x, *post_y, z_post, new_stretch)
+    )(stretch, flow, *flow_x, *post_y, z_post, new_stretch)
     (new_mass,) = call(add_all, [box])(
-        inner_settled, outer_settled, spread, z_last, *last_y, *last_corners, *last_x[::-1]
+        inner_settled, outer_settled, spread, z_last, *last_y, *last_corners, *last_x[::-1], outer_done
     )
     return (fresh, new_stretch, new_mass)
 

time: 42.3 us -> 41.2 us (0.974)
  waiting for transfers between devices: 6.34 us -> 4.13 us
  starting transfers between devices: 22.4 us -> 23.5 us
    ppermute x9 -> x10, starting transfers between devices: 13.5 us -> 15.7 us  [swapped(): lax.ppermute(second, axis, behind)]
    ppermute x3, waiting for transfers between devices: 2.52 us -> 0.78 us  [both_ways(): lax.ppermute(rows, 'gz', [(i, (i + 1) % devices) for i in range(devices)])]
    ppermute x3, starting transfers between devices: 4.61 us -> 3.6 us  [both_ways(): lax.ppermute(rows, 'gz', [(i, (i + 1) % devices) for i in range(devices)])]
    ppermute x9 -> x10, waiting for transfers between devices: 3.79 us -> 2.79 us  [swapped(): lax.ppermute(second, axis, behind)]
    ppermute x9 -> x10, waiting for transfers between devices: 0.02 us -> 0.56 us  [swapped(): lax.ppermute(first, axis, ahead)]
    ppermute x9 -> x10, starting transfers between devices: 4.3 us -> 4.19 us  [swapped(): lax.ppermute(first, axis, ahead)]
  transfers between devices with their start and end apart: 21 -> 23, of which waited for: 7 -> 6; matrix products, arithmetic and copies ran while one was open for 0% -> 0% of each run, Pallas kernels for 20% -> 21%
where the time goes in v5:
time: 41.2 us; the launch traced here: 40.9 us
  starting transfers between devices  23.5 us (57%)
  Pallas kernels  12.5 us (30%)
  waiting for transfers between devices  4.13 us (10%)
  between operations  0.83 us (2%)
    ppermute x10, starting transfers between devices, swapped(): lax.ppermute(second, axis, behind)  15.7 us
    ppermute x10, starting transfers between devices, swapped(): lax.ppermute(first, axis, ahead)  4.19 us
    ppermute x3, starting transfers between devices, both_ways(): lax.ppermute(rows, 'gz', [(i, (i + 1) % devices) for i in range(devices)])  3.6 us
    ppermute x10, waiting for transfers between devices, swapped(): lax.ppermute(second, axis, behind)  2.79 us
    pallas_call x1, Pallas kernels, shards(): call(moments, [(19, *box), (5, *box)], specs=[remote], scratch=[pltpu.Sem...  1.74 us
    pallas_call x1, Pallas kernels, shards(): call(store, [(19, *box)], out_specs=[remote], scratch=[pltpu.SemaphoreTyp...  1.7 us
    pallas_call x1, Pallas kernels, shards(): call(first_faces, [(6, *box), jax.ShapeDtypeStruct(box, jnp.int32), (8, b...  1.38 us
    pallas_call x1, Pallas kernels, shards(): call(restretch_inner, [(6, *box), mark], out_specs=[remote, pl.BlockSpec(...  1.19 us
  transfers between devices with their start and end apart: 23, of which 6 were waited for; matrix products, arithmetic and copies ran while one was open for 0% of the time, Pallas kernels for 21%

profile of v5, /device:TPU:0, one launch (start us, length us, event | category | flops | bytes accessed | tf_op | source)
XLA Modules:
  0.0 40.9 jit_solution(1976819921766637874)
XLA Ops:
  0.6 1.4 %shard_map.95 = (f32[6,4,32,256]{3,2,1,0:T(8,128)S(1)}, s32[4,32,256]{2,1,0:T(8,128)S(1)}, f32[8,128]{1,0:T(8,128)S(1)}, f32[16,256]{1,0:T(8,128)S(1)}, f32[16,2...) custom-call(f32[6,4,32,256]{3,2,1,0:T(8,128)} %stretch_in.1, s32[4,32,256]{2,1,0:T(8,128)} %flags_in.1), custom_call_target="tpu_custom_call" | custom-call | flops 327680 | bytes 1966080 | tf_op jit(solution)/shard_map/pallas_call | solution.py:1028
  2.0 3.1 %collective-permute-start.3 = (f32[4,32,256]{2,1,0:T(8,128)S(1)}, f32[4,32,256]{2,1,0:T(8,128)S(1)}, u32[]{:S(2)}, u32[]{:S(2)}) collective-permute-start(f32[4,32,256]{2,1,0:T(8,128)S(1)} %get-tuple-element.57), channel_id=1, source_target_pairs={{0,8},{8,0},{16,24},{24,16},{1,9},{9,1},{17,25},{25,17},{2,10},{10... | collective-permute-start | bytes 393224 | tf_op jit(solution)/shard_map/ppermute | solution.py:984
  5.1 2.5 %collective-permute-start.4 = (f32[4,32,256]{2,1,0:T(8,128)S(1)}, f32[4,32,256]{2,1,0:T(8,128)S(1)}, u32[]{:S(2)}, u32[]{:S(2)}) collective-permute-start(f32[4,32,256]{2,1,0:T(8,128)S(1)} %get-tuple-element.58), channel_id=1, source_target_pairs={{0,24},{8,16},{16,8},{24,0},{1,25},{9,17},{17,9},{25,1},{2,26},{10... | collective-permute-start | bytes 393224 | tf_op jit(solution)/shard_map/ppermute | solution.py:984
  7.6 0.0 collective-permute-start.1
  7.6 1.6 %collective-permute-start.2 = (f32[16,256]{1,0:T(8,128)S(1)}, f32[16,256]{1,0:T(8,128)S(1)}, u32[]{:S(2)}, u32[]{:S(2)}) collective-permute-start(f32[16,256]{1,0:T(8,128)S(1)} %get-tuple-element.54), channel_id=1, source_target_pairs={{0,6},{2,4},{4,2},{6,0},{1,7},{3,5},{5,3},{7,1},{8,14},{10,12},{12... | collective-permute-start | bytes 49160 | tf_op jit(solution)/shard_map/ppermute | solution.py:984
  9.2 1.5 %collective-permute-start = (f32[8,128]{1,0:T(8,128)S(1)}, f32[8,128]{1,0:T(8,128)S(1)}, u32[]{:S(2)}, u32[]{:S(2)}) collective-permute-start(f32[8,128]{1,0:T(8,128)S(1)} %get-tuple-element.52), channel_id=1, source_target_pairs={{0,1},{1,0},{2,3},{3,2},{4,5},{5,4},{6,7},{7,6},{8,9},{9,8},{10,11... | collective-permute-start | bytes 12296 | tf_op jit(solution)/shard_map/ppermute | solution.py:989
  10.7 1.7 %shard_map.94 = (f32[19,4,32,256]{3,2,1,0:T(8,128)S(1)}, f32[5,4,32,256]{3,2,1,0:T(8,128)S(1)}) custom-call(f32[19,4,32,256]{3,2,1,0:T(8,128)} %pops_in.1), custom_call_target="tpu_custom_call" | custom-call | flops 1966080 | bytes 4915200 | tf_op jit(solution)/shard_map/pallas_call | solution.py:1056
  12.5 0.3 collective-permute-done.z_rows
  12.8 0.0 collective-permute-done.1.y_first
  12.8 0.0 collective-permute-done.2.y_second
  12.8 0.8 %shard_map.96 = (f32[19,2,32,256]{3,2,1,0:T(8,128)S(1)}, f32[3,2,32,256]{3,2,1,0:T(8,128)S(1)}) custom-call(f32[19,4,32,256]{3,2,1,0:T(8,128)S(1)} %get-tuple-element.49.pops, f32[6,4,32,256]{3,2,1,0:T(8,128)S(1)} %get-tuple-element.50.stretch, f32[5,4,32,256]{3,2,1,0:T(8,128)S(1)} %get-tuple-element.51.flow, f32[8,128]{1,0:T(8,128)S(1)} %collective-permute-done.z_rows, ...), custom_call_target="tpu_custom_call" | custom-call | flops 4915200 | bytes 4915200 | tf_op jit(solution)/shard_map/pallas_call | solution.py:1067
  13.6 0.0 collective-permute-done.3.x_first.gas_first
  13.6 0.1 collective-permute-done.4.x_second.gas_second
  13.7 1.0 %shard_map.97 = (f32[19,2,32,256]{3,2,1,0:T(8,128)S(1)}, f32[3,2,32,256]{3,2,1,0:T(8,128)S(1)}, f32[24,128]{1,0:T(8,128)S(1)}, f32[5,32,256]{2,1,0:T(8,128)S(1)}...) custom-call(f32[19,4,32,256]{3,2,1,0:T(8,128)S(1)} %get-tuple-element.49.pops, ...), custom_call_target="tpu_custom_call" | custom-call | flops 4915200 | bytes 4915200 | tf_op jit(solution)/shard_map/pallas_call | solution.py:1073
  14.7 0.0 collective-permute-start.5
  14.8 1.6 %collective-permute-start.6 = (f32[40,256]{1,0:T(8,128)S(1)}, f32[40,256]{1,0:T(8,128)S(1)}, u32[]{:S(2)}, u32[]{:S(2)}) collective-permute-start(f32[40,256]{1,0:T(8,128)S(1)} %get-tuple-element.63), channel_id=1, source_target_pairs={{0,6},{2,4},{4,2},{6,0},{1,7},{3,5},{5,3},{7,1},{8,14},{10,12},{12... | collective-permute-start | bytes 122888 | tf_op jit(solution)/shard_map/ppermute | solution.py:984
  16.4 1.5 %collective-permute-start.7 = (f32[24,128]{1,0:T(8,128)S(1)}, f32[24,128]{1,0:T(8,128)S(1)}, u32[]{:S(2)}, u32[]{:S(2)}) collective-permute-start(f32[24,128]{1,0:T(8,128)S(1)} %get-tuple-element.64), channel_id=1, source_target_pairs={{0,1},{1,0},{2,3},{3,2},{4,5},{5,4},{6,7},{7,6},{8,9},{9,8},{10,11... | collective-permute-start | bytes 36872 | tf_op jit(solution)/shard_map/ppermute | solution.py:989
  17.9 0.6 %collective-permute-start.10 = (f32[5,32,256]{2,1,0:T(8,128)S(1)}, f32[5,32,256]{2,1,0:T(8,128)S(1)}, u32[]{:S(2)}, u32[]{:S(2)}) collective-permute-start(f32[5,32,256]{2,1,0:T(8,128)S(1)} %get-tuple-element.74), channel_id=1, source_target_pairs={{0,8},{8,0},{16,24},{24,16},{1,9},{9,1},{17,25},{25,17},{2,10},{10... | collective-permute-start | bytes 491528 | tf_op jit(solution)/shard_map/ppermute | solution.py:984
  18.5 2.6 %collective-permute-start.11 = (f32[5,32,256]{2,1,0:T(8,128)S(1)}, f32[5,32,256]{2,1,0:T(8,128)S(1)}, u32[]{:S(2)}, u32[]{:S(2)}) collective-permute-start(f32[5,32,256]{2,1,0:T(8,128)S(1)} %get-tuple-element.75), channel_id=1, source_target_pairs={{0,24},{8,16},{16,8},{24,0},{1,25},{9,17},{17,9},{25,1},{2,26},{10... | collective-permute-start | bytes 491528 | tf_op jit(solution)/shard_map/ppermute | solution.py:984
  21.1 0.0 collective-permute-done.7.z_rows.refs_0_
  21.1 0.0 collective-permute-done.5.y_first.refs_1_
  21.1 0.0 collective-permute-done.6.y_second.refs_2_
  21.2 0.0 copy-start
  21.2 0.1 collective-permute-start.8
  21.3 0.1 collective-permute-start.12
  21.3 2.1 %collective-permute-start.13 = (f32[32,128]{1,0:T(8,128)S(1)}, f32[32,128]{1,0:T(8,128)S(1)}, u32[]{:S(2)}, u32[]{:S(2)}) collective-permute-start(f32[32,128]{1,0:T(8,128)S(1)} %get-tuple-element.77), channel_id=1, source_target_pairs={{0,24},{8,16},{16,8},{24,0},{1,25},{9,17},{17,9},{25,1},{2,26},{10... | collective-permute-start | bytes 49160 | tf_op jit(solution)/shard_map/ppermute | solution.py:984
  23.5 0.0 collective-permute-done.8.corner_first
  23.5 0.0 collective-permute-start.9
  23.5 0.0 copy-done.1
  23.5 0.0 copy-done.2
  23.5 0.0 copy-done.3
  23.5 0.3 shard_map.99
  23.9 1.2 %shard_map.102 = (f32[6,4,32,256]{3,2,1,0:T(8,128)}, f32[8,128]{1,0:T(8,128)S(1)}) custom-call(f32[6,4,32,256]{3,2,1,0:T(8,128)S(1)} %get-tuple-element.50.stretch, f32[5,4,32,256]{3,2,1,0:T(8,128)S(1)} %get-tuple-element.51.flow, f32[40,256]{1,0:T(8,128)S(1)} %collective-permute-done.5.y_first.refs_1_, ...), custom_call_target="tpu_custom_call" | custom-call | flops 2621440 | bytes 1310720 | tf_op jit(solution)/shard_map/pallas_call | solution.py:1111
  25.1 0.9 %shard_map.98 = (f32[15,2,32,256]{3,2,1,0:T(8,128)S(1)}, f32[15,2,32,256]{3,2,1,0:T(8,128)S(1)}, f32[4,32,256]{2,1,0:T(8,128)S(1)}, f32[4,32,256]{2,1,0:T(8,128)S(1)}) custom-call(f32[19,2,32,256]{3,2,1,0:T(8,128)S(1)} %get-tuple-element.55.inner.inner_post, f32[19,2,32,256]{3,2,1,0:T(8,128)S(1)} %get-tuple-element.59.outer_post.post, ...), custom_call_target="tpu_custom_call" | custom-call | flops 11468800 | bytes 6553600 | tf_op jit(solution)/shard_map/pallas_call | solution.py:1091
  26.0 0.7 %collective-permute-done.9.corner_second = f32[24,128]{1,0:T(8,128)S(1)} collective-permute-done((f32[24,128]{1,0:T(8,128)S(1)}, f32[24,128]{1,0:T(8,128)S(1)}, u32[]{:S(2)}, u32[]{:S(2)}) %collective-permute-start.9) | collective-permute-done | bytes 12320 | tf_op jit(solution)/shard_map/ppermute | solution.py:984
  26.7 0.0 copy-done
  26.7 0.6 %shard_map.101 = (f32[4,2,32,256]{3,2,1,0:T(8,128)S(1)}, f32[4,2,32,256]{3,2,1,0:T(8,128)S(1)}, f32[2,32,256]{2,1,0:T(8,128)S(1)}, f32[2,32,256]{2,1,0:T(8,128)S...) custom-call(f32[19,2,32,256]{3,2,1,0:T(8,128)S(1)} %get-tuple-element.55.inner.inner_post, ...), custom_call_target="tpu_custom_call" | custom-call | flops 3276800 | bytes 1966080 | tf_op jit(solution)/shard_map/pallas_call | solution.py:1105
  27.3 0.0 collective-permute-done.12.edges_first
  27.3 2.0 %collective-permute-done.13.edges_second = f32[32,128]{1,0:T(8,128)S(1)} collective-permute-done((f32[32,128]{1,0:T(8,128)S(1)}, f32[32,128]{1,0:T(8,128)S(1)}, u32[]{:S(2)}, u32[]{:S(2)}) %collective-permute-start.13) | collective-permute-done | bytes 16416 | tf_op jit(solution)/shard_map/ppermute | solution.py:984
  29.2 0.0 collective-permute-done.10.x_first
  29.2 0.0 collective-permute-done.11.x_second
  29.3 0.7 %shard_map.103 = (f32[5,2,32,256]{3,2,1,0:T(8,128)S(1)}, f32[3,32,256]{2,1,0:T(8,128)S(1)}, f32[3,32,256]{2,1,0:T(8,128)S(1)}, f32[2,32,256]{2,1,0:T(8,128)S(1)}...) custom-call(f32[19,2,32,256]{3,2,1,0:T(8,128)S(1)} %get-tuple-element.59.outer, ...), custom_call_target="tpu_custom_call" | custom-call | flops 4915200 | bytes 3276800 | tf_op jit(solution)/shard_map/pallas_call | solution.py:1118
  30.0 0.6 %collective-permute-start.16 = (f32[16,128]{1,0:T(8,128)S(1)}, f32[16,128]{1,0:T(8,128)S(1)}, u32[]{:S(2)}, u32[]{:S(2)}) collective-permute-start(f32[16,128]{1,0:T(8,128)S(1)} %get-tuple-element.89), channel_id=1, source_target_pairs={{0,1},{1,0},{2,3},{3,2},{4,5},{5,4},{6,7},{7,6},{8,9},{9,8},{10,11... | collective-permute-start | bytes 24584 | tf_op jit(solution)/shard_map/ppermute | solution.py:989
  30.6 0.0 collective-permute-start.17
  30.6 0.6 %collective-permute-start.18 = (f32[8,256]{1,0:T(8,128)S(1)}, f32[8,256]{1,0:T(8,128)S(1)}, u32[]{:S(2)}, u32[]{:S(2)}) collective-permute-start(f32[8,256]{1,0:T(8,128)S(1)} %get-tuple-element.91), channel_id=1, source_target_pairs={{0,6},{2,4},{4,2},{6,0},{1,7},{3,5},{5,3},{7,1},{8,14},{10,12},{12... | collective-permute-start | bytes 24584 | tf_op jit(solution)/shard_map/ppermute | solution.py:984
  31.2 0.3 collective-permute-start.14
  31.5 1.7 %collective-permute-start.15 = (f32[3,32,256]{2,1,0:T(8,128)S(1)}, f32[3,32,256]{2,1,0:T(8,128)S(1)}, u32[]{:S(2)}, u32[]{:S(2)}) collective-permute-start(f32[3,32,256]{2,1,0:T(8,128)S(1)} %get-tuple-element.83), channel_id=1, source_target_pairs={{0,24},{8,16},{16,8},{24,0},{1,25},{9,17},{17,9},{25,1},{2,26},{10... | collective-permute-start | bytes 294920 | tf_op jit(solution)/shard_map/ppermute | solution.py:984
  33.3 0.4 %collective-permute-done.16.z_rows = f32[16,128]{1,0:T(8,128)S(1)} collective-permute-done((f32[16,128]{1,0:T(8,128)S(1)}, f32[16,128]{1,0:T(8,128)S(1)}, u32[]{:S(2)}, u32[]{:S(2)}) %collective-permute-start.16) | collective-permute-done | bytes 8224 | tf_op jit(solution)/shard_map/ppermute | solution.py:989
  33.7 0.0 collective-permute-done.17.y_first
  33.7 0.0 collective-permute-done.18.y_second
  33.7 0.2 shard_map.106
  33.9 1.7 %collective-permute-start.21 = (f32[32,256]{1,0:T(8,128)S(1)}, f32[32,256]{1,0:T(8,128)S(1)}, u32[]{:S(2)}, u32[]{:S(2)}) collective-permute-start(f32[32,256]{1,0:T(8,128)S(1)} %get-tuple-element.92), channel_id=1, source_target_pairs={{0,24},{8,16},{16,8},{24,0},{1,25},{9,17},{17,9},{25,1},{2,26},{10... | collective-permute-start | bytes 98312 | tf_op jit(solution)/shard_map/ppermute | solution.py:984
  35.6 0.0 collective-permute-start.22
  35.6 0.0 collective-permute-start.19
  35.6 0.5 %collective-permute-done.14.x_first = f32[3,32,256]{2,1,0:T(8,128)S(1)} collective-permute-done((f32[3,32,256]{2,1,0:T(8,128)S(1)}, f32[3,32,256]{2,1,0:T(8,128)S(1)}, u32[]{:S(2)}, u32[]{:S(2)}) %collective-permute-start.14) | collective-permute-done | bytes 98336 | tf_op jit(solution)/shard_map/ppermute | solution.py:984
  36.2 1.1 %collective-permute-start.20 = (f32[16,128]{1,0:T(8,128)S(1)}, f32[16,128]{1,0:T(8,128)S(1)}, u32[]{:S(2)}, u32[]{:S(2)}) collective-permute-start(f32[16,128]{1,0:T(8,128)S(1)} %collective-permute-done.16.z_rows), channel_id=1, source_target_pairs={{0,6},{2,4},{4,2},{6,0},{1,7},{3,5},{5,3},{7,1},{8,14},{10,12},{12... | collective-permute-start | bytes 24584 | tf_op jit(solution)/shard_map/ppermute | solution.py:984
  37.2 1.7 %shard_map.104 = f32[19,4,32,256]{3,2,1,0:T(8,128)} custom-call(f32[15,2,32,256]{3,2,1,0:T(8,128)S(1)} %get-tuple-element.65.inner, f32[15,2,32,256]{3,2,1,0:T(8,128)S(1)} %get-tuple-element.66.outer, f32[4,2,32,256]{3,2,1,0:T(8,128)S(1)} %get-tuple-element.70.inner_slanted, f32[4,2,32,256]{3,2,1,0:T(8,128)S(1)} %get-tuple-element.71.outer_slanted, ...), custom_call_target="tpu_custom_call" | custom-call | bytes 5242880 | tf_op jit(solution)/shard_map/pallas_call | solution.py:1154
  39.0 0.0 collective-permute-done.15.x_second
  39.0 1.1 %shard_map.105 = (f32[6,4,32,256]{3,2,1,0:T(8,128)}, f32[8,128]{1,0:T(8,128)S(1)}) custom-call(f32[6,4,32,256]{3,2,1,0:T(8,128)S(1)} %get-tuple-element.50.stretch, f32[5,4,32,256]{3,2,1,0:T(8,128)S(1)} %get-tuple-element.51.flow, f32[3,32,256]{2,1,0:T(8,128)S(1)} %collective-permute-done.14.x_first, ...), custom_call_target="tpu_custom_call", output_to_operand_aliasing={{0}: (7, {})} | custom-call | flops 2621440 | bytes 1310720 | tf_op jit(solution)/shard_map/pallas_call | solution.py:1161
  40.0 0.0 collective-permute-done.19.corner_first
  40.1 0.0 collective-permute-done.20.corner_second
  40.1 0.0 collective-permute-done.21.x_second
  40.1 0.0 collective-permute-done.22.x_first
  40.1 0.9 %shard_map.107 = f32[4,32,256]{2,1,0:T(8,128)} custom-call(f32[2,32,256]{2,1,0:T(8,128)S(1)} %get-tuple-element.86.inner_settled, f32[2,32,256]{2,1,0:T(8,128)S(1)} %get-tuple-element.87.outer_settled, f32[6,32,256]{2,1,0:T(8,128)S(1)} %get-tuple-element.88.spread, f32[16,128]{1,0:T(8,128)S(1)} %collective-permute-done.16.z_rows, ...), custom_call_target="tpu_custom_call" | custom-call | tf_op jit(solution)/shard_map/pallas_call | solution.py:1172
  (4 shorter events, 0.0 us)
Async XLA Ops:
  2.0 11.5 %collective-permute-start.3 = (f32[4,32,256]{2,1,0:T(8,128)S(1)}, f32[4,32,256]{2,1,0:T(8,128)S(1)}, u32[]{:S(2)}, u32[]{:S(2)}) collective-permute-start(f32[4,32,256]{2,1,0:T(8,128)S(1)} %get-tuple-element.57), channel_id=1, source_target_pairs={{0,8},{8,0},{16,24},{24,16},{1,9},{9,1},{17,25},{25,17},{2,10},{10... | collective-permute-start | bytes 393224 | tf_op jit(solution)/shard_map/ppermute | solution.py:984
  5.1 8.6 %collective-permute-start.4 = (f32[4,32,256]{2,1,0:T(8,128)S(1)}, f32[4,32,256]{2,1,0:T(8,128)S(1)}, u32[]{:S(2)}, u32[]{:S(2)}) collective-permute-start(f32[4,32,256]{2,1,0:T(8,128)S(1)} %get-tuple-element.58), channel_id=1, source_target_pairs={{0,24},{8,16},{16,8},{24,0},{1,25},{9,17},{17,9},{25,1},{2,26},{10... | collective-permute-start | bytes 393224 | tf_op jit(solution)/shard_map/ppermute | solution.py:984
  7.6 5.2 %collective-permute-start.1 = (f32[16,256]{1,0:T(8,128)S(1)}, f32[16,256]{1,0:T(8,128)S(1)}, u32[]{:S(2)}, u32[]{:S(2)}) collective-permute-start(f32[16,256]{1,0:T(8,128)S(1)} %get-tuple-element.53), channel_id=1, source_target_pairs={{0,2},{2,0},{4,6},{6,4},{1,3},{3,1},{5,7},{7,5},{8,10},{10,8},{12,... | collective-permute-start | bytes 49160 | tf_op jit(solution)/shard_map/ppermute | solution.py:984
  7.6 5.2 %collective-permute-start.2 = (f32[16,256]{1,0:T(8,128)S(1)}, f32[16,256]{1,0:T(8,128)S(1)}, u32[]{:S(2)}, u32[]{:S(2)}) collective-permute-start(f32[16,256]{1,0:T(8,128)S(1)} %get-tuple-element.54), channel_id=1, source_target_pairs={{0,6},{2,4},{4,2},{6,0},{1,7},{3,5},{5,3},{7,1},{8,14},{10,12},{12... | collective-permute-start | bytes 49160 | tf_op jit(solution)/shard_map/ppermute | solution.py:984
  9.2 3.6 %collective-permute-start = (f32[8,128]{1,0:T(8,128)S(1)}, f32[8,128]{1,0:T(8,128)S(1)}, u32[]{:S(2)}, u32[]{:S(2)}) collective-permute-start(f32[8,128]{1,0:T(8,128)S(1)} %get-tuple-element.52), channel_id=1, source_target_pairs={{0,1},{1,0},{2,3},{3,2},{4,5},{5,4},{6,7},{7,6},{8,9},{9,8},{10,11... | collective-permute-start | bytes 12296 | tf_op jit(solution)/shard_map/ppermute | solution.py:989
  14.7 6.4 %collective-permute-start.5 = (f32[40,256]{1,0:T(8,128)S(1)}, f32[40,256]{1,0:T(8,128)S(1)}, u32[]{:S(2)}, u32[]{:S(2)}) collective-permute-start(f32[40,256]{1,0:T(8,128)S(1)} %get-tuple-element.62), channel_id=1, source_target_pairs={{0,2},{2,0},{4,6},{6,4},{1,3},{3,1},{5,7},{7,5},{8,10},{10,8},{12,... | collective-permute-start | bytes 122888 | tf_op jit(solution)/shard_map/ppermute | solution.py:984
  14.8 6.4 %collective-permute-start.6 = (f32[40,256]{1,0:T(8,128)S(1)}, f32[40,256]{1,0:T(8,128)S(1)}, u32[]{:S(2)}, u32[]{:S(2)}) collective-permute-start(f32[40,256]{1,0:T(8,128)S(1)} %get-tuple-element.63), channel_id=1, source_target_pairs={{0,6},{2,4},{4,2},{6,0},{1,7},{3,5},{5,3},{7,1},{8,14},{10,12},{12... | collective-permute-start | bytes 122888 | tf_op jit(solution)/shard_map/ppermute | solution.py:984
  16.4 4.7 %collective-permute-start.7 = (f32[24,128]{1,0:T(8,128)S(1)}, f32[24,128]{1,0:T(8,128)S(1)}, u32[]{:S(2)}, u32[]{:S(2)}) collective-permute-start(f32[24,128]{1,0:T(8,128)S(1)} %get-tuple-element.64), channel_id=1, source_target_pairs={{0,1},{1,0},{2,3},{3,2},{4,5},{5,4},{6,7},{7,6},{8,9},{9,8},{10,11... | collective-permute-start | bytes 36872 | tf_op jit(solution)/shard_map/ppermute | solution.py:989
  17.9 11.3 %collective-permute-start.10 = (f32[5,32,256]{2,1,0:T(8,128)S(1)}, f32[5,32,256]{2,1,0:T(8,128)S(1)}, u32[]{:S(2)}, u32[]{:S(2)}) collective-permute-start(f32[5,32,256]{2,1,0:T(8,128)S(1)} %get-tuple-element.74), channel_id=1, source_target_pairs={{0,8},{8,0},{16,24},{24,16},{1,9},{9,1},{17,25},{25,17},{2,10},{10... | collective-permute-start | bytes 491528 | tf_op jit(solution)/shard_map/ppermute | solution.py:984
  18.5 5.0 %copy-start.1 = (s32[1024]{0:T(1024)S(1)}, s32[1024]{0:T(1024)}, u32[]{:S(2)}) copy-start(s32[1024]{0:T(1024)} %param.11) | copy-start | bytes 12292
  18.5 5.0 %copy-start.2 = (s32[1024]{0:T(1024)S(1)}, s32[1024]{0:T(1024)}, u32[]{:S(2)}) copy-start(s32[1024]{0:T(1024)} %param.12) | copy-start | bytes 12292
  18.5 5.0 %copy-start.3 = (s32[1024]{0:T(1024)S(1)}, s32[1024]{0:T(1024)}, u32[]{:S(2)}) copy-start(s32[1024]{0:T(1024)} %param.13) | copy-start | bytes 12292
  18.5 10.8 %collective-permute-start.11 = (f32[5,32,256]{2,1,0:T(8,128)S(1)}, f32[5,32,256]{2,1,0:T(8,128)S(1)}, u32[]{:S(2)}, u32[]{:S(2)}) collective-permute-start(f32[5,32,256]{2,1,0:T(8,128)S(1)} %get-tuple-element.75), channel_id=1, source_target_pairs={{0,24},{8,16},{16,8},{24,0},{1,25},{9,17},{17,9},{25,1},{2,26},{10... | collective-permute-start | bytes 491528 | tf_op jit(solution)/shard_map/ppermute | solution.py:984
  21.2 5.5 %copy-start = (f32[4,32,256]{2,1,0:T(8,128)S(1)}, f32[4,32,256]{2,1,0:T(8,128)}, u32[]{:S(2)}) copy-start(f32[4,32,256]{2,1,0:T(8,128)} %mass.3) | copy-start | bytes 393220
  21.2 2.3 %collective-permute-start.8 = (f32[24,128]{1,0:T(8,128)S(1)}, f32[24,128]{1,0:T(8,128)S(1)}, u32[]{:S(2)}, u32[]{:S(2)}) collective-permute-start(f32[24,128]{1,0:T(8,128)S(1)} %get-tuple-element.67), channel_id=1, source_target_pairs={{0,2},{2,0},{4,6},{6,4},{1,3},{3,1},{5,7},{7,5},{8,10},{10,8},{12,... | collective-permute-start | bytes 36872 | tf_op jit(solution)/shard_map/ppermute | solution.py:984
  21.3 6.0 %collective-permute-start.12 = (f32[32,128]{1,0:T(8,128)S(1)}, f32[32,128]{1,0:T(8,128)S(1)}, u32[]{:S(2)}, u32[]{:S(2)}) collective-permute-start(f32[32,128]{1,0:T(8,128)S(1)} %get-tuple-element.76), channel_id=1, source_target_pairs={{0,8},{8,0},{16,24},{24,16},{1,9},{9,1},{17,25},{25,17},{2,10},{10... | collective-permute-start | bytes 49160 | tf_op jit(solution)/shard_map/ppermute | solution.py:984
  21.3 7.9 %collective-permute-start.13 = (f32[32,128]{1,0:T(8,128)S(1)}, f32[32,128]{1,0:T(8,128)S(1)}, u32[]{:S(2)}, u32[]{:S(2)}) collective-permute-start(f32[32,128]{1,0:T(8,128)S(1)} %get-tuple-element.77), channel_id=1, source_target_pairs={{0,24},{8,16},{16,8},{24,0},{1,25},{9,17},{17,9},{25,1},{2,26},{10... | collective-permute-start | bytes 49160 | tf_op jit(solution)/shard_map/ppermute | solution.py:984
  23.5 3.2 %collective-permute-start.9 = (f32[24,128]{1,0:T(8,128)S(1)}, f32[24,128]{1,0:T(8,128)S(1)}, u32[]{:S(2)}, u32[]{:S(2)}) collective-permute-start(f32[24,128]{1,0:T(8,128)S(1)} %get-tuple-element.67), channel_id=1, source_target_pairs={{0,6},{2,4},{4,2},{6,0},{1,7},{3,5},{5,3},{7,1},{8,14},{10,12},{12... | collective-permute-start | bytes 36872 | tf_op jit(solution)/shard_map/ppermute | solution.py:984
  30.0 3.7 %collective-permute-start.16 = (f32[16,128]{1,0:T(8,128)S(1)}, f32[16,128]{1,0:T(8,128)S(1)}, u32[]{:S(2)}, u32[]{:S(2)}) collective-permute-start(f32[16,128]{1,0:T(8,128)S(1)} %get-tuple-element.89), channel_id=1, source_target_pairs={{0,1},{1,0},{2,3},{3,2},{4,5},{5,4},{6,7},{7,6},{8,9},{9,8},{10,11... | collective-permute-start | bytes 24584 | tf_op jit(solution)/shard_map/ppermute | solution.py:989
  30.6 3.1 %collective-permute-start.17 = (f32[8,256]{1,0:T(8,128)S(1)}, f32[8,256]{1,0:T(8,128)S(1)}, u32[]{:S(2)}, u32[]{:S(2)}) collective-permute-start(f32[8,256]{1,0:T(8,128)S(1)} %get-tuple-element.90), channel_id=1, source_target_pairs={{0,2},{2,0},{4,6},{6,4},{1,3},{3,1},{5,7},{7,5},{8,10},{10,8},{12,... | collective-permute-start | bytes 24584 | tf_op jit(solution)/shard_map/ppermute | solution.py:984
  30.6 3.1 %collective-permute-start.18 = (f32[8,256]{1,0:T(8,128)S(1)}, f32[8,256]{1,0:T(8,128)S(1)}, u32[]{:S(2)}, u32[]{:S(2)}) collective-permute-start(f32[8,256]{1,0:T(8,128)S(1)} %get-tuple-element.91), channel_id=1, source_target_pairs={{0,6},{2,4},{4,2},{6,0},{1,7},{3,5},{5,3},{7,1},{8,14},{10,12},{12... | collective-permute-start | bytes 24584 | tf_op jit(solution)/shard_map/ppermute | solution.py:984
  31.2 5.0 %collective-permute-start.14 = (f32[3,32,256]{2,1,0:T(8,128)S(1)}, f32[3,32,256]{2,1,0:T(8,128)S(1)}, u32[]{:S(2)}, u32[]{:S(2)}) collective-permute-start(f32[3,32,256]{2,1,0:T(8,128)S(1)} %get-tuple-element.82), channel_id=1, source_target_pairs={{0,8},{8,0},{16,24},{24,16},{1,9},{9,1},{17,25},{25,17},{2,10},{10... | collective-permute-start | bytes 294920 | tf_op jit(solution)/shard_map/ppermute | solution.py:984
  31.5 7.4 %collective-permute-start.15 = (f32[3,32,256]{2,1,0:T(8,128)S(1)}, f32[3,32,256]{2,1,0:T(8,128)S(1)}, u32[]{:S(2)}, u32[]{:S(2)}) collective-permute-start(f32[3,32,256]{2,1,0:T(8,128)S(1)} %get-tuple-element.83), channel_id=1, source_target_pairs={{0,24},{8,16},{16,8},{24,0},{1,25},{9,17},{17,9},{25,1},{2,26},{10... | collective-permute-start | bytes 294920 | tf_op jit(solution)/shard_map/ppermute | solution.py:984
  33.9 6.2 %collective-permute-start.21 = (f32[32,256]{1,0:T(8,128)S(1)}, f32[32,256]{1,0:T(8,128)S(1)}, u32[]{:S(2)}, u32[]{:S(2)}) collective-permute-start(f32[32,256]{1,0:T(8,128)S(1)} %get-tuple-element.92), channel_id=1, source_target_pairs={{0,24},{8,16},{16,8},{24,0},{1,25},{9,17},{17,9},{25,1},{2,26},{10... | collective-permute-start | bytes 98312 | tf_op jit(solution)/shard_map/ppermute | solution.py:984
  35.6 4.4 %collective-permute-start.22 = (f32[32,256]{1,0:T(8,128)S(1)}, f32[32,256]{1,0:T(8,128)S(1)}, u32[]{:S(2)}, u32[]{:S(2)}) collective-permute-start(f32[32,256]{1,0:T(8,128)S(1)} %get-tuple-element.93), channel_id=1, source_target_pairs={{0,8},{8,0},{16,24},{24,16},{1,9},{9,1},{17,25},{25,17},{2,10},{10... | collective-permute-start | bytes 98312 | tf_op jit(solution)/shard_map/ppermute | solution.py:984
  35.6 4.4 %collective-permute-start.19 = (f32[16,128]{1,0:T(8,128)S(1)}, f32[16,128]{1,0:T(8,128)S(1)}, u32[]{:S(2)}, u32[]{:S(2)}) collective-permute-start(f32[16,128]{1,0:T(8,128)S(1)} %collective-permute-done.16.z_rows), channel_id=1, source_target_pairs={{0,2},{2,0},{4,6},{6,4},{1,3},{3,1},{5,7},{7,5},{8,10},{10,8},{12,... | collective-permute-start | bytes 24584 | tf_op jit(solution)/shard_map/ppermute | solution.py:984
  36.2 3.9 %collective-permute-start.20 = (f32[16,128]{1,0:T(8,128)S(1)}, f32[16,128]{1,0:T(8,128)S(1)}, u32[]{:S(2)}, u32[]{:S(2)}) collective-permute-start(f32[16,128]{1,0:T(8,128)S(1)} %collective-permute-done.16.z_rows), channel_id=1, source_target_pairs={{0,6},{2,4},{4,2},{6,0},{1,7},{3,5},{5,3},{7,1},{8,14},{10,12},{12... | collective-permute-start | bytes 24584 | tf_op jit(solution)/shard_map/ppermute | solution.py:984

commit v6 on v5

--- a/solution.py
+++ b/solution.py
@@ -468,7 +468,13 @@
     y_second,
     z_rows,
     inner_stretch,
+    inner,
+    outer,
+    inner_slanted,
+    outer_slanted,
+    late,
     new_stretch,
+    fresh,
     mark,
     updated,
     below,
@@ -477,8 +483,12 @@
     y_above,
     z_halo,
     sems,
+    store_sems,
 ):
     bx = stretch.shape[1]
+    moves = stored(inner, outer, inner_slanted, outer_slanted, late, fresh, store_sems)
+    for copy in moves:
+        copy.start()
     flip_x = odd("gx")
     for comp in range(3):
         below[comp] = jnp.where(flip_x, x_first[comp], x_second[comp])
@@ -494,11 +504,11 @@
         )
         copies[-1].start()
     mark[...] = jnp.zeros(mark.shape, jnp.float32)
-    for copy in copies:
+    for copy in copies + moves:
         copy.wait()
 
 
-def store(inner, outer, inner_slanted, outer_slanted, late, fresh, sems):
+def stored(inner, outer, inner_slanted, outer_slanted, late, fresh, sems):
     bx = fresh.shape[1]
     moves = [
         (inner, fresh.at[0:first_slanted, 1 : bx - 1]),
@@ -515,14 +525,10 @@
             if index in order:
                 moves.append((late.at[order.index(index), place], fresh.at[index, x]))
             start = index + 1
-    copies = [
+    return [
         pltpu.make_async_copy(source, target, sems.at[place])
         for place, (source, target) in enumerate(moves)
     ]
-    for copy in copies:
-        copy.start()
-    for copy in copies:
-        copy.wait()
 
 
 up_edges = ((0, y_up.index(7)), (0, gas_slot), (1, y_down.index(9)), (1, gas_slot))
@@ -765,8 +771,8 @@
     changes,
     gas_first,
     gas_second,
+    x_second,
     x_first,
-    x_second,
     edges_first,
     edges_second,
     inner_excess,
@@ -1138,7 +1144,7 @@
         totals,
         changes,
         *first_x,
-        *post_x,
+        *post_x[::-1],
         *edges_x,
         inner_excess,
         inner_heading,
@@ -1151,24 +1157,29 @@
     flow_x = swapped(v_one, v_two, "gx")
     x_one, x_two = call(add_faces, [face, face], cost=(4 * 10**9, 0))(spread, z_last, *last_y)
     last_x = swapped(x_one, x_two, "gx")
-    (fresh,) = call(
-        store,
-        [(19, *box)],
-        out_specs=[remote],
-        scratch=[pltpu.SemaphoreType.DMA((32,))],
-        cost=(0, 160 * cells),
-    )(inner, outer, inner_slanted, outer_slanted, late)
-    new_stretch, outer_done = call(
+    new_stretch, fresh, outer_done = call(
         restretch_outer,
-        [(6, *box), mark],
-        specs=[pl.BlockSpec()] * 7 + [remote],
-        out_specs=[remote, pl.BlockSpec()],
+        [(6, *box), (19, *box), mark],
+        specs=[pl.BlockSpec()] * 7 + [remote] + [pl.BlockSpec()] * 5,
+        out_specs=[remote, remote, pl.BlockSpec()],
         scratch=[(6, *ends), (3, *face), (3, *face)]
         + sides_y
-        + [pltpu.SemaphoreType.DMA((2,))],
-        cost=(80 * cells, 40 * cells),
+        + [pltpu.SemaphoreType.DMA((2,)), pltpu.SemaphoreType.DMA((32,))],
+        cost=(80 * cells, 200 * cells),
         aliases={7: 0},
-    )(stretch, flow, *flow_x, *post_y, z_post, new_stretch)
+    )(
+        stretch,
+        flow,
+        *flow_x,
+        *post_y,
+        z_post,
+        new_stretch,
+        inner,
+        outer,
+        inner_slanted,
+        outer_slanted,
+        late,
+    )
     (new_mass,) = call(add_all, [box])(
         inner_settled, outer_settled, spread, z_last, *last_y, *last_corners, *last_x[::-1], outer_done
     )

time: 41.2 us -> 43.4 us (1.053); the launches traced: 40.9 us -> 42.6 us
  waiting for transfers between devices: 4.13 us -> 7.19 us
  starting transfers between devices: 23.5 us -> 22.7 us
  Pallas kernels: 12.5 us -> 11.9 us
    ppermute x10, waiting for transfers between devices: 0.56 us -> 3.68 us  [swapped(): lax.ppermute(first, axis, ahead)]
    ppermute x10, starting transfers between devices: 15.7 us -> 13.6 us  [swapped(): lax.ppermute(second, axis, behind)]
    ppermute x10, starting transfers between devices: 4.19 us -> 5.47 us  [swapped(): lax.ppermute(first, axis, ahead)]
    pallas_call x2 -> x1, Pallas kernels: 2.77 us -> 2.15 us  [shards(): call(restretch_outer, [(6, *box), (19, *box), mark], specs=[pl.BlockSpec(...]
  transfers between devices with their start and end apart: 23 -> 23, of which waited for: 6 -> 8; matrix products, arithmetic and copies ran while one was open for 0% -> 0% of each run, Pallas kernels for 21% -> 18%
where the time goes in v6:
time: 43.4 us; the launch traced here: 42.6 us
  starting transfers between devices  22.7 us (52%)
  Pallas kernels  11.9 us (27%)
  waiting for transfers between devices  7.19 us (17%)
  between operations  0.78 us (2%)
    ppermute x10, starting transfers between devices, swapped(): lax.ppermute(second, axis, behind)  13.6 us
    ppermute x10, starting transfers between devices, swapped(): lax.ppermute(first, axis, ahead)  5.47 us
    ppermute x10, waiting for transfers between devices, swapped(): lax.ppermute(first, axis, ahead)  3.68 us
    ppermute x3, starting transfers between devices, both_ways(): lax.ppermute(rows, 'gz', [(i, (i + 1) % devices) for i in range(devices)])  3.6 us
    ppermute x10, waiting for transfers between devices, swapped(): lax.ppermute(second, axis, behind)  2.54 us
    pallas_call x1, Pallas kernels, shards(): call(restretch_outer, [(6, *box), (19, *box), mark], specs=[pl.BlockSpec(...  2.15 us
    pallas_call x1, Pallas kernels, shards(): call(moments, [(19, *box), (5, *box)], specs=[remote], scratch=[pltpu.Sem...  1.74 us
    pallas_call x1, Pallas kernels, shards(): call(first_faces, [(6, *box), jax.ShapeDtypeStruct(box, jnp.int32), (8, b...  1.38 us
  transfers between devices with their start and end apart: 23, of which 8 were waited for; matrix products, arithmetic and copies ran while one was open for 0% of the time, Pallas kernels for 18%

profile of v6, /device:TPU:0, one launch (start us, length us, event | category | flops | bytes accessed | tf_op | source)
XLA Modules:
  0.0 42.6 jit_solution(1636492386956856037)
XLA Ops:
  0.6 1.4 %shard_map.94 = (f32[6,4,32,256]{3,2,1,0:T(8,128)S(1)}, s32[4,32,256]{2,1,0:T(8,128)S(1)}, f32[8,128]{1,0:T(8,128)S(1)}, f32[16,256]{1,0:T(8,128)S(1)}, f32[16,2...) custom-call(f32[6,4,32,256]{3,2,1,0:T(8,128)} %stretch_in.1, s32[4,32,256]{2,1,0:T(8,128)} %flags_in.1), custom_call_target="tpu_custom_call" | custom-call | flops 327680 | bytes 1966080 | tf_op jit(solution)/shard_map/pallas_call | solution.py:1034
  2.0 3.1 %collective-permute-start = (f32[4,32,256]{2,1,0:T(8,128)S(1)}, f32[4,32,256]{2,1,0:T(8,128)S(1)}, u32[]{:S(2)}, u32[]{:S(2)}) collective-permute-start(f32[4,32,256]{2,1,0:T(8,128)S(1)} %get-tuple-element.54), channel_id=1, source_target_pairs={{0,8},{8,0},{16,24},{24,16},{1,9},{9,1},{17,25},{25,17},{2,10},{10... | collective-permute-start | bytes 393224 | tf_op jit(solution)/shard_map/ppermute | solution.py:990
  5.1 2.5 %collective-permute-start.1 = (f32[4,32,256]{2,1,0:T(8,128)S(1)}, f32[4,32,256]{2,1,0:T(8,128)S(1)}, u32[]{:S(2)}, u32[]{:S(2)}) collective-permute-start(f32[4,32,256]{2,1,0:T(8,128)S(1)} %get-tuple-element.55), channel_id=1, source_target_pairs={{0,24},{8,16},{16,8},{24,0},{1,25},{9,17},{17,9},{25,1},{2,26},{10... | collective-permute-start | bytes 393224 | tf_op jit(solution)/shard_map/ppermute | solution.py:990
  7.6 0.0 collective-permute-start.2
  7.6 1.6 %collective-permute-start.3 = (f32[16,256]{1,0:T(8,128)S(1)}, f32[16,256]{1,0:T(8,128)S(1)}, u32[]{:S(2)}, u32[]{:S(2)}) collective-permute-start(f32[16,256]{1,0:T(8,128)S(1)} %get-tuple-element.57), channel_id=1, source_target_pairs={{0,6},{2,4},{4,2},{6,0},{1,7},{3,5},{5,3},{7,1},{8,14},{10,12},{12... | collective-permute-start | bytes 49160 | tf_op jit(solution)/shard_map/ppermute | solution.py:990
  9.2 1.5 %collective-permute-start.4 = (f32[8,128]{1,0:T(8,128)S(1)}, f32[8,128]{1,0:T(8,128)S(1)}, u32[]{:S(2)}, u32[]{:S(2)}) collective-permute-start(f32[8,128]{1,0:T(8,128)S(1)} %get-tuple-element.58), channel_id=1, source_target_pairs={{0,1},{1,0},{2,3},{3,2},{4,5},{5,4},{6,7},{7,6},{8,9},{9,8},{10,11... | collective-permute-start | bytes 12296 | tf_op jit(solution)/shard_map/ppermute | solution.py:995
  10.7 1.7 %shard_map.95 = (f32[19,4,32,256]{3,2,1,0:T(8,128)S(1)}, f32[5,4,32,256]{3,2,1,0:T(8,128)S(1)}) custom-call(f32[19,4,32,256]{3,2,1,0:T(8,128)} %pops_in.1), custom_call_target="tpu_custom_call" | custom-call | flops 1966080 | bytes 4915200 | tf_op jit(solution)/shard_map/pallas_call | solution.py:1062
  12.5 0.3 collective-permute-done.4.z_rows
  12.8 0.0 collective-permute-done.2.y_first
  12.8 0.0 collective-permute-done.3.y_second
  12.8 0.8 %shard_map.96 = (f32[19,2,32,256]{3,2,1,0:T(8,128)S(1)}, f32[3,2,32,256]{3,2,1,0:T(8,128)S(1)}) custom-call(f32[19,4,32,256]{3,2,1,0:T(8,128)S(1)} %get-tuple-element.52.pops, f32[6,4,32,256]{3,2,1,0:T(8,128)S(1)} %get-tuple-element.50.stretch, f32[5,4,32,256]{3,2,1,0:T(8,128)S(1)} %get-tuple-element.51.flow, f32[8,128]{1,0:T(8,128)S(1)} %collective-permute-done.4.z_rows, ...), custom_call_target="tpu_custom_call" | custom-call | flops 4915200 | bytes 4915200 | tf_op jit(solution)/shard_map/pallas_call | solution.py:1073
  13.6 0.0 collective-permute-done.x_first.gas_first
  13.6 0.1 collective-permute-done.1.x_second.gas_second
  13.7 1.0 %shard_map.97 = (f32[19,2,32,256]{3,2,1,0:T(8,128)S(1)}, f32[3,2,32,256]{3,2,1,0:T(8,128)S(1)}, f32[24,128]{1,0:T(8,128)S(1)}, f32[5,32,256]{2,1,0:T(8,128)S(1)}...) custom-call(f32[19,4,32,256]{3,2,1,0:T(8,128)S(1)} %get-tuple-element.52.pops, ...), custom_call_target="tpu_custom_call" | custom-call | flops 4915200 | bytes 4915200 | tf_op jit(solution)/shard_map/pallas_call | solution.py:1079
  14.7 0.0 collective-permute-start.5
  14.8 1.6 %collective-permute-start.6 = (f32[40,256]{1,0:T(8,128)S(1)}, f32[40,256]{1,0:T(8,128)S(1)}, u32[]{:S(2)}, u32[]{:S(2)}) collective-permute-start(f32[40,256]{1,0:T(8,128)S(1)} %get-tuple-element.64), channel_id=1, source_target_pairs={{0,6},{2,4},{4,2},{6,0},{1,7},{3,5},{5,3},{7,1},{8,14},{10,12},{12... | collective-permute-start | bytes 122888 | tf_op jit(solution)/shard_map/ppermute | solution.py:990
  16.4 1.5 %collective-permute-start.7 = (f32[24,128]{1,0:T(8,128)S(1)}, f32[24,128]{1,0:T(8,128)S(1)}, u32[]{:S(2)}, u32[]{:S(2)}) collective-permute-start(f32[24,128]{1,0:T(8,128)S(1)} %get-tuple-element.65), channel_id=1, source_target_pairs={{0,1},{1,0},{2,3},{3,2},{4,5},{5,4},{6,7},{7,6},{8,9},{9,8},{10,11... | collective-permute-start | bytes 36872 | tf_op jit(solution)/shard_map/ppermute | solution.py:995
  17.9 1.5 %collective-permute-start.10 = (f32[5,32,256]{2,1,0:T(8,128)S(1)}, f32[5,32,256]{2,1,0:T(8,128)S(1)}, u32[]{:S(2)}, u32[]{:S(2)}) collective-permute-start(f32[5,32,256]{2,1,0:T(8,128)S(1)} %get-tuple-element.71), channel_id=1, source_target_pairs={{0,24},{8,16},{16,8},{24,0},{1,25},{9,17},{17,9},{25,1},{2,26},{10... | collective-permute-start | bytes 491528 | tf_op jit(solution)/shard_map/ppermute | solution.py:990
  19.4 0.0 copy-start.1
  19.4 0.8 %collective-permute-start.11 = (f32[5,32,256]{2,1,0:T(8,128)S(1)}, f32[5,32,256]{2,1,0:T(8,128)S(1)}, u32[]{:S(2)}, u32[]{:S(2)}) collective-permute-start(f32[5,32,256]{2,1,0:T(8,128)S(1)} %get-tuple-element.72), channel_id=1, source_target_pairs={{0,8},{8,0},{16,24},{24,16},{1,9},{9,1},{17,25},{25,17},{2,10},{10... | collective-permute-start | bytes 491528 | tf_op jit(solution)/shard_map/ppermute | solution.py:990
  20.2 0.0 collective-permute-done.7.refs_0_.z_rows
  20.2 0.0 collective-permute-done.5.refs_1_.y_first
  20.2 0.0 collective-permute-done.6.refs_2_.y_second
  20.3 0.0 copy-start
  20.3 0.1 collective-permute-start.8
  20.4 1.2 %collective-permute-start.12 = (f32[32,128]{1,0:T(8,128)S(1)}, f32[32,128]{1,0:T(8,128)S(1)}, u32[]{:S(2)}, u32[]{:S(2)}) collective-permute-start(f32[32,128]{1,0:T(8,128)S(1)} %get-tuple-element.73), channel_id=1, source_target_pairs={{0,8},{8,0},{16,24},{24,16},{1,9},{9,1},{17,25},{25,17},{2,10},{10... | collective-permute-start | bytes 49160 | tf_op jit(solution)/shard_map/ppermute | solution.py:990
  21.6 2.3 %collective-permute-start.13 = (f32[32,128]{1,0:T(8,128)S(1)}, f32[32,128]{1,0:T(8,128)S(1)}, u32[]{:S(2)}, u32[]{:S(2)}) collective-permute-start(f32[32,128]{1,0:T(8,128)S(1)} %get-tuple-element.74), channel_id=1, source_target_pairs={{0,24},{8,16},{16,8},{24,0},{1,25},{9,17},{17,9},{25,1},{2,26},{10... | collective-permute-start | bytes 49160 | tf_op jit(solution)/shard_map/ppermute | solution.py:990
  24.0 0.0 collective-permute-done.8.corner_first
  24.0 0.0 collective-permute-start.9
  24.0 0.0 copy-done.1
  24.0 0.0 copy-done.2
  24.0 0.0 copy-done.3
  24.0 0.3 shard_map.98
  24.3 1.2 %shard_map.102 = (f32[6,4,32,256]{3,2,1,0:T(8,128)}, f32[8,128]{1,0:T(8,128)S(1)}) custom-call(f32[6,4,32,256]{3,2,1,0:T(8,128)S(1)} %get-tuple-element.50.stretch, f32[5,4,32,256]{3,2,1,0:T(8,128)S(1)} %get-tuple-element.51.flow, f32[40,256]{1,0:T(8,128)S(1)} %collective-permute-done.5.refs_1_.y_first, ...), custom_call_target="tpu_custom_call" | custom-call | flops 2621440 | bytes 1310720 | tf_op jit(solution)/shard_map/pallas_call | solution.py:1117
  25.5 0.9 %shard_map.100 = (f32[15,2,32,256]{3,2,1,0:T(8,128)S(1)}, f32[15,2,32,256]{3,2,1,0:T(8,128)S(1)}, f32[4,32,256]{2,1,0:T(8,128)S(1)}, f32[4,32,256]{2,1,0:T(8,128)S(1)}) custom-call(f32[19,2,32,256]{3,2,1,0:T(8,128)S(1)} %get-tuple-element.59.inner.inner_post, f32[19,2,32,256]{3,2,1,0:T(8,128)S(1)} %get-tuple-element.60.outer_post.post, ...), custom_call_target="tpu_custom_call" | custom-call | flops 11468800 | bytes 6553600 | tf_op jit(solution)/shard_map/pallas_call | solution.py:1097
  26.5 0.7 %collective-permute-done.9.corner_second = f32[24,128]{1,0:T(8,128)S(1)} collective-permute-done((f32[24,128]{1,0:T(8,128)S(1)}, f32[24,128]{1,0:T(8,128)S(1)}, u32[]{:S(2)}, u32[]{:S(2)}) %collective-permute-start.9) | collective-permute-done | bytes 12320 | tf_op jit(solution)/shard_map/ppermute | solution.py:990
  27.1 0.0 copy-done
  27.2 0.6 %shard_map.101 = (f32[4,2,32,256]{3,2,1,0:T(8,128)S(1)}, f32[4,2,32,256]{3,2,1,0:T(8,128)S(1)}, f32[2,32,256]{2,1,0:T(8,128)S(1)}, f32[2,32,256]{2,1,0:T(8,128)S...) custom-call(f32[19,2,32,256]{3,2,1,0:T(8,128)S(1)} %get-tuple-element.59.inner.inner_post, ...), custom_call_target="tpu_custom_call" | custom-call | flops 3276800 | bytes 1966080 | tf_op jit(solution)/shard_map/pallas_call | solution.py:1111
  27.7 1.3 %collective-permute-done.12.edges_first = f32[32,128]{1,0:T(8,128)S(1)} collective-permute-done((f32[32,128]{1,0:T(8,128)S(1)}, f32[32,128]{1,0:T(8,128)S(1)}, u32[]{:S(2)}, u32[]{:S(2)}) %collective-permute-start.12) | collective-permute-done | bytes 16416 | tf_op jit(solution)/shard_map/ppermute | solution.py:990
  29.0 0.8 %collective-permute-done.13.edges_second = f32[32,128]{1,0:T(8,128)S(1)} collective-permute-done((f32[32,128]{1,0:T(8,128)S(1)}, f32[32,128]{1,0:T(8,128)S(1)}, u32[]{:S(2)}, u32[]{:S(2)}) %collective-permute-start.13) | collective-permute-done | bytes 16416 | tf_op jit(solution)/shard_map/ppermute | solution.py:990
  29.8 0.0 collective-permute-done.10.x_second
  29.8 0.0 collective-permute-done.11.x_first
  29.9 0.7 %shard_map.103 = (f32[5,2,32,256]{3,2,1,0:T(8,128)S(1)}, f32[3,32,256]{2,1,0:T(8,128)S(1)}, f32[3,32,256]{2,1,0:T(8,128)S(1)}, f32[2,32,256]{2,1,0:T(8,128)S(1)}...) custom-call(f32[19,2,32,256]{3,2,1,0:T(8,128)S(1)} %get-tuple-element.60.outer, ...), custom_call_target="tpu_custom_call" | custom-call | flops 4915200 | bytes 3276800 | tf_op jit(solution)/shard_map/pallas_call | solution.py:1124
  30.6 0.6 %collective-permute-start.16 = (f32[16,128]{1,0:T(8,128)S(1)}, f32[16,128]{1,0:T(8,128)S(1)}, u32[]{:S(2)}, u32[]{:S(2)}) collective-permute-start(f32[16,128]{1,0:T(8,128)S(1)} %get-tuple-element.91), channel_id=1, source_target_pairs={{0,1},{1,0},{2,3},{3,2},{4,5},{5,4},{6,7},{7,6},{8,9},{9,8},{10,11... | collective-permute-start | bytes 24584 | tf_op jit(solution)/shard_map/ppermute | solution.py:995
  31.2 0.0 collective-permute-start.17
  31.2 0.6 %collective-permute-start.18 = (f32[8,256]{1,0:T(8,128)S(1)}, f32[8,256]{1,0:T(8,128)S(1)}, u32[]{:S(2)}, u32[]{:S(2)}) collective-permute-start(f32[8,256]{1,0:T(8,128)S(1)} %get-tuple-element.93), channel_id=1, source_target_pairs={{0,6},{2,4},{4,2},{6,0},{1,7},{3,5},{5,3},{7,1},{8,14},{10,12},{12... | collective-permute-start | bytes 24584 | tf_op jit(solution)/shard_map/ppermute | solution.py:990
  31.8 0.0 collective-permute-start.14
  31.8 1.9 %collective-permute-start.15 = (f32[3,32,256]{2,1,0:T(8,128)S(1)}, f32[3,32,256]{2,1,0:T(8,128)S(1)}, u32[]{:S(2)}, u32[]{:S(2)}) collective-permute-start(f32[3,32,256]{2,1,0:T(8,128)S(1)} %get-tuple-element.79), channel_id=1, source_target_pairs={{0,24},{8,16},{16,8},{24,0},{1,25},{9,17},{17,9},{25,1},{2,26},{10... | collective-permute-start | bytes 294920 | tf_op jit(solution)/shard_map/ppermute | solution.py:990
  33.7 0.6 %collective-permute-done.16.z_rows = f32[16,128]{1,0:T(8,128)S(1)} collective-permute-done((f32[16,128]{1,0:T(8,128)S(1)}, f32[16,128]{1,0:T(8,128)S(1)}, u32[]{:S(2)}, u32[]{:S(2)}) %collective-permute-start.16) | collective-permute-done | bytes 8224 | tf_op jit(solution)/shard_map/ppermute | solution.py:995
  34.3 0.0 collective-permute-done.17.y_first
  34.3 0.0 collective-permute-done.18.y_second
  34.3 0.2 shard_map.105
  34.5 1.6 %collective-permute-start.21 = (f32[32,256]{1,0:T(8,128)S(1)}, f32[32,256]{1,0:T(8,128)S(1)}, u32[]{:S(2)}, u32[]{:S(2)}) collective-permute-start(f32[32,256]{1,0:T(8,128)S(1)} %get-tuple-element.94), channel_id=1, source_target_pairs={{0,24},{8,16},{16,8},{24,0},{1,25},{9,17},{17,9},{25,1},{2,26},{10... | collective-permute-start | bytes 98312 | tf_op jit(solution)/shard_map/ppermute | solution.py:990
  36.1 0.0 collective-permute-start.22
  36.1 0.1 collective-permute-start.19
  36.3 2.4 %collective-permute-done.14.x_first = f32[3,32,256]{2,1,0:T(8,128)S(1)} collective-permute-done((f32[3,32,256]{2,1,0:T(8,128)S(1)}, f32[3,32,256]{2,1,0:T(8,128)S(1)}, u32[]{:S(2)}, u32[]{:S(2)}) %collective-permute-start.14) | collective-permute-done | bytes 98336 | tf_op jit(solution)/shard_map/ppermute | solution.py:990
  38.6 0.0 collective-permute-start.20
  38.6 0.0 collective-permute-done.15.x_second
  38.6 2.2 %shard_map.104 = (f32[6,4,32,256]{3,2,1,0:T(8,128)}, f32[19,4,32,256]{3,2,1,0:T(8,128)}, f32[8,128]{1,0:T(8,128)S(1)}) custom-call(f32[6,4,32,256]{3,2,1,0:T(8,128)S(1)} %get-tuple-element.50.stretch, f32[5,4,32,256]{3,2,1,0:T(8,128)S(1)} %get-tuple-element.51.flow, ...), custom_call_target="tpu_custom_call", output_to_operand_aliasing={{0}: (7, {})} | custom-call | flops 2621440 | bytes 6553600 | tf_op jit(solution)/shard_map/pallas_call | solution.py:1160
  40.8 0.0 collective-permute-done.19.corner_first
  40.8 0.9 %collective-permute-done.20.corner_second = f32[16,128]{1,0:T(8,128)S(1)} collective-permute-done((f32[16,128]{1,0:T(8,128)S(1)}, f32[16,128]{1,0:T(8,128)S(1)}, u32[]{:S(2)}, u32[]{:S(2)}) %collective-permute-start.20) | collective-permute-done | bytes 8224 | tf_op jit(solution)/shard_map/ppermute | solution.py:990
  41.7 0.0 collective-permute-done.21.x_second
  41.7 0.0 collective-permute-done.22.x_first
  41.7 0.9 %shard_map.106 = f32[4,32,256]{2,1,0:T(8,128)} custom-call(f32[2,32,256]{2,1,0:T(8,128)S(1)} %get-tuple-element.88.inner_settled, f32[2,32,256]{2,1,0:T(8,128)S(1)} %get-tuple-element.89.outer_settled, f32[6,32,256]{2,1,0:T(8,128)S(1)} %get-tuple-element.90.spread, f32[16,128]{1,0:T(8,128)S(1)} %collective-permute-done.16.z_rows, ...), custom_call_target="tpu_custom_call" | custom-call | tf_op jit(solution)/shard_map/pallas_call | solution.py:1183
  (3 shorter events, 0.0 us)
Async XLA Ops:
  2.0 11.5 %collective-permute-start = (f32[4,32,256]{2,1,0:T(8,128)S(1)}, f32[4,32,256]{2,1,0:T(8,128)S(1)}, u32[]{:S(2)}, u32[]{:S(2)}) collective-permute-start(f32[4,32,256]{2,1,0:T(8,128)S(1)} %get-tuple-element.54), channel_id=1, source_target_pairs={{0,8},{8,0},{16,24},{24,16},{1,9},{9,1},{17,25},{25,17},{2,10},{10... | collective-permute-start | bytes 393224 | tf_op jit(solution)/shard_map/ppermute | solution.py:990
  5.1 8.6 %collective-permute-start.1 = (f32[4,32,256]{2,1,0:T(8,128)S(1)}, f32[4,32,256]{2,1,0:T(8,128)S(1)}, u32[]{:S(2)}, u32[]{:S(2)}) collective-permute-start(f32[4,32,256]{2,1,0:T(8,128)S(1)} %get-tuple-element.55), channel_id=1, source_target_pairs={{0,24},{8,16},{16,8},{24,0},{1,25},{9,17},{17,9},{25,1},{2,26},{10... | collective-permute-start | bytes 393224 | tf_op jit(solution)/shard_map/ppermute | solution.py:990
  7.6 5.2 %collective-permute-start.2 = (f32[16,256]{1,0:T(8,128)S(1)}, f32[16,256]{1,0:T(8,128)S(1)}, u32[]{:S(2)}, u32[]{:S(2)}) collective-permute-start(f32[16,256]{1,0:T(8,128)S(1)} %get-tuple-element.56), channel_id=1, source_target_pairs={{0,2},{2,0},{4,6},{6,4},{1,3},{3,1},{5,7},{7,5},{8,10},{10,8},{12,... | collective-permute-start | bytes 49160 | tf_op jit(solution)/shard_map/ppermute | solution.py:990
  7.6 5.2 %collective-permute-start.3 = (f32[16,256]{1,0:T(8,128)S(1)}, f32[16,256]{1,0:T(8,128)S(1)}, u32[]{:S(2)}, u32[]{:S(2)}) collective-permute-start(f32[16,256]{1,0:T(8,128)S(1)} %get-tuple-element.57), channel_id=1, source_target_pairs={{0,6},{2,4},{4,2},{6,0},{1,7},{3,5},{5,3},{7,1},{8,14},{10,12},{12... | collective-permute-start | bytes 49160 | tf_op jit(solution)/shard_map/ppermute | solution.py:990
  9.2 3.6 %collective-permute-start.4 = (f32[8,128]{1,0:T(8,128)S(1)}, f32[8,128]{1,0:T(8,128)S(1)}, u32[]{:S(2)}, u32[]{:S(2)}) collective-permute-start(f32[8,128]{1,0:T(8,128)S(1)} %get-tuple-element.58), channel_id=1, source_target_pairs={{0,1},{1,0},{2,3},{3,2},{4,5},{5,4},{6,7},{7,6},{8,9},{9,8},{10,11... | collective-permute-start | bytes 12296 | tf_op jit(solution)/shard_map/ppermute | solution.py:995
  14.7 5.5 %collective-permute-start.5 = (f32[40,256]{1,0:T(8,128)S(1)}, f32[40,256]{1,0:T(8,128)S(1)}, u32[]{:S(2)}, u32[]{:S(2)}) collective-permute-start(f32[40,256]{1,0:T(8,128)S(1)} %get-tuple-element.63), channel_id=1, source_target_pairs={{0,2},{2,0},{4,6},{6,4},{1,3},{3,1},{5,7},{7,5},{8,10},{10,8},{12,... | collective-permute-start | bytes 122888 | tf_op jit(solution)/shard_map/ppermute | solution.py:990
  14.8 5.5 %collective-permute-start.6 = (f32[40,256]{1,0:T(8,128)S(1)}, f32[40,256]{1,0:T(8,128)S(1)}, u32[]{:S(2)}, u32[]{:S(2)}) collective-permute-start(f32[40,256]{1,0:T(8,128)S(1)} %get-tuple-element.64), channel_id=1, source_target_pairs={{0,6},{2,4},{4,2},{6,0},{1,7},{3,5},{5,3},{7,1},{8,14},{10,12},{12... | collective-permute-start | bytes 122888 | tf_op jit(solution)/shard_map/ppermute | solution.py:990
  16.4 3.8 %collective-permute-start.7 = (f32[24,128]{1,0:T(8,128)S(1)}, f32[24,128]{1,0:T(8,128)S(1)}, u32[]{:S(2)}, u32[]{:S(2)}) collective-permute-start(f32[24,128]{1,0:T(8,128)S(1)} %get-tuple-element.65), channel_id=1, source_target_pairs={{0,1},{1,0},{2,3},{3,2},{4,5},{5,4},{6,7},{7,6},{8,9},{9,8},{10,11... | collective-permute-start | bytes 36872 | tf_op jit(solution)/shard_map/ppermute | solution.py:995
  17.9 11.9 %collective-permute-start.10 = (f32[5,32,256]{2,1,0:T(8,128)S(1)}, f32[5,32,256]{2,1,0:T(8,128)S(1)}, u32[]{:S(2)}, u32[]{:S(2)}) collective-permute-start(f32[5,32,256]{2,1,0:T(8,128)S(1)} %get-tuple-element.71), channel_id=1, source_target_pairs={{0,24},{8,16},{16,8},{24,0},{1,25},{9,17},{17,9},{25,1},{2,26},{10... | collective-permute-start | bytes 491528 | tf_op jit(solution)/shard_map/ppermute | solution.py:990
  19.4 4.6 %copy-start.1 = (s32[1024]{0:T(1024)S(1)}, s32[1024]{0:T(1024)}, u32[]{:S(2)}) copy-start(s32[1024]{0:T(1024)} %param.11) | copy-start | bytes 12292
  19.4 4.6 %copy-start.2 = (s32[1024]{0:T(1024)S(1)}, s32[1024]{0:T(1024)}, u32[]{:S(2)}) copy-start(s32[1024]{0:T(1024)} %param.12) | copy-start | bytes 12292
  19.4 4.6 %copy-start.3 = (s32[1024]{0:T(1024)S(1)}, s32[1024]{0:T(1024)}, u32[]{:S(2)}) copy-start(s32[1024]{0:T(1024)} %param.13) | copy-start | bytes 12292
  19.4 10.5 %collective-permute-start.11 = (f32[5,32,256]{2,1,0:T(8,128)S(1)}, f32[5,32,256]{2,1,0:T(8,128)S(1)}, u32[]{:S(2)}, u32[]{:S(2)}) collective-permute-start(f32[5,32,256]{2,1,0:T(8,128)S(1)} %get-tuple-element.72), channel_id=1, source_target_pairs={{0,8},{8,0},{16,24},{24,16},{1,9},{9,1},{17,25},{25,17},{2,10},{10... | collective-permute-start | bytes 491528 | tf_op jit(solution)/shard_map/ppermute | solution.py:990
  20.3 6.9 %copy-start = (f32[4,32,256]{2,1,0:T(8,128)S(1)}, f32[4,32,256]{2,1,0:T(8,128)}, u32[]{:S(2)}) copy-start(f32[4,32,256]{2,1,0:T(8,128)} %mass.3) | copy-start | bytes 393220
  20.3 3.7 %collective-permute-start.8 = (f32[24,128]{1,0:T(8,128)S(1)}, f32[24,128]{1,0:T(8,128)S(1)}, u32[]{:S(2)}, u32[]{:S(2)}) collective-permute-start(f32[24,128]{1,0:T(8,128)S(1)} %get-tuple-element.66), channel_id=1, source_target_pairs={{0,2},{2,0},{4,6},{6,4},{1,3},{3,1},{5,7},{7,5},{8,10},{10,8},{12,... | collective-permute-start | bytes 36872 | tf_op jit(solution)/shard_map/ppermute | solution.py:990
  20.4 8.7 %collective-permute-start.12 = (f32[32,128]{1,0:T(8,128)S(1)}, f32[32,128]{1,0:T(8,128)S(1)}, u32[]{:S(2)}, u32[]{:S(2)}) collective-permute-start(f32[32,128]{1,0:T(8,128)S(1)} %get-tuple-element.73), channel_id=1, source_target_pairs={{0,8},{8,0},{16,24},{24,16},{1,9},{9,1},{17,25},{25,17},{2,10},{10... | collective-permute-start | bytes 49160 | tf_op jit(solution)/shard_map/ppermute | solution.py:990
  21.6 8.2 %collective-permute-start.13 = (f32[32,128]{1,0:T(8,128)S(1)}, f32[32,128]{1,0:T(8,128)S(1)}, u32[]{:S(2)}, u32[]{:S(2)}) collective-permute-start(f32[32,128]{1,0:T(8,128)S(1)} %get-tuple-element.74), channel_id=1, source_target_pairs={{0,24},{8,16},{16,8},{24,0},{1,25},{9,17},{17,9},{25,1},{2,26},{10... | collective-permute-start | bytes 49160 | tf_op jit(solution)/shard_map/ppermute | solution.py:990
  24.0 3.2 %collective-permute-start.9 = (f32[24,128]{1,0:T(8,128)S(1)}, f32[24,128]{1,0:T(8,128)S(1)}, u32[]{:S(2)}, u32[]{:S(2)}) collective-permute-start(f32[24,128]{1,0:T(8,128)S(1)} %get-tuple-element.66), channel_id=1, source_target_pairs={{0,6},{2,4},{4,2},{6,0},{1,7},{3,5},{5,3},{7,1},{8,14},{10,12},{12... | collective-permute-start | bytes 36872 | tf_op jit(solution)/shard_map/ppermute | solution.py:990
  30.6 3.7 %collective-permute-start.16 = (f32[16,128]{1,0:T(8,128)S(1)}, f32[16,128]{1,0:T(8,128)S(1)}, u32[]{:S(2)}, u32[]{:S(2)}) collective-permute-start(f32[16,128]{1,0:T(8,128)S(1)} %get-tuple-element.91), channel_id=1, source_target_pairs={{0,1},{1,0},{2,3},{3,2},{4,5},{5,4},{6,7},{7,6},{8,9},{9,8},{10,11... | collective-permute-start | bytes 24584 | tf_op jit(solution)/shard_map/ppermute | solution.py:995
  31.2 3.1 %collective-permute-start.17 = (f32[8,256]{1,0:T(8,128)S(1)}, f32[8,256]{1,0:T(8,128)S(1)}, u32[]{:S(2)}, u32[]{:S(2)}) collective-permute-start(f32[8,256]{1,0:T(8,128)S(1)} %get-tuple-element.92), channel_id=1, source_target_pairs={{0,2},{2,0},{4,6},{6,4},{1,3},{3,1},{5,7},{7,5},{8,10},{10,8},{12,... | collective-permute-start | bytes 24584 | tf_op jit(solution)/shard_map/ppermute | solution.py:990
  31.2 3.1 %collective-permute-start.18 = (f32[8,256]{1,0:T(8,128)S(1)}, f32[8,256]{1,0:T(8,128)S(1)}, u32[]{:S(2)}, u32[]{:S(2)}) collective-permute-start(f32[8,256]{1,0:T(8,128)S(1)} %get-tuple-element.93), channel_id=1, source_target_pairs={{0,6},{2,4},{4,2},{6,0},{1,7},{3,5},{5,3},{7,1},{8,14},{10,12},{12... | collective-permute-start | bytes 24584 | tf_op jit(solution)/shard_map/ppermute | solution.py:990
  31.8 6.8 %collective-permute-start.14 = (f32[3,32,256]{2,1,0:T(8,128)S(1)}, f32[3,32,256]{2,1,0:T(8,128)S(1)}, u32[]{:S(2)}, u32[]{:S(2)}) collective-permute-start(f32[3,32,256]{2,1,0:T(8,128)S(1)} %get-tuple-element.78), channel_id=1, source_target_pairs={{0,8},{8,0},{16,24},{24,16},{1,9},{9,1},{17,25},{25,17},{2,10},{10... | collective-permute-start | bytes 294920 | tf_op jit(solution)/shard_map/ppermute | solution.py:990
  31.8 6.8 %collective-permute-start.15 = (f32[3,32,256]{2,1,0:T(8,128)S(1)}, f32[3,32,256]{2,1,0:T(8,128)S(1)}, u32[]{:S(2)}, u32[]{:S(2)}) collective-permute-start(f32[3,32,256]{2,1,0:T(8,128)S(1)} %get-tuple-element.79), channel_id=1, source_target_pairs={{0,24},{8,16},{16,8},{24,0},{1,25},{9,17},{17,9},{25,1},{2,26},{10... | collective-permute-start | bytes 294920 | tf_op jit(solution)/shard_map/ppermute | solution.py:990
  34.5 7.2 %collective-permute-start.21 = (f32[32,256]{1,0:T(8,128)S(1)}, f32[32,256]{1,0:T(8,128)S(1)}, u32[]{:S(2)}, u32[]{:S(2)}) collective-permute-start(f32[32,256]{1,0:T(8,128)S(1)} %get-tuple-element.94), channel_id=1, source_target_pairs={{0,24},{8,16},{16,8},{24,0},{1,25},{9,17},{17,9},{25,1},{2,26},{10... | collective-permute-start | bytes 98312 | tf_op jit(solution)/shard_map/ppermute | solution.py:990
  36.1 5.6 %collective-permute-start.22 = (f32[32,256]{1,0:T(8,128)S(1)}, f32[32,256]{1,0:T(8,128)S(1)}, u32[]{:S(2)}, u32[]{:S(2)}) collective-permute-start(f32[32,256]{1,0:T(8,128)S(1)} %get-tuple-element.95), channel_id=1, source_target_pairs={{0,8},{8,0},{16,24},{24,16},{1,9},{9,1},{17,25},{25,17},{2,10},{10... | collective-permute-start | bytes 98312 | tf_op jit(solution)/shard_map/ppermute | solution.py:990
  36.1 4.7 %collective-permute-start.19 = (f32[16,128]{1,0:T(8,128)S(1)}, f32[16,128]{1,0:T(8,128)S(1)}, u32[]{:S(2)}, u32[]{:S(2)}) collective-permute-start(f32[16,128]{1,0:T(8,128)S(1)} %collective-permute-done.16.z_rows), channel_id=1, source_target_pairs={{0,2},{2,0},{4,6},{6,4},{1,3},{3,1},{5,7},{7,5},{8,10},{10,8},{12,... | collective-permute-start | bytes 24584 | tf_op jit(solution)/shard_map/ppermute | solution.py:990
  38.6 3.1 %collective-permute-start.20 = (f32[16,128]{1,0:T(8,128)S(1)}, f32[16,128]{1,0:T(8,128)S(1)}, u32[]{:S(2)}, u32[]{:S(2)}) collective-permute-start(f32[16,128]{1,0:T(8,128)S(1)} %collective-permute-done.16.z_rows), channel_id=1, source_target_pairs={{0,6},{2,4},{4,2},{6,0},{1,7},{3,5},{5,3},{7,1},{8,14},{10,12},{12... | collective-permute-start | bytes 24584 | tf_op jit(solution)/shard_map/ppermute | solution.py:990

commit v7 on v6

--- a/solution.py
+++ b/solution.py
@@ -400,6 +400,8 @@
         up, down = (post[x_up[slot], 1], post[x_down[slot], 0])
         ahead[slot] = jnp.where(flip_x, down, up)
         behind[slot] = jnp.where(flip_x, up, down)
+    for comp in range(3):
+        ahead[5 + comp] = jnp.where(flip_x, flow[comp, 0], flow[comp, bx - 1])
 
 
 def restretch_plane(x, place, stretch, flow, halos, updated):
@@ -491,8 +493,8 @@
         copy.start()
     flip_x = odd("gx")
     for comp in range(3):
-        below[comp] = jnp.where(flip_x, x_first[comp], x_second[comp])
-        above[comp] = jnp.where(flip_x, x_second[comp], x_first[comp])
+        below[comp] = jnp.where(flip_x, x_first[5 + comp], x_second[comp])
+        above[comp] = jnp.where(flip_x, x_second[comp], x_first[5 + comp])
     swapped_rows(y_first, y_second, range(speed_slot, sides), y_below, y_above, 0)
     z_halo[...] = row_columns(z_rows[...]).reshape(z_halo.shape)
     halos = (below, above, y_below, y_above, z_halo)
@@ -771,8 +773,8 @@
     changes,
     gas_first,
     gas_second,
+    x_first,
     x_second,
-    x_first,
     edges_first,
     edges_second,
     inner_excess,
@@ -780,7 +782,6 @@
     flow,
     after,
     late,
-    v_first,
     v_second,
     settled,
     spread,
@@ -803,7 +804,6 @@
 
     for comp in range(3):
         up, down = (flow[comp, bx - 1], flow[comp, 0])
-        v_first[comp] = jnp.where(flip_x, down, up)
         v_second[comp] = jnp.where(flip_x, up, down)
     for slot in range(5):
         below[slot] = jnp.where(flip_x, x_first[slot], x_second[slot])
@@ -983,11 +983,20 @@
         new_mass[x] = total
 
 
+def swapped_ahead(array, axis):
+    devices = lax.axis_size(axis)
+    pairing = [(i, (i + 1) % devices if i % 2 == 0 else i - 1) for i in range(devices)]
+    return lax.ppermute(array, axis, pairing)
+
+
+def swapped_behind(array, axis):
+    devices = lax.axis_size(axis)
+    pairing = [(i, (i - 1) % devices if i % 2 == 0 else (i + 1) % devices) for i in range(devices)]
+    return lax.ppermute(array, axis, pairing)
+
+
 def swapped(first, second, axis):
-    devices = lax.axis_size(axis)
-    ahead = [(i, (i + 1) % devices if i % 2 == 0 else i - 1) for i in range(devices)]
-    behind = [(i, (i - 1) % devices if i % 2 == 0 else (i + 1) % devices) for i in range(devices)]
-    return lax.ppermute(first, axis, ahead), lax.ppermute(second, axis, behind)
+    return swapped_ahead(first, axis), swapped_behind(second, axis)
 
 
 def both_ways(rows, lower):
@@ -1078,7 +1087,7 @@
     )(pops, stretch, flow, z_first, *y_first)
     outer_post, outer_shift, z_out, x_one, x_two, y_one, y_two = call(
         collide_outer,
-        [(19, *ends), (3, *ends), columns, (5, *face), (5, *face), rows, rows],
+        [(19, *ends), (3, *ends), columns, (8, *face), (5, *face), rows, rows],
         scratch=[(4, *face), (4, *face)] + sides_y + [box],
         cost=(150 * cells, 150 * cells),
     )(pops, stretch, flags, flow, *first_x, *y_first, z_first, inner_post)
@@ -1121,11 +1130,10 @@
         scratch=[(6, *inside)] + sides_y + [pltpu.SemaphoreType.DMA],
         cost=(80 * cells, 40 * cells),
     )(stretch, flow, *post_y, z_post)
-    late, v_one, v_two, outer_settled, spread, y_one, y_two, z_out = call(
+    late, v_two, outer_settled, spread, y_one, y_two, z_out = call(
         stream_late,
         [
             (5, *ends),
-            (3, *face),
             (3, *face),
             ends,
             (bx + 2, *face),
@@ -1144,7 +1152,7 @@
         totals,
         changes,
         *first_x,
-        *post_x[::-1],
+        *post_x,
         *edges_x,
         inner_excess,
         inner_heading,
@@ -1154,7 +1162,7 @@
     z_last = both_ways(z_out, 8)
     last_y = swapped(y_one, y_two, "gy")
     last_corners = swapped(z_last, z_last, "gy")
-    flow_x = swapped(v_one, v_two, "gx")
+    flow_x = (post_x[0], swapped_behind(v_two, "gx"))
     x_one, x_two = call(add_faces, [face, face], cost=(4 * 10**9, 0))(spread, z_last, *last_y)
     last_x = swapped(x_one, x_two, "gx")
     new_stretch, fresh, outer_done = call(

time: 43.4 us -> 43.1 us (level); the launches traced: 42.6 us -> 42.9 us
    ppermute x3, waiting for transfers between devices: 0.97 us -> 1.66 us  [both_ways(): lax.ppermute(rows, 'gz', [(i, (i + 1) % devices) for i in range(devices)])]
    ppermute x20 -> x19, waiting for transfers between devices: 6.22 us -> 5.81 us  [the longest x10 5.01 us: swapped_behind(): return lax.ppermute(array, axis, pairing)]
    ppermute x20 -> x19, starting transfers between devices: 19.1 us -> 19.2 us  [the longest x10 15.3 us: swapped_behind(): return lax.ppermute(array, axis, pairing)]
  transfers between devices with their start and end apart: 23 -> 22, of which waited for: 8 -> 7; matrix products, arithmetic and copies ran while one was open for 0% -> 0% of each run, Pallas kernels for 18% -> 18%
where the time goes in v7:
time: 43.1 us; the launch traced here: 42.9 us
  starting transfers between devices  22.8 us (53%)
  Pallas kernels  11.9 us (28%)
  waiting for transfers between devices  7.46 us (17%)
  between operations  0.81 us (2%)
    ppermute x10, starting transfers between devices, swapped_behind(): return lax.ppermute(array, axis, pairing)  15.3 us
    ppermute x10, waiting for transfers between devices, swapped_behind(): return lax.ppermute(array, axis, pairing)  5.01 us
    ppermute x9, starting transfers between devices, swapped_ahead(): return lax.ppermute(array, axis, pairing)  3.86 us
    ppermute x3, starting transfers between devices, both_ways(): lax.ppermute(rows, 'gz', [(i, (i + 1) % devices) for i in range(devices)])  3.59 us
    pallas_call x1, Pallas kernels, shards(): call(restretch_outer, [(6, *box), (19, *box), mark], specs=[pl.BlockSpec(...  2.16 us
    pallas_call x1, Pallas kernels, shards(): call(moments, [(19, *box), (5, *box)], specs=[remote], scratch=[pltpu.Sem...  1.74 us
    ppermute x3, waiting for transfers between devices, both_ways(): lax.ppermute(rows, 'gz', [(i, (i + 1) % devices) for i in range(devices)])  1.66 us
    pallas_call x1, Pallas kernels, shards(): call(first_faces, [(6, *box), jax.ShapeDtypeStruct(box, jnp.int32), (8, b...  1.38 us
  transfers between devices with their start and end apart: 22, of which 7 were waited for; matrix products, arithmetic and copies ran while one was open for 0% of the time, Pallas kernels for 18%

profile of v7, /device:TPU:0, one launch (start us, length us, event | category | flops | bytes accessed | tf_op | source)
XLA Modules:
  0.0 42.9 jit_solution(6714234738257582456)
XLA Ops:
  0.6 1.4 %shard_map.94 = (f32[6,4,32,256]{3,2,1,0:T(8,128)S(1)}, s32[4,32,256]{2,1,0:T(8,128)S(1)}, f32[8,128]{1,0:T(8,128)S(1)}, f32[16,256]{1,0:T(8,128)S(1)}, f32[16,2...) custom-call(f32[6,4,32,256]{3,2,1,0:T(8,128)} %stretch_in.1, s32[4,32,256]{2,1,0:T(8,128)} %flags_in.1), custom_call_target="tpu_custom_call" | custom-call | flops 327680 | bytes 1966080 | tf_op jit(solution)/shard_map/pallas_call | solution.py:1043
  2.0 3.1 %collective-permute-start = (f32[4,32,256]{2,1,0:T(8,128)S(1)}, f32[4,32,256]{2,1,0:T(8,128)S(1)}, u32[]{:S(2)}, u32[]{:S(2)}) collective-permute-start(f32[4,32,256]{2,1,0:T(8,128)S(1)} %get-tuple-element.53), channel_id=1, source_target_pairs={{0,8},{8,0},{16,24},{24,16},{1,9},{9,1},{17,25},{25,17},{2,10},{10... | collective-permute-start | bytes 393224 | tf_op jit(solution)/shard_map/ppermute | solution.py:989
  5.1 2.5 %collective-permute-start.1 = (f32[4,32,256]{2,1,0:T(8,128)S(1)}, f32[4,32,256]{2,1,0:T(8,128)S(1)}, u32[]{:S(2)}, u32[]{:S(2)}) collective-permute-start(f32[4,32,256]{2,1,0:T(8,128)S(1)} %get-tuple-element.54), channel_id=1, source_target_pairs={{0,24},{8,16},{16,8},{24,0},{1,25},{9,17},{17,9},{25,1},{2,26},{10... | collective-permute-start | bytes 393224 | tf_op jit(solution)/shard_map/ppermute | solution.py:995
  7.6 0.0 collective-permute-start.2
  7.6 1.6 %collective-permute-start.3 = (f32[16,256]{1,0:T(8,128)S(1)}, f32[16,256]{1,0:T(8,128)S(1)}, u32[]{:S(2)}, u32[]{:S(2)}) collective-permute-start(f32[16,256]{1,0:T(8,128)S(1)} %get-tuple-element.56), channel_id=1, source_target_pairs={{0,6},{2,4},{4,2},{6,0},{1,7},{3,5},{5,3},{7,1},{8,14},{10,12},{12... | collective-permute-start | bytes 49160 | tf_op jit(solution)/shard_map/ppermute | solution.py:995
  9.2 1.5 %collective-permute-start.4 = (f32[8,128]{1,0:T(8,128)S(1)}, f32[8,128]{1,0:T(8,128)S(1)}, u32[]{:S(2)}, u32[]{:S(2)}) collective-permute-start(f32[8,128]{1,0:T(8,128)S(1)} %get-tuple-element.57), channel_id=1, source_target_pairs={{0,1},{1,0},{2,3},{3,2},{4,5},{5,4},{6,7},{7,6},{8,9},{9,8},{10,11... | collective-permute-start | bytes 12296 | tf_op jit(solution)/shard_map/ppermute | solution.py:1004
  10.7 1.7 %shard_map.95 = (f32[19,4,32,256]{3,2,1,0:T(8,128)S(1)}, f32[5,4,32,256]{3,2,1,0:T(8,128)S(1)}) custom-call(f32[19,4,32,256]{3,2,1,0:T(8,128)} %pops_in.1), custom_call_target="tpu_custom_call" | custom-call | flops 1966080 | bytes 4915200 | tf_op jit(solution)/shard_map/pallas_call | solution.py:1071
  12.5 0.3 collective-permute-done.4.z_rows
  12.8 0.0 collective-permute-done.2.y_first
  12.8 0.0 collective-permute-done.3.y_second
  12.8 0.8 %shard_map.96 = (f32[19,2,32,256]{3,2,1,0:T(8,128)S(1)}, f32[3,2,32,256]{3,2,1,0:T(8,128)S(1)}) custom-call(f32[19,4,32,256]{3,2,1,0:T(8,128)S(1)} %get-tuple-element.51.pops, f32[6,4,32,256]{3,2,1,0:T(8,128)S(1)} %get-tuple-element.49.stretch, f32[5,4,32,256]{3,2,1,0:T(8,128)S(1)} %get-tuple-element.50.flow, f32[8,128]{1,0:T(8,128)S(1)} %collective-permute-done.4.z_rows, ...), custom_call_target="tpu_custom_call" | custom-call | flops 4915200 | bytes 4915200 | tf_op jit(solution)/shard_map/pallas_call | solution.py:1082
  13.6 0.0 collective-permute-done.x_first.gas_first
  13.6 0.1 collective-permute-done.1.x_second.gas_second
  13.7 1.0 %shard_map.97 = (f32[19,2,32,256]{3,2,1,0:T(8,128)S(1)}, f32[3,2,32,256]{3,2,1,0:T(8,128)S(1)}, f32[24,128]{1,0:T(8,128)S(1)}, f32[8,32,256]{2,1,0:T(8,128)S(1)}...) custom-call(f32[19,4,32,256]{3,2,1,0:T(8,128)S(1)} %get-tuple-element.51.pops, ...), custom_call_target="tpu_custom_call" | custom-call | flops 4915200 | bytes 4915200 | tf_op jit(solution)/shard_map/pallas_call | solution.py:1088
  14.7 0.0 collective-permute-start.6
  14.8 1.6 %collective-permute-start.7 = (f32[40,256]{1,0:T(8,128)S(1)}, f32[40,256]{1,0:T(8,128)S(1)}, u32[]{:S(2)}, u32[]{:S(2)}) collective-permute-start(f32[40,256]{1,0:T(8,128)S(1)} %get-tuple-element.64), channel_id=1, source_target_pairs={{0,6},{2,4},{4,2},{6,0},{1,7},{3,5},{5,3},{7,1},{8,14},{10,12},{12... | collective-permute-start | bytes 122888 | tf_op jit(solution)/shard_map/ppermute | solution.py:995
  16.4 1.5 %collective-permute-start.8 = (f32[24,128]{1,0:T(8,128)S(1)}, f32[24,128]{1,0:T(8,128)S(1)}, u32[]{:S(2)}, u32[]{:S(2)}) collective-permute-start(f32[24,128]{1,0:T(8,128)S(1)} %get-tuple-element.65), channel_id=1, source_target_pairs={{0,1},{1,0},{2,3},{3,2},{4,5},{5,4},{6,7},{7,6},{8,9},{9,8},{10,11... | collective-permute-start | bytes 36872 | tf_op jit(solution)/shard_map/ppermute | solution.py:1004
  17.9 0.6 %collective-permute-start.5 = (f32[8,32,256]{2,1,0:T(8,128)S(1)}, f32[8,32,256]{2,1,0:T(8,128)S(1)}, u32[]{:S(2)}, u32[]{:S(2)}) collective-permute-start(f32[8,32,256]{2,1,0:T(8,128)S(1)} %get-tuple-element.59), channel_id=1, source_target_pairs={{0,8},{8,0},{16,24},{24,16},{1,9},{9,1},{17,25},{25,17},{2,10},{10... | collective-permute-start | bytes 786440 | tf_op jit(solution)/shard_map/ppermute | solution.py:989
  18.5 0.0 copy-start.1
  18.5 0.0 copy-start.2
  18.5 0.0 copy-start.3
  18.5 2.6 %collective-permute-start.11 = (f32[5,32,256]{2,1,0:T(8,128)S(1)}, f32[5,32,256]{2,1,0:T(8,128)S(1)}, u32[]{:S(2)}, u32[]{:S(2)}) collective-permute-start(f32[5,32,256]{2,1,0:T(8,128)S(1)} %get-tuple-element.71), channel_id=1, source_target_pairs={{0,24},{8,16},{16,8},{24,0},{1,25},{9,17},{17,9},{25,1},{2,26},{10... | collective-permute-start | bytes 491528 | tf_op jit(solution)/shard_map/ppermute | solution.py:995
  21.1 0.0 collective-permute-done.8.refs_0_.z_rows
  21.1 0.0 collective-permute-done.6.refs_1_.y_first
  21.1 0.0 collective-permute-done.7.refs_2_.y_second
  21.2 0.0 copy-start
  21.2 0.1 collective-permute-start.9
  21.3 0.1 collective-permute-start.12
  21.3 2.1 %collective-permute-start.13 = (f32[32,128]{1,0:T(8,128)S(1)}, f32[32,128]{1,0:T(8,128)S(1)}, u32[]{:S(2)}, u32[]{:S(2)}) collective-permute-start(f32[32,128]{1,0:T(8,128)S(1)} %get-tuple-element.73), channel_id=1, source_target_pairs={{0,24},{8,16},{16,8},{24,0},{1,25},{9,17},{17,9},{25,1},{2,26},{10... | collective-permute-start | bytes 49160 | tf_op jit(solution)/shard_map/ppermute | solution.py:995
  23.5 0.0 collective-permute-done.9.corner_first
  23.5 0.0 collective-permute-start.10
  23.5 0.0 copy-done.1
  23.5 0.0 copy-done.2
  23.5 0.0 copy-done.3
  23.5 0.3 shard_map.98
  23.9 1.2 %shard_map.102 = (f32[6,4,32,256]{3,2,1,0:T(8,128)}, f32[8,128]{1,0:T(8,128)S(1)}) custom-call(f32[6,4,32,256]{3,2,1,0:T(8,128)S(1)} %get-tuple-element.49.stretch, f32[5,4,32,256]{3,2,1,0:T(8,128)S(1)} %get-tuple-element.50.flow, f32[40,256]{1,0:T(8,128)S(1)} %collective-permute-done.6.refs_1_.y_first, ...), custom_call_target="tpu_custom_call" | custom-call | flops 2621440 | bytes 1310720 | tf_op jit(solution)/shard_map/pallas_call | solution.py:1126
  25.1 0.9 %shard_map.100 = (f32[15,2,32,256]{3,2,1,0:T(8,128)S(1)}, f32[15,2,32,256]{3,2,1,0:T(8,128)S(1)}, f32[4,32,256]{2,1,0:T(8,128)S(1)}, f32[4,32,256]{2,1,0:T(8,128)S(1)}) custom-call(f32[19,2,32,256]{3,2,1,0:T(8,128)S(1)} %get-tuple-element.58.inner.inner_post, f32[19,2,32,256]{3,2,1,0:T(8,128)S(1)} %get-tuple-element.60.outer_post.post, ...), custom_call_target="tpu_custom_call" | custom-call | flops 11468800 | bytes 6553600 | tf_op jit(solution)/shard_map/pallas_call | solution.py:1106
  26.0 0.7 %collective-permute-done.10.corner_second = f32[24,128]{1,0:T(8,128)S(1)} collective-permute-done((f32[24,128]{1,0:T(8,128)S(1)}, f32[24,128]{1,0:T(8,128)S(1)}, u32[]{:S(2)}, u32[]{:S(2)}) %collective-permute-start.10) | collective-permute-done | bytes 12320 | tf_op jit(solution)/shard_map/ppermute | solution.py:995
  26.7 0.0 copy-done
  26.7 0.6 %shard_map.101 = (f32[4,2,32,256]{3,2,1,0:T(8,128)S(1)}, f32[4,2,32,256]{3,2,1,0:T(8,128)S(1)}, f32[2,32,256]{2,1,0:T(8,128)S(1)}, f32[2,32,256]{2,1,0:T(8,128)S...) custom-call(f32[19,2,32,256]{3,2,1,0:T(8,128)S(1)} %get-tuple-element.58.inner.inner_post, ...), custom_call_target="tpu_custom_call" | custom-call | flops 3276800 | bytes 1966080 | tf_op jit(solution)/shard_map/pallas_call | solution.py:1120
  27.3 0.8 %collective-permute-done.12.edges_first = f32[32,128]{1,0:T(8,128)S(1)} collective-permute-done((f32[32,128]{1,0:T(8,128)S(1)}, f32[32,128]{1,0:T(8,128)S(1)}, u32[]{:S(2)}, u32[]{:S(2)}) %collective-permute-start.12) | collective-permute-done | bytes 16416 | tf_op jit(solution)/shard_map/ppermute | solution.py:989
  28.0 3.3 %collective-permute-done.13.edges_second = f32[32,128]{1,0:T(8,128)S(1)} collective-permute-done((f32[32,128]{1,0:T(8,128)S(1)}, f32[32,128]{1,0:T(8,128)S(1)}, u32[]{:S(2)}, u32[]{:S(2)}) %collective-permute-start.13) | collective-permute-done | bytes 16416 | tf_op jit(solution)/shard_map/ppermute | solution.py:995
  31.3 0.0 collective-permute-done.11.x_second
  31.3 0.0 collective-permute-done.5.x_first
  31.3 0.8 %shard_map.103 = (f32[5,2,32,256]{3,2,1,0:T(8,128)S(1)}, f32[3,32,256]{2,1,0:T(8,128)S(1)}, f32[2,32,256]{2,1,0:T(8,128)S(1)}, f32[6,32,256]{2,1,0:T(8,128)S(1)}...) custom-call(f32[19,2,32,256]{3,2,1,0:T(8,128)S(1)} %get-tuple-element.60.outer_post.post, ...), custom_call_target="tpu_custom_call" | custom-call | flops 4915200 | bytes 3276800 | tf_op jit(solution)/shard_map/pallas_call | solution.py:1133
  32.1 0.6 %collective-permute-start.15 = (f32[16,128]{1,0:T(8,128)S(1)}, f32[16,128]{1,0:T(8,128)S(1)}, u32[]{:S(2)}, u32[]{:S(2)}) collective-permute-start(f32[16,128]{1,0:T(8,128)S(1)} %get-tuple-element.89), channel_id=1, source_target_pairs={{0,1},{1,0},{2,3},{3,2},{4,5},{5,4},{6,7},{7,6},{8,9},{9,8},{10,11... | collective-permute-start | bytes 24584 | tf_op jit(solution)/shard_map/ppermute | solution.py:1004
  32.6 0.0 collective-permute-start.16
  32.6 0.6 %collective-permute-start.17 = (f32[8,256]{1,0:T(8,128)S(1)}, f32[8,256]{1,0:T(8,128)S(1)}, u32[]{:S(2)}, u32[]{:S(2)}) collective-permute-start(f32[8,256]{1,0:T(8,128)S(1)} %get-tuple-element.91), channel_id=1, source_target_pairs={{0,6},{2,4},{4,2},{6,0},{1,7},{3,5},{5,3},{7,1},{8,14},{10,12},{12... | collective-permute-start | bytes 24584 | tf_op jit(solution)/shard_map/ppermute | solution.py:995
  33.3 1.2 %collective-permute-start.14 = (f32[3,32,256]{2,1,0:T(8,128)S(1)}, f32[3,32,256]{2,1,0:T(8,128)S(1)}, u32[]{:S(2)}, u32[]{:S(2)}) collective-permute-start(f32[3,32,256]{2,1,0:T(8,128)S(1)} %get-tuple-element.77), channel_id=1, source_target_pairs={{0,24},{8,16},{16,8},{24,0},{1,25},{9,17},{17,9},{25,1},{2,26},{10... | collective-permute-start | bytes 294920 | tf_op jit(solution)/shard_map/ppermute | solution.py:995
  34.5 1.3 %collective-permute-done.15.z_rows = f32[16,128]{1,0:T(8,128)S(1)} collective-permute-done((f32[16,128]{1,0:T(8,128)S(1)}, f32[16,128]{1,0:T(8,128)S(1)}, u32[]{:S(2)}, u32[]{:S(2)}) %collective-permute-start.15) | collective-permute-done | bytes 8224 | tf_op jit(solution)/shard_map/ppermute | solution.py:1004
  35.8 0.0 collective-permute-done.16.y_first
  35.8 0.0 collective-permute-done.17.y_second
  35.8 0.2 shard_map.105
  35.9 1.4 %collective-permute-start.20 = (f32[32,256]{1,0:T(8,128)S(1)}, f32[32,256]{1,0:T(8,128)S(1)}, u32[]{:S(2)}, u32[]{:S(2)}) collective-permute-start(f32[32,256]{1,0:T(8,128)S(1)} %get-tuple-element.92), channel_id=1, source_target_pairs={{0,24},{8,16},{16,8},{24,0},{1,25},{9,17},{17,9},{25,1},{2,26},{10... | collective-permute-start | bytes 98312 | tf_op jit(solution)/shard_map/ppermute | solution.py:995
  37.4 0.0 collective-permute-start.21
  37.4 0.0 collective-permute-start.18
  37.4 1.6 %collective-permute-start.19 = (f32[16,128]{1,0:T(8,128)S(1)}, f32[16,128]{1,0:T(8,128)S(1)}, u32[]{:S(2)}, u32[]{:S(2)}) collective-permute-start(f32[16,128]{1,0:T(8,128)S(1)} %collective-permute-done.15.z_rows), channel_id=1, source_target_pairs={{0,6},{2,4},{4,2},{6,0},{1,7},{3,5},{5,3},{7,1},{8,14},{10,12},{12... | collective-permute-start | bytes 24584 | tf_op jit(solution)/shard_map/ppermute | solution.py:995
  39.0 0.9 %collective-permute-done.14.x_second = f32[3,32,256]{2,1,0:T(8,128)S(1)} collective-permute-done((f32[3,32,256]{2,1,0:T(8,128)S(1)}, f32[3,32,256]{2,1,0:T(8,128)S(1)}, u32[]{:S(2)}, u32[]{:S(2)}) %collective-permute-start.14) | collective-permute-done | bytes 98336 | tf_op jit(solution)/shard_map/ppermute | solution.py:995
  39.9 2.2 %shard_map.104 = (f32[6,4,32,256]{3,2,1,0:T(8,128)}, f32[19,4,32,256]{3,2,1,0:T(8,128)}, f32[8,128]{1,0:T(8,128)S(1)}) custom-call(f32[6,4,32,256]{3,2,1,0:T(8,128)S(1)} %get-tuple-element.49.stretch, f32[5,4,32,256]{3,2,1,0:T(8,128)S(1)} %get-tuple-element.50.flow, ...), custom_call_target="tpu_custom_call", output_to_operand_aliasing={{0}: (7, {})} | custom-call | flops 2621440 | bytes 6553600 | tf_op jit(solution)/shard_map/pallas_call | solution.py:1168
  42.0 0.0 collective-permute-done.18.corner_first
  42.1 0.0 collective-permute-done.19.corner_second
  42.1 0.0 collective-permute-done.20.x_second
  42.1 0.0 collective-permute-done.21.x_first
  42.1 0.9 %shard_map.106 = f32[4,32,256]{2,1,0:T(8,128)} custom-call(f32[2,32,256]{2,1,0:T(8,128)S(1)} %get-tuple-element.86.inner_settled, f32[2,32,256]{2,1,0:T(8,128)S(1)} %get-tuple-element.87.outer_settled, f32[6,32,256]{2,1,0:T(8,128)S(1)} %get-tuple-element.88.spread, f32[16,128]{1,0:T(8,128)S(1)} %collective-permute-done.15.z_rows, ...), custom_call_target="tpu_custom_call" | custom-call | tf_op jit(solution)/shard_map/pallas_call | solution.py:1191
  (1 shorter events, 0.0 us)
Async XLA Ops:
  2.0 11.5 %collective-permute-start = (f32[4,32,256]{2,1,0:T(8,128)S(1)}, f32[4,32,256]{2,1,0:T(8,128)S(1)}, u32[]{:S(2)}, u32[]{:S(2)}) collective-permute-start(f32[4,32,256]{2,1,0:T(8,128)S(1)} %get-tuple-element.53), channel_id=1, source_target_pairs={{0,8},{8,0},{16,24},{24,16},{1,9},{9,1},{17,25},{25,17},{2,10},{10... | collective-permute-start | bytes 393224 | tf_op jit(solution)/shard_map/ppermute | solution.py:989
  5.1 8.6 %collective-permute-start.1 = (f32[4,32,256]{2,1,0:T(8,128)S(1)}, f32[4,32,256]{2,1,0:T(8,128)S(1)}, u32[]{:S(2)}, u32[]{:S(2)}) collective-permute-start(f32[4,32,256]{2,1,0:T(8,128)S(1)} %get-tuple-element.54), channel_id=1, source_target_pairs={{0,24},{8,16},{16,8},{24,0},{1,25},{9,17},{17,9},{25,1},{2,26},{10... | collective-permute-start | bytes 393224 | tf_op jit(solution)/shard_map/ppermute | solution.py:995
  7.6 5.2 %collective-permute-start.2 = (f32[16,256]{1,0:T(8,128)S(1)}, f32[16,256]{1,0:T(8,128)S(1)}, u32[]{:S(2)}, u32[]{:S(2)}) collective-permute-start(f32[16,256]{1,0:T(8,128)S(1)} %get-tuple-element.55), channel_id=1, source_target_pairs={{0,2},{2,0},{4,6},{6,4},{1,3},{3,1},{5,7},{7,5},{8,10},{10,8},{12,... | collective-permute-start | bytes 49160 | tf_op jit(solution)/shard_map/ppermute | solution.py:989
  7.6 5.2 %collective-permute-start.3 = (f32[16,256]{1,0:T(8,128)S(1)}, f32[16,256]{1,0:T(8,128)S(1)}, u32[]{:S(2)}, u32[]{:S(2)}) collective-permute-start(f32[16,256]{1,0:T(8,128)S(1)} %get-tuple-element.56), channel_id=1, source_target_pairs={{0,6},{2,4},{4,2},{6,0},{1,7},{3,5},{5,3},{7,1},{8,14},{10,12},{12... | collective-permute-start | bytes 49160 | tf_op jit(solution)/shard_map/ppermute | solution.py:995
  9.2 3.6 %collective-permute-start.4 = (f32[8,128]{1,0:T(8,128)S(1)}, f32[8,128]{1,0:T(8,128)S(1)}, u32[]{:S(2)}, u32[]{:S(2)}) collective-permute-start(f32[8,128]{1,0:T(8,128)S(1)} %get-tuple-element.57), channel_id=1, source_target_pairs={{0,1},{1,0},{2,3},{3,2},{4,5},{5,4},{6,7},{7,6},{8,9},{9,8},{10,11... | collective-permute-start | bytes 12296 | tf_op jit(solution)/shard_map/ppermute | solution.py:1004
  14.7 6.4 %collective-permute-start.6 = (f32[40,256]{1,0:T(8,128)S(1)}, f32[40,256]{1,0:T(8,128)S(1)}, u32[]{:S(2)}, u32[]{:S(2)}) collective-permute-start(f32[40,256]{1,0:T(8,128)S(1)} %get-tuple-element.63), channel_id=1, source_target_pairs={{0,2},{2,0},{4,6},{6,4},{1,3},{3,1},{5,7},{7,5},{8,10},{10,8},{12,... | collective-permute-start | bytes 122888 | tf_op jit(solution)/shard_map/ppermute | solution.py:989
  14.8 6.4 %collective-permute-start.7 = (f32[40,256]{1,0:T(8,128)S(1)}, f32[40,256]{1,0:T(8,128)S(1)}, u32[]{:S(2)}, u32[]{:S(2)}) collective-permute-start(f32[40,256]{1,0:T(8,128)S(1)} %get-tuple-element.64), channel_id=1, source_target_pairs={{0,6},{2,4},{4,2},{6,0},{1,7},{3,5},{5,3},{7,1},{8,14},{10,12},{12... | collective-permute-start | bytes 122888 | tf_op jit(solution)/shard_map/ppermute | solution.py:995
  16.4 4.7 %collective-permute-start.8 = (f32[24,128]{1,0:T(8,128)S(1)}, f32[24,128]{1,0:T(8,128)S(1)}, u32[]{:S(2)}, u32[]{:S(2)}) collective-permute-start(f32[24,128]{1,0:T(8,128)S(1)} %get-tuple-element.65), channel_id=1, source_target_pairs={{0,1},{1,0},{2,3},{3,2},{4,5},{5,4},{6,7},{7,6},{8,9},{9,8},{10,11... | collective-permute-start | bytes 36872 | tf_op jit(solution)/shard_map/ppermute | solution.py:1004
  17.9 13.4 %collective-permute-start.5 = (f32[8,32,256]{2,1,0:T(8,128)S(1)}, f32[8,32,256]{2,1,0:T(8,128)S(1)}, u32[]{:S(2)}, u32[]{:S(2)}) collective-permute-start(f32[8,32,256]{2,1,0:T(8,128)S(1)} %get-tuple-element.59), channel_id=1, source_target_pairs={{0,8},{8,0},{16,24},{24,16},{1,9},{9,1},{17,25},{25,17},{2,10},{10... | collective-permute-start | bytes 786440 | tf_op jit(solution)/shard_map/ppermute | solution.py:989
  18.5 5.0 %copy-start.1 = (s32[1024]{0:T(1024)S(1)}, s32[1024]{0:T(1024)}, u32[]{:S(2)}) copy-start(s32[1024]{0:T(1024)} %param.11) | copy-start | bytes 12292
  18.5 5.0 %copy-start.2 = (s32[1024]{0:T(1024)S(1)}, s32[1024]{0:T(1024)}, u32[]{:S(2)}) copy-start(s32[1024]{0:T(1024)} %param.12) | copy-start | bytes 12292
  18.5 5.0 %copy-start.3 = (s32[1024]{0:T(1024)S(1)}, s32[1024]{0:T(1024)}, u32[]{:S(2)}) copy-start(s32[1024]{0:T(1024)} %param.13) | copy-start | bytes 12292
  18.5 12.8 %collective-permute-start.11 = (f32[5,32,256]{2,1,0:T(8,128)S(1)}, f32[5,32,256]{2,1,0:T(8,128)S(1)}, u32[]{:S(2)}, u32[]{:S(2)}) collective-permute-start(f32[5,32,256]{2,1,0:T(8,128)S(1)} %get-tuple-element.71), channel_id=1, source_target_pairs={{0,24},{8,16},{16,8},{24,0},{1,25},{9,17},{17,9},{25,1},{2,26},{10... | collective-permute-start | bytes 491528 | tf_op jit(solution)/shard_map/ppermute | solution.py:995
  21.2 5.5 %copy-start = (f32[4,32,256]{2,1,0:T(8,128)S(1)}, f32[4,32,256]{2,1,0:T(8,128)}, u32[]{:S(2)}) copy-start(f32[4,32,256]{2,1,0:T(8,128)} %mass.3) | copy-start | bytes 393220
  21.2 2.3 %collective-permute-start.9 = (f32[24,128]{1,0:T(8,128)S(1)}, f32[24,128]{1,0:T(8,128)S(1)}, u32[]{:S(2)}, u32[]{:S(2)}) collective-permute-start(f32[24,128]{1,0:T(8,128)S(1)} %get-tuple-element.66), channel_id=1, source_target_pairs={{0,2},{2,0},{4,6},{6,4},{1,3},{3,1},{5,7},{7,5},{8,10},{10,8},{12,... | collective-permute-start | bytes 36872 | tf_op jit(solution)/shard_map/ppermute | solution.py:989
  21.3 6.8 %collective-permute-start.12 = (f32[32,128]{1,0:T(8,128)S(1)}, f32[32,128]{1,0:T(8,128)S(1)}, u32[]{:S(2)}, u32[]{:S(2)}) collective-permute-start(f32[32,128]{1,0:T(8,128)S(1)} %get-tuple-element.72), channel_id=1, source_target_pairs={{0,8},{8,0},{16,24},{24,16},{1,9},{9,1},{17,25},{25,17},{2,10},{10... | collective-permute-start | bytes 49160 | tf_op jit(solution)/shard_map/ppermute | solution.py:989
  21.3 10.0 %collective-permute-start.13 = (f32[32,128]{1,0:T(8,128)S(1)}, f32[32,128]{1,0:T(8,128)S(1)}, u32[]{:S(2)}, u32[]{:S(2)}) collective-permute-start(f32[32,128]{1,0:T(8,128)S(1)} %get-tuple-element.73), channel_id=1, source_target_pairs={{0,24},{8,16},{16,8},{24,0},{1,25},{9,17},{17,9},{25,1},{2,26},{10... | collective-permute-start | bytes 49160 | tf_op jit(solution)/shard_map/ppermute | solution.py:995
  23.5 3.2 %collective-permute-start.10 = (f32[24,128]{1,0:T(8,128)S(1)}, f32[24,128]{1,0:T(8,128)S(1)}, u32[]{:S(2)}, u32[]{:S(2)}) collective-permute-start(f32[24,128]{1,0:T(8,128)S(1)} %get-tuple-element.66), channel_id=1, source_target_pairs={{0,6},{2,4},{4,2},{6,0},{1,7},{3,5},{5,3},{7,1},{8,14},{10,12},{12... | collective-permute-start | bytes 36872 | tf_op jit(solution)/shard_map/ppermute | solution.py:995
  32.1 3.7 %collective-permute-start.15 = (f32[16,128]{1,0:T(8,128)S(1)}, f32[16,128]{1,0:T(8,128)S(1)}, u32[]{:S(2)}, u32[]{:S(2)}) collective-permute-start(f32[16,128]{1,0:T(8,128)S(1)} %get-tuple-element.89), channel_id=1, source_target_pairs={{0,1},{1,0},{2,3},{3,2},{4,5},{5,4},{6,7},{7,6},{8,9},{9,8},{10,11... | collective-permute-start | bytes 24584 | tf_op jit(solution)/shard_map/ppermute | solution.py:1004
  32.6 3.1 %collective-permute-start.16 = (f32[8,256]{1,0:T(8,128)S(1)}, f32[8,256]{1,0:T(8,128)S(1)}, u32[]{:S(2)}, u32[]{:S(2)}) collective-permute-start(f32[8,256]{1,0:T(8,128)S(1)} %get-tuple-element.90), channel_id=1, source_target_pairs={{0,2},{2,0},{4,6},{6,4},{1,3},{3,1},{5,7},{7,5},{8,10},{10,8},{12,... | collective-permute-start | bytes 24584 | tf_op jit(solution)/shard_map/ppermute | solution.py:989
  32.6 3.1 %collective-permute-start.17 = (f32[8,256]{1,0:T(8,128)S(1)}, f32[8,256]{1,0:T(8,128)S(1)}, u32[]{:S(2)}, u32[]{:S(2)}) collective-permute-start(f32[8,256]{1,0:T(8,128)S(1)} %get-tuple-element.91), channel_id=1, source_target_pairs={{0,6},{2,4},{4,2},{6,0},{1,7},{3,5},{5,3},{7,1},{8,14},{10,12},{12... | collective-permute-start | bytes 24584 | tf_op jit(solution)/shard_map/ppermute | solution.py:995
  33.3 6.6 %collective-permute-start.14 = (f32[3,32,256]{2,1,0:T(8,128)S(1)}, f32[3,32,256]{2,1,0:T(8,128)S(1)}, u32[]{:S(2)}, u32[]{:S(2)}) collective-permute-start(f32[3,32,256]{2,1,0:T(8,128)S(1)} %get-tuple-element.77), channel_id=1, source_target_pairs={{0,24},{8,16},{16,8},{24,0},{1,25},{9,17},{17,9},{25,1},{2,26},{10... | collective-permute-start | bytes 294920 | tf_op jit(solution)/shard_map/ppermute | solution.py:995
  35.9 6.1 %collective-permute-start.20 = (f32[32,256]{1,0:T(8,128)S(1)}, f32[32,256]{1,0:T(8,128)S(1)}, u32[]{:S(2)}, u32[]{:S(2)}) collective-permute-start(f32[32,256]{1,0:T(8,128)S(1)} %get-tuple-element.92), channel_id=1, source_target_pairs={{0,24},{8,16},{16,8},{24,0},{1,25},{9,17},{17,9},{25,1},{2,26},{10... | collective-permute-start | bytes 98312 | tf_op jit(solution)/shard_map/ppermute | solution.py:995
  37.4 4.7 %collective-permute-start.21 = (f32[32,256]{1,0:T(8,128)S(1)}, f32[32,256]{1,0:T(8,128)S(1)}, u32[]{:S(2)}, u32[]{:S(2)}) collective-permute-start(f32[32,256]{1,0:T(8,128)S(1)} %get-tuple-element.93), channel_id=1, source_target_pairs={{0,8},{8,0},{16,24},{24,16},{1,9},{9,1},{17,25},{25,17},{2,10},{10... | collective-permute-start | bytes 98312 | tf_op jit(solution)/shard_map/ppermute | solution.py:989
  37.4 4.7 %collective-permute-start.18 = (f32[16,128]{1,0:T(8,128)S(1)}, f32[16,128]{1,0:T(8,128)S(1)}, u32[]{:S(2)}, u32[]{:S(2)}) collective-permute-start(f32[16,128]{1,0:T(8,128)S(1)} %collective-permute-done.15.z_rows), channel_id=1, source_target_pairs={{0,2},{2,0},{4,6},{6,4},{1,3},{3,1},{5,7},{7,5},{8,10},{10,8},{12,... | collective-permute-start | bytes 24584 | tf_op jit(solution)/shard_map/ppermute | solution.py:989
  37.4 4.7 %collective-permute-start.19 = (f32[16,128]{1,0:T(8,128)S(1)}, f32[16,128]{1,0:T(8,128)S(1)}, u32[]{:S(2)}, u32[]{:S(2)}) collective-permute-start(f32[16,128]{1,0:T(8,128)S(1)} %collective-permute-done.15.z_rows), channel_id=1, source_target_pairs={{0,6},{2,4},{4,2},{6,0},{1,7},{3,5},{5,3},{7,1},{8,14},{10,12},{12... | collective-permute-start | bytes 24584 | tf_op jit(solution)/shard_map/ppermute | solution.py:995

commit v8 on v5

--- a/solution.py
+++ b/solution.py
@@ -400,6 +400,7 @@
         up, down = (post[x_up[slot], 1], post[x_down[slot], 0])
         ahead[slot] = jnp.where(flip_x, down, up)
         behind[slot] = jnp.where(flip_x, up, down)
+    behind[5] = jnp.where(flip_x, flow[0, bx - 1], flow[0, 0])
 
 
 def restretch_plane(x, place, stretch, flow, halos, updated):
@@ -464,6 +465,7 @@
     flow,
     x_first,
     x_second,
+    post_second,
     y_first,
     y_second,
     z_rows,
@@ -481,8 +483,9 @@
     bx = stretch.shape[1]
     flip_x = odd("gx")
     for comp in range(3):
-        below[comp] = jnp.where(flip_x, x_first[comp], x_second[comp])
-        above[comp] = jnp.where(flip_x, x_second[comp], x_first[comp])
+        second = post_second[5] if comp == 0 else x_second[comp - 1]
+        below[comp] = jnp.where(flip_x, x_first[comp], second)
+        above[comp] = jnp.where(flip_x, second, x_first[comp])
     swapped_rows(y_first, y_second, range(speed_slot, sides), y_below, y_above, 0)
     z_halo[...] = row_columns(z_rows[...]).reshape(z_halo.shape)
     halos = (below, above, y_below, y_above, z_halo)
@@ -798,7 +801,8 @@
     for comp in range(3):
         up, down = (flow[comp, bx - 1], flow[comp, 0])
         v_first[comp] = jnp.where(flip_x, down, up)
-        v_second[comp] = jnp.where(flip_x, up, down)
+        if comp > 0:
+            v_second[comp - 1] = jnp.where(flip_x, up, down)
     for slot in range(5):
         below[slot] = jnp.where(flip_x, x_first[slot], x_second[slot])
         above[slot] = jnp.where(flip_x, x_second[slot], x_first[slot])
@@ -1072,7 +1076,7 @@
     )(pops, stretch, flow, z_first, *y_first)
     outer_post, outer_shift, z_out, x_one, x_two, y_one, y_two = call(
         collide_outer,
-        [(19, *ends), (3, *ends), columns, (5, *face), (5, *face), rows, rows],
+        [(19, *ends), (3, *ends), columns, (5, *face), (6, *face), rows, rows],
         scratch=[(4, *face), (4, *face)] + sides_y + [box],
         cost=(150 * cells, 150 * cells),
     )(pops, stretch, flags, flow, *first_x, *y_first, z_first, inner_post)
@@ -1081,7 +1085,7 @@
     post_x = swapped(x_one, x_two, "gx")
     edges = (4 * (bz // lanes) + columns[0], lanes)
     x_one, x_two, corner = call(
-        lambda *refs: forward_edges(*refs, bx=bx), [edges, edges, columns], cost=(4 * 10**9, 0)
+        lambda *refs: forward_edges(*refs, bx=bx), [edges, edges, columns], cost=(135 * 10**7, 0)
     )(z_post, *post_y)
     corners = swapped(corner, corner, "gy")
     edges_x = swapped(x_one, x_two, "gx")
@@ -1120,7 +1124,7 @@
         [
             (5, *ends),
             (3, *face),
-            (3, *face),
+            (2, *face),
             ends,
             (bx + 2, *face),
             (8, bz),
@@ -1161,14 +1165,14 @@
     new_stretch, outer_done = call(
         restretch_outer,
         [(6, *box), mark],
-        specs=[pl.BlockSpec()] * 7 + [remote],
+        specs=[pl.BlockSpec()] * 8 + [remote],
         out_specs=[remote, pl.BlockSpec()],
         scratch=[(6, *ends), (3, *face), (3, *face)]
         + sides_y
         + [pltpu.SemaphoreType.DMA((2,))],
         cost=(80 * cells, 40 * cells),
-        aliases={7: 0},
-    )(stretch, flow, *flow_x, *post_y, z_post, new_stretch)
+        aliases={8: 0},
+    )(stretch, flow, *flow_x, post_x[1], *post_y, z_post, new_stretch)
     (new_mass,) = call(add_all, [box])(
         inner_settled, outer_settled, spread, z_last, *last_y, *last_corners, *last_x[::-1], outer_done
     )

time: 41.2 us -> 43.1 us (1.046); the launches traced: 40.9 us -> 42.4 us
  starting transfers between devices: 23.5 us -> 24.3 us
  waiting for transfers between devices: 4.13 us -> 4.78 us
    ppermute x10, starting transfers between devices: 15.7 us -> 13.9 us  [swapped(): lax.ppermute(second, axis, behind)]
    ppermute x10, starting transfers between devices: 4.19 us -> 5.78 us  [swapped(): lax.ppermute(first, axis, ahead)]
    ppermute x3, starting transfers between devices: 3.6 us -> 4.61 us  [both_ways(): lax.ppermute(rows, 'gz', [(i, (i + 1) % devices) for i in range(devices)])]
    ppermute x3, waiting for transfers between devices: 0.78 us -> 1.67 us  [both_ways(): lax.ppermute(rows, 'gz', [(i, (i + 1) % devices) for i in range(devices)])]
    ppermute x10, waiting for transfers between devices: 0.56 us -> 0.03 us  [swapped(): lax.ppermute(first, axis, ahead)]
  transfers between devices with their start and end apart: 23 -> 23, of which waited for: 6 -> 7; matrix products, arithmetic and copies ran while one was open for 0% -> 0% of each run, Pallas kernels for 21% -> 20%
where the time goes in v8:
time: 43.1 us; the launch traced here: 42.4 us
  starting transfers between devices  24.3 us (56%)
  Pallas kernels  12.5 us (29%)
  waiting for transfers between devices  4.78 us (11%)
  between operations  0.79 us (2%)
    ppermute x10, starting transfers between devices, swapped(): lax.ppermute(second, axis, behind)  13.9 us
    ppermute x10, starting transfers between devices, swapped(): lax.ppermute(first, axis, ahead)  5.78 us
    ppermute x3, starting transfers between devices, both_ways(): lax.ppermute(rows, 'gz', [(i, (i + 1) % devices) for i in range(devices)])  4.61 us
    ppermute x10, waiting for transfers between devices, swapped(): lax.ppermute(second, axis, behind)  3.09 us
    pallas_call x1, Pallas kernels, shards(): call(moments, [(19, *box), (5, *box)], specs=[remote], scratch=[pltpu.Sem...  1.74 us
    pallas_call x1, Pallas kernels, shards(): call(store, [(19, *box)], out_specs=[remote], scratch=[pltpu.SemaphoreTyp...  1.7 us
    ppermute x3, waiting for transfers between devices, both_ways(): lax.ppermute(rows, 'gz', [(i, (i + 1) % devices) for i in range(devices)])  1.67 us
    pallas_call x1, Pallas kernels, shards(): call(first_faces, [(6, *box), jax.ShapeDtypeStruct(box, jnp.int32), (8, b...  1.38 us
  transfers between devices with their start and end apart: 23, of which 7 were waited for; matrix products, arithmetic and copies ran while one was open for 0% of the time, Pallas kernels for 20%

profile of v8, /device:TPU:0, one launch (start us, length us, event | category | flops | bytes accessed | tf_op | source)
XLA Modules:
  0.0 42.4 jit_solution(7870243067800469060)
XLA Ops:
  0.6 1.4 %shard_map.95 = (f32[6,4,32,256]{3,2,1,0:T(8,128)S(1)}, s32[4,32,256]{2,1,0:T(8,128)S(1)}, f32[8,128]{1,0:T(8,128)S(1)}, f32[16,256]{1,0:T(8,128)S(1)}, f32[16,2...) custom-call(f32[6,4,32,256]{3,2,1,0:T(8,128)} %stretch_in.1, s32[4,32,256]{2,1,0:T(8,128)} %flags_in.1), custom_call_target="tpu_custom_call" | custom-call | flops 327680 | bytes 1966080 | tf_op jit(solution)/shard_map/pallas_call | solution.py:1032
  2.0 3.1 %collective-permute-start.3 = (f32[4,32,256]{2,1,0:T(8,128)S(1)}, f32[4,32,256]{2,1,0:T(8,128)S(1)}, u32[]{:S(2)}, u32[]{:S(2)}) collective-permute-start(f32[4,32,256]{2,1,0:T(8,128)S(1)} %get-tuple-element.57), channel_id=1, source_target_pairs={{0,8},{8,0},{16,24},{24,16},{1,9},{9,1},{17,25},{25,17},{2,10},{10... | collective-permute-start | bytes 393224 | tf_op jit(solution)/shard_map/ppermute | solution.py:988
  5.1 2.5 %collective-permute-start.4 = (f32[4,32,256]{2,1,0:T(8,128)S(1)}, f32[4,32,256]{2,1,0:T(8,128)S(1)}, u32[]{:S(2)}, u32[]{:S(2)}) collective-permute-start(f32[4,32,256]{2,1,0:T(8,128)S(1)} %get-tuple-element.58), channel_id=1, source_target_pairs={{0,24},{8,16},{16,8},{24,0},{1,25},{9,17},{17,9},{25,1},{2,26},{10... | collective-permute-start | bytes 393224 | tf_op jit(solution)/shard_map/ppermute | solution.py:988
  7.6 0.0 collective-permute-start.1
  7.6 1.6 %collective-permute-start.2 = (f32[16,256]{1,0:T(8,128)S(1)}, f32[16,256]{1,0:T(8,128)S(1)}, u32[]{:S(2)}, u32[]{:S(2)}) collective-permute-start(f32[16,256]{1,0:T(8,128)S(1)} %get-tuple-element.54), channel_id=1, source_target_pairs={{0,6},{2,4},{4,2},{6,0},{1,7},{3,5},{5,3},{7,1},{8,14},{10,12},{12... | collective-permute-start | bytes 49160 | tf_op jit(solution)/shard_map/ppermute | solution.py:988
  9.2 1.5 %collective-permute-start = (f32[8,128]{1,0:T(8,128)S(1)}, f32[8,128]{1,0:T(8,128)S(1)}, u32[]{:S(2)}, u32[]{:S(2)}) collective-permute-start(f32[8,128]{1,0:T(8,128)S(1)} %get-tuple-element.52), channel_id=1, source_target_pairs={{0,1},{1,0},{2,3},{3,2},{4,5},{5,4},{6,7},{7,6},{8,9},{9,8},{10,11... | collective-permute-start | bytes 12296 | tf_op jit(solution)/shard_map/ppermute | solution.py:993
  10.7 1.7 %shard_map.94 = (f32[19,4,32,256]{3,2,1,0:T(8,128)S(1)}, f32[5,4,32,256]{3,2,1,0:T(8,128)S(1)}) custom-call(f32[19,4,32,256]{3,2,1,0:T(8,128)} %pops_in.1), custom_call_target="tpu_custom_call" | custom-call | flops 1966080 | bytes 4915200 | tf_op jit(solution)/shard_map/pallas_call | solution.py:1060
  12.5 0.3 collective-permute-done.z_rows
  12.8 0.0 collective-permute-done.1.y_first
  12.8 0.0 collective-permute-done.2.y_second
  12.8 0.8 %shard_map.96 = (f32[19,2,32,256]{3,2,1,0:T(8,128)S(1)}, f32[3,2,32,256]{3,2,1,0:T(8,128)S(1)}) custom-call(f32[19,4,32,256]{3,2,1,0:T(8,128)S(1)} %get-tuple-element.49.pops, f32[6,4,32,256]{3,2,1,0:T(8,128)S(1)} %get-tuple-element.50.stretch, f32[5,4,32,256]{3,2,1,0:T(8,128)S(1)} %get-tuple-element.51.flow, f32[8,128]{1,0:T(8,128)S(1)} %collective-permute-done.z_rows, ...), custom_call_target="tpu_custom_call" | custom-call | flops 4915200 | bytes 4915200 | tf_op jit(solution)/shard_map/pallas_call | solution.py:1071
  13.6 0.0 collective-permute-done.3.x_first.gas_first
  13.6 0.1 collective-permute-done.4.x_second.gas_second
  13.7 1.0 %shard_map.97 = (f32[19,2,32,256]{3,2,1,0:T(8,128)S(1)}, f32[3,2,32,256]{3,2,1,0:T(8,128)S(1)}, f32[24,128]{1,0:T(8,128)S(1)}, f32[5,32,256]{2,1,0:T(8,128)S(1)}...) custom-call(f32[19,4,32,256]{3,2,1,0:T(8,128)S(1)} %get-tuple-element.49.pops, ...), custom_call_target="tpu_custom_call" | custom-call | flops 4915200 | bytes 4915200 | tf_op jit(solution)/shard_map/pallas_call | solution.py:1077
  14.7 1.5 %collective-permute-start.11 = (f32[6,32,256]{2,1,0:T(8,128)S(1)}, f32[6,32,256]{2,1,0:T(8,128)S(1)}, u32[]{:S(2)}, u32[]{:S(2)}) collective-permute-start(f32[6,32,256]{2,1,0:T(8,128)S(1)} %get-tuple-element.75), channel_id=1, source_target_pairs={{0,24},{8,16},{16,8},{24,0},{1,25},{9,17},{17,9},{25,1},{2,26},{10... | collective-permute-start | bytes 589832 | tf_op jit(solution)/shard_map/ppermute | solution.py:988
  16.2 0.0 collective-permute-start.5
  16.2 1.6 %collective-permute-start.6 = (f32[40,256]{1,0:T(8,128)S(1)}, f32[40,256]{1,0:T(8,128)S(1)}, u32[]{:S(2)}, u32[]{:S(2)}) collective-permute-start(f32[40,256]{1,0:T(8,128)S(1)} %get-tuple-element.63), channel_id=1, source_target_pairs={{0,6},{2,4},{4,2},{6,0},{1,7},{3,5},{5,3},{7,1},{8,14},{10,12},{12... | collective-permute-start | bytes 122888 | tf_op jit(solution)/shard_map/ppermute | solution.py:988
  17.8 1.5 %collective-permute-start.7 = (f32[24,128]{1,0:T(8,128)S(1)}, f32[24,128]{1,0:T(8,128)S(1)}, u32[]{:S(2)}, u32[]{:S(2)}) collective-permute-start(f32[24,128]{1,0:T(8,128)S(1)} %get-tuple-element.64), channel_id=1, source_target_pairs={{0,1},{1,0},{2,3},{3,2},{4,5},{5,4},{6,7},{7,6},{8,9},{9,8},{10,11... | collective-permute-start | bytes 36872 | tf_op jit(solution)/shard_map/ppermute | solution.py:993
  19.4 0.8 %collective-permute-start.10 = (f32[5,32,256]{2,1,0:T(8,128)S(1)}, f32[5,32,256]{2,1,0:T(8,128)S(1)}, u32[]{:S(2)}, u32[]{:S(2)}) collective-permute-start(f32[5,32,256]{2,1,0:T(8,128)S(1)} %get-tuple-element.74), channel_id=1, source_target_pairs={{0,8},{8,0},{16,24},{24,16},{1,9},{9,1},{17,25},{25,17},{2,10},{10... | collective-permute-start | bytes 491528 | tf_op jit(solution)/shard_map/ppermute | solution.py:988
  20.2 1.3 %collective-permute-done.7.z_rows.refs_0_ = f32[24,128]{1,0:T(8,128)S(1)} collective-permute-done((f32[24,128]{1,0:T(8,128)S(1)}, f32[24,128]{1,0:T(8,128)S(1)}, u32[]{:S(2)}, u32[]{:S(2)}) %collective-permute-start.7) | collective-permute-done | bytes 12320 | tf_op jit(solution)/shard_map/ppermute | solution.py:993
  21.5 0.0 collective-permute-done.5.y_first.refs_1_
  21.5 0.0 collective-permute-done.6.y_second.refs_2_
  21.6 0.0 copy-start
  21.6 0.1 collective-permute-start.8
  21.7 0.9 %collective-permute-start.12 = (f32[32,128]{1,0:T(8,128)S(1)}, f32[32,128]{1,0:T(8,128)S(1)}, u32[]{:S(2)}, u32[]{:S(2)}) collective-permute-start(f32[32,128]{1,0:T(8,128)S(1)} %get-tuple-element.76), channel_id=1, source_target_pairs={{0,8},{8,0},{16,24},{24,16},{1,9},{9,1},{17,25},{25,17},{2,10},{10... | collective-permute-start | bytes 49160 | tf_op jit(solution)/shard_map/ppermute | solution.py:988
  22.6 1.6 %collective-permute-start.13 = (f32[32,128]{1,0:T(8,128)S(1)}, f32[32,128]{1,0:T(8,128)S(1)}, u32[]{:S(2)}, u32[]{:S(2)}) collective-permute-start(f32[32,128]{1,0:T(8,128)S(1)} %get-tuple-element.77), channel_id=1, source_target_pairs={{0,24},{8,16},{16,8},{24,0},{1,25},{9,17},{17,9},{25,1},{2,26},{10... | collective-permute-start | bytes 49160 | tf_op jit(solution)/shard_map/ppermute | solution.py:988
  24.1 0.0 collective-permute-done.8.corner_first
  24.1 0.2 collective-permute-start.9
  24.4 0.0 copy-done.1
  24.4 0.0 copy-done.2
  24.4 0.0 copy-done.3
  24.4 0.3 shard_map.99
  24.7 1.2 %shard_map.102 = (f32[6,4,32,256]{3,2,1,0:T(8,128)}, f32[8,128]{1,0:T(8,128)S(1)}) custom-call(f32[6,4,32,256]{3,2,1,0:T(8,128)S(1)} %get-tuple-element.50.stretch, f32[5,4,32,256]{3,2,1,0:T(8,128)S(1)} %get-tuple-element.51.flow, f32[40,256]{1,0:T(8,128)S(1)} %collective-permute-done.5.y_first.refs_1_, ...), custom_call_target="tpu_custom_call" | custom-call | flops 2621440 | bytes 1310720 | tf_op jit(solution)/shard_map/pallas_call | solution.py:1115
  25.9 0.9 %shard_map.98 = (f32[15,2,32,256]{3,2,1,0:T(8,128)S(1)}, f32[15,2,32,256]{3,2,1,0:T(8,128)S(1)}, f32[4,32,256]{2,1,0:T(8,128)S(1)}, f32[4,32,256]{2,1,0:T(8,128)S(1)}) custom-call(f32[19,2,32,256]{3,2,1,0:T(8,128)S(1)} %get-tuple-element.55.inner.inner_post, f32[19,2,32,256]{3,2,1,0:T(8,128)S(1)} %get-tuple-element.59.outer_post.post, ...), custom_call_target="tpu_custom_call" | custom-call | flops 11468800 | bytes 6553600 | tf_op jit(solution)/shard_map/pallas_call | solution.py:1095
  26.9 0.4 collective-permute-done.9.corner_second
  27.3 0.0 copy-done
  27.3 0.6 %shard_map.101 = (f32[4,2,32,256]{3,2,1,0:T(8,128)S(1)}, f32[4,2,32,256]{3,2,1,0:T(8,128)S(1)}, f32[2,32,256]{2,1,0:T(8,128)S(1)}, f32[2,32,256]{2,1,0:T(8,128)S...) custom-call(f32[19,2,32,256]{3,2,1,0:T(8,128)S(1)} %get-tuple-element.55.inner.inner_post, ...), custom_call_target="tpu_custom_call" | custom-call | flops 3276800 | bytes 1966080 | tf_op jit(solution)/shard_map/pallas_call | solution.py:1109
  27.9 0.0 collective-permute-done.12.edges_first
  27.9 0.2 collective-permute-done.13.edges_second
  28.1 0.0 collective-permute-done.10.x_first
  28.1 0.0 collective-permute-done.11.x_second.post_second
  28.1 0.8 %shard_map.103 = (f32[5,2,32,256]{3,2,1,0:T(8,128)S(1)}, f32[3,32,256]{2,1,0:T(8,128)S(1)}, f32[2,32,256]{2,1,0:T(8,128)S(1)}, f32[2,32,256]{2,1,0:T(8,128)S(1)}...) custom-call(f32[19,2,32,256]{3,2,1,0:T(8,128)S(1)} %get-tuple-element.59.outer, ...), custom_call_target="tpu_custom_call" | custom-call | flops 4915200 | bytes 3276800 | tf_op jit(solution)/shard_map/pallas_call | solution.py:1122
  28.9 1.6 %collective-permute-start.16 = (f32[16,128]{1,0:T(8,128)S(1)}, f32[16,128]{1,0:T(8,128)S(1)}, u32[]{:S(2)}, u32[]{:S(2)}) collective-permute-start(f32[16,128]{1,0:T(8,128)S(1)} %get-tuple-element.89), channel_id=1, source_target_pairs={{0,1},{1,0},{2,3},{3,2},{4,5},{5,4},{6,7},{7,6},{8,9},{9,8},{10,11... | collective-permute-start | bytes 24584 | tf_op jit(solution)/shard_map/ppermute | solution.py:993
  30.4 0.0 collective-permute-start.17
  30.4 1.0 %collective-permute-start.18 = (f32[8,256]{1,0:T(8,128)S(1)}, f32[8,256]{1,0:T(8,128)S(1)}, u32[]{:S(2)}, u32[]{:S(2)}) collective-permute-start(f32[8,256]{1,0:T(8,128)S(1)} %get-tuple-element.91), channel_id=1, source_target_pairs={{0,6},{2,4},{4,2},{6,0},{1,7},{3,5},{5,3},{7,1},{8,14},{10,12},{12... | collective-permute-start | bytes 24584 | tf_op jit(solution)/shard_map/ppermute | solution.py:988
  31.4 0.9 %collective-permute-start.14 = (f32[3,32,256]{2,1,0:T(8,128)S(1)}, f32[3,32,256]{2,1,0:T(8,128)S(1)}, u32[]{:S(2)}, u32[]{:S(2)}) collective-permute-start(f32[3,32,256]{2,1,0:T(8,128)S(1)} %get-tuple-element.82), channel_id=1, source_target_pairs={{0,8},{8,0},{16,24},{24,16},{1,9},{9,1},{17,25},{25,17},{2,10},{10... | collective-permute-start | bytes 294920 | tf_op jit(solution)/shard_map/ppermute | solution.py:988
  32.3 1.5 %collective-permute-start.15 = (f32[2,32,256]{2,1,0:T(8,128)S(1)}, f32[2,32,256]{2,1,0:T(8,128)S(1)}, u32[]{:S(2)}, u32[]{:S(2)}) collective-permute-start(f32[2,32,256]{2,1,0:T(8,128)S(1)} %get-tuple-element.83), channel_id=1, source_target_pairs={{0,24},{8,16},{16,8},{24,0},{1,25},{9,17},{17,9},{25,1},{2,26},{10... | collective-permute-start | bytes 196616 | tf_op jit(solution)/shard_map/ppermute | solution.py:988
  33.8 0.0 collective-permute-done.16.z_rows
  33.8 0.0 collective-permute-done.17.y_first
  33.8 0.0 collective-permute-done.18.y_second
  33.8 0.2 shard_map.106
  34.0 2.4 %collective-permute-start.21 = (f32[32,256]{1,0:T(8,128)S(1)}, f32[32,256]{1,0:T(8,128)S(1)}, u32[]{:S(2)}, u32[]{:S(2)}) collective-permute-start(f32[32,256]{1,0:T(8,128)S(1)} %get-tuple-element.92), channel_id=1, source_target_pairs={{0,24},{8,16},{16,8},{24,0},{1,25},{9,17},{17,9},{25,1},{2,26},{10... | collective-permute-start | bytes 98312 | tf_op jit(solution)/shard_map/ppermute | solution.py:988
  36.4 0.0 collective-permute-start.22
  36.4 0.0 collective-permute-start.19
  36.4 2.0 %collective-permute-done.15.x_second = f32[2,32,256]{2,1,0:T(8,128)S(1)} collective-permute-done((f32[2,32,256]{2,1,0:T(8,128)S(1)}, f32[2,32,256]{2,1,0:T(8,128)S(1)}, u32[]{:S(2)}, u32[]{:S(2)}) %collective-permute-start.15) | collective-permute-done | bytes 65568 | tf_op jit(solution)/shard_map/ppermute | solution.py:988
  38.4 0.0 collective-permute-start.20
  38.4 1.7 %shard_map.104 = f32[19,4,32,256]{3,2,1,0:T(8,128)} custom-call(f32[15,2,32,256]{3,2,1,0:T(8,128)S(1)} %get-tuple-element.65.inner, f32[15,2,32,256]{3,2,1,0:T(8,128)S(1)} %get-tuple-element.66.outer, f32[4,2,32,256]{3,2,1,0:T(8,128)S(1)} %get-tuple-element.70.inner_slanted, f32[4,2,32,256]{3,2,1,0:T(8,128)S(1)} %get-tuple-element.71.outer_slanted, ...), custom_call_target="tpu_custom_call" | custom-call | bytes 5242880 | tf_op jit(solution)/shard_map/pallas_call | solution.py:1158
  40.1 0.0 collective-permute-done.14.x_first
  40.2 1.1 %shard_map.105 = (f32[6,4,32,256]{3,2,1,0:T(8,128)}, f32[8,128]{1,0:T(8,128)S(1)}) custom-call(f32[6,4,32,256]{3,2,1,0:T(8,128)S(1)} %get-tuple-element.50.stretch, f32[5,4,32,256]{3,2,1,0:T(8,128)S(1)} %get-tuple-element.51.flow, f32[3,32,256]{2,1,0:T(8,128)S(1)} %collective-permute-done.14.x_first, ...), custom_call_target="tpu_custom_call", output_to_operand_aliasing={{0}: (8, {})} | custom-call | flops 2621440 | bytes 1310720 | tf_op jit(solution)/shard_map/pallas_call | solution.py:1165
  41.2 0.0 collective-permute-done.19.corner_first
  41.2 0.3 collective-permute-done.20.corner_second
  41.5 0.0 collective-permute-done.21.x_second
  41.5 0.0 collective-permute-done.22.x_first
  41.5 0.9 %shard_map.107 = f32[4,32,256]{2,1,0:T(8,128)} custom-call(f32[2,32,256]{2,1,0:T(8,128)S(1)} %get-tuple-element.86.inner_settled, f32[2,32,256]{2,1,0:T(8,128)S(1)} %get-tuple-element.87.outer_settled, f32[6,32,256]{2,1,0:T(8,128)S(1)} %get-tuple-element.88.spread, f32[16,128]{1,0:T(8,128)S(1)} %collective-permute-done.16.z_rows, ...), custom_call_target="tpu_custom_call" | custom-call | tf_op jit(solution)/shard_map/pallas_call | solution.py:1176
  (4 shorter events, 0.0 us)
Async XLA Ops:
  2.0 11.5 %collective-permute-start.3 = (f32[4,32,256]{2,1,0:T(8,128)S(1)}, f32[4,32,256]{2,1,0:T(8,128)S(1)}, u32[]{:S(2)}, u32[]{:S(2)}) collective-permute-start(f32[4,32,256]{2,1,0:T(8,128)S(1)} %get-tuple-element.57), channel_id=1, source_target_pairs={{0,8},{8,0},{16,24},{24,16},{1,9},{9,1},{17,25},{25,17},{2,10},{10... | collective-permute-start | bytes 393224 | tf_op jit(solution)/shard_map/ppermute | solution.py:988
  5.1 8.6 %collective-permute-start.4 = (f32[4,32,256]{2,1,0:T(8,128)S(1)}, f32[4,32,256]{2,1,0:T(8,128)S(1)}, u32[]{:S(2)}, u32[]{:S(2)}) collective-permute-start(f32[4,32,256]{2,1,0:T(8,128)S(1)} %get-tuple-element.58), channel_id=1, source_target_pairs={{0,24},{8,16},{16,8},{24,0},{1,25},{9,17},{17,9},{25,1},{2,26},{10... | collective-permute-start | bytes 393224 | tf_op jit(solution)/shard_map/ppermute | solution.py:988
  7.6 5.2 %collective-permute-start.1 = (f32[16,256]{1,0:T(8,128)S(1)}, f32[16,256]{1,0:T(8,128)S(1)}, u32[]{:S(2)}, u32[]{:S(2)}) collective-permute-start(f32[16,256]{1,0:T(8,128)S(1)} %get-tuple-element.53), channel_id=1, source_target_pairs={{0,2},{2,0},{4,6},{6,4},{1,3},{3,1},{5,7},{7,5},{8,10},{10,8},{12,... | collective-permute-start | bytes 49160 | tf_op jit(solution)/shard_map/ppermute | solution.py:988
  7.6 5.2 %collective-permute-start.2 = (f32[16,256]{1,0:T(8,128)S(1)}, f32[16,256]{1,0:T(8,128)S(1)}, u32[]{:S(2)}, u32[]{:S(2)}) collective-permute-start(f32[16,256]{1,0:T(8,128)S(1)} %get-tuple-element.54), channel_id=1, source_target_pairs={{0,6},{2,4},{4,2},{6,0},{1,7},{3,5},{5,3},{7,1},{8,14},{10,12},{12... | collective-permute-start | bytes 49160 | tf_op jit(solution)/shard_map/ppermute | solution.py:988
  9.2 3.6 %collective-permute-start = (f32[8,128]{1,0:T(8,128)S(1)}, f32[8,128]{1,0:T(8,128)S(1)}, u32[]{:S(2)}, u32[]{:S(2)}) collective-permute-start(f32[8,128]{1,0:T(8,128)S(1)} %get-tuple-element.52), channel_id=1, source_target_pairs={{0,1},{1,0},{2,3},{3,2},{4,5},{5,4},{6,7},{7,6},{8,9},{9,8},{10,11... | collective-permute-start | bytes 12296 | tf_op jit(solution)/shard_map/ppermute | solution.py:993
  14.7 13.4 %collective-permute-start.11 = (f32[6,32,256]{2,1,0:T(8,128)S(1)}, f32[6,32,256]{2,1,0:T(8,128)S(1)}, u32[]{:S(2)}, u32[]{:S(2)}) collective-permute-start(f32[6,32,256]{2,1,0:T(8,128)S(1)} %get-tuple-element.75), channel_id=1, source_target_pairs={{0,24},{8,16},{16,8},{24,0},{1,25},{9,17},{17,9},{25,1},{2,26},{10... | collective-permute-start | bytes 589832 | tf_op jit(solution)/shard_map/ppermute | solution.py:988
  16.2 5.3 %collective-permute-start.5 = (f32[40,256]{1,0:T(8,128)S(1)}, f32[40,256]{1,0:T(8,128)S(1)}, u32[]{:S(2)}, u32[]{:S(2)}) collective-permute-start(f32[40,256]{1,0:T(8,128)S(1)} %get-tuple-element.62), channel_id=1, source_target_pairs={{0,2},{2,0},{4,6},{6,4},{1,3},{3,1},{5,7},{7,5},{8,10},{10,8},{12,... | collective-permute-start | bytes 122888 | tf_op jit(solution)/shard_map/ppermute | solution.py:988
  16.2 5.3 %collective-permute-start.6 = (f32[40,256]{1,0:T(8,128)S(1)}, f32[40,256]{1,0:T(8,128)S(1)}, u32[]{:S(2)}, u32[]{:S(2)}) collective-permute-start(f32[40,256]{1,0:T(8,128)S(1)} %get-tuple-element.63), channel_id=1, source_target_pairs={{0,6},{2,4},{4,2},{6,0},{1,7},{3,5},{5,3},{7,1},{8,14},{10,12},{12... | collective-permute-start | bytes 122888 | tf_op jit(solution)/shard_map/ppermute | solution.py:988
  17.8 3.7 %collective-permute-start.7 = (f32[24,128]{1,0:T(8,128)S(1)}, f32[24,128]{1,0:T(8,128)S(1)}, u32[]{:S(2)}, u32[]{:S(2)}) collective-permute-start(f32[24,128]{1,0:T(8,128)S(1)} %get-tuple-element.64), channel_id=1, source_target_pairs={{0,1},{1,0},{2,3},{3,2},{4,5},{5,4},{6,7},{7,6},{8,9},{9,8},{10,11... | collective-permute-start | bytes 36872 | tf_op jit(solution)/shard_map/ppermute | solution.py:993
  19.3 5.0 %copy-start.1 = (s32[1024]{0:T(1024)S(1)}, s32[1024]{0:T(1024)}, u32[]{:S(2)}) copy-start(s32[1024]{0:T(1024)} %param.11) | copy-start | bytes 12292
  19.4 5.0 %copy-start.2 = (s32[1024]{0:T(1024)S(1)}, s32[1024]{0:T(1024)}, u32[]{:S(2)}) copy-start(s32[1024]{0:T(1024)} %param.12) | copy-start | bytes 12292
  19.4 5.0 %copy-start.3 = (s32[1024]{0:T(1024)S(1)}, s32[1024]{0:T(1024)}, u32[]{:S(2)}) copy-start(s32[1024]{0:T(1024)} %param.13) | copy-start | bytes 12292
  19.4 8.7 %collective-permute-start.10 = (f32[5,32,256]{2,1,0:T(8,128)S(1)}, f32[5,32,256]{2,1,0:T(8,128)S(1)}, u32[]{:S(2)}, u32[]{:S(2)}) collective-permute-start(f32[5,32,256]{2,1,0:T(8,128)S(1)} %get-tuple-element.74), channel_id=1, source_target_pairs={{0,8},{8,0},{16,24},{24,16},{1,9},{9,1},{17,25},{25,17},{2,10},{10... | collective-permute-start | bytes 491528 | tf_op jit(solution)/shard_map/ppermute | solution.py:988
  21.6 5.7 %copy-start = (f32[4,32,256]{2,1,0:T(8,128)S(1)}, f32[4,32,256]{2,1,0:T(8,128)}, u32[]{:S(2)}) copy-start(f32[4,32,256]{2,1,0:T(8,128)} %mass.3) | copy-start | bytes 393220
  21.6 2.6 %collective-permute-start.8 = (f32[24,128]{1,0:T(8,128)S(1)}, f32[24,128]{1,0:T(8,128)S(1)}, u32[]{:S(2)}, u32[]{:S(2)}) collective-permute-start(f32[24,128]{1,0:T(8,128)S(1)} %get-tuple-element.67), channel_id=1, source_target_pairs={{0,2},{2,0},{4,6},{6,4},{1,3},{3,1},{5,7},{7,5},{8,10},{10,8},{12,... | collective-permute-start | bytes 36872 | tf_op jit(solution)/shard_map/ppermute | solution.py:988
  21.7 6.2 %collective-permute-start.12 = (f32[32,128]{1,0:T(8,128)S(1)}, f32[32,128]{1,0:T(8,128)S(1)}, u32[]{:S(2)}, u32[]{:S(2)}) collective-permute-start(f32[32,128]{1,0:T(8,128)S(1)} %get-tuple-element.76), channel_id=1, source_target_pairs={{0,8},{8,0},{16,24},{24,16},{1,9},{9,1},{17,25},{25,17},{2,10},{10... | collective-permute-start | bytes 49160 | tf_op jit(solution)/shard_map/ppermute | solution.py:988
  22.6 5.5 %collective-permute-start.13 = (f32[32,128]{1,0:T(8,128)S(1)}, f32[32,128]{1,0:T(8,128)S(1)}, u32[]{:S(2)}, u32[]{:S(2)}) collective-permute-start(f32[32,128]{1,0:T(8,128)S(1)} %get-tuple-element.77), channel_id=1, source_target_pairs={{0,24},{8,16},{16,8},{24,0},{1,25},{9,17},{17,9},{25,1},{2,26},{10... | collective-permute-start | bytes 49160 | tf_op jit(solution)/shard_map/ppermute | solution.py:988
  24.1 3.1 %collective-permute-start.9 = (f32[24,128]{1,0:T(8,128)S(1)}, f32[24,128]{1,0:T(8,128)S(1)}, u32[]{:S(2)}, u32[]{:S(2)}) collective-permute-start(f32[24,128]{1,0:T(8,128)S(1)} %get-tuple-element.67), channel_id=1, source_target_pairs={{0,6},{2,4},{4,2},{6,0},{1,7},{3,5},{5,3},{7,1},{8,14},{10,12},{12... | collective-permute-start | bytes 36872 | tf_op jit(solution)/shard_map/ppermute | solution.py:988
  28.9 4.9 %collective-permute-start.16 = (f32[16,128]{1,0:T(8,128)S(1)}, f32[16,128]{1,0:T(8,128)S(1)}, u32[]{:S(2)}, u32[]{:S(2)}) collective-permute-start(f32[16,128]{1,0:T(8,128)S(1)} %get-tuple-element.89), channel_id=1, source_target_pairs={{0,1},{1,0},{2,3},{3,2},{4,5},{5,4},{6,7},{7,6},{8,9},{9,8},{10,11... | collective-permute-start | bytes 24584 | tf_op jit(solution)/shard_map/ppermute | solution.py:993
  30.4 3.4 %collective-permute-start.17 = (f32[8,256]{1,0:T(8,128)S(1)}, f32[8,256]{1,0:T(8,128)S(1)}, u32[]{:S(2)}, u32[]{:S(2)}) collective-permute-start(f32[8,256]{1,0:T(8,128)S(1)} %get-tuple-element.90), channel_id=1, source_target_pairs={{0,2},{2,0},{4,6},{6,4},{1,3},{3,1},{5,7},{7,5},{8,10},{10,8},{12,... | collective-permute-start | bytes 24584 | tf_op jit(solution)/shard_map/ppermute | solution.py:988
  30.4 3.4 %collective-permute-start.18 = (f32[8,256]{1,0:T(8,128)S(1)}, f32[8,256]{1,0:T(8,128)S(1)}, u32[]{:S(2)}, u32[]{:S(2)}) collective-permute-start(f32[8,256]{1,0:T(8,128)S(1)} %get-tuple-element.91), channel_id=1, source_target_pairs={{0,6},{2,4},{4,2},{6,0},{1,7},{3,5},{5,3},{7,1},{8,14},{10,12},{12... | collective-permute-start | bytes 24584 | tf_op jit(solution)/shard_map/ppermute | solution.py:988
  31.4 8.7 %collective-permute-start.14 = (f32[3,32,256]{2,1,0:T(8,128)S(1)}, f32[3,32,256]{2,1,0:T(8,128)S(1)}, u32[]{:S(2)}, u32[]{:S(2)}) collective-permute-start(f32[3,32,256]{2,1,0:T(8,128)S(1)} %get-tuple-element.82), channel_id=1, source_target_pairs={{0,8},{8,0},{16,24},{24,16},{1,9},{9,1},{17,25},{25,17},{2,10},{10... | collective-permute-start | bytes 294920 | tf_op jit(solution)/shard_map/ppermute | solution.py:988
  32.3 6.1 %collective-permute-start.15 = (f32[2,32,256]{2,1,0:T(8,128)S(1)}, f32[2,32,256]{2,1,0:T(8,128)S(1)}, u32[]{:S(2)}, u32[]{:S(2)}) collective-permute-start(f32[2,32,256]{2,1,0:T(8,128)S(1)} %get-tuple-element.83), channel_id=1, source_target_pairs={{0,24},{8,16},{16,8},{24,0},{1,25},{9,17},{17,9},{25,1},{2,26},{10... | collective-permute-start | bytes 196616 | tf_op jit(solution)/shard_map/ppermute | solution.py:988
  34.0 7.5 %collective-permute-start.21 = (f32[32,256]{1,0:T(8,128)S(1)}, f32[32,256]{1,0:T(8,128)S(1)}, u32[]{:S(2)}, u32[]{:S(2)}) collective-permute-start(f32[32,256]{1,0:T(8,128)S(1)} %get-tuple-element.92), channel_id=1, source_target_pairs={{0,24},{8,16},{16,8},{24,0},{1,25},{9,17},{17,9},{25,1},{2,26},{10... | collective-permute-start | bytes 98312 | tf_op jit(solution)/shard_map/ppermute | solution.py:988
  36.4 5.1 %collective-permute-start.22 = (f32[32,256]{1,0:T(8,128)S(1)}, f32[32,256]{1,0:T(8,128)S(1)}, u32[]{:S(2)}, u32[]{:S(2)}) collective-permute-start(f32[32,256]{1,0:T(8,128)S(1)} %get-tuple-element.93), channel_id=1, source_target_pairs={{0,8},{8,0},{16,24},{24,16},{1,9},{9,1},{17,25},{25,17},{2,10},{10... | collective-permute-start | bytes 98312 | tf_op jit(solution)/shard_map/ppermute | solution.py:988
  36.4 4.8 %collective-permute-start.19 = (f32[16,128]{1,0:T(8,128)S(1)}, f32[16,128]{1,0:T(8,128)S(1)}, u32[]{:S(2)}, u32[]{:S(2)}) collective-permute-start(f32[16,128]{1,0:T(8,128)S(1)} %collective-permute-done.16.z_rows), channel_id=1, source_target_pairs={{0,2},{2,0},{4,6},{6,4},{1,3},{3,1},{5,7},{7,5},{8,10},{10,8},{12,... | collective-permute-start | bytes 24584 | tf_op jit(solution)/shard_map/ppermute | solution.py:988
  38.4 3.1 %collective-permute-start.20 = (f32[16,128]{1,0:T(8,128)S(1)}, f32[16,128]{1,0:T(8,128)S(1)}, u32[]{:S(2)}, u32[]{:S(2)}) collective-permute-start(f32[16,128]{1,0:T(8,128)S(1)} %collective-permute-done.16.z_rows), channel_id=1, source_target_pairs={{0,6},{2,4},{4,2},{6,0},{1,7},{3,5},{5,3},{7,1},{8,14},{10,12},{12... | collective-permute-start | bytes 24584 | tf_op jit(solution)/shard_map/ppermute | solution.py:988

commit v9 on v5

--- a/solution.py
+++ b/solution.py
@@ -105,7 +105,7 @@
     return total
 
 
-def conversions(source, kind, heading, code, *, columns):
+def conversions(source, kind, heading, code, mark, *, columns):
     count = source.shape[1]
     value = (heading[...] + 32 * kind[...]).astype(jnp.float32)
     row, column = (source[...] // columns, source[...] % columns)
@@ -114,6 +114,7 @@
     code[...] = lax.dot_general(
         by_row, by_column, (((1,), (1,)), ((), ())), preferred_element_type=jnp.float32
     )
+    mark[...] = jnp.zeros(mark.shape, jnp.float32)
 
 
 def odd(axis):
@@ -400,6 +401,8 @@
         up, down = (post[x_up[slot], 1], post[x_down[slot], 0])
         ahead[slot] = jnp.where(flip_x, down, up)
         behind[slot] = jnp.where(flip_x, up, down)
+    for comp in range(3):
+        behind[5 + comp] = jnp.where(flip_x, flow[comp, bx - 1], flow[comp, 0])
 
 
 def restretch_plane(x, place, stretch, flow, halos, updated):
@@ -481,8 +484,8 @@
     bx = stretch.shape[1]
     flip_x = odd("gx")
     for comp in range(3):
-        below[comp] = jnp.where(flip_x, x_first[comp], x_second[comp])
-        above[comp] = jnp.where(flip_x, x_second[comp], x_first[comp])
+        below[comp] = jnp.where(flip_x, x_first[comp], x_second[5 + comp])
+        above[comp] = jnp.where(flip_x, x_second[5 + comp], x_first[comp])
     swapped_rows(y_first, y_second, range(speed_slot, sides), y_below, y_above, 0)
     z_halo[...] = row_columns(z_rows[...]).reshape(z_halo.shape)
     halos = (below, above, y_below, y_above, z_halo)
@@ -529,7 +532,7 @@
 down_edges = ((0, y_up.index(10)), (0, gas_slot), (1, y_down.index(8)), (1, gas_slot))
 
 
-def forward_edges(z_rows, y_first, y_second, first_out, second_out, corner, *, bx):
+def forward_edges(z_rows, y_first, y_second, after, first_out, second_out, corner, *, bx):
     halves = y_first.shape[1] // lanes
     flip_x, flip_y = (odd("gx"), odd("gy"))
     for half in range(halves):
@@ -775,7 +778,6 @@
     after,
     late,
     v_first,
-    v_second,
     settled,
     spread,
     line_first,
@@ -798,7 +800,6 @@
     for comp in range(3):
         up, down = (flow[comp, bx - 1], flow[comp, 0])
         v_first[comp] = jnp.where(flip_x, down, up)
-        v_second[comp] = jnp.where(flip_x, up, down)
     for slot in range(5):
         below[slot] = jnp.where(flip_x, x_first[slot], x_second[slot])
         above[slot] = jnp.where(flip_x, x_second[slot], x_first[slot])
@@ -977,11 +978,20 @@
         new_mass[x] = total
 
 
+def swapped_ahead(array, axis):
+    devices = lax.axis_size(axis)
+    pairing = [(i, (i + 1) % devices if i % 2 == 0 else i - 1) for i in range(devices)]
+    return lax.ppermute(array, axis, pairing)
+
+
+def swapped_behind(array, axis):
+    devices = lax.axis_size(axis)
+    pairing = [(i, (i - 1) % devices if i % 2 == 0 else (i + 1) % devices) for i in range(devices)]
+    return lax.ppermute(array, axis, pairing)
+
+
 def swapped(first, second, axis):
-    devices = lax.axis_size(axis)
-    ahead = [(i, (i + 1) % devices if i % 2 == 0 else i - 1) for i in range(devices)]
-    behind = [(i, (i - 1) % devices if i % 2 == 0 else (i + 1) % devices) for i in range(devices)]
-    return lax.ppermute(first, axis, ahead), lax.ppermute(second, axis, behind)
+    return swapped_ahead(first, axis), swapped_behind(second, axis)
 
 
 def both_ways(rows, lower):
@@ -1046,9 +1056,9 @@
 
     entries = conv_source.shape[0]
     mark = (tall, lanes)
-    (code,) = call(
+    code, code_done = call(
         lambda *refs: conversions(*refs, columns=bz),
-        [(bx * by, bz)],
+        [(bx * by, bz), mark],
         cost=(40 * cells, 4 * cells),
     )(*(array.reshape(1, entries) for array in (conv_source, conv_kind, conv_direction)))
     code = code.reshape(box)
@@ -1072,7 +1082,7 @@
     )(pops, stretch, flow, z_first, *y_first)
     outer_post, outer_shift, z_out, x_one, x_two, y_one, y_two = call(
         collide_outer,
-        [(19, *ends), (3, *ends), columns, (5, *face), (5, *face), rows, rows],
+        [(19, *ends), (3, *ends), columns, (5, *face), (8, *face), rows, rows],
         scratch=[(4, *face), (4, *face)] + sides_y + [box],
         cost=(150 * cells, 150 * cells),
     )(pops, stretch, flags, flow, *first_x, *y_first, z_first, inner_post)
@@ -1081,8 +1091,8 @@
     post_x = swapped(x_one, x_two, "gx")
     edges = (4 * (bz // lanes) + columns[0], lanes)
     x_one, x_two, corner = call(
-        lambda *refs: forward_edges(*refs, bx=bx), [edges, edges, columns], cost=(4 * 10**9, 0)
-    )(z_post, *post_y)
+        lambda *refs: forward_edges(*refs, bx=bx), [edges, edges, columns], cost=(17 * 10**8, 0)
+    )(z_post, *post_y, code_done)
     corners = swapped(corner, corner, "gy")
     edges_x = swapped(x_one, x_two, "gx")
 
@@ -1115,11 +1125,10 @@
         scratch=[(6, *inside)] + sides_y + [pltpu.SemaphoreType.DMA],
         cost=(80 * cells, 40 * cells),
     )(stretch, flow, *post_y, z_post)
-    late, v_one, v_two, outer_settled, spread, y_one, y_two, z_out = call(
+    late, v_one, outer_settled, spread, y_one, y_two, z_out = call(
         stream_late,
         [
             (5, *ends),
-            (3, *face),
             (3, *face),
             ends,
             (bx + 2, *face),
@@ -1148,7 +1157,7 @@
     z_last = both_ways(z_out, 8)
     last_y = swapped(y_one, y_two, "gy")
     last_corners = swapped(z_last, z_last, "gy")
-    flow_x = swapped(v_one, v_two, "gx")
+    flow_x = (swapped_ahead(v_one, "gx"), post_x[1])
     x_one, x_two = call(add_faces, [face, face], cost=(4 * 10**9, 0))(spread, z_last, *last_y)
     last_x = swapped(x_one, x_two, "gx")
     (fresh,) = call(

time: 41.2 us -> 41.7 us (1.012)
  starting transfers between devices: 23.5 us -> 24.6 us
  waiting for transfers between devices: 4.13 us -> 3.64 us
    ppermute x20 -> x19, waiting for transfers between devices: 3.35 us -> 2.21 us  [the longest x9 2.08 us: swapped_behind(): return lax.ppermute(array, axis, pairing)]
    ppermute x3, starting transfers between devices: 3.6 us -> 4.38 us  [both_ways(): lax.ppermute(rows, 'gz', [(i, (i + 1) % devices) for i in range(devices)])]
    ppermute x3, waiting for transfers between devices: 0.78 us -> 1.42 us  [both_ways(): lax.ppermute(rows, 'gz', [(i, (i + 1) % devices) for i in range(devices)])]
    ppermute x20 -> x19, starting transfers between devices: 19.9 us -> 20.2 us  [the longest x9 14 us: swapped_behind(): return lax.ppermute(array, axis, pairing)]
  transfers between devices with their start and end apart: 23 -> 22, of which waited for: 6 -> 8; matrix products, arithmetic and copies ran while one was open for 0% -> 0% of each run, Pallas kernels for 21% -> 20%
where the time goes in v9:
time: 41.7 us; the launch traced here: 41.5 us
  starting transfers between devices  24.6 us (59%)
  Pallas kernels  12.5 us (30%)
  waiting for transfers between devices  3.64 us (9%)
  between operations  0.8 us (2%)
    ppermute x9, starting transfers between devices, swapped_behind(): return lax.ppermute(array, axis, pairing)  14 us
    ppermute x10, starting transfers between devices, swapped_ahead(): return lax.ppermute(array, axis, pairing)  6.15 us
    ppermute x3, starting transfers between devices, both_ways(): lax.ppermute(rows, 'gz', [(i, (i + 1) % devices) for i in range(devices)])  4.38 us
    ppermute x9, waiting for transfers between devices, swapped_behind(): return lax.ppermute(array, axis, pairing)  2.08 us
    pallas_call x1, Pallas kernels, shards(): call(moments, [(19, *box), (5, *box)], specs=[remote], scratch=[pltpu.Sem...  1.74 us
    pallas_call x1, Pallas kernels, shards(): call(store, [(19, *box)], out_specs=[remote], scratch=[pltpu.SemaphoreTyp...  1.7 us
    ppermute x3, waiting for transfers between devices, both_ways(): lax.ppermute(rows, 'gz', [(i, (i + 1) % devices) for i in range(devices)])  1.42 us
    pallas_call x1, Pallas kernels, shards(): call(first_faces, [(6, *box), jax.ShapeDtypeStruct(box, jnp.int32), (8, b...  1.38 us
  transfers between devices with their start and end apart: 22, of which 8 were waited for; matrix products, arithmetic and copies ran while one was open for 0% of the time, Pallas kernels for 20%

profile of v9, /device:TPU:0, one launch (start us, length us, event | category | flops | bytes accessed | tf_op | source)
XLA Modules:
  0.0 41.5 jit_solution(13631408962579426704)
XLA Ops:
  0.6 1.4 %shard_map.95 = (f32[6,4,32,256]{3,2,1,0:T(8,128)S(1)}, s32[4,32,256]{2,1,0:T(8,128)S(1)}, f32[8,128]{1,0:T(8,128)S(1)}, f32[16,256]{1,0:T(8,128)S(1)}, f32[16,2...) custom-call(f32[6,4,32,256]{3,2,1,0:T(8,128)} %stretch_in.1, s32[4,32,256]{2,1,0:T(8,128)} %flags_in.1), custom_call_target="tpu_custom_call" | custom-call | flops 327680 | bytes 1966080 | tf_op jit(solution)/shard_map/pallas_call | solution.py:1038
  2.0 3.1 %collective-permute-start.3 = (f32[4,32,256]{2,1,0:T(8,128)S(1)}, f32[4,32,256]{2,1,0:T(8,128)S(1)}, u32[]{:S(2)}, u32[]{:S(2)}) collective-permute-start(f32[4,32,256]{2,1,0:T(8,128)S(1)} %get-tuple-element.58), channel_id=1, source_target_pairs={{0,8},{8,0},{16,24},{24,16},{1,9},{9,1},{17,25},{25,17},{2,10},{10... | collective-permute-start | bytes 393224 | tf_op jit(solution)/shard_map/ppermute | solution.py:984
  5.1 2.5 %collective-permute-start.4 = (f32[4,32,256]{2,1,0:T(8,128)S(1)}, f32[4,32,256]{2,1,0:T(8,128)S(1)}, u32[]{:S(2)}, u32[]{:S(2)}) collective-permute-start(f32[4,32,256]{2,1,0:T(8,128)S(1)} %get-tuple-element.59), channel_id=1, source_target_pairs={{0,24},{8,16},{16,8},{24,0},{1,25},{9,17},{17,9},{25,1},{2,26},{10... | collective-permute-start | bytes 393224 | tf_op jit(solution)/shard_map/ppermute | solution.py:990
  7.6 0.0 collective-permute-start.1
  7.6 1.6 %collective-permute-start.2 = (f32[16,256]{1,0:T(8,128)S(1)}, f32[16,256]{1,0:T(8,128)S(1)}, u32[]{:S(2)}, u32[]{:S(2)}) collective-permute-start(f32[16,256]{1,0:T(8,128)S(1)} %get-tuple-element.55), channel_id=1, source_target_pairs={{0,6},{2,4},{4,2},{6,0},{1,7},{3,5},{5,3},{7,1},{8,14},{10,12},{12... | collective-permute-start | bytes 49160 | tf_op jit(solution)/shard_map/ppermute | solution.py:990
  9.2 1.5 %collective-permute-start = (f32[8,128]{1,0:T(8,128)S(1)}, f32[8,128]{1,0:T(8,128)S(1)}, u32[]{:S(2)}, u32[]{:S(2)}) collective-permute-start(f32[8,128]{1,0:T(8,128)S(1)} %get-tuple-element.53), channel_id=1, source_target_pairs={{0,1},{1,0},{2,3},{3,2},{4,5},{5,4},{6,7},{7,6},{8,9},{9,8},{10,11... | collective-permute-start | bytes 12296 | tf_op jit(solution)/shard_map/ppermute | solution.py:999
  10.7 1.7 %shard_map.94 = (f32[19,4,32,256]{3,2,1,0:T(8,128)S(1)}, f32[5,4,32,256]{3,2,1,0:T(8,128)S(1)}) custom-call(f32[19,4,32,256]{3,2,1,0:T(8,128)} %pops_in.1), custom_call_target="tpu_custom_call" | custom-call | flops 1966080 | bytes 4915200 | tf_op jit(solution)/shard_map/pallas_call | solution.py:1066
  12.5 0.3 collective-permute-done.z_rows
  12.8 0.0 collective-permute-done.1.y_first
  12.8 0.0 collective-permute-done.2.y_second
  12.8 0.8 %shard_map.96 = (f32[19,2,32,256]{3,2,1,0:T(8,128)S(1)}, f32[3,2,32,256]{3,2,1,0:T(8,128)S(1)}) custom-call(f32[19,4,32,256]{3,2,1,0:T(8,128)S(1)} %get-tuple-element.50.pops, f32[6,4,32,256]{3,2,1,0:T(8,128)S(1)} %get-tuple-element.51.stretch, f32[5,4,32,256]{3,2,1,0:T(8,128)S(1)} %get-tuple-element.52.flow, f32[8,128]{1,0:T(8,128)S(1)} %collective-permute-done.z_rows, ...), custom_call_target="tpu_custom_call" | custom-call | flops 4915200 | bytes 4915200 | tf_op jit(solution)/shard_map/pallas_call | solution.py:1077
  13.6 0.0 collective-permute-done.3.x_first.gas_first
  13.6 0.1 collective-permute-done.4.x_second.gas_second
  13.7 0.0 copy-start.1
  13.7 0.0 copy-start.2
  13.7 1.0 %shard_map.97 = (f32[19,2,32,256]{3,2,1,0:T(8,128)S(1)}, f32[3,2,32,256]{3,2,1,0:T(8,128)S(1)}, f32[24,128]{1,0:T(8,128)S(1)}, f32[5,32,256]{2,1,0:T(8,128)S(1)}...) custom-call(f32[19,4,32,256]{3,2,1,0:T(8,128)S(1)} %get-tuple-element.50.pops, ...), custom_call_target="tpu_custom_call" | custom-call | flops 4915200 | bytes 4915200 | tf_op jit(solution)/shard_map/pallas_call | solution.py:1083
  14.7 1.5 %collective-permute-start.11 = (f32[8,32,256]{2,1,0:T(8,128)S(1)}, f32[8,32,256]{2,1,0:T(8,128)S(1)}, u32[]{:S(2)}, u32[]{:S(2)}) collective-permute-start(f32[8,32,256]{2,1,0:T(8,128)S(1)} %get-tuple-element.78), channel_id=1, source_target_pairs={{0,24},{8,16},{16,8},{24,0},{1,25},{9,17},{17,9},{25,1},{2,26},{10... | collective-permute-start | bytes 786440 | tf_op jit(solution)/shard_map/ppermute | solution.py:990
  16.2 0.0 collective-permute-start.5
  16.2 1.6 %collective-permute-start.6 = (f32[40,256]{1,0:T(8,128)S(1)}, f32[40,256]{1,0:T(8,128)S(1)}, u32[]{:S(2)}, u32[]{:S(2)}) collective-permute-start(f32[40,256]{1,0:T(8,128)S(1)} %get-tuple-element.64), channel_id=1, source_target_pairs={{0,6},{2,4},{4,2},{6,0},{1,7},{3,5},{5,3},{7,1},{8,14},{10,12},{12... | collective-permute-start | bytes 122888 | tf_op jit(solution)/shard_map/ppermute | solution.py:990
  17.8 1.5 %collective-permute-start.7 = (f32[24,128]{1,0:T(8,128)S(1)}, f32[24,128]{1,0:T(8,128)S(1)}, u32[]{:S(2)}, u32[]{:S(2)}) collective-permute-start(f32[24,128]{1,0:T(8,128)S(1)} %get-tuple-element.65), channel_id=1, source_target_pairs={{0,1},{1,0},{2,3},{3,2},{4,5},{5,4},{6,7},{7,6},{8,9},{9,8},{10,11... | collective-permute-start | bytes 36872 | tf_op jit(solution)/shard_map/ppermute | solution.py:999
  19.4 0.0 copy-done.1
  19.4 0.0 copy-done.2
  19.4 0.0 copy-done.3
  19.4 0.3 shard_map.99
  19.7 0.9 %collective-permute-start.10 = (f32[5,32,256]{2,1,0:T(8,128)S(1)}, f32[5,32,256]{2,1,0:T(8,128)S(1)}, u32[]{:S(2)}, u32[]{:S(2)}) collective-permute-start(f32[5,32,256]{2,1,0:T(8,128)S(1)} %get-tuple-element.77), channel_id=1, source_target_pairs={{0,8},{8,0},{16,24},{24,16},{1,9},{9,1},{17,25},{25,17},{2,10},{10... | collective-permute-start | bytes 491528 | tf_op jit(solution)/shard_map/ppermute | solution.py:984
  20.6 0.9 %collective-permute-done.7.z_rows.refs_0_ = f32[24,128]{1,0:T(8,128)S(1)} collective-permute-done((f32[24,128]{1,0:T(8,128)S(1)}, f32[24,128]{1,0:T(8,128)S(1)}, u32[]{:S(2)}, u32[]{:S(2)}) %collective-permute-start.7) | collective-permute-done | bytes 12320 | tf_op jit(solution)/shard_map/ppermute | solution.py:999
  21.5 0.0 collective-permute-done.5.y_first.refs_1_
  21.5 0.0 collective-permute-done.6.y_second.refs_2_
  21.6 0.0 copy-start
  21.6 0.1 collective-permute-start.8
  21.7 0.9 %collective-permute-start.12 = (f32[32,128]{1,0:T(8,128)S(1)}, f32[32,128]{1,0:T(8,128)S(1)}, u32[]{:S(2)}, u32[]{:S(2)}) collective-permute-start(f32[32,128]{1,0:T(8,128)S(1)} %get-tuple-element.79), channel_id=1, source_target_pairs={{0,8},{8,0},{16,24},{24,16},{1,9},{9,1},{17,25},{25,17},{2,10},{10... | collective-permute-start | bytes 49160 | tf_op jit(solution)/shard_map/ppermute | solution.py:984
  22.6 1.8 %collective-permute-start.13 = (f32[32,128]{1,0:T(8,128)S(1)}, f32[32,128]{1,0:T(8,128)S(1)}, u32[]{:S(2)}, u32[]{:S(2)}) collective-permute-start(f32[32,128]{1,0:T(8,128)S(1)} %get-tuple-element.80), channel_id=1, source_target_pairs={{0,24},{8,16},{16,8},{24,0},{1,25},{9,17},{17,9},{25,1},{2,26},{10... | collective-permute-start | bytes 49160 | tf_op jit(solution)/shard_map/ppermute | solution.py:990
  24.3 0.0 collective-permute-done.8.corner_first
  24.3 0.0 collective-permute-start.9
  24.4 1.2 %shard_map.102 = (f32[6,4,32,256]{3,2,1,0:T(8,128)}, f32[8,128]{1,0:T(8,128)S(1)}) custom-call(f32[6,4,32,256]{3,2,1,0:T(8,128)S(1)} %get-tuple-element.51.stretch, f32[5,4,32,256]{3,2,1,0:T(8,128)S(1)} %get-tuple-element.52.flow, f32[40,256]{1,0:T(8,128)S(1)} %collective-permute-done.5.y_first.refs_1_, ...), custom_call_target="tpu_custom_call" | custom-call | flops 2621440 | bytes 1310720 | tf_op jit(solution)/shard_map/pallas_call | solution.py:1121
  25.6 0.9 %shard_map.98 = (f32[15,2,32,256]{3,2,1,0:T(8,128)S(1)}, f32[15,2,32,256]{3,2,1,0:T(8,128)S(1)}, f32[4,32,256]{2,1,0:T(8,128)S(1)}, f32[4,32,256]{2,1,0:T(8,128)S(1)}) custom-call(f32[19,2,32,256]{3,2,1,0:T(8,128)S(1)} %get-tuple-element.56.inner.inner_post, f32[19,2,32,256]{3,2,1,0:T(8,128)S(1)} %get-tuple-element.60.outer_post.post, ...), custom_call_target="tpu_custom_call" | custom-call | flops 11468800 | bytes 6553600 | tf_op jit(solution)/shard_map/pallas_call | solution.py:1101
  26.5 1.0 %collective-permute-done.9.corner_second = f32[24,128]{1,0:T(8,128)S(1)} collective-permute-done((f32[24,128]{1,0:T(8,128)S(1)}, f32[24,128]{1,0:T(8,128)S(1)}, u32[]{:S(2)}, u32[]{:S(2)}) %collective-permute-start.9) | collective-permute-done | bytes 12320 | tf_op jit(solution)/shard_map/ppermute | solution.py:990
  27.5 0.0 copy-done
  27.5 0.6 %shard_map.101 = (f32[4,2,32,256]{3,2,1,0:T(8,128)S(1)}, f32[4,2,32,256]{3,2,1,0:T(8,128)S(1)}, f32[2,32,256]{2,1,0:T(8,128)S(1)}, f32[2,32,256]{2,1,0:T(8,128)S...) custom-call(f32[19,2,32,256]{3,2,1,0:T(8,128)S(1)} %get-tuple-element.56.inner.inner_post, ...), custom_call_target="tpu_custom_call" | custom-call | flops 3276800 | bytes 1966080 | tf_op jit(solution)/shard_map/pallas_call | solution.py:1115
  28.1 0.1 collective-permute-done.12.edges_first
  28.2 0.2 collective-permute-done.13.edges_second
  28.4 0.0 collective-permute-done.10.x_first
  28.4 0.0 collective-permute-done.11.x_second
  28.5 0.8 %shard_map.103 = (f32[5,2,32,256]{3,2,1,0:T(8,128)S(1)}, f32[3,32,256]{2,1,0:T(8,128)S(1)}, f32[2,32,256]{2,1,0:T(8,128)S(1)}, f32[6,32,256]{2,1,0:T(8,128)S(1)}...) custom-call(f32[19,2,32,256]{3,2,1,0:T(8,128)S(1)} %get-tuple-element.60.outer_post.post, ...), custom_call_target="tpu_custom_call" | custom-call | flops 4915200 | bytes 3276800 | tf_op jit(solution)/shard_map/pallas_call | solution.py:1128
  29.2 1.3 %collective-permute-start.15 = (f32[16,128]{1,0:T(8,128)S(1)}, f32[16,128]{1,0:T(8,128)S(1)}, u32[]{:S(2)}, u32[]{:S(2)}) collective-permute-start(f32[16,128]{1,0:T(8,128)S(1)} %get-tuple-element.91), channel_id=1, source_target_pairs={{0,1},{1,0},{2,3},{3,2},{4,5},{5,4},{6,7},{7,6},{8,9},{9,8},{10,11... | collective-permute-start | bytes 24584 | tf_op jit(solution)/shard_map/ppermute | solution.py:999
  30.5 0.0 collective-permute-start.16
  30.5 1.4 %collective-permute-start.17 = (f32[8,256]{1,0:T(8,128)S(1)}, f32[8,256]{1,0:T(8,128)S(1)}, u32[]{:S(2)}, u32[]{:S(2)}) collective-permute-start(f32[8,256]{1,0:T(8,128)S(1)} %get-tuple-element.93), channel_id=1, source_target_pairs={{0,6},{2,4},{4,2},{6,0},{1,7},{3,5},{5,3},{7,1},{8,14},{10,12},{12... | collective-permute-start | bytes 24584 | tf_op jit(solution)/shard_map/ppermute | solution.py:990
  31.9 0.8 %collective-permute-start.14 = (f32[3,32,256]{2,1,0:T(8,128)S(1)}, f32[3,32,256]{2,1,0:T(8,128)S(1)}, u32[]{:S(2)}, u32[]{:S(2)}) collective-permute-start(f32[3,32,256]{2,1,0:T(8,128)S(1)} %get-tuple-element.85), channel_id=1, source_target_pairs={{0,8},{8,0},{16,24},{24,16},{1,9},{9,1},{17,25},{25,17},{2,10},{10... | collective-permute-start | bytes 294920 | tf_op jit(solution)/shard_map/ppermute | solution.py:984
  32.8 0.1 collective-permute-done.15.z_rows
  32.9 0.0 collective-permute-done.16.y_first
  32.9 0.7 %collective-permute-done.17.y_second = f32[8,256]{1,0:T(8,128)S(1)} collective-permute-done((f32[8,256]{1,0:T(8,128)S(1)}, f32[8,256]{1,0:T(8,128)S(1)}, u32[]{:S(2)}, u32[]{:S(2)}) %collective-permute-start.17) | collective-permute-done | bytes 8224 | tf_op jit(solution)/shard_map/ppermute | solution.py:990
  33.6 0.2 shard_map.106
  33.8 2.1 %collective-permute-start.20 = (f32[32,256]{1,0:T(8,128)S(1)}, f32[32,256]{1,0:T(8,128)S(1)}, u32[]{:S(2)}, u32[]{:S(2)}) collective-permute-start(f32[32,256]{1,0:T(8,128)S(1)} %get-tuple-element.94), channel_id=1, source_target_pairs={{0,24},{8,16},{16,8},{24,0},{1,25},{9,17},{17,9},{25,1},{2,26},{10... | collective-permute-start | bytes 98312 | tf_op jit(solution)/shard_map/ppermute | solution.py:990
  35.9 0.3 collective-permute-start.21
  36.2 0.0 collective-permute-start.18
  36.2 1.6 %collective-permute-start.19 = (f32[16,128]{1,0:T(8,128)S(1)}, f32[16,128]{1,0:T(8,128)S(1)}, u32[]{:S(2)}, u32[]{:S(2)}) collective-permute-start(f32[16,128]{1,0:T(8,128)S(1)} %collective-permute-done.15.z_rows), channel_id=1, source_target_pairs={{0,6},{2,4},{4,2},{6,0},{1,7},{3,5},{5,3},{7,1},{8,14},{10,12},{12... | collective-permute-start | bytes 24584 | tf_op jit(solution)/shard_map/ppermute | solution.py:990
  37.8 1.7 %shard_map.104 = f32[19,4,32,256]{3,2,1,0:T(8,128)} custom-call(f32[15,2,32,256]{3,2,1,0:T(8,128)S(1)} %get-tuple-element.66.inner, f32[15,2,32,256]{3,2,1,0:T(8,128)S(1)} %get-tuple-element.67.outer, f32[4,2,32,256]{3,2,1,0:T(8,128)S(1)} %get-tuple-element.73.inner_slanted, f32[4,2,32,256]{3,2,1,0:T(8,128)S(1)} %get-tuple-element.74.outer_slanted, ...), custom_call_target="tpu_custom_call" | custom-call | bytes 5242880 | tf_op jit(solution)/shard_map/pallas_call | solution.py:1163
  39.5 0.0 collective-permute-done.14.x_first
  39.5 1.1 %shard_map.105 = (f32[6,4,32,256]{3,2,1,0:T(8,128)}, f32[8,128]{1,0:T(8,128)S(1)}) custom-call(f32[6,4,32,256]{3,2,1,0:T(8,128)S(1)} %get-tuple-element.51.stretch, f32[5,4,32,256]{3,2,1,0:T(8,128)S(1)} %get-tuple-element.52.flow, f32[3,32,256]{2,1,0:T(8,128)S(1)} %collective-permute-done.14.x_first, ...), custom_call_target="tpu_custom_call", output_to_operand_aliasing={{0}: (7, {})} | custom-call | flops 2621440 | bytes 1310720 | tf_op jit(solution)/shard_map/pallas_call | solution.py:1170
  40.6 0.0 collective-permute-done.18.corner_first
  40.6 0.0 collective-permute-done.19.corner_second
  40.6 0.0 collective-permute-done.20.x_second
  40.7 0.0 collective-permute-done.21.x_first
  40.7 0.9 %shard_map.107 = f32[4,32,256]{2,1,0:T(8,128)} custom-call(f32[2,32,256]{2,1,0:T(8,128)S(1)} %get-tuple-element.88.inner_settled, f32[2,32,256]{2,1,0:T(8,128)S(1)} %get-tuple-element.89.outer_settled, f32[6,32,256]{2,1,0:T(8,128)S(1)} %get-tuple-element.90.spread, f32[16,128]{1,0:T(8,128)S(1)} %collective-permute-done.15.z_rows, ...), custom_call_target="tpu_custom_call" | custom-call | tf_op jit(solution)/shard_map/pallas_call | solution.py:1181
  (2 shorter events, 0.0 us)
Async XLA Ops:
  2.0 11.5 %collective-permute-start.3 = (f32[4,32,256]{2,1,0:T(8,128)S(1)}, f32[4,32,256]{2,1,0:T(8,128)S(1)}, u32[]{:S(2)}, u32[]{:S(2)}) collective-permute-start(f32[4,32,256]{2,1,0:T(8,128)S(1)} %get-tuple-element.58), channel_id=1, source_target_pairs={{0,8},{8,0},{16,24},{24,16},{1,9},{9,1},{17,25},{25,17},{2,10},{10... | collective-permute-start | bytes 393224 | tf_op jit(solution)/shard_map/ppermute | solution.py:984
  5.1 8.6 %collective-permute-start.4 = (f32[4,32,256]{2,1,0:T(8,128)S(1)}, f32[4,32,256]{2,1,0:T(8,128)S(1)}, u32[]{:S(2)}, u32[]{:S(2)}) collective-permute-start(f32[4,32,256]{2,1,0:T(8,128)S(1)} %get-tuple-element.59), channel_id=1, source_target_pairs={{0,24},{8,16},{16,8},{24,0},{1,25},{9,17},{17,9},{25,1},{2,26},{10... | collective-permute-start | bytes 393224 | tf_op jit(solution)/shard_map/ppermute | solution.py:990
  7.6 5.2 %collective-permute-start.1 = (f32[16,256]{1,0:T(8,128)S(1)}, f32[16,256]{1,0:T(8,128)S(1)}, u32[]{:S(2)}, u32[]{:S(2)}) collective-permute-start(f32[16,256]{1,0:T(8,128)S(1)} %get-tuple-element.54), channel_id=1, source_target_pairs={{0,2},{2,0},{4,6},{6,4},{1,3},{3,1},{5,7},{7,5},{8,10},{10,8},{12,... | collective-permute-start | bytes 49160 | tf_op jit(solution)/shard_map/ppermute | solution.py:984
  7.6 5.2 %collective-permute-start.2 = (f32[16,256]{1,0:T(8,128)S(1)}, f32[16,256]{1,0:T(8,128)S(1)}, u32[]{:S(2)}, u32[]{:S(2)}) collective-permute-start(f32[16,256]{1,0:T(8,128)S(1)} %get-tuple-element.55), channel_id=1, source_target_pairs={{0,6},{2,4},{4,2},{6,0},{1,7},{3,5},{5,3},{7,1},{8,14},{10,12},{12... | collective-permute-start | bytes 49160 | tf_op jit(solution)/shard_map/ppermute | solution.py:990
  9.2 3.6 %collective-permute-start = (f32[8,128]{1,0:T(8,128)S(1)}, f32[8,128]{1,0:T(8,128)S(1)}, u32[]{:S(2)}, u32[]{:S(2)}) collective-permute-start(f32[8,128]{1,0:T(8,128)S(1)} %get-tuple-element.53), channel_id=1, source_target_pairs={{0,1},{1,0},{2,3},{3,2},{4,5},{5,4},{6,7},{7,6},{8,9},{9,8},{10,11... | collective-permute-start | bytes 12296 | tf_op jit(solution)/shard_map/ppermute | solution.py:999
  13.7 5.7 %copy-start.1 = (s32[1024]{0:T(1024)S(1)}, s32[1024]{0:T(1024)}, u32[]{:S(2)}) copy-start(s32[1024]{0:T(1024)} %param.11) | copy-start | bytes 12292
  13.7 5.7 %copy-start.2 = (s32[1024]{0:T(1024)S(1)}, s32[1024]{0:T(1024)}, u32[]{:S(2)}) copy-start(s32[1024]{0:T(1024)} %param.12) | copy-start | bytes 12292
  13.7 5.7 %copy-start.3 = (s32[1024]{0:T(1024)S(1)}, s32[1024]{0:T(1024)}, u32[]{:S(2)}) copy-start(s32[1024]{0:T(1024)} %param.13) | copy-start | bytes 12292
  14.7 13.7 %collective-permute-start.11 = (f32[8,32,256]{2,1,0:T(8,128)S(1)}, f32[8,32,256]{2,1,0:T(8,128)S(1)}, u32[]{:S(2)}, u32[]{:S(2)}) collective-permute-start(f32[8,32,256]{2,1,0:T(8,128)S(1)} %get-tuple-element.78), channel_id=1, source_target_pairs={{0,24},{8,16},{16,8},{24,0},{1,25},{9,17},{17,9},{25,1},{2,26},{10... | collective-permute-start | bytes 786440 | tf_op jit(solution)/shard_map/ppermute | solution.py:990
  16.2 5.3 %collective-permute-start.5 = (f32[40,256]{1,0:T(8,128)S(1)}, f32[40,256]{1,0:T(8,128)S(1)}, u32[]{:S(2)}, u32[]{:S(2)}) collective-permute-start(f32[40,256]{1,0:T(8,128)S(1)} %get-tuple-element.63), channel_id=1, source_target_pairs={{0,2},{2,0},{4,6},{6,4},{1,3},{3,1},{5,7},{7,5},{8,10},{10,8},{12,... | collective-permute-start | bytes 122888 | tf_op jit(solution)/shard_map/ppermute | solution.py:984
  16.2 5.3 %collective-permute-start.6 = (f32[40,256]{1,0:T(8,128)S(1)}, f32[40,256]{1,0:T(8,128)S(1)}, u32[]{:S(2)}, u32[]{:S(2)}) collective-permute-start(f32[40,256]{1,0:T(8,128)S(1)} %get-tuple-element.64), channel_id=1, source_target_pairs={{0,6},{2,4},{4,2},{6,0},{1,7},{3,5},{5,3},{7,1},{8,14},{10,12},{12... | collective-permute-start | bytes 122888 | tf_op jit(solution)/shard_map/ppermute | solution.py:990
  17.8 3.7 %collective-permute-start.7 = (f32[24,128]{1,0:T(8,128)S(1)}, f32[24,128]{1,0:T(8,128)S(1)}, u32[]{:S(2)}, u32[]{:S(2)}) collective-permute-start(f32[24,128]{1,0:T(8,128)S(1)} %get-tuple-element.65), channel_id=1, source_target_pairs={{0,1},{1,0},{2,3},{3,2},{4,5},{5,4},{6,7},{7,6},{8,9},{9,8},{10,11... | collective-permute-start | bytes 36872 | tf_op jit(solution)/shard_map/ppermute | solution.py:999
  19.7 8.7 %collective-permute-start.10 = (f32[5,32,256]{2,1,0:T(8,128)S(1)}, f32[5,32,256]{2,1,0:T(8,128)S(1)}, u32[]{:S(2)}, u32[]{:S(2)}) collective-permute-start(f32[5,32,256]{2,1,0:T(8,128)S(1)} %get-tuple-element.77), channel_id=1, source_target_pairs={{0,8},{8,0},{16,24},{24,16},{1,9},{9,1},{17,25},{25,17},{2,10},{10... | collective-permute-start | bytes 491528 | tf_op jit(solution)/shard_map/ppermute | solution.py:984
  21.6 5.9 %copy-start = (f32[4,32,256]{2,1,0:T(8,128)S(1)}, f32[4,32,256]{2,1,0:T(8,128)}, u32[]{:S(2)}) copy-start(f32[4,32,256]{2,1,0:T(8,128)} %mass.3) | copy-start | bytes 393220
  21.6 2.8 %collective-permute-start.8 = (f32[24,128]{1,0:T(8,128)S(1)}, f32[24,128]{1,0:T(8,128)S(1)}, u32[]{:S(2)}, u32[]{:S(2)}) collective-permute-start(f32[24,128]{1,0:T(8,128)S(1)} %get-tuple-element.70), channel_id=1, source_target_pairs={{0,2},{2,0},{4,6},{6,4},{1,3},{3,1},{5,7},{7,5},{8,10},{10,8},{12,... | collective-permute-start | bytes 36872 | tf_op jit(solution)/shard_map/ppermute | solution.py:984
  21.7 6.6 %collective-permute-start.12 = (f32[32,128]{1,0:T(8,128)S(1)}, f32[32,128]{1,0:T(8,128)S(1)}, u32[]{:S(2)}, u32[]{:S(2)}) collective-permute-start(f32[32,128]{1,0:T(8,128)S(1)} %get-tuple-element.79), channel_id=1, source_target_pairs={{0,8},{8,0},{16,24},{24,16},{1,9},{9,1},{17,25},{25,17},{2,10},{10... | collective-permute-start | bytes 49160 | tf_op jit(solution)/shard_map/ppermute | solution.py:984
  22.6 5.9 %collective-permute-start.13 = (f32[32,128]{1,0:T(8,128)S(1)}, f32[32,128]{1,0:T(8,128)S(1)}, u32[]{:S(2)}, u32[]{:S(2)}) collective-permute-start(f32[32,128]{1,0:T(8,128)S(1)} %get-tuple-element.80), channel_id=1, source_target_pairs={{0,24},{8,16},{16,8},{24,0},{1,25},{9,17},{17,9},{25,1},{2,26},{10... | collective-permute-start | bytes 49160 | tf_op jit(solution)/shard_map/ppermute | solution.py:990
  24.3 3.2 %collective-permute-start.9 = (f32[24,128]{1,0:T(8,128)S(1)}, f32[24,128]{1,0:T(8,128)S(1)}, u32[]{:S(2)}, u32[]{:S(2)}) collective-permute-start(f32[24,128]{1,0:T(8,128)S(1)} %get-tuple-element.70), channel_id=1, source_target_pairs={{0,6},{2,4},{4,2},{6,0},{1,7},{3,5},{5,3},{7,1},{8,14},{10,12},{12... | collective-permute-start | bytes 36872 | tf_op jit(solution)/shard_map/ppermute | solution.py:990
  29.2 3.7 %collective-permute-start.15 = (f32[16,128]{1,0:T(8,128)S(1)}, f32[16,128]{1,0:T(8,128)S(1)}, u32[]{:S(2)}, u32[]{:S(2)}) collective-permute-start(f32[16,128]{1,0:T(8,128)S(1)} %get-tuple-element.91), channel_id=1, source_target_pairs={{0,1},{1,0},{2,3},{3,2},{4,5},{5,4},{6,7},{7,6},{8,9},{9,8},{10,11... | collective-permute-start | bytes 24584 | tf_op jit(solution)/shard_map/ppermute | solution.py:999
  30.5 2.4 %collective-permute-start.16 = (f32[8,256]{1,0:T(8,128)S(1)}, f32[8,256]{1,0:T(8,128)S(1)}, u32[]{:S(2)}, u32[]{:S(2)}) collective-permute-start(f32[8,256]{1,0:T(8,128)S(1)} %get-tuple-element.92), channel_id=1, source_target_pairs={{0,2},{2,0},{4,6},{6,4},{1,3},{3,1},{5,7},{7,5},{8,10},{10,8},{12,... | collective-permute-start | bytes 24584 | tf_op jit(solution)/shard_map/ppermute | solution.py:984
  30.5 3.1 %collective-permute-start.17 = (f32[8,256]{1,0:T(8,128)S(1)}, f32[8,256]{1,0:T(8,128)S(1)}, u32[]{:S(2)}, u32[]{:S(2)}) collective-permute-start(f32[8,256]{1,0:T(8,128)S(1)} %get-tuple-element.93), channel_id=1, source_target_pairs={{0,6},{2,4},{4,2},{6,0},{1,7},{3,5},{5,3},{7,1},{8,14},{10,12},{12... | collective-permute-start | bytes 24584 | tf_op jit(solution)/shard_map/ppermute | solution.py:990
  31.9 7.6 %collective-permute-start.14 = (f32[3,32,256]{2,1,0:T(8,128)S(1)}, f32[3,32,256]{2,1,0:T(8,128)S(1)}, u32[]{:S(2)}, u32[]{:S(2)}) collective-permute-start(f32[3,32,256]{2,1,0:T(8,128)S(1)} %get-tuple-element.85), channel_id=1, source_target_pairs={{0,8},{8,0},{16,24},{24,16},{1,9},{9,1},{17,25},{25,17},{2,10},{10... | collective-permute-start | bytes 294920 | tf_op jit(solution)/shard_map/ppermute | solution.py:984
  33.8 6.8 %collective-permute-start.20 = (f32[32,256]{1,0:T(8,128)S(1)}, f32[32,256]{1,0:T(8,128)S(1)}, u32[]{:S(2)}, u32[]{:S(2)}) collective-permute-start(f32[32,256]{1,0:T(8,128)S(1)} %get-tuple-element.94), channel_id=1, source_target_pairs={{0,24},{8,16},{16,8},{24,0},{1,25},{9,17},{17,9},{25,1},{2,26},{10... | collective-permute-start | bytes 98312 | tf_op jit(solution)/shard_map/ppermute | solution.py:990
  35.9 4.8 %collective-permute-start.21 = (f32[32,256]{1,0:T(8,128)S(1)}, f32[32,256]{1,0:T(8,128)S(1)}, u32[]{:S(2)}, u32[]{:S(2)}) collective-permute-start(f32[32,256]{1,0:T(8,128)S(1)} %get-tuple-element.95), channel_id=1, source_target_pairs={{0,8},{8,0},{16,24},{24,16},{1,9},{9,1},{17,25},{25,17},{2,10},{10... | collective-permute-start | bytes 98312 | tf_op jit(solution)/shard_map/ppermute | solution.py:984
  36.2 4.4 %collective-permute-start.18 = (f32[16,128]{1,0:T(8,128)S(1)}, f32[16,128]{1,0:T(8,128)S(1)}, u32[]{:S(2)}, u32[]{:S(2)}) collective-permute-start(f32[16,128]{1,0:T(8,128)S(1)} %collective-permute-done.15.z_rows), channel_id=1, source_target_pairs={{0,2},{2,0},{4,6},{6,4},{1,3},{3,1},{5,7},{7,5},{8,10},{10,8},{12,... | collective-permute-start | bytes 24584 | tf_op jit(solution)/shard_map/ppermute | solution.py:984
  36.2 4.4 %collective-permute-start.19 = (f32[16,128]{1,0:T(8,128)S(1)}, f32[16,128]{1,0:T(8,128)S(1)}, u32[]{:S(2)}, u32[]{:S(2)}) collective-permute-start(f32[16,128]{1,0:T(8,128)S(1)} %collective-permute-done.15.z_rows), channel_id=1, source_target_pairs={{0,6},{2,4},{4,2},{6,0},{1,7},{3,5},{5,3},{7,1},{8,14},{10,12},{12... | collective-permute-start | bytes 24584 | tf_op jit(solution)/shard_map/ppermute | solution.py:990

commit v10 on v7

--- a/solution.py
+++ b/solution.py
@@ -105,7 +105,7 @@
     return total
 
 
-def conversions(source, kind, heading, code, *, columns):
+def conversions(source, kind, heading, code, mark, *, columns):
     count = source.shape[1]
     value = (heading[...] + 32 * kind[...]).astype(jnp.float32)
     row, column = (source[...] // columns, source[...] % columns)
@@ -114,6 +114,7 @@
     code[...] = lax.dot_general(
         by_row, by_column, (((1,), (1,)), ((), ())), preferred_element_type=jnp.float32
     )
+    mark[...] = jnp.zeros(mark.shape, jnp.float32)
 
 
 def odd(axis):
@@ -401,7 +402,7 @@
         ahead[slot] = jnp.where(flip_x, down, up)
         behind[slot] = jnp.where(flip_x, up, down)
     for comp in range(3):
-        ahead[5 + comp] = jnp.where(flip_x, flow[comp, 0], flow[comp, bx - 1])
+        behind[5 + comp] = jnp.where(flip_x, flow[comp, bx - 1], flow[comp, 0])
 
 
 def restretch_plane(x, place, stretch, flow, halos, updated):
@@ -493,8 +494,8 @@
         copy.start()
     flip_x = odd("gx")
     for comp in range(3):
-        below[comp] = jnp.where(flip_x, x_first[5 + comp], x_second[comp])
-        above[comp] = jnp.where(flip_x, x_second[comp], x_first[5 + comp])
+        below[comp] = jnp.where(flip_x, x_first[comp], x_second[5 + comp])
+        above[comp] = jnp.where(flip_x, x_second[5 + comp], x_first[comp])
     swapped_rows(y_first, y_second, range(speed_slot, sides), y_below, y_above, 0)
     z_halo[...] = row_columns(z_rows[...]).reshape(z_halo.shape)
     halos = (below, above, y_below, y_above, z_halo)
@@ -537,7 +538,7 @@
 down_edges = ((0, y_up.index(10)), (0, gas_slot), (1, y_down.index(8)), (1, gas_slot))
 
 
-def forward_edges(z_rows, y_first, y_second, first_out, second_out, corner, *, bx):
+def forward_edges(z_rows, y_first, y_second, after, first_out, second_out, corner, *, bx):
     halves = y_first.shape[1] // lanes
     flip_x, flip_y = (odd("gx"), odd("gy"))
     for half in range(halves):
@@ -782,7 +783,7 @@
     flow,
     after,
     late,
-    v_second,
+    v_first,
     settled,
     spread,
     line_first,
@@ -804,7 +805,7 @@
 
     for comp in range(3):
         up, down = (flow[comp, bx - 1], flow[comp, 0])
-        v_second[comp] = jnp.where(flip_x, up, down)
+        v_first[comp] = jnp.where(flip_x, down, up)
     for slot in range(5):
         below[slot] = jnp.where(flip_x, x_first[slot], x_second[slot])
         above[slot] = jnp.where(flip_x, x_second[slot], x_first[slot])
@@ -1061,9 +1062,9 @@
 
     entries = conv_source.shape[0]
     mark = (tall, lanes)
-    (code,) = call(
+    code, code_done = call(
         lambda *refs: conversions(*refs, columns=bz),
-        [(bx * by, bz)],
+        [(bx * by, bz), mark],
         cost=(40 * cells, 4 * cells),
     )(*(array.reshape(1, entries) for array in (conv_source, conv_kind, conv_direction)))
     code = code.reshape(box)
@@ -1087,7 +1088,7 @@
     )(pops, stretch, flow, z_first, *y_first)
     outer_post, outer_shift, z_out, x_one, x_two, y_one, y_two = call(
         collide_outer,
-        [(19, *ends), (3, *ends), columns, (8, *face), (5, *face), rows, rows],
+        [(19, *ends), (3, *ends), columns, (5, *face), (8, *face), rows, rows],
         scratch=[(4, *face), (4, *face)] + sides_y + [box],
         cost=(150 * cells, 150 * cells),
     )(pops, stretch, flags, flow, *first_x, *y_first, z_first, inner_post)
@@ -1096,8 +1097,8 @@
     post_x = swapped(x_one, x_two, "gx")
     edges = (4 * (bz // lanes) + columns[0], lanes)
     x_one, x_two, corner = call(
-        lambda *refs: forward_edges(*refs, bx=bx), [edges, edges, columns], cost=(4 * 10**9, 0)
-    )(z_post, *post_y)
+        lambda *refs: forward_edges(*refs, bx=bx), [edges, edges, columns], cost=(17 * 10**8, 0)
+    )(z_post, *post_y, code_done)
     corners = swapped(corner, corner, "gy")
     edges_x = swapped(x_one, x_two, "gx")
 
@@ -1130,7 +1131,7 @@
         scratch=[(6, *inside)] + sides_y + [pltpu.SemaphoreType.DMA],
         cost=(80 * cells, 40 * cells),
     )(stretch, flow, *post_y, z_post)
-    late, v_two, outer_settled, spread, y_one, y_two, z_out = call(
+    late, v_one, outer_settled, spread, y_one, y_two, z_out = call(
         stream_late,
         [
             (5, *ends),
@@ -1162,7 +1163,7 @@
     z_last = both_ways(z_out, 8)
     last_y = swapped(y_one, y_two, "gy")
     last_corners = swapped(z_last, z_last, "gy")
-    flow_x = (post_x[0], swapped_behind(v_two, "gx"))
+    flow_x = (swapped_ahead(v_one, "gx"), post_x[1])
     x_one, x_two = call(add_faces, [face, face], cost=(4 * 10**9, 0))(spread, z_last, *last_y)
     last_x = swapped(x_one, x_two, "gx")
     new_stretch, fresh, outer_done = call(

time: 43.1 us -> 41.1 us (0.954)
  waiting for transfers between devices: 7.46 us -> 3.71 us
  starting transfers between devices: 22.8 us -> 24.6 us
    ppermute x10 -> x9, waiting for transfers between devices: 5.01 us -> 2.08 us  [swapped_behind(): return lax.ppermute(array, axis, pairing)]
    ppermute x9 -> x10, starting transfers between devices: 3.86 us -> 6.15 us  [swapped_ahead(): return lax.ppermute(array, axis, pairing)]
    ppermute x10 -> x9, starting transfers between devices: 15.3 us -> 14 us  [swapped_behind(): return lax.ppermute(array, axis, pairing)]
    ppermute x3, starting transfers between devices: 3.59 us -> 4.38 us  [both_ways(): lax.ppermute(rows, 'gz', [(i, (i + 1) % devices) for i in range(devices)])]
    ppermute x9 -> x10, waiting for transfers between devices: 0.79 us -> 0.21 us  [swapped_ahead(): return lax.ppermute(array, axis, pairing)]
  transfers between devices with their start and end apart: 22 -> 22, of which waited for: 7 -> 9; matrix products, arithmetic and copies ran while one was open for 0% -> 0% of each run, Pallas kernels for 18% -> 19%
where the time goes in v10:
time: 41.1 us; the launch traced here: 41 us
  starting transfers between devices  24.6 us (60%)
  Pallas kernels  11.9 us (29%)
  waiting for transfers between devices  3.71 us (9%)
  between operations  0.78 us (2%)
    ppermute x9, starting transfers between devices, swapped_behind(): return lax.ppermute(array, axis, pairing)  14 us
    ppermute x10, starting transfers between devices, swapped_ahead(): return lax.ppermute(array, axis, pairing)  6.15 us
    ppermute x3, starting transfers between devices, both_ways(): lax.ppermute(rows, 'gz', [(i, (i + 1) % devices) for i in range(devices)])  4.38 us
    pallas_call x1, Pallas kernels, shards(): call(restretch_outer, [(6, *box), (19, *box), mark], specs=[pl.BlockSpec(...  2.16 us
    ppermute x9, waiting for transfers between devices, swapped_behind(): return lax.ppermute(array, axis, pairing)  2.08 us
    pallas_call x1, Pallas kernels, shards(): call(moments, [(19, *box), (5, *box)], specs=[remote], scratch=[pltpu.Sem...  1.74 us
    ppermute x3, waiting for transfers between devices, both_ways(): lax.ppermute(rows, 'gz', [(i, (i + 1) % devices) for i in range(devices)])  1.42 us
    pallas_call x1, Pallas kernels, shards(): call(first_faces, [(6, *box), jax.ShapeDtypeStruct(box, jnp.int32), (8, b...  1.38 us
  transfers between devices with their start and end apart: 22, of which 9 were waited for; matrix products, arithmetic and copies ran while one was open for 0% of the time, Pallas kernels for 19%

profile of v10, /device:TPU:0, one launch (start us, length us, event | category | flops | bytes accessed | tf_op | source)
XLA Modules:
  0.0 41.0 jit_solution(7378843007651982367)
XLA Ops:
  0.6 1.4 %shard_map.94 = (f32[6,4,32,256]{3,2,1,0:T(8,128)S(1)}, s32[4,32,256]{2,1,0:T(8,128)S(1)}, f32[8,128]{1,0:T(8,128)S(1)}, f32[16,256]{1,0:T(8,128)S(1)}, f32[16,2...) custom-call(f32[6,4,32,256]{3,2,1,0:T(8,128)} %stretch_in.1, s32[4,32,256]{2,1,0:T(8,128)} %flags_in.1), custom_call_target="tpu_custom_call" | custom-call | flops 327680 | bytes 1966080 | tf_op jit(solution)/shard_map/pallas_call | solution.py:1044
  2.0 3.1 %collective-permute-start = (f32[4,32,256]{2,1,0:T(8,128)S(1)}, f32[4,32,256]{2,1,0:T(8,128)S(1)}, u32[]{:S(2)}, u32[]{:S(2)}) collective-permute-start(f32[4,32,256]{2,1,0:T(8,128)S(1)} %get-tuple-element.55), channel_id=1, source_target_pairs={{0,8},{8,0},{16,24},{24,16},{1,9},{9,1},{17,25},{25,17},{2,10},{10... | collective-permute-start | bytes 393224 | tf_op jit(solution)/shard_map/ppermute | solution.py:990
  5.1 2.5 %collective-permute-start.1 = (f32[4,32,256]{2,1,0:T(8,128)S(1)}, f32[4,32,256]{2,1,0:T(8,128)S(1)}, u32[]{:S(2)}, u32[]{:S(2)}) collective-permute-start(f32[4,32,256]{2,1,0:T(8,128)S(1)} %get-tuple-element.56), channel_id=1, source_target_pairs={{0,24},{8,16},{16,8},{24,0},{1,25},{9,17},{17,9},{25,1},{2,26},{10... | collective-permute-start | bytes 393224 | tf_op jit(solution)/shard_map/ppermute | solution.py:996
  7.6 0.0 collective-permute-start.2
  7.6 1.6 %collective-permute-start.3 = (f32[16,256]{1,0:T(8,128)S(1)}, f32[16,256]{1,0:T(8,128)S(1)}, u32[]{:S(2)}, u32[]{:S(2)}) collective-permute-start(f32[16,256]{1,0:T(8,128)S(1)} %get-tuple-element.58), channel_id=1, source_target_pairs={{0,6},{2,4},{4,2},{6,0},{1,7},{3,5},{5,3},{7,1},{8,14},{10,12},{12... | collective-permute-start | bytes 49160 | tf_op jit(solution)/shard_map/ppermute | solution.py:996
  9.2 1.5 %collective-permute-start.4 = (f32[8,128]{1,0:T(8,128)S(1)}, f32[8,128]{1,0:T(8,128)S(1)}, u32[]{:S(2)}, u32[]{:S(2)}) collective-permute-start(f32[8,128]{1,0:T(8,128)S(1)} %get-tuple-element.59), channel_id=1, source_target_pairs={{0,1},{1,0},{2,3},{3,2},{4,5},{5,4},{6,7},{7,6},{8,9},{9,8},{10,11... | collective-permute-start | bytes 12296 | tf_op jit(solution)/shard_map/ppermute | solution.py:1005
  10.7 1.7 %shard_map.95 = (f32[19,4,32,256]{3,2,1,0:T(8,128)S(1)}, f32[5,4,32,256]{3,2,1,0:T(8,128)S(1)}) custom-call(f32[19,4,32,256]{3,2,1,0:T(8,128)} %pops_in.1), custom_call_target="tpu_custom_call" | custom-call | flops 1966080 | bytes 4915200 | tf_op jit(solution)/shard_map/pallas_call | solution.py:1072
  12.5 0.3 collective-permute-done.4.z_rows
  12.8 0.0 collective-permute-done.2.y_first
  12.8 0.0 collective-permute-done.3.y_second
  12.8 0.8 %shard_map.96 = (f32[19,2,32,256]{3,2,1,0:T(8,128)S(1)}, f32[3,2,32,256]{3,2,1,0:T(8,128)S(1)}) custom-call(f32[19,4,32,256]{3,2,1,0:T(8,128)S(1)} %get-tuple-element.53.pops, f32[6,4,32,256]{3,2,1,0:T(8,128)S(1)} %get-tuple-element.51.stretch, f32[5,4,32,256]{3,2,1,0:T(8,128)S(1)} %get-tuple-element.52.flow, f32[8,128]{1,0:T(8,128)S(1)} %collective-permute-done.4.z_rows, ...), custom_call_target="tpu_custom_call" | custom-call | flops 4915200 | bytes 4915200 | tf_op jit(solution)/shard_map/pallas_call | solution.py:1083
  13.6 0.0 collective-permute-done.x_first.gas_first
  13.6 0.1 collective-permute-done.1.x_second.gas_second
  13.7 0.0 copy-start.1
  13.7 0.0 copy-start.2
  13.7 0.0 copy-start.3
  13.7 1.0 %shard_map.97 = (f32[19,2,32,256]{3,2,1,0:T(8,128)S(1)}, f32[3,2,32,256]{3,2,1,0:T(8,128)S(1)}, f32[24,128]{1,0:T(8,128)S(1)}, f32[5,32,256]{2,1,0:T(8,128)S(1)}...) custom-call(f32[19,4,32,256]{3,2,1,0:T(8,128)S(1)} %get-tuple-element.53.pops, ...), custom_call_target="tpu_custom_call" | custom-call | flops 4915200 | bytes 4915200 | tf_op jit(solution)/shard_map/pallas_call | solution.py:1089
  14.7 1.5 %collective-permute-start.11 = (f32[8,32,256]{2,1,0:T(8,128)S(1)}, f32[8,32,256]{2,1,0:T(8,128)S(1)}, u32[]{:S(2)}, u32[]{:S(2)}) collective-permute-start(f32[8,32,256]{2,1,0:T(8,128)S(1)} %get-tuple-element.75), channel_id=1, source_target_pairs={{0,24},{8,16},{16,8},{24,0},{1,25},{9,17},{17,9},{25,1},{2,26},{10... | collective-permute-start | bytes 786440 | tf_op jit(solution)/shard_map/ppermute | solution.py:996
  16.2 0.0 collective-permute-start.5
  16.2 1.6 %collective-permute-start.6 = (f32[40,256]{1,0:T(8,128)S(1)}, f32[40,256]{1,0:T(8,128)S(1)}, u32[]{:S(2)}, u32[]{:S(2)}) collective-permute-start(f32[40,256]{1,0:T(8,128)S(1)} %get-tuple-element.66), channel_id=1, source_target_pairs={{0,6},{2,4},{4,2},{6,0},{1,7},{3,5},{5,3},{7,1},{8,14},{10,12},{12... | collective-permute-start | bytes 122888 | tf_op jit(solution)/shard_map/ppermute | solution.py:996
  17.9 1.5 %collective-permute-start.7 = (f32[24,128]{1,0:T(8,128)S(1)}, f32[24,128]{1,0:T(8,128)S(1)}, u32[]{:S(2)}, u32[]{:S(2)}) collective-permute-start(f32[24,128]{1,0:T(8,128)S(1)} %get-tuple-element.67), channel_id=1, source_target_pairs={{0,1},{1,0},{2,3},{3,2},{4,5},{5,4},{6,7},{7,6},{8,9},{9,8},{10,11... | collective-permute-start | bytes 36872 | tf_op jit(solution)/shard_map/ppermute | solution.py:1005
  19.4 0.0 copy-done.1
  19.4 0.0 copy-done.2
  19.4 0.0 copy-done.3
  19.4 0.3 shard_map.98
  19.7 0.9 %collective-permute-start.10 = (f32[5,32,256]{2,1,0:T(8,128)S(1)}, f32[5,32,256]{2,1,0:T(8,128)S(1)}, u32[]{:S(2)}, u32[]{:S(2)}) collective-permute-start(f32[5,32,256]{2,1,0:T(8,128)S(1)} %get-tuple-element.74), channel_id=1, source_target_pairs={{0,8},{8,0},{16,24},{24,16},{1,9},{9,1},{17,25},{25,17},{2,10},{10... | collective-permute-start | bytes 491528 | tf_op jit(solution)/shard_map/ppermute | solution.py:990
  20.6 0.9 %collective-permute-done.7.refs_0_.z_rows = f32[24,128]{1,0:T(8,128)S(1)} collective-permute-done((f32[24,128]{1,0:T(8,128)S(1)}, f32[24,128]{1,0:T(8,128)S(1)}, u32[]{:S(2)}, u32[]{:S(2)}) %collective-permute-start.7) | collective-permute-done | bytes 12320 | tf_op jit(solution)/shard_map/ppermute | solution.py:1005
  21.5 0.0 collective-permute-done.5.refs_1_.y_first
  21.6 0.0 collective-permute-done.6.refs_2_.y_second
  21.6 0.0 copy-start
  21.6 0.1 collective-permute-start.8
  21.7 0.9 %collective-permute-start.12 = (f32[32,128]{1,0:T(8,128)S(1)}, f32[32,128]{1,0:T(8,128)S(1)}, u32[]{:S(2)}, u32[]{:S(2)}) collective-permute-start(f32[32,128]{1,0:T(8,128)S(1)} %get-tuple-element.76), channel_id=1, source_target_pairs={{0,8},{8,0},{16,24},{24,16},{1,9},{9,1},{17,25},{25,17},{2,10},{10... | collective-permute-start | bytes 49160 | tf_op jit(solution)/shard_map/ppermute | solution.py:990
  22.6 1.8 %collective-permute-start.13 = (f32[32,128]{1,0:T(8,128)S(1)}, f32[32,128]{1,0:T(8,128)S(1)}, u32[]{:S(2)}, u32[]{:S(2)}) collective-permute-start(f32[32,128]{1,0:T(8,128)S(1)} %get-tuple-element.77), channel_id=1, source_target_pairs={{0,24},{8,16},{16,8},{24,0},{1,25},{9,17},{17,9},{25,1},{2,26},{10... | collective-permute-start | bytes 49160 | tf_op jit(solution)/shard_map/ppermute | solution.py:996
  24.3 0.0 collective-permute-done.8.corner_first
  24.3 0.0 collective-permute-start.9
  24.4 1.2 %shard_map.102 = (f32[6,4,32,256]{3,2,1,0:T(8,128)}, f32[8,128]{1,0:T(8,128)S(1)}) custom-call(f32[6,4,32,256]{3,2,1,0:T(8,128)S(1)} %get-tuple-element.51.stretch, f32[5,4,32,256]{3,2,1,0:T(8,128)S(1)} %get-tuple-element.52.flow, f32[40,256]{1,0:T(8,128)S(1)} %collective-permute-done.5.refs_1_.y_first, ...), custom_call_target="tpu_custom_call" | custom-call | flops 2621440 | bytes 1310720 | tf_op jit(solution)/shard_map/pallas_call | solution.py:1127
  25.6 0.9 %shard_map.100 = (f32[15,2,32,256]{3,2,1,0:T(8,128)S(1)}, f32[15,2,32,256]{3,2,1,0:T(8,128)S(1)}, f32[4,32,256]{2,1,0:T(8,128)S(1)}, f32[4,32,256]{2,1,0:T(8,128)S(1)}) custom-call(f32[19,2,32,256]{3,2,1,0:T(8,128)S(1)} %get-tuple-element.60.inner.inner_post, f32[19,2,32,256]{3,2,1,0:T(8,128)S(1)} %get-tuple-element.61.outer_post.post, ...), custom_call_target="tpu_custom_call" | custom-call | flops 11468800 | bytes 6553600 | tf_op jit(solution)/shard_map/pallas_call | solution.py:1107
  26.5 1.0 %collective-permute-done.9.corner_second = f32[24,128]{1,0:T(8,128)S(1)} collective-permute-done((f32[24,128]{1,0:T(8,128)S(1)}, f32[24,128]{1,0:T(8,128)S(1)}, u32[]{:S(2)}, u32[]{:S(2)}) %collective-permute-start.9) | collective-permute-done | bytes 12320 | tf_op jit(solution)/shard_map/ppermute | solution.py:996
  27.5 0.0 copy-done
  27.5 0.6 %shard_map.101 = (f32[4,2,32,256]{3,2,1,0:T(8,128)S(1)}, f32[4,2,32,256]{3,2,1,0:T(8,128)S(1)}, f32[2,32,256]{2,1,0:T(8,128)S(1)}, f32[2,32,256]{2,1,0:T(8,128)S...) custom-call(f32[19,2,32,256]{3,2,1,0:T(8,128)S(1)} %get-tuple-element.60.inner.inner_post, ...), custom_call_target="tpu_custom_call" | custom-call | flops 3276800 | bytes 1966080 | tf_op jit(solution)/shard_map/pallas_call | solution.py:1121
  28.1 0.1 collective-permute-done.12.edges_first
  28.2 0.2 collective-permute-done.13.edges_second
  28.5 0.0 collective-permute-done.10.x_first
  28.5 0.0 collective-permute-done.11.x_second
  28.5 0.8 %shard_map.103 = (f32[5,2,32,256]{3,2,1,0:T(8,128)S(1)}, f32[3,32,256]{2,1,0:T(8,128)S(1)}, f32[2,32,256]{2,1,0:T(8,128)S(1)}, f32[6,32,256]{2,1,0:T(8,128)S(1)}...) custom-call(f32[19,2,32,256]{3,2,1,0:T(8,128)S(1)} %get-tuple-element.61.outer_post.post, ...), custom_call_target="tpu_custom_call" | custom-call | flops 4915200 | bytes 3276800 | tf_op jit(solution)/shard_map/pallas_call | solution.py:1134
  29.2 1.3 %collective-permute-start.15 = (f32[16,128]{1,0:T(8,128)S(1)}, f32[16,128]{1,0:T(8,128)S(1)}, u32[]{:S(2)}, u32[]{:S(2)}) collective-permute-start(f32[16,128]{1,0:T(8,128)S(1)} %get-tuple-element.93), channel_id=1, source_target_pairs={{0,1},{1,0},{2,3},{3,2},{4,5},{5,4},{6,7},{7,6},{8,9},{9,8},{10,11... | collective-permute-start | bytes 24584 | tf_op jit(solution)/shard_map/ppermute | solution.py:1005
  30.5 0.0 collective-permute-start.16
  30.6 1.4 %collective-permute-start.17 = (f32[8,256]{1,0:T(8,128)S(1)}, f32[8,256]{1,0:T(8,128)S(1)}, u32[]{:S(2)}, u32[]{:S(2)}) collective-permute-start(f32[8,256]{1,0:T(8,128)S(1)} %get-tuple-element.95), channel_id=1, source_target_pairs={{0,6},{2,4},{4,2},{6,0},{1,7},{3,5},{5,3},{7,1},{8,14},{10,12},{12... | collective-permute-start | bytes 24584 | tf_op jit(solution)/shard_map/ppermute | solution.py:996
  31.9 0.8 %collective-permute-start.14 = (f32[3,32,256]{2,1,0:T(8,128)S(1)}, f32[3,32,256]{2,1,0:T(8,128)S(1)}, u32[]{:S(2)}, u32[]{:S(2)}) collective-permute-start(f32[3,32,256]{2,1,0:T(8,128)S(1)} %get-tuple-element.81), channel_id=1, source_target_pairs={{0,8},{8,0},{16,24},{24,16},{1,9},{9,1},{17,25},{25,17},{2,10},{10... | collective-permute-start | bytes 294920 | tf_op jit(solution)/shard_map/ppermute | solution.py:990
  32.8 0.1 collective-permute-done.15.z_rows
  32.9 0.0 collective-permute-done.16.y_first
  32.9 0.7 %collective-permute-done.17.y_second = f32[8,256]{1,0:T(8,128)S(1)} collective-permute-done((f32[8,256]{1,0:T(8,128)S(1)}, f32[8,256]{1,0:T(8,128)S(1)}, u32[]{:S(2)}, u32[]{:S(2)}) %collective-permute-start.17) | collective-permute-done | bytes 8224 | tf_op jit(solution)/shard_map/ppermute | solution.py:996
  33.6 0.2 shard_map.105
  33.8 2.1 %collective-permute-start.20 = (f32[32,256]{1,0:T(8,128)S(1)}, f32[32,256]{1,0:T(8,128)S(1)}, u32[]{:S(2)}, u32[]{:S(2)}) collective-permute-start(f32[32,256]{1,0:T(8,128)S(1)} %get-tuple-element.96), channel_id=1, source_target_pairs={{0,24},{8,16},{16,8},{24,0},{1,25},{9,17},{17,9},{25,1},{2,26},{10... | collective-permute-start | bytes 98312 | tf_op jit(solution)/shard_map/ppermute | solution.py:996
  35.9 0.3 collective-permute-start.21
  36.2 0.0 collective-permute-start.18
  36.2 1.6 %collective-permute-start.19 = (f32[16,128]{1,0:T(8,128)S(1)}, f32[16,128]{1,0:T(8,128)S(1)}, u32[]{:S(2)}, u32[]{:S(2)}) collective-permute-start(f32[16,128]{1,0:T(8,128)S(1)} %collective-permute-done.15.z_rows), channel_id=1, source_target_pairs={{0,6},{2,4},{4,2},{6,0},{1,7},{3,5},{5,3},{7,1},{8,14},{10,12},{12... | collective-permute-start | bytes 24584 | tf_op jit(solution)/shard_map/ppermute | solution.py:996
  37.8 0.0 collective-permute-done.14.x_first
  37.8 2.2 %shard_map.104 = (f32[6,4,32,256]{3,2,1,0:T(8,128)}, f32[19,4,32,256]{3,2,1,0:T(8,128)}, f32[8,128]{1,0:T(8,128)S(1)}) custom-call(f32[6,4,32,256]{3,2,1,0:T(8,128)S(1)} %get-tuple-element.51.stretch, f32[5,4,32,256]{3,2,1,0:T(8,128)S(1)} %get-tuple-element.52.flow, ...), custom_call_target="tpu_custom_call", output_to_operand_aliasing={{0}: (7, {})} | custom-call | flops 2621440 | bytes 6553600 | tf_op jit(solution)/shard_map/pallas_call | solution.py:1169
  40.0 0.0 collective-permute-done.18.corner_first
  40.0 0.0 collective-permute-done.19.corner_second
  40.0 0.0 collective-permute-done.20.x_second
  40.0 0.1 collective-permute-done.21.x_first
  40.1 0.9 %shard_map.106 = f32[4,32,256]{2,1,0:T(8,128)} custom-call(f32[2,32,256]{2,1,0:T(8,128)S(1)} %get-tuple-element.90.inner_settled, f32[2,32,256]{2,1,0:T(8,128)S(1)} %get-tuple-element.91.outer_settled, f32[6,32,256]{2,1,0:T(8,128)S(1)} %get-tuple-element.92.spread, f32[16,128]{1,0:T(8,128)S(1)} %collective-permute-done.15.z_rows, ...), custom_call_target="tpu_custom_call" | custom-call | tf_op jit(solution)/shard_map/pallas_call | solution.py:1192
  (1 shorter events, 0.0 us)
Async XLA Ops:
  2.0 11.5 %collective-permute-start = (f32[4,32,256]{2,1,0:T(8,128)S(1)}, f32[4,32,256]{2,1,0:T(8,128)S(1)}, u32[]{:S(2)}, u32[]{:S(2)}) collective-permute-start(f32[4,32,256]{2,1,0:T(8,128)S(1)} %get-tuple-element.55), channel_id=1, source_target_pairs={{0,8},{8,0},{16,24},{24,16},{1,9},{9,1},{17,25},{25,17},{2,10},{10... | collective-permute-start | bytes 393224 | tf_op jit(solution)/shard_map/ppermute | solution.py:990
  5.1 8.6 %collective-permute-start.1 = (f32[4,32,256]{2,1,0:T(8,128)S(1)}, f32[4,32,256]{2,1,0:T(8,128)S(1)}, u32[]{:S(2)}, u32[]{:S(2)}) collective-permute-start(f32[4,32,256]{2,1,0:T(8,128)S(1)} %get-tuple-element.56), channel_id=1, source_target_pairs={{0,24},{8,16},{16,8},{24,0},{1,25},{9,17},{17,9},{25,1},{2,26},{10... | collective-permute-start | bytes 393224 | tf_op jit(solution)/shard_map/ppermute | solution.py:996
  7.6 5.2 %collective-permute-start.2 = (f32[16,256]{1,0:T(8,128)S(1)}, f32[16,256]{1,0:T(8,128)S(1)}, u32[]{:S(2)}, u32[]{:S(2)}) collective-permute-start(f32[16,256]{1,0:T(8,128)S(1)} %get-tuple-element.57), channel_id=1, source_target_pairs={{0,2},{2,0},{4,6},{6,4},{1,3},{3,1},{5,7},{7,5},{8,10},{10,8},{12,... | collective-permute-start | bytes 49160 | tf_op jit(solution)/shard_map/ppermute | solution.py:990
  7.6 5.2 %collective-permute-start.3 = (f32[16,256]{1,0:T(8,128)S(1)}, f32[16,256]{1,0:T(8,128)S(1)}, u32[]{:S(2)}, u32[]{:S(2)}) collective-permute-start(f32[16,256]{1,0:T(8,128)S(1)} %get-tuple-element.58), channel_id=1, source_target_pairs={{0,6},{2,4},{4,2},{6,0},{1,7},{3,5},{5,3},{7,1},{8,14},{10,12},{12... | collective-permute-start | bytes 49160 | tf_op jit(solution)/shard_map/ppermute | solution.py:996
  9.2 3.6 %collective-permute-start.4 = (f32[8,128]{1,0:T(8,128)S(1)}, f32[8,128]{1,0:T(8,128)S(1)}, u32[]{:S(2)}, u32[]{:S(2)}) collective-permute-start(f32[8,128]{1,0:T(8,128)S(1)} %get-tuple-element.59), channel_id=1, source_target_pairs={{0,1},{1,0},{2,3},{3,2},{4,5},{5,4},{6,7},{7,6},{8,9},{9,8},{10,11... | collective-permute-start | bytes 12296 | tf_op jit(solution)/shard_map/ppermute | solution.py:1005
  13.7 5.7 %copy-start.1 = (s32[1024]{0:T(1024)S(1)}, s32[1024]{0:T(1024)}, u32[]{:S(2)}) copy-start(s32[1024]{0:T(1024)} %param.11) | copy-start | bytes 12292
  13.7 5.7 %copy-start.2 = (s32[1024]{0:T(1024)S(1)}, s32[1024]{0:T(1024)}, u32[]{:S(2)}) copy-start(s32[1024]{0:T(1024)} %param.12) | copy-start | bytes 12292
  13.7 5.7 %copy-start.3 = (s32[1024]{0:T(1024)S(1)}, s32[1024]{0:T(1024)}, u32[]{:S(2)}) copy-start(s32[1024]{0:T(1024)} %param.13) | copy-start | bytes 12292
  14.7 13.7 %collective-permute-start.11 = (f32[8,32,256]{2,1,0:T(8,128)S(1)}, f32[8,32,256]{2,1,0:T(8,128)S(1)}, u32[]{:S(2)}, u32[]{:S(2)}) collective-permute-start(f32[8,32,256]{2,1,0:T(8,128)S(1)} %get-tuple-element.75), channel_id=1, source_target_pairs={{0,24},{8,16},{16,8},{24,0},{1,25},{9,17},{17,9},{25,1},{2,26},{10... | collective-permute-start | bytes 786440 | tf_op jit(solution)/shard_map/ppermute | solution.py:996
  16.2 5.3 %collective-permute-start.5 = (f32[40,256]{1,0:T(8,128)S(1)}, f32[40,256]{1,0:T(8,128)S(1)}, u32[]{:S(2)}, u32[]{:S(2)}) collective-permute-start(f32[40,256]{1,0:T(8,128)S(1)} %get-tuple-element.65), channel_id=1, source_target_pairs={{0,2},{2,0},{4,6},{6,4},{1,3},{3,1},{5,7},{7,5},{8,10},{10,8},{12,... | collective-permute-start | bytes 122888 | tf_op jit(solution)/shard_map/ppermute | solution.py:990
  16.2 5.3 %collective-permute-start.6 = (f32[40,256]{1,0:T(8,128)S(1)}, f32[40,256]{1,0:T(8,128)S(1)}, u32[]{:S(2)}, u32[]{:S(2)}) collective-permute-start(f32[40,256]{1,0:T(8,128)S(1)} %get-tuple-element.66), channel_id=1, source_target_pairs={{0,6},{2,4},{4,2},{6,0},{1,7},{3,5},{5,3},{7,1},{8,14},{10,12},{12... | collective-permute-start | bytes 122888 | tf_op jit(solution)/shard_map/ppermute | solution.py:996
  17.9 3.7 %collective-permute-start.7 = (f32[24,128]{1,0:T(8,128)S(1)}, f32[24,128]{1,0:T(8,128)S(1)}, u32[]{:S(2)}, u32[]{:S(2)}) collective-permute-start(f32[24,128]{1,0:T(8,128)S(1)} %get-tuple-element.67), channel_id=1, source_target_pairs={{0,1},{1,0},{2,3},{3,2},{4,5},{5,4},{6,7},{7,6},{8,9},{9,8},{10,11... | collective-permute-start | bytes 36872 | tf_op jit(solution)/shard_map/ppermute | solution.py:1005
  19.7 8.7 %collective-permute-start.10 = (f32[5,32,256]{2,1,0:T(8,128)S(1)}, f32[5,32,256]{2,1,0:T(8,128)S(1)}, u32[]{:S(2)}, u32[]{:S(2)}) collective-permute-start(f32[5,32,256]{2,1,0:T(8,128)S(1)} %get-tuple-element.74), channel_id=1, source_target_pairs={{0,8},{8,0},{16,24},{24,16},{1,9},{9,1},{17,25},{25,17},{2,10},{10... | collective-permute-start | bytes 491528 | tf_op jit(solution)/shard_map/ppermute | solution.py:990
  21.6 5.9 %copy-start = (f32[4,32,256]{2,1,0:T(8,128)S(1)}, f32[4,32,256]{2,1,0:T(8,128)}, u32[]{:S(2)}) copy-start(f32[4,32,256]{2,1,0:T(8,128)} %mass.3) | copy-start | bytes 393220
  21.6 2.8 %collective-permute-start.8 = (f32[24,128]{1,0:T(8,128)S(1)}, f32[24,128]{1,0:T(8,128)S(1)}, u32[]{:S(2)}, u32[]{:S(2)}) collective-permute-start(f32[24,128]{1,0:T(8,128)S(1)} %get-tuple-element.69), channel_id=1, source_target_pairs={{0,2},{2,0},{4,6},{6,4},{1,3},{3,1},{5,7},{7,5},{8,10},{10,8},{12,... | collective-permute-start | bytes 36872 | tf_op jit(solution)/shard_map/ppermute | solution.py:990
  21.7 6.6 %collective-permute-start.12 = (f32[32,128]{1,0:T(8,128)S(1)}, f32[32,128]{1,0:T(8,128)S(1)}, u32[]{:S(2)}, u32[]{:S(2)}) collective-permute-start(f32[32,128]{1,0:T(8,128)S(1)} %get-tuple-element.76), channel_id=1, source_target_pairs={{0,8},{8,0},{16,24},{24,16},{1,9},{9,1},{17,25},{25,17},{2,10},{10... | collective-permute-start | bytes 49160 | tf_op jit(solution)/shard_map/ppermute | solution.py:990
  22.6 5.9 %collective-permute-start.13 = (f32[32,128]{1,0:T(8,128)S(1)}, f32[32,128]{1,0:T(8,128)S(1)}, u32[]{:S(2)}, u32[]{:S(2)}) collective-permute-start(f32[32,128]{1,0:T(8,128)S(1)} %get-tuple-element.77), channel_id=1, source_target_pairs={{0,24},{8,16},{16,8},{24,0},{1,25},{9,17},{17,9},{25,1},{2,26},{10... | collective-permute-start | bytes 49160 | tf_op jit(solution)/shard_map/ppermute | solution.py:996
  24.3 3.2 %collective-permute-start.9 = (f32[24,128]{1,0:T(8,128)S(1)}, f32[24,128]{1,0:T(8,128)S(1)}, u32[]{:S(2)}, u32[]{:S(2)}) collective-permute-start(f32[24,128]{1,0:T(8,128)S(1)} %get-tuple-element.69), channel_id=1, source_target_pairs={{0,6},{2,4},{4,2},{6,0},{1,7},{3,5},{5,3},{7,1},{8,14},{10,12},{12... | collective-permute-start | bytes 36872 | tf_op jit(solution)/shard_map/ppermute | solution.py:996
  29.2 3.7 %collective-permute-start.15 = (f32[16,128]{1,0:T(8,128)S(1)}, f32[16,128]{1,0:T(8,128)S(1)}, u32[]{:S(2)}, u32[]{:S(2)}) collective-permute-start(f32[16,128]{1,0:T(8,128)S(1)} %get-tuple-element.93), channel_id=1, source_target_pairs={{0,1},{1,0},{2,3},{3,2},{4,5},{5,4},{6,7},{7,6},{8,9},{9,8},{10,11... | collective-permute-start | bytes 24584 | tf_op jit(solution)/shard_map/ppermute | solution.py:1005
  30.5 2.4 %collective-permute-start.16 = (f32[8,256]{1,0:T(8,128)S(1)}, f32[8,256]{1,0:T(8,128)S(1)}, u32[]{:S(2)}, u32[]{:S(2)}) collective-permute-start(f32[8,256]{1,0:T(8,128)S(1)} %get-tuple-element.94), channel_id=1, source_target_pairs={{0,2},{2,0},{4,6},{6,4},{1,3},{3,1},{5,7},{7,5},{8,10},{10,8},{12,... | collective-permute-start | bytes 24584 | tf_op jit(solution)/shard_map/ppermute | solution.py:990
  30.6 3.1 %collective-permute-start.17 = (f32[8,256]{1,0:T(8,128)S(1)}, f32[8,256]{1,0:T(8,128)S(1)}, u32[]{:S(2)}, u32[]{:S(2)}) collective-permute-start(f32[8,256]{1,0:T(8,128)S(1)} %get-tuple-element.95), channel_id=1, source_target_pairs={{0,6},{2,4},{4,2},{6,0},{1,7},{3,5},{5,3},{7,1},{8,14},{10,12},{12... | collective-permute-start | bytes 24584 | tf_op jit(solution)/shard_map/ppermute | solution.py:996
  31.9 5.9 %collective-permute-start.14 = (f32[3,32,256]{2,1,0:T(8,128)S(1)}, f32[3,32,256]{2,1,0:T(8,128)S(1)}, u32[]{:S(2)}, u32[]{:S(2)}) collective-permute-start(f32[3,32,256]{2,1,0:T(8,128)S(1)} %get-tuple-element.81), channel_id=1, source_target_pairs={{0,8},{8,0},{16,24},{24,16},{1,9},{9,1},{17,25},{25,17},{2,10},{10... | collective-permute-start | bytes 294920 | tf_op jit(solution)/shard_map/ppermute | solution.py:990
  33.8 6.2 %collective-permute-start.20 = (f32[32,256]{1,0:T(8,128)S(1)}, f32[32,256]{1,0:T(8,128)S(1)}, u32[]{:S(2)}, u32[]{:S(2)}) collective-permute-start(f32[32,256]{1,0:T(8,128)S(1)} %get-tuple-element.96), channel_id=1, source_target_pairs={{0,24},{8,16},{16,8},{24,0},{1,25},{9,17},{17,9},{25,1},{2,26},{10... | collective-permute-start | bytes 98312 | tf_op jit(solution)/shard_map/ppermute | solution.py:996
  35.9 4.2 %collective-permute-start.21 = (f32[32,256]{1,0:T(8,128)S(1)}, f32[32,256]{1,0:T(8,128)S(1)}, u32[]{:S(2)}, u32[]{:S(2)}) collective-permute-start(f32[32,256]{1,0:T(8,128)S(1)} %get-tuple-element.97), channel_id=1, source_target_pairs={{0,8},{8,0},{16,24},{24,16},{1,9},{9,1},{17,25},{25,17},{2,10},{10... | collective-permute-start | bytes 98312 | tf_op jit(solution)/shard_map/ppermute | solution.py:990
  36.2 3.8 %collective-permute-start.18 = (f32[16,128]{1,0:T(8,128)S(1)}, f32[16,128]{1,0:T(8,128)S(1)}, u32[]{:S(2)}, u32[]{:S(2)}) collective-permute-start(f32[16,128]{1,0:T(8,128)S(1)} %collective-permute-done.15.z_rows), channel_id=1, source_target_pairs={{0,2},{2,0},{4,6},{6,4},{1,3},{3,1},{5,7},{7,5},{8,10},{10,8},{12,... | collective-permute-start | bytes 24584 | tf_op jit(solution)/shard_map/ppermute | solution.py:990
  36.2 3.8 %collective-permute-start.19 = (f32[16,128]{1,0:T(8,128)S(1)}, f32[16,128]{1,0:T(8,128)S(1)}, u32[]{:S(2)}, u32[]{:S(2)}) collective-permute-start(f32[16,128]{1,0:T(8,128)S(1)} %collective-permute-done.15.z_rows), channel_id=1, source_target_pairs={{0,6},{2,4},{4,2},{6,0},{1,7},{3,5},{5,3},{7,1},{8,14},{10,12},{12... | collective-permute-start | bytes 24584 | tf_op jit(solution)/shard_map/ppermute | solution.py:996

commit v11 on v10

--- a/solution.py
+++ b/solution.py
@@ -471,11 +471,10 @@
     y_second,
     z_rows,
     inner_stretch,
-    inner,
     outer,
-    inner_slanted,
     outer_slanted,
     late,
+    inner_fresh,
     new_stretch,
     fresh,
     mark,
@@ -489,7 +488,7 @@
     store_sems,
 ):
     bx = stretch.shape[1]
-    moves = stored(inner, outer, inner_slanted, outer_slanted, late, fresh, store_sems)
+    moves = stored(outer, outer_slanted, late, fresh, store_sems)
     for copy in moves:
         copy.start()
     flip_x = odd("gx")
@@ -511,12 +510,9 @@
         copy.wait()
 
 
-def stored(inner, outer, inner_slanted, outer_slanted, late, fresh, sems):
+def stored(outer, outer_slanted, late, fresh, sems):
     bx = fresh.shape[1]
-    moves = [
-        (inner, fresh.at[0:first_slanted, 1 : bx - 1]),
-        (inner_slanted, fresh.at[first_slanted:, 1 : bx - 1]),
-    ]
+    moves = []
     for place, x in enumerate((0, bx - 1)):
         moves.append((outer_slanted.at[:, place], fresh.at[first_slanted:, x]))
         order = (x_up, x_down)[place]
@@ -532,6 +528,23 @@
         pltpu.make_async_copy(source, target, sems.at[place])
         for place, (source, target) in enumerate(moves)
     ]
+
+
+def store_inner(inner, inner_slanted, after, fresh, mark, sems):
+    bx = fresh.shape[1]
+    copies = [
+        pltpu.make_async_copy(
+            inner, fresh.at[0:first_slanted, 1 : bx - 1], sems.at[0]
+        ),
+        pltpu.make_async_copy(
+            inner_slanted, fresh.at[first_slanted:, 1 : bx - 1], sems.at[1]
+        ),
+    ]
+    for copy in copies:
+        copy.start()
+    mark[...] = jnp.zeros(mark.shape, jnp.float32)
+    for copy in copies:
+        copy.wait()
 
 
 up_edges = ((0, y_up.index(7)), (0, gas_slot), (1, y_down.index(9)), (1, gas_slot))
@@ -933,7 +946,7 @@
     return total + jnp.where(row_at == by - 1, y_above[target : target + 1, :], 0.0)
 
 
-def add_faces(spread, z_rows, y_first, y_second, first, second):
+def add_faces(spread, z_rows, y_first, y_second, after, first, second):
     last = spread.shape[0] - 1
     flip_x, flip_y = (odd("gx"), odd("gy"))
     tile = row_columns(z_rows[...])
@@ -1164,18 +1177,28 @@
     last_y = swapped(y_one, y_two, "gy")
     last_corners = swapped(z_last, z_last, "gy")
     flow_x = (swapped_ahead(v_one, "gx"), post_x[1])
-    x_one, x_two = call(add_faces, [face, face], cost=(4 * 10**9, 0))(spread, z_last, *last_y)
+    fresh, inner_stored = call(
+        store_inner,
+        [(19, *box), mark],
+        specs=[pl.BlockSpec()] * 2 + [anywhere],
+        out_specs=[remote, pl.BlockSpec()],
+        scratch=[pltpu.SemaphoreType.DMA((2,))],
+        cost=(0, 80 * cells),
+    )(inner, inner_slanted, late)
+    x_one, x_two = call(add_faces, [face, face], cost=(4 * 10**9, 0))(
+        spread, z_last, *last_y, inner_stored
+    )
     last_x = swapped(x_one, x_two, "gx")
     new_stretch, fresh, outer_done = call(
         restretch_outer,
         [(6, *box), (19, *box), mark],
-        specs=[pl.BlockSpec()] * 7 + [remote] + [pl.BlockSpec()] * 5,
+        specs=[pl.BlockSpec()] * 7 + [remote] + [pl.BlockSpec()] * 3 + [remote],
         out_specs=[remote, remote, pl.BlockSpec()],
         scratch=[(6, *ends), (3, *face), (3, *face)]
         + sides_y
         + [pltpu.SemaphoreType.DMA((2,)), pltpu.SemaphoreType.DMA((32,))],
         cost=(80 * cells, 200 * cells),
-        aliases={7: 0},
+        aliases={7: 0, 11: 1},
     )(
         stretch,
         flow,
@@ -1183,11 +1206,10 @@
         *post_y,
         z_post,
         new_stretch,
-        inner,
         outer,
-        inner_slanted,
         outer_slanted,
         late,
+        fresh,
     )
     (new_mass,) = call(add_all, [box])(
         inner_settled, outer_settled, spread, z_last, *last_y, *last_corners, *last_x[::-1], outer_done

time: 41.1 us -> 41.7 us (1.015)
  Pallas kernels: 11.9 us -> 12.5 us
    pallas_call x0 -> x1, Pallas kernels: none -> 1.04 us  [shards(): call(store_inner, [(19, *box), mark], specs=[pl.BlockSpec()] * 2 + [anywh...]
    ppermute x10, waiting for transfers between devices: 0.21 us -> 0.95 us  [swapped_ahead(): return lax.ppermute(array, axis, pairing)]
    ppermute x9, waiting for transfers between devices: 2.08 us -> 1.58 us  [swapped_behind(): return lax.ppermute(array, axis, pairing)]
  transfers between devices with their start and end apart: 22 -> 22, of which waited for: 9 -> 8; matrix products, arithmetic and copies ran while one was open for 0% -> 0% of each run, Pallas kernels for 19% -> 21%
where the time goes in v11:
time: 41.7 us; the launch traced here: 41.5 us
  starting transfers between devices  24.4 us (59%)
  Pallas kernels  12.5 us (30%)
  waiting for transfers between devices  3.82 us (9%)
  between operations  0.8 us (2%)
    ppermute x9, starting transfers between devices, swapped_behind(): return lax.ppermute(array, axis, pairing)  14.2 us
    ppermute x10, starting transfers between devices, swapped_ahead(): return lax.ppermute(array, axis, pairing)  5.81 us
    ppermute x3, starting transfers between devices, both_ways(): lax.ppermute(rows, 'gz', [(i, (i + 1) % devices) for i in range(devices)])  4.38 us
    pallas_call x1, Pallas kernels, shards(): call(restretch_outer, [(6, *box), (19, *box), mark], specs=[pl.BlockSpec(...  1.75 us
    pallas_call x1, Pallas kernels, shards(): call(moments, [(19, *box), (5, *box)], specs=[remote], scratch=[pltpu.Sem...  1.74 us
    ppermute x9, waiting for transfers between devices, swapped_behind(): return lax.ppermute(array, axis, pairing)  1.58 us
    pallas_call x1, Pallas kernels, shards(): call(first_faces, [(6, *box), jax.ShapeDtypeStruct(box, jnp.int32), (8, b...  1.38 us
    ppermute x3, waiting for transfers between devices, both_ways(): lax.ppermute(rows, 'gz', [(i, (i + 1) % devices) for i in range(devices)])  1.28 us
  transfers between devices with their start and end apart: 22, of which 8 were waited for; matrix products, arithmetic and copies ran while one was open for 0% of the time, Pallas kernels for 21%

profile of v11, /device:TPU:0, one launch (start us, length us, event | category | flops | bytes accessed | tf_op | source)
XLA Modules:
  0.0 41.5 jit_solution(532451900746909526)
XLA Ops:
  0.6 1.4 %shard_map.94 = (f32[6,4,32,256]{3,2,1,0:T(8,128)S(1)}, s32[4,32,256]{2,1,0:T(8,128)S(1)}, f32[8,128]{1,0:T(8,128)S(1)}, f32[16,256]{1,0:T(8,128)S(1)}, f32[16,2...) custom-call(f32[6,4,32,256]{3,2,1,0:T(8,128)} %stretch_in.1, s32[4,32,256]{2,1,0:T(8,128)} %flags_in.1), custom_call_target="tpu_custom_call" | custom-call | flops 327680 | bytes 1966080 | tf_op jit(solution)/shard_map/pallas_call | solution.py:1057
  2.0 3.1 %collective-permute-start = (f32[4,32,256]{2,1,0:T(8,128)S(1)}, f32[4,32,256]{2,1,0:T(8,128)S(1)}, u32[]{:S(2)}, u32[]{:S(2)}) collective-permute-start(f32[4,32,256]{2,1,0:T(8,128)S(1)} %get-tuple-element.57), channel_id=1, source_target_pairs={{0,8},{8,0},{16,24},{24,16},{1,9},{9,1},{17,25},{25,17},{2,10},{10... | collective-permute-start | bytes 393224 | tf_op jit(solution)/shard_map/ppermute | solution.py:1003
  5.1 2.5 %collective-permute-start.1 = (f32[4,32,256]{2,1,0:T(8,128)S(1)}, f32[4,32,256]{2,1,0:T(8,128)S(1)}, u32[]{:S(2)}, u32[]{:S(2)}) collective-permute-start(f32[4,32,256]{2,1,0:T(8,128)S(1)} %get-tuple-element.58), channel_id=1, source_target_pairs={{0,24},{8,16},{16,8},{24,0},{1,25},{9,17},{17,9},{25,1},{2,26},{10... | collective-permute-start | bytes 393224 | tf_op jit(solution)/shard_map/ppermute | solution.py:1009
  7.6 0.0 collective-permute-start.2
  7.6 1.6 %collective-permute-start.3 = (f32[16,256]{1,0:T(8,128)S(1)}, f32[16,256]{1,0:T(8,128)S(1)}, u32[]{:S(2)}, u32[]{:S(2)}) collective-permute-start(f32[16,256]{1,0:T(8,128)S(1)} %get-tuple-element.60), channel_id=1, source_target_pairs={{0,6},{2,4},{4,2},{6,0},{1,7},{3,5},{5,3},{7,1},{8,14},{10,12},{12... | collective-permute-start | bytes 49160 | tf_op jit(solution)/shard_map/ppermute | solution.py:1009
  9.2 1.5 %collective-permute-start.4 = (f32[8,128]{1,0:T(8,128)S(1)}, f32[8,128]{1,0:T(8,128)S(1)}, u32[]{:S(2)}, u32[]{:S(2)}) collective-permute-start(f32[8,128]{1,0:T(8,128)S(1)} %get-tuple-element.61), channel_id=1, source_target_pairs={{0,1},{1,0},{2,3},{3,2},{4,5},{5,4},{6,7},{7,6},{8,9},{9,8},{10,11... | collective-permute-start | bytes 12296 | tf_op jit(solution)/shard_map/ppermute | solution.py:1018
  10.7 1.7 %shard_map.95 = (f32[19,4,32,256]{3,2,1,0:T(8,128)S(1)}, f32[5,4,32,256]{3,2,1,0:T(8,128)S(1)}) custom-call(f32[19,4,32,256]{3,2,1,0:T(8,128)} %pops_in.1), custom_call_target="tpu_custom_call" | custom-call | flops 1966080 | bytes 4915200 | tf_op jit(solution)/shard_map/pallas_call | solution.py:1085
  12.5 0.3 collective-permute-done.4.z_rows
  12.8 0.0 collective-permute-done.2.y_first
  12.8 0.0 collective-permute-done.3.y_second
  12.8 0.8 %shard_map.96 = (f32[19,2,32,256]{3,2,1,0:T(8,128)S(1)}, f32[3,2,32,256]{3,2,1,0:T(8,128)S(1)}) custom-call(f32[19,4,32,256]{3,2,1,0:T(8,128)S(1)} %get-tuple-element.55.pops, f32[6,4,32,256]{3,2,1,0:T(8,128)S(1)} %get-tuple-element.53.stretch, f32[5,4,32,256]{3,2,1,0:T(8,128)S(1)} %get-tuple-element.54.flow, f32[8,128]{1,0:T(8,128)S(1)} %collective-permute-done.4.z_rows, ...), custom_call_target="tpu_custom_call" | custom-call | flops 4915200 | bytes 4915200 | tf_op jit(solution)/shard_map/pallas_call | solution.py:1096
  13.6 0.0 collective-permute-done.x_first.gas_first
  13.6 0.1 collective-permute-done.1.x_second.gas_second
  13.7 0.0 copy-start.1
  13.7 0.0 copy-start.2
  13.7 1.0 %shard_map.97 = (f32[19,2,32,256]{3,2,1,0:T(8,128)S(1)}, f32[3,2,32,256]{3,2,1,0:T(8,128)S(1)}, f32[24,128]{1,0:T(8,128)S(1)}, f32[5,32,256]{2,1,0:T(8,128)S(1)}...) custom-call(f32[19,4,32,256]{3,2,1,0:T(8,128)S(1)} %get-tuple-element.55.pops, ...), custom_call_target="tpu_custom_call" | custom-call | flops 4915200 | bytes 4915200 | tf_op jit(solution)/shard_map/pallas_call | solution.py:1102
  14.7 1.5 %collective-permute-start.11 = (f32[8,32,256]{2,1,0:T(8,128)S(1)}, f32[8,32,256]{2,1,0:T(8,128)S(1)}, u32[]{:S(2)}, u32[]{:S(2)}) collective-permute-start(f32[8,32,256]{2,1,0:T(8,128)S(1)} %get-tuple-element.77), channel_id=1, source_target_pairs={{0,24},{8,16},{16,8},{24,0},{1,25},{9,17},{17,9},{25,1},{2,26},{10... | collective-permute-start | bytes 786440 | tf_op jit(solution)/shard_map/ppermute | solution.py:1009
  16.2 0.0 collective-permute-start.5
  16.2 1.6 %collective-permute-start.6 = (f32[40,256]{1,0:T(8,128)S(1)}, f32[40,256]{1,0:T(8,128)S(1)}, u32[]{:S(2)}, u32[]{:S(2)}) collective-permute-start(f32[40,256]{1,0:T(8,128)S(1)} %get-tuple-element.68), channel_id=1, source_target_pairs={{0,6},{2,4},{4,2},{6,0},{1,7},{3,5},{5,3},{7,1},{8,14},{10,12},{12... | collective-permute-start | bytes 122888 | tf_op jit(solution)/shard_map/ppermute | solution.py:1009
  17.8 1.5 %collective-permute-start.7 = (f32[24,128]{1,0:T(8,128)S(1)}, f32[24,128]{1,0:T(8,128)S(1)}, u32[]{:S(2)}, u32[]{:S(2)}) collective-permute-start(f32[24,128]{1,0:T(8,128)S(1)} %get-tuple-element.69), channel_id=1, source_target_pairs={{0,1},{1,0},{2,3},{3,2},{4,5},{5,4},{6,7},{7,6},{8,9},{9,8},{10,11... | collective-permute-start | bytes 36872 | tf_op jit(solution)/shard_map/ppermute | solution.py:1018
  19.4 0.0 copy-done.1
  19.4 0.0 copy-done.2
  19.4 0.0 copy-done.3
  19.4 0.3 shard_map.98
  19.7 0.9 %collective-permute-start.10 = (f32[5,32,256]{2,1,0:T(8,128)S(1)}, f32[5,32,256]{2,1,0:T(8,128)S(1)}, u32[]{:S(2)}, u32[]{:S(2)}) collective-permute-start(f32[5,32,256]{2,1,0:T(8,128)S(1)} %get-tuple-element.76), channel_id=1, source_target_pairs={{0,8},{8,0},{16,24},{24,16},{1,9},{9,1},{17,25},{25,17},{2,10},{10... | collective-permute-start | bytes 491528 | tf_op jit(solution)/shard_map/ppermute | solution.py:1003
  20.6 0.9 %collective-permute-done.7.refs_0_.z_rows = f32[24,128]{1,0:T(8,128)S(1)} collective-permute-done((f32[24,128]{1,0:T(8,128)S(1)}, f32[24,128]{1,0:T(8,128)S(1)}, u32[]{:S(2)}, u32[]{:S(2)}) %collective-permute-start.7) | collective-permute-done | bytes 12320 | tf_op jit(solution)/shard_map/ppermute | solution.py:1018
  21.5 0.0 collective-permute-done.5.refs_1_.y_first
  21.5 0.0 collective-permute-done.6.refs_2_.y_second
  21.6 0.0 copy-start
  21.6 0.1 collective-permute-start.8
  21.7 0.9 %collective-permute-start.12 = (f32[32,128]{1,0:T(8,128)S(1)}, f32[32,128]{1,0:T(8,128)S(1)}, u32[]{:S(2)}, u32[]{:S(2)}) collective-permute-start(f32[32,128]{1,0:T(8,128)S(1)} %get-tuple-element.78), channel_id=1, source_target_pairs={{0,8},{8,0},{16,24},{24,16},{1,9},{9,1},{17,25},{25,17},{2,10},{10... | collective-permute-start | bytes 49160 | tf_op jit(solution)/shard_map/ppermute | solution.py:1003
  22.6 1.8 %collective-permute-start.13 = (f32[32,128]{1,0:T(8,128)S(1)}, f32[32,128]{1,0:T(8,128)S(1)}, u32[]{:S(2)}, u32[]{:S(2)}) collective-permute-start(f32[32,128]{1,0:T(8,128)S(1)} %get-tuple-element.79), channel_id=1, source_target_pairs={{0,24},{8,16},{16,8},{24,0},{1,25},{9,17},{17,9},{25,1},{2,26},{10... | collective-permute-start | bytes 49160 | tf_op jit(solution)/shard_map/ppermute | solution.py:1009
  24.3 0.0 collective-permute-done.8.corner_first
  24.3 0.0 collective-permute-start.9
  24.4 1.2 %shard_map.102 = (f32[6,4,32,256]{3,2,1,0:T(8,128)}, f32[8,128]{1,0:T(8,128)S(1)}) custom-call(f32[6,4,32,256]{3,2,1,0:T(8,128)S(1)} %get-tuple-element.53.stretch, f32[5,4,32,256]{3,2,1,0:T(8,128)S(1)} %get-tuple-element.54.flow, f32[40,256]{1,0:T(8,128)S(1)} %collective-permute-done.5.refs_1_.y_first, ...), custom_call_target="tpu_custom_call" | custom-call | flops 2621440 | bytes 1310720 | tf_op jit(solution)/shard_map/pallas_call | solution.py:1140
  25.6 0.9 %shard_map.100 = (f32[15,2,32,256]{3,2,1,0:T(8,128)S(1)}, f32[15,2,32,256]{3,2,1,0:T(8,128)S(1)}, f32[4,32,256]{2,1,0:T(8,128)S(1)}, f32[4,32,256]{2,1,0:T(8,128)S(1)}) custom-call(f32[19,2,32,256]{3,2,1,0:T(8,128)S(1)} %get-tuple-element.62.inner.inner_post, f32[19,2,32,256]{3,2,1,0:T(8,128)S(1)} %get-tuple-element.63.outer_post.post, ...), custom_call_target="tpu_custom_call" | custom-call | flops 11468800 | bytes 6553600 | tf_op jit(solution)/shard_map/pallas_call | solution.py:1120
  26.5 1.0 %collective-permute-done.9.corner_second = f32[24,128]{1,0:T(8,128)S(1)} collective-permute-done((f32[24,128]{1,0:T(8,128)S(1)}, f32[24,128]{1,0:T(8,128)S(1)}, u32[]{:S(2)}, u32[]{:S(2)}) %collective-permute-start.9) | collective-permute-done | bytes 12320 | tf_op jit(solution)/shard_map/ppermute | solution.py:1009
  27.5 0.0 copy-done
  27.5 0.6 %shard_map.101 = (f32[4,2,32,256]{3,2,1,0:T(8,128)S(1)}, f32[4,2,32,256]{3,2,1,0:T(8,128)S(1)}, f32[2,32,256]{2,1,0:T(8,128)S(1)}, f32[2,32,256]{2,1,0:T(8,128)S...) custom-call(f32[19,2,32,256]{3,2,1,0:T(8,128)S(1)} %get-tuple-element.62.inner.inner_post, ...), custom_call_target="tpu_custom_call" | custom-call | flops 3276800 | bytes 1966080 | tf_op jit(solution)/shard_map/pallas_call | solution.py:1134
  28.1 0.1 collective-permute-done.12.edges_first
  28.2 0.2 collective-permute-done.13.edges_second
  28.4 0.0 collective-permute-done.10.x_first
  28.5 0.0 collective-permute-done.11.x_second
  28.5 0.8 %shard_map.103 = (f32[5,2,32,256]{3,2,1,0:T(8,128)S(1)}, f32[3,32,256]{2,1,0:T(8,128)S(1)}, f32[2,32,256]{2,1,0:T(8,128)S(1)}, f32[6,32,256]{2,1,0:T(8,128)S(1)}...) custom-call(f32[19,2,32,256]{3,2,1,0:T(8,128)S(1)} %get-tuple-element.63.outer_post.post, ...), custom_call_target="tpu_custom_call" | custom-call | flops 4915200 | bytes 3276800 | tf_op jit(solution)/shard_map/pallas_call | solution.py:1147
  29.2 1.3 %collective-permute-start.15 = (f32[16,128]{1,0:T(8,128)S(1)}, f32[16,128]{1,0:T(8,128)S(1)}, u32[]{:S(2)}, u32[]{:S(2)}) collective-permute-start(f32[16,128]{1,0:T(8,128)S(1)} %get-tuple-element.96), channel_id=1, source_target_pairs={{0,1},{1,0},{2,3},{3,2},{4,5},{5,4},{6,7},{7,6},{8,9},{9,8},{10,11... | collective-permute-start | bytes 24584 | tf_op jit(solution)/shard_map/ppermute | solution.py:1018
  30.5 0.0 collective-permute-start.16
  30.5 1.4 %collective-permute-start.17 = (f32[8,256]{1,0:T(8,128)S(1)}, f32[8,256]{1,0:T(8,128)S(1)}, u32[]{:S(2)}, u32[]{:S(2)}) collective-permute-start(f32[8,256]{1,0:T(8,128)S(1)} %get-tuple-element.98), channel_id=1, source_target_pairs={{0,6},{2,4},{4,2},{6,0},{1,7},{3,5},{5,3},{7,1},{8,14},{10,12},{12... | collective-permute-start | bytes 24584 | tf_op jit(solution)/shard_map/ppermute | solution.py:1009
  31.9 0.8 %collective-permute-start.14 = (f32[3,32,256]{2,1,0:T(8,128)S(1)}, f32[3,32,256]{2,1,0:T(8,128)S(1)}, u32[]{:S(2)}, u32[]{:S(2)}) collective-permute-start(f32[3,32,256]{2,1,0:T(8,128)S(1)} %get-tuple-element.83), channel_id=1, source_target_pairs={{0,8},{8,0},{16,24},{24,16},{1,9},{9,1},{17,25},{25,17},{2,10},{10... | collective-permute-start | bytes 294920 | tf_op jit(solution)/shard_map/ppermute | solution.py:1003
  32.8 1.0 %shard_map.104 = (f32[19,4,32,256]{3,2,1,0:T(8,128)}, f32[8,128]{1,0:T(8,128)S(1)}) custom-call(f32[15,2,32,256]{3,2,1,0:T(8,128)S(1)} %get-tuple-element.88.inner, f32[4,2,32,256]{3,2,1,0:T(8,128)S(1)} %get-tuple-element.89.inner_slanted, f32[5,2,32,256]{3,2,1,0:T(8,128)S(1)} %get-tuple-element.87.after.late), custom_call_target="tpu_custom_call" | custom-call | bytes 2621440 | tf_op jit(solution)/shard_map/pallas_call | solution.py:1180
  33.8 0.0 collective-permute-done.15.z_rows
  33.8 0.0 collective-permute-done.16.y_first
  33.8 0.0 collective-permute-done.17.y_second
  33.8 0.2 shard_map.106
  34.0 2.7 %collective-permute-start.20 = (f32[32,256]{1,0:T(8,128)S(1)}, f32[32,256]{1,0:T(8,128)S(1)}, u32[]{:S(2)}, u32[]{:S(2)}) collective-permute-start(f32[32,256]{1,0:T(8,128)S(1)} %get-tuple-element.100), channel_id=1, source_target_pairs={{0,24},{8,16},{16,8},{24,0},{1,25},{9,17},{17,9},{25,1},{2,26},{10... | collective-permute-start | bytes 98312 | tf_op jit(solution)/shard_map/ppermute | solution.py:1009
  36.7 0.0 collective-permute-start.21
  36.7 0.0 collective-permute-start.18
  36.7 1.1 %collective-permute-start.19 = (f32[16,128]{1,0:T(8,128)S(1)}, f32[16,128]{1,0:T(8,128)S(1)}, u32[]{:S(2)}, u32[]{:S(2)}) collective-permute-start(f32[16,128]{1,0:T(8,128)S(1)} %collective-permute-done.15.z_rows), channel_id=1, source_target_pairs={{0,6},{2,4},{4,2},{6,0},{1,7},{3,5},{5,3},{7,1},{8,14},{10,12},{12... | collective-permute-start | bytes 24584 | tf_op jit(solution)/shard_map/ppermute | solution.py:1009
  37.8 0.0 collective-permute-done.14.x_first
  37.8 1.8 %shard_map.105 = (f32[6,4,32,256]{3,2,1,0:T(8,128)}, f32[19,4,32,256]{3,2,1,0:T(8,128)}, f32[8,128]{1,0:T(8,128)S(1)}) custom-call(f32[6,4,32,256]{3,2,1,0:T(8,128)S(1)} %get-tuple-element.53.stretch, f32[5,4,32,256]{3,2,1,0:T(8,128)S(1)} %get-tuple-element.54.flow, ...), custom_call_target="tpu_custom_call", output_to_operand_aliasing={{0}: (7, {}), {1}: (11, {})} | custom-call | flops 2621440 | bytes 6553600 | tf_op jit(solution)/shard_map/pallas_call | solution.py:1192
  39.6 0.0 collective-permute-done.18.corner_first
  39.6 0.2 collective-permute-done.19.corner_second
  39.8 0.0 collective-permute-done.20.x_second
  39.8 0.8 %collective-permute-done.21.x_first = f32[32,256]{1,0:T(8,128)S(1)} collective-permute-done((f32[32,256]{1,0:T(8,128)S(1)}, f32[32,256]{1,0:T(8,128)S(1)}, u32[]{:S(2)}, u32[]{:S(2)}) %collective-permute-start.21) | collective-permute-done | bytes 32800 | tf_op jit(solution)/shard_map/ppermute | solution.py:1003
  40.6 0.9 %shard_map.107 = f32[4,32,256]{2,1,0:T(8,128)} custom-call(f32[2,32,256]{2,1,0:T(8,128)S(1)} %get-tuple-element.93.inner_settled, f32[2,32,256]{2,1,0:T(8,128)S(1)} %get-tuple-element.94.outer_settled, f32[6,32,256]{2,1,0:T(8,128)S(1)} %get-tuple-element.95.spread, f32[16,128]{1,0:T(8,128)S(1)} %collective-permute-done.15.z_rows, ...), custom_call_target="tpu_custom_call" | custom-call | tf_op jit(solution)/shard_map/pallas_call | solution.py:1214
  (2 shorter events, 0.0 us)
Async XLA Ops:
  2.0 11.5 %collective-permute-start = (f32[4,32,256]{2,1,0:T(8,128)S(1)}, f32[4,32,256]{2,1,0:T(8,128)S(1)}, u32[]{:S(2)}, u32[]{:S(2)}) collective-permute-start(f32[4,32,256]{2,1,0:T(8,128)S(1)} %get-tuple-element.57), channel_id=1, source_target_pairs={{0,8},{8,0},{16,24},{24,16},{1,9},{9,1},{17,25},{25,17},{2,10},{10... | collective-permute-start | bytes 393224 | tf_op jit(solution)/shard_map/ppermute | solution.py:1003
  5.1 8.6 %collective-permute-start.1 = (f32[4,32,256]{2,1,0:T(8,128)S(1)}, f32[4,32,256]{2,1,0:T(8,128)S(1)}, u32[]{:S(2)}, u32[]{:S(2)}) collective-permute-start(f32[4,32,256]{2,1,0:T(8,128)S(1)} %get-tuple-element.58), channel_id=1, source_target_pairs={{0,24},{8,16},{16,8},{24,0},{1,25},{9,17},{17,9},{25,1},{2,26},{10... | collective-permute-start | bytes 393224 | tf_op jit(solution)/shard_map/ppermute | solution.py:1009
  7.6 5.2 %collective-permute-start.2 = (f32[16,256]{1,0:T(8,128)S(1)}, f32[16,256]{1,0:T(8,128)S(1)}, u32[]{:S(2)}, u32[]{:S(2)}) collective-permute-start(f32[16,256]{1,0:T(8,128)S(1)} %get-tuple-element.59), channel_id=1, source_target_pairs={{0,2},{2,0},{4,6},{6,4},{1,3},{3,1},{5,7},{7,5},{8,10},{10,8},{12,... | collective-permute-start | bytes 49160 | tf_op jit(solution)/shard_map/ppermute | solution.py:1003
  7.6 5.2 %collective-permute-start.3 = (f32[16,256]{1,0:T(8,128)S(1)}, f32[16,256]{1,0:T(8,128)S(1)}, u32[]{:S(2)}, u32[]{:S(2)}) collective-permute-start(f32[16,256]{1,0:T(8,128)S(1)} %get-tuple-element.60), channel_id=1, source_target_pairs={{0,6},{2,4},{4,2},{6,0},{1,7},{3,5},{5,3},{7,1},{8,14},{10,12},{12... | collective-permute-start | bytes 49160 | tf_op jit(solution)/shard_map/ppermute | solution.py:1009
  9.2 3.6 %collective-permute-start.4 = (f32[8,128]{1,0:T(8,128)S(1)}, f32[8,128]{1,0:T(8,128)S(1)}, u32[]{:S(2)}, u32[]{:S(2)}) collective-permute-start(f32[8,128]{1,0:T(8,128)S(1)} %get-tuple-element.61), channel_id=1, source_target_pairs={{0,1},{1,0},{2,3},{3,2},{4,5},{5,4},{6,7},{7,6},{8,9},{9,8},{10,11... | collective-permute-start | bytes 12296 | tf_op jit(solution)/shard_map/ppermute | solution.py:1018
  13.7 5.7 %copy-start.1 = (s32[1024]{0:T(1024)S(1)}, s32[1024]{0:T(1024)}, u32[]{:S(2)}) copy-start(s32[1024]{0:T(1024)} %param.11) | copy-start | bytes 12292
  13.7 5.7 %copy-start.2 = (s32[1024]{0:T(1024)S(1)}, s32[1024]{0:T(1024)}, u32[]{:S(2)}) copy-start(s32[1024]{0:T(1024)} %param.12) | copy-start | bytes 12292
  13.7 5.7 %copy-start.3 = (s32[1024]{0:T(1024)S(1)}, s32[1024]{0:T(1024)}, u32[]{:S(2)}) copy-start(s32[1024]{0:T(1024)} %param.13) | copy-start | bytes 12292
  14.7 13.7 %collective-permute-start.11 = (f32[8,32,256]{2,1,0:T(8,128)S(1)}, f32[8,32,256]{2,1,0:T(8,128)S(1)}, u32[]{:S(2)}, u32[]{:S(2)}) collective-permute-start(f32[8,32,256]{2,1,0:T(8,128)S(1)} %get-tuple-element.77), channel_id=1, source_target_pairs={{0,24},{8,16},{16,8},{24,0},{1,25},{9,17},{17,9},{25,1},{2,26},{10... | collective-permute-start | bytes 786440 | tf_op jit(solution)/shard_map/ppermute | solution.py:1009
  16.2 5.3 %collective-permute-start.5 = (f32[40,256]{1,0:T(8,128)S(1)}, f32[40,256]{1,0:T(8,128)S(1)}, u32[]{:S(2)}, u32[]{:S(2)}) collective-permute-start(f32[40,256]{1,0:T(8,128)S(1)} %get-tuple-element.67), channel_id=1, source_target_pairs={{0,2},{2,0},{4,6},{6,4},{1,3},{3,1},{5,7},{7,5},{8,10},{10,8},{12,... | collective-permute-start | bytes 122888 | tf_op jit(solution)/shard_map/ppermute | solution.py:1003
  16.2 5.3 %collective-permute-start.6 = (f32[40,256]{1,0:T(8,128)S(1)}, f32[40,256]{1,0:T(8,128)S(1)}, u32[]{:S(2)}, u32[]{:S(2)}) collective-permute-start(f32[40,256]{1,0:T(8,128)S(1)} %get-tuple-element.68), channel_id=1, source_target_pairs={{0,6},{2,4},{4,2},{6,0},{1,7},{3,5},{5,3},{7,1},{8,14},{10,12},{12... | collective-permute-start | bytes 122888 | tf_op jit(solution)/shard_map/ppermute | solution.py:1009
  17.8 3.7 %collective-permute-start.7 = (f32[24,128]{1,0:T(8,128)S(1)}, f32[24,128]{1,0:T(8,128)S(1)}, u32[]{:S(2)}, u32[]{:S(2)}) collective-permute-start(f32[24,128]{1,0:T(8,128)S(1)} %get-tuple-element.69), channel_id=1, source_target_pairs={{0,1},{1,0},{2,3},{3,2},{4,5},{5,4},{6,7},{7,6},{8,9},{9,8},{10,11... | collective-permute-start | bytes 36872 | tf_op jit(solution)/shard_map/ppermute | solution.py:1018
  19.7 8.7 %collective-permute-start.10 = (f32[5,32,256]{2,1,0:T(8,128)S(1)}, f32[5,32,256]{2,1,0:T(8,128)S(1)}, u32[]{:S(2)}, u32[]{:S(2)}) collective-permute-start(f32[5,32,256]{2,1,0:T(8,128)S(1)} %get-tuple-element.76), channel_id=1, source_target_pairs={{0,8},{8,0},{16,24},{24,16},{1,9},{9,1},{17,25},{25,17},{2,10},{10... | collective-permute-start | bytes 491528 | tf_op jit(solution)/shard_map/ppermute | solution.py:1003
  21.6 6.0 %copy-start = (f32[4,32,256]{2,1,0:T(8,128)S(1)}, f32[4,32,256]{2,1,0:T(8,128)}, u32[]{:S(2)}) copy-start(f32[4,32,256]{2,1,0:T(8,128)} %mass.3) | copy-start | bytes 393220
  21.6 2.8 %collective-permute-start.8 = (f32[24,128]{1,0:T(8,128)S(1)}, f32[24,128]{1,0:T(8,128)S(1)}, u32[]{:S(2)}, u32[]{:S(2)}) collective-permute-start(f32[24,128]{1,0:T(8,128)S(1)} %get-tuple-element.71), channel_id=1, source_target_pairs={{0,2},{2,0},{4,6},{6,4},{1,3},{3,1},{5,7},{7,5},{8,10},{10,8},{12,... | collective-permute-start | bytes 36872 | tf_op jit(solution)/shard_map/ppermute | solution.py:1003
  21.7 6.6 %collective-permute-start.12 = (f32[32,128]{1,0:T(8,128)S(1)}, f32[32,128]{1,0:T(8,128)S(1)}, u32[]{:S(2)}, u32[]{:S(2)}) collective-permute-start(f32[32,128]{1,0:T(8,128)S(1)} %get-tuple-element.78), channel_id=1, source_target_pairs={{0,8},{8,0},{16,24},{24,16},{1,9},{9,1},{17,25},{25,17},{2,10},{10... | collective-permute-start | bytes 49160 | tf_op jit(solution)/shard_map/ppermute | solution.py:1003
  22.6 5.9 %collective-permute-start.13 = (f32[32,128]{1,0:T(8,128)S(1)}, f32[32,128]{1,0:T(8,128)S(1)}, u32[]{:S(2)}, u32[]{:S(2)}) collective-permute-start(f32[32,128]{1,0:T(8,128)S(1)} %get-tuple-element.79), channel_id=1, source_target_pairs={{0,24},{8,16},{16,8},{24,0},{1,25},{9,17},{17,9},{25,1},{2,26},{10... | collective-permute-start | bytes 49160 | tf_op jit(solution)/shard_map/ppermute | solution.py:1009
  24.3 3.2 %collective-permute-start.9 = (f32[24,128]{1,0:T(8,128)S(1)}, f32[24,128]{1,0:T(8,128)S(1)}, u32[]{:S(2)}, u32[]{:S(2)}) collective-permute-start(f32[24,128]{1,0:T(8,128)S(1)} %get-tuple-element.71), channel_id=1, source_target_pairs={{0,6},{2,4},{4,2},{6,0},{1,7},{3,5},{5,3},{7,1},{8,14},{10,12},{12... | collective-permute-start | bytes 36872 | tf_op jit(solution)/shard_map/ppermute | solution.py:1009
  29.2 4.6 %collective-permute-start.15 = (f32[16,128]{1,0:T(8,128)S(1)}, f32[16,128]{1,0:T(8,128)S(1)}, u32[]{:S(2)}, u32[]{:S(2)}) collective-permute-start(f32[16,128]{1,0:T(8,128)S(1)} %get-tuple-element.96), channel_id=1, source_target_pairs={{0,1},{1,0},{2,3},{3,2},{4,5},{5,4},{6,7},{7,6},{8,9},{9,8},{10,11... | collective-permute-start | bytes 24584 | tf_op jit(solution)/shard_map/ppermute | solution.py:1018
  30.5 3.3 %collective-permute-start.16 = (f32[8,256]{1,0:T(8,128)S(1)}, f32[8,256]{1,0:T(8,128)S(1)}, u32[]{:S(2)}, u32[]{:S(2)}) collective-permute-start(f32[8,256]{1,0:T(8,128)S(1)} %get-tuple-element.97), channel_id=1, source_target_pairs={{0,2},{2,0},{4,6},{6,4},{1,3},{3,1},{5,7},{7,5},{8,10},{10,8},{12,... | collective-permute-start | bytes 24584 | tf_op jit(solution)/shard_map/ppermute | solution.py:1003
  30.5 3.3 %collective-permute-start.17 = (f32[8,256]{1,0:T(8,128)S(1)}, f32[8,256]{1,0:T(8,128)S(1)}, u32[]{:S(2)}, u32[]{:S(2)}) collective-permute-start(f32[8,256]{1,0:T(8,128)S(1)} %get-tuple-element.98), channel_id=1, source_target_pairs={{0,6},{2,4},{4,2},{6,0},{1,7},{3,5},{5,3},{7,1},{8,14},{10,12},{12... | collective-permute-start | bytes 24584 | tf_op jit(solution)/shard_map/ppermute | solution.py:1009
  31.9 5.9 %collective-permute-start.14 = (f32[3,32,256]{2,1,0:T(8,128)S(1)}, f32[3,32,256]{2,1,0:T(8,128)S(1)}, u32[]{:S(2)}, u32[]{:S(2)}) collective-permute-start(f32[3,32,256]{2,1,0:T(8,128)S(1)} %get-tuple-element.83), channel_id=1, source_target_pairs={{0,8},{8,0},{16,24},{24,16},{1,9},{9,1},{17,25},{25,17},{2,10},{10... | collective-permute-start | bytes 294920 | tf_op jit(solution)/shard_map/ppermute | solution.py:1003
  34.0 5.8 %collective-permute-start.20 = (f32[32,256]{1,0:T(8,128)S(1)}, f32[32,256]{1,0:T(8,128)S(1)}, u32[]{:S(2)}, u32[]{:S(2)}) collective-permute-start(f32[32,256]{1,0:T(8,128)S(1)} %get-tuple-element.100), channel_id=1, source_target_pairs={{0,24},{8,16},{16,8},{24,0},{1,25},{9,17},{17,9},{25,1},{2,26},{10... | collective-permute-start | bytes 98312 | tf_op jit(solution)/shard_map/ppermute | solution.py:1009
  36.7 3.9 %collective-permute-start.21 = (f32[32,256]{1,0:T(8,128)S(1)}, f32[32,256]{1,0:T(8,128)S(1)}, u32[]{:S(2)}, u32[]{:S(2)}) collective-permute-start(f32[32,256]{1,0:T(8,128)S(1)} %get-tuple-element.101), channel_id=1, source_target_pairs={{0,8},{8,0},{16,24},{24,16},{1,9},{9,1},{17,25},{25,17},{2,10},{10... | collective-permute-start | bytes 98312 | tf_op jit(solution)/shard_map/ppermute | solution.py:1003
  36.7 2.9 %collective-permute-start.18 = (f32[16,128]{1,0:T(8,128)S(1)}, f32[16,128]{1,0:T(8,128)S(1)}, u32[]{:S(2)}, u32[]{:S(2)}) collective-permute-start(f32[16,128]{1,0:T(8,128)S(1)} %collective-permute-done.15.z_rows), channel_id=1, source_target_pairs={{0,2},{2,0},{4,6},{6,4},{1,3},{3,1},{5,7},{7,5},{8,10},{10,8},{12,... | collective-permute-start | bytes 24584 | tf_op jit(solution)/shard_map/ppermute | solution.py:1003
  36.7 3.1 %collective-permute-start.19 = (f32[16,128]{1,0:T(8,128)S(1)}, f32[16,128]{1,0:T(8,128)S(1)}, u32[]{:S(2)}, u32[]{:S(2)}) collective-permute-start(f32[16,128]{1,0:T(8,128)S(1)} %collective-permute-done.15.z_rows), channel_id=1, source_target_pairs={{0,6},{2,4},{4,2},{6,0},{1,7},{3,5},{5,3},{7,1},{8,14},{10,12},{12... | collective-permute-start | bytes 24584 | tf_op jit(solution)/shard_map/ppermute | solution.py:1009

commit v12 on v10

--- a/solution.py
+++ b/solution.py
@@ -471,11 +471,11 @@
     y_second,
     z_rows,
     inner_stretch,
-    inner,
     outer,
     inner_slanted,
     outer_slanted,
     late,
+    inner_fresh,
     new_stretch,
     fresh,
     mark,
@@ -489,7 +489,7 @@
     store_sems,
 ):
     bx = stretch.shape[1]
-    moves = stored(inner, outer, inner_slanted, outer_slanted, late, fresh, store_sems)
+    moves = stored(outer, inner_slanted, outer_slanted, late, fresh, store_sems)
     for copy in moves:
         copy.start()
     flip_x = odd("gx")
@@ -511,12 +511,9 @@
         copy.wait()
 
 
-def stored(inner, outer, inner_slanted, outer_slanted, late, fresh, sems):
+def stored(outer, inner_slanted, outer_slanted, late, fresh, sems):
     bx = fresh.shape[1]
-    moves = [
-        (inner, fresh.at[0:first_slanted, 1 : bx - 1]),
-        (inner_slanted, fresh.at[first_slanted:, 1 : bx - 1]),
-    ]
+    moves = [(inner_slanted, fresh.at[first_slanted:, 1 : bx - 1])]
     for place, x in enumerate((0, bx - 1)):
         moves.append((outer_slanted.at[:, place], fresh.at[first_slanted:, x]))
         order = (x_up, x_down)[place]
@@ -532,6 +529,13 @@
         pltpu.make_async_copy(source, target, sems.at[place])
         for place, (source, target) in enumerate(moves)
     ]
+
+
+def store_inner(inner, fresh, mark, sem):
+    copy = pltpu.make_async_copy(inner, fresh.at[0:first_slanted, 1 : fresh.shape[1] - 1], sem)
+    copy.start()
+    mark[...] = jnp.zeros(mark.shape, jnp.float32)
+    copy.wait()
 
 
 up_edges = ((0, y_up.index(7)), (0, gas_slot), (1, y_down.index(9)), (1, gas_slot))
@@ -720,6 +724,7 @@
     corner_second,
     totals,
     changes,
+    after,
     inner,
     outer,
     settled,
@@ -1110,6 +1115,13 @@
         scratch=rims,
         cost=(350 * cells, 200 * cells),
     )(*posts, flags, *post_y, z_post)
+    fresh, inner_stored = call(
+        store_inner,
+        [(19, *box), mark],
+        out_specs=[remote, pl.BlockSpec()],
+        scratch=[pltpu.SemaphoreType.DMA],
+        cost=(0, 60 * cells),
+    )(inner)
     (
         inner_slanted,
         outer_slanted,
@@ -1123,7 +1135,7 @@
         [(4, *inside), (4, *ends), inside, inside, inside, ends, ends],
         scratch=rims,
         cost=(100 * cells, 60 * cells),
-    )(*posts, mass, flags, code, *post_y, z_post, *corners, totals, changes)
+    )(*posts, mass, flags, code, *post_y, z_post, *corners, totals, changes, inner_stored)
     new_stretch, inner_done = call(
         restretch_inner,
         [(6, *box), mark],
@@ -1164,18 +1176,20 @@
     last_y = swapped(y_one, y_two, "gy")
     last_corners = swapped(z_last, z_last, "gy")
     flow_x = (swapped_ahead(v_one, "gx"), post_x[1])
-    x_one, x_two = call(add_faces, [face, face], cost=(4 * 10**9, 0))(spread, z_last, *last_y)
+    x_one, x_two = call(add_faces, [face, face], cost=(4 * 10**9, 0))(
+        spread, z_last, *last_y
+    )
     last_x = swapped(x_one, x_two, "gx")
     new_stretch, fresh, outer_done = call(
         restretch_outer,
         [(6, *box), (19, *box), mark],
-        specs=[pl.BlockSpec()] * 7 + [remote] + [pl.BlockSpec()] * 5,
+        specs=[pl.BlockSpec()] * 7 + [remote] + [pl.BlockSpec()] * 4 + [remote],
         out_specs=[remote, remote, pl.BlockSpec()],
         scratch=[(6, *ends), (3, *face), (3, *face)]
         + sides_y
         + [pltpu.SemaphoreType.DMA((2,)), pltpu.SemaphoreType.DMA((32,))],
         cost=(80 * cells, 200 * cells),
-        aliases={7: 0},
+        aliases={7: 0, 12: 1},
     )(
         stretch,
         flow,
@@ -1183,11 +1197,11 @@
         *post_y,
         z_post,
         new_stretch,
-        inner,
         outer,
         inner_slanted,
         outer_slanted,
         late,
+        fresh,
     )
     (new_mass,) = call(add_all, [box])(
         inner_settled, outer_settled, spread, z_last, *last_y, *last_corners, *last_x[::-1], outer_done

time: 41.1 us -> 41.2 us (level)
  waiting for transfers between devices: 3.71 us -> 3.07 us
  Pallas kernels: 11.9 us -> 12.5 us
    pallas_call x0 -> x1, Pallas kernels: none -> 0.96 us  [shards(): call(store_inner, [(19, *box), mark], out_specs=[remote, pl.BlockSpec()],...]
    ppermute x9, waiting for transfers between devices: 2.08 us -> 1.3 us  [swapped_behind(): return lax.ppermute(array, axis, pairing)]
  transfers between devices with their start and end apart: 22 -> 22, of which waited for: 9 -> 8; matrix products, arithmetic and copies ran while one was open for 0% -> 0% of each run, Pallas kernels for 19% -> 21%
where the time goes in v12:
time: 41.2 us; the launch traced here: 41 us
  starting transfers between devices  24.7 us (60%)
  Pallas kernels  12.5 us (30%)
  waiting for transfers between devices  3.07 us (7%)
  between operations  0.77 us (2%)
    ppermute x9, starting transfers between devices, swapped_behind(): return lax.ppermute(array, axis, pairing)  14.4 us
    ppermute x10, starting transfers between devices, swapped_ahead(): return lax.ppermute(array, axis, pairing)  5.94 us
    ppermute x3, starting transfers between devices, both_ways(): lax.ppermute(rows, 'gz', [(i, (i + 1) % devices) for i in range(devices)])  4.37 us
    pallas_call x1, Pallas kernels, shards(): call(restretch_outer, [(6, *box), (19, *box), mark], specs=[pl.BlockSpec(...  1.84 us
    pallas_call x1, Pallas kernels, shards(): call(moments, [(19, *box), (5, *box)], specs=[remote], scratch=[pltpu.Sem...  1.74 us
    pallas_call x1, Pallas kernels, shards(): call(first_faces, [(6, *box), jax.ShapeDtypeStruct(box, jnp.int32), (8, b...  1.38 us
    ppermute x9, waiting for transfers between devices, swapped_behind(): return lax.ppermute(array, axis, pairing)  1.3 us
    ppermute x3, waiting for transfers between devices, both_ways(): lax.ppermute(rows, 'gz', [(i, (i + 1) % devices) for i in range(devices)])  1.28 us
  transfers between devices with their start and end apart: 22, of which 8 were waited for; matrix products, arithmetic and copies ran while one was open for 0% of the time, Pallas kernels for 21%

profile of v12, /device:TPU:0, one launch (start us, length us, event | category | flops | bytes accessed | tf_op | source)
XLA Modules:
  0.0 41.0 jit_solution(12446152623289051725)
XLA Ops:
  0.6 1.4 %shard_map.94 = (f32[6,4,32,256]{3,2,1,0:T(8,128)S(1)}, s32[4,32,256]{2,1,0:T(8,128)S(1)}, f32[8,128]{1,0:T(8,128)S(1)}, f32[16,256]{1,0:T(8,128)S(1)}, f32[16,2...) custom-call(f32[6,4,32,256]{3,2,1,0:T(8,128)} %stretch_in.1, s32[4,32,256]{2,1,0:T(8,128)} %flags_in.1), custom_call_target="tpu_custom_call" | custom-call | flops 327680 | bytes 1966080 | tf_op jit(solution)/shard_map/pallas_call | solution.py:1049
  2.0 3.1 %collective-permute-start = (f32[4,32,256]{2,1,0:T(8,128)S(1)}, f32[4,32,256]{2,1,0:T(8,128)S(1)}, u32[]{:S(2)}, u32[]{:S(2)}) collective-permute-start(f32[4,32,256]{2,1,0:T(8,128)S(1)} %get-tuple-element.57), channel_id=1, source_target_pairs={{0,8},{8,0},{16,24},{24,16},{1,9},{9,1},{17,25},{25,17},{2,10},{10... | collective-permute-start | bytes 393224 | tf_op jit(solution)/shard_map/ppermute | solution.py:995
  5.1 2.5 %collective-permute-start.1 = (f32[4,32,256]{2,1,0:T(8,128)S(1)}, f32[4,32,256]{2,1,0:T(8,128)S(1)}, u32[]{:S(2)}, u32[]{:S(2)}) collective-permute-start(f32[4,32,256]{2,1,0:T(8,128)S(1)} %get-tuple-element.58), channel_id=1, source_target_pairs={{0,24},{8,16},{16,8},{24,0},{1,25},{9,17},{17,9},{25,1},{2,26},{10... | collective-permute-start | bytes 393224 | tf_op jit(solution)/shard_map/ppermute | solution.py:1001
  7.6 0.0 collective-permute-start.2
  7.6 1.6 %collective-permute-start.3 = (f32[16,256]{1,0:T(8,128)S(1)}, f32[16,256]{1,0:T(8,128)S(1)}, u32[]{:S(2)}, u32[]{:S(2)}) collective-permute-start(f32[16,256]{1,0:T(8,128)S(1)} %get-tuple-element.60), channel_id=1, source_target_pairs={{0,6},{2,4},{4,2},{6,0},{1,7},{3,5},{5,3},{7,1},{8,14},{10,12},{12... | collective-permute-start | bytes 49160 | tf_op jit(solution)/shard_map/ppermute | solution.py:1001
  9.2 1.5 %collective-permute-start.4 = (f32[8,128]{1,0:T(8,128)S(1)}, f32[8,128]{1,0:T(8,128)S(1)}, u32[]{:S(2)}, u32[]{:S(2)}) collective-permute-start(f32[8,128]{1,0:T(8,128)S(1)} %get-tuple-element.61), channel_id=1, source_target_pairs={{0,1},{1,0},{2,3},{3,2},{4,5},{5,4},{6,7},{7,6},{8,9},{9,8},{10,11... | collective-permute-start | bytes 12296 | tf_op jit(solution)/shard_map/ppermute | solution.py:1010
  10.7 1.7 %shard_map.95 = (f32[19,4,32,256]{3,2,1,0:T(8,128)S(1)}, f32[5,4,32,256]{3,2,1,0:T(8,128)S(1)}) custom-call(f32[19,4,32,256]{3,2,1,0:T(8,128)} %pops_in.1), custom_call_target="tpu_custom_call" | custom-call | flops 1966080 | bytes 4915200 | tf_op jit(solution)/shard_map/pallas_call | solution.py:1077
  12.5 0.3 collective-permute-done.4.z_rows
  12.8 0.0 collective-permute-done.2.y_first
  12.8 0.0 collective-permute-done.3.y_second
  12.8 0.8 %shard_map.96 = (f32[19,2,32,256]{3,2,1,0:T(8,128)S(1)}, f32[3,2,32,256]{3,2,1,0:T(8,128)S(1)}) custom-call(f32[19,4,32,256]{3,2,1,0:T(8,128)S(1)} %get-tuple-element.55.pops, f32[6,4,32,256]{3,2,1,0:T(8,128)S(1)} %get-tuple-element.53.stretch, f32[5,4,32,256]{3,2,1,0:T(8,128)S(1)} %get-tuple-element.54.flow, f32[8,128]{1,0:T(8,128)S(1)} %collective-permute-done.4.z_rows, ...), custom_call_target="tpu_custom_call" | custom-call | flops 4915200 | bytes 4915200 | tf_op jit(solution)/shard_map/pallas_call | solution.py:1088
  13.6 0.0 collective-permute-done.x_first.gas_first
  13.6 0.1 collective-permute-done.1.x_second.gas_second
  13.7 0.0 copy-start.1
  13.7 0.0 copy-start.2
  13.7 0.0 copy-start.3
  13.7 1.0 %shard_map.97 = (f32[19,2,32,256]{3,2,1,0:T(8,128)S(1)}, f32[3,2,32,256]{3,2,1,0:T(8,128)S(1)}, f32[24,128]{1,0:T(8,128)S(1)}, f32[5,32,256]{2,1,0:T(8,128)S(1)}...) custom-call(f32[19,4,32,256]{3,2,1,0:T(8,128)S(1)} %get-tuple-element.55.pops, ...), custom_call_target="tpu_custom_call" | custom-call | flops 4915200 | bytes 4915200 | tf_op jit(solution)/shard_map/pallas_call | solution.py:1094
  14.7 1.5 %collective-permute-start.11 = (f32[8,32,256]{2,1,0:T(8,128)S(1)}, f32[8,32,256]{2,1,0:T(8,128)S(1)}, u32[]{:S(2)}, u32[]{:S(2)}) collective-permute-start(f32[8,32,256]{2,1,0:T(8,128)S(1)} %get-tuple-element.79), channel_id=1, source_target_pairs={{0,24},{8,16},{16,8},{24,0},{1,25},{9,17},{17,9},{25,1},{2,26},{10... | collective-permute-start | bytes 786440 | tf_op jit(solution)/shard_map/ppermute | solution.py:1001
  16.2 0.0 collective-permute-start.5
  16.2 1.6 %collective-permute-start.6 = (f32[40,256]{1,0:T(8,128)S(1)}, f32[40,256]{1,0:T(8,128)S(1)}, u32[]{:S(2)}, u32[]{:S(2)}) collective-permute-start(f32[40,256]{1,0:T(8,128)S(1)} %get-tuple-element.68), channel_id=1, source_target_pairs={{0,6},{2,4},{4,2},{6,0},{1,7},{3,5},{5,3},{7,1},{8,14},{10,12},{12... | collective-permute-start | bytes 122888 | tf_op jit(solution)/shard_map/ppermute | solution.py:1001
  17.8 1.5 %collective-permute-start.7 = (f32[24,128]{1,0:T(8,128)S(1)}, f32[24,128]{1,0:T(8,128)S(1)}, u32[]{:S(2)}, u32[]{:S(2)}) collective-permute-start(f32[24,128]{1,0:T(8,128)S(1)} %get-tuple-element.69), channel_id=1, source_target_pairs={{0,1},{1,0},{2,3},{3,2},{4,5},{5,4},{6,7},{7,6},{8,9},{9,8},{10,11... | collective-permute-start | bytes 36872 | tf_op jit(solution)/shard_map/ppermute | solution.py:1010
  19.4 0.0 copy-done.1
  19.4 0.0 copy-done.2
  19.4 0.0 copy-done.3
  19.4 0.3 shard_map.98
  19.7 0.9 %collective-permute-start.10 = (f32[5,32,256]{2,1,0:T(8,128)S(1)}, f32[5,32,256]{2,1,0:T(8,128)S(1)}, u32[]{:S(2)}, u32[]{:S(2)}) collective-permute-start(f32[5,32,256]{2,1,0:T(8,128)S(1)} %get-tuple-element.78), channel_id=1, source_target_pairs={{0,8},{8,0},{16,24},{24,16},{1,9},{9,1},{17,25},{25,17},{2,10},{10... | collective-permute-start | bytes 491528 | tf_op jit(solution)/shard_map/ppermute | solution.py:995
  20.6 0.9 %collective-permute-done.7.refs_0_.z_rows = f32[24,128]{1,0:T(8,128)S(1)} collective-permute-done((f32[24,128]{1,0:T(8,128)S(1)}, f32[24,128]{1,0:T(8,128)S(1)}, u32[]{:S(2)}, u32[]{:S(2)}) %collective-permute-start.7) | collective-permute-done | bytes 12320 | tf_op jit(solution)/shard_map/ppermute | solution.py:1010
  21.5 0.0 collective-permute-done.5.refs_1_.y_first
  21.5 0.0 collective-permute-done.6.refs_2_.y_second
  21.6 0.1 collective-permute-start.8
  21.7 0.9 %collective-permute-start.12 = (f32[32,128]{1,0:T(8,128)S(1)}, f32[32,128]{1,0:T(8,128)S(1)}, u32[]{:S(2)}, u32[]{:S(2)}) collective-permute-start(f32[32,128]{1,0:T(8,128)S(1)} %get-tuple-element.80), channel_id=1, source_target_pairs={{0,8},{8,0},{16,24},{24,16},{1,9},{9,1},{17,25},{25,17},{2,10},{10... | collective-permute-start | bytes 49160 | tf_op jit(solution)/shard_map/ppermute | solution.py:995
  22.6 1.8 %collective-permute-start.13 = (f32[32,128]{1,0:T(8,128)S(1)}, f32[32,128]{1,0:T(8,128)S(1)}, u32[]{:S(2)}, u32[]{:S(2)}) collective-permute-start(f32[32,128]{1,0:T(8,128)S(1)} %get-tuple-element.81), channel_id=1, source_target_pairs={{0,24},{8,16},{16,8},{24,0},{1,25},{9,17},{17,9},{25,1},{2,26},{10... | collective-permute-start | bytes 49160 | tf_op jit(solution)/shard_map/ppermute | solution.py:1001
  24.3 0.0 collective-permute-done.8.corner_first
  24.3 0.0 collective-permute-start.9
  24.4 0.9 %shard_map.100 = (f32[15,2,32,256]{3,2,1,0:T(8,128)S(1)}, f32[15,2,32,256]{3,2,1,0:T(8,128)S(1)}, f32[4,32,256]{2,1,0:T(8,128)S(1)}, f32[4,32,256]{2,1,0:T(8,128)S(1)}) custom-call(f32[19,2,32,256]{3,2,1,0:T(8,128)S(1)} %get-tuple-element.62.inner.inner_post, f32[19,2,32,256]{3,2,1,0:T(8,128)S(1)} %get-tuple-element.63.outer_post.post, ...), custom_call_target="tpu_custom_call" | custom-call | flops 11468800 | bytes 6553600 | tf_op jit(solution)/shard_map/pallas_call | solution.py:1112
  25.3 1.0 %shard_map.101 = (f32[19,4,32,256]{3,2,1,0:T(8,128)}, f32[8,128]{1,0:T(8,128)S(1)}) custom-call(f32[15,2,32,256]{3,2,1,0:T(8,128)S(1)} %get-tuple-element.74.inner), custom_call_target="tpu_custom_call" | custom-call | bytes 1966080 | tf_op jit(solution)/shard_map/pallas_call | solution.py:1118
  26.3 1.2 %shard_map.103 = (f32[6,4,32,256]{3,2,1,0:T(8,128)}, f32[8,128]{1,0:T(8,128)S(1)}) custom-call(f32[6,4,32,256]{3,2,1,0:T(8,128)S(1)} %get-tuple-element.53.stretch, f32[5,4,32,256]{3,2,1,0:T(8,128)S(1)} %get-tuple-element.54.flow, f32[40,256]{1,0:T(8,128)S(1)} %collective-permute-done.5.refs_1_.y_first, ...), custom_call_target="tpu_custom_call" | custom-call | flops 2621440 | bytes 1310720 | tf_op jit(solution)/shard_map/pallas_call | solution.py:1139
  27.5 0.0 collective-permute-done.9.corner_second
  27.5 0.0 copy-done
  27.5 0.6 %shard_map.102 = (f32[4,2,32,256]{3,2,1,0:T(8,128)S(1)}, f32[4,2,32,256]{3,2,1,0:T(8,128)S(1)}, f32[2,32,256]{2,1,0:T(8,128)S(1)}, f32[2,32,256]{2,1,0:T(8,128)S...) custom-call(f32[19,2,32,256]{3,2,1,0:T(8,128)S(1)} %get-tuple-element.62.inner.inner_post, ...), custom_call_target="tpu_custom_call" | custom-call | flops 3276800 | bytes 1966080 | tf_op jit(solution)/shard_map/pallas_call | solution.py:1133
  28.1 0.1 collective-permute-done.12.edges_first
  28.2 0.2 collective-permute-done.13.edges_second
  28.4 0.0 collective-permute-done.10.x_first
  28.5 0.0 collective-permute-done.11.x_second
  28.5 0.8 %shard_map.104 = (f32[5,2,32,256]{3,2,1,0:T(8,128)S(1)}, f32[3,32,256]{2,1,0:T(8,128)S(1)}, f32[2,32,256]{2,1,0:T(8,128)S(1)}, f32[6,32,256]{2,1,0:T(8,128)S(1)}...) custom-call(f32[19,2,32,256]{3,2,1,0:T(8,128)S(1)} %get-tuple-element.63.outer_post.post, ...), custom_call_target="tpu_custom_call" | custom-call | flops 4915200 | bytes 3276800 | tf_op jit(solution)/shard_map/pallas_call | solution.py:1146
  29.2 1.3 %collective-permute-start.15 = (f32[16,128]{1,0:T(8,128)S(1)}, f32[16,128]{1,0:T(8,128)S(1)}, u32[]{:S(2)}, u32[]{:S(2)}) collective-permute-start(f32[16,128]{1,0:T(8,128)S(1)} %get-tuple-element.97), channel_id=1, source_target_pairs={{0,1},{1,0},{2,3},{3,2},{4,5},{5,4},{6,7},{7,6},{8,9},{9,8},{10,11... | collective-permute-start | bytes 24584 | tf_op jit(solution)/shard_map/ppermute | solution.py:1010
  30.5 0.1 collective-permute-start.16
  30.6 1.5 %collective-permute-start.17 = (f32[8,256]{1,0:T(8,128)S(1)}, f32[8,256]{1,0:T(8,128)S(1)}, u32[]{:S(2)}, u32[]{:S(2)}) collective-permute-start(f32[8,256]{1,0:T(8,128)S(1)} %get-tuple-element.99), channel_id=1, source_target_pairs={{0,6},{2,4},{4,2},{6,0},{1,7},{3,5},{5,3},{7,1},{8,14},{10,12},{12... | collective-permute-start | bytes 24584 | tf_op jit(solution)/shard_map/ppermute | solution.py:1001
  32.1 0.9 %collective-permute-start.14 = (f32[3,32,256]{2,1,0:T(8,128)S(1)}, f32[3,32,256]{2,1,0:T(8,128)S(1)}, u32[]{:S(2)}, u32[]{:S(2)}) collective-permute-start(f32[3,32,256]{2,1,0:T(8,128)S(1)} %get-tuple-element.85), channel_id=1, source_target_pairs={{0,8},{8,0},{16,24},{24,16},{1,9},{9,1},{17,25},{25,17},{2,10},{10... | collective-permute-start | bytes 294920 | tf_op jit(solution)/shard_map/ppermute | solution.py:995
  32.9 0.0 collective-permute-done.15.z_rows
  32.9 0.0 collective-permute-done.16.y_first
  32.9 0.8 %collective-permute-done.17.y_second = f32[8,256]{1,0:T(8,128)S(1)} collective-permute-done((f32[8,256]{1,0:T(8,128)S(1)}, f32[8,256]{1,0:T(8,128)S(1)}, u32[]{:S(2)}, u32[]{:S(2)}) %collective-permute-start.17) | collective-permute-done | bytes 8224 | tf_op jit(solution)/shard_map/ppermute | solution.py:1001
  33.7 0.2 shard_map.106
  33.9 2.3 %collective-permute-start.20 = (f32[32,256]{1,0:T(8,128)S(1)}, f32[32,256]{1,0:T(8,128)S(1)}, u32[]{:S(2)}, u32[]{:S(2)}) collective-permute-start(f32[32,256]{1,0:T(8,128)S(1)} %get-tuple-element.100), channel_id=1, source_target_pairs={{0,24},{8,16},{16,8},{24,0},{1,25},{9,17},{17,9},{25,1},{2,26},{10... | collective-permute-start | bytes 98312 | tf_op jit(solution)/shard_map/ppermute | solution.py:1001
  36.2 0.0 collective-permute-start.21
  36.2 0.0 collective-permute-start.18
  36.2 1.6 %collective-permute-start.19 = (f32[16,128]{1,0:T(8,128)S(1)}, f32[16,128]{1,0:T(8,128)S(1)}, u32[]{:S(2)}, u32[]{:S(2)}) collective-permute-start(f32[16,128]{1,0:T(8,128)S(1)} %collective-permute-done.15.z_rows), channel_id=1, source_target_pairs={{0,6},{2,4},{4,2},{6,0},{1,7},{3,5},{5,3},{7,1},{8,14},{10,12},{12... | collective-permute-start | bytes 24584 | tf_op jit(solution)/shard_map/ppermute | solution.py:1001
  37.8 0.0 collective-permute-done.14.x_first
  37.8 1.8 %shard_map.105 = (f32[6,4,32,256]{3,2,1,0:T(8,128)}, f32[19,4,32,256]{3,2,1,0:T(8,128)}, f32[8,128]{1,0:T(8,128)S(1)}) custom-call(f32[6,4,32,256]{3,2,1,0:T(8,128)S(1)} %get-tuple-element.53.stretch, f32[5,4,32,256]{3,2,1,0:T(8,128)S(1)} %get-tuple-element.54.flow, ...), custom_call_target="tpu_custom_call", output_to_operand_aliasing={{0}: (7, {}), {1}: (12, {})} | custom-call | flops 2621440 | bytes 6553600 | tf_op jit(solution)/shard_map/pallas_call | solution.py:1183
  39.7 0.0 collective-permute-done.18.corner_first
  39.7 0.0 collective-permute-done.19.corner_second
  39.7 0.1 collective-permute-done.20.x_second
  39.8 0.3 collective-permute-done.21.x_first
  40.2 0.9 %shard_map.107 = f32[4,32,256]{2,1,0:T(8,128)} custom-call(f32[2,32,256]{2,1,0:T(8,128)S(1)} %get-tuple-element.94.inner_settled, f32[2,32,256]{2,1,0:T(8,128)S(1)} %get-tuple-element.95.outer_settled, f32[6,32,256]{2,1,0:T(8,128)S(1)} %get-tuple-element.96.spread, f32[16,128]{1,0:T(8,128)S(1)} %collective-permute-done.15.z_rows, ...), custom_call_target="tpu_custom_call" | custom-call | tf_op jit(solution)/shard_map/pallas_call | solution.py:1206
  (2 shorter events, 0.0 us)
Async XLA Ops:
  2.0 11.6 %collective-permute-start = (f32[4,32,256]{2,1,0:T(8,128)S(1)}, f32[4,32,256]{2,1,0:T(8,128)S(1)}, u32[]{:S(2)}, u32[]{:S(2)}) collective-permute-start(f32[4,32,256]{2,1,0:T(8,128)S(1)} %get-tuple-element.57), channel_id=1, source_target_pairs={{0,8},{8,0},{16,24},{24,16},{1,9},{9,1},{17,25},{25,17},{2,10},{10... | collective-permute-start | bytes 393224 | tf_op jit(solution)/shard_map/ppermute | solution.py:995
  5.1 8.6 %collective-permute-start.1 = (f32[4,32,256]{2,1,0:T(8,128)S(1)}, f32[4,32,256]{2,1,0:T(8,128)S(1)}, u32[]{:S(2)}, u32[]{:S(2)}) collective-permute-start(f32[4,32,256]{2,1,0:T(8,128)S(1)} %get-tuple-element.58), channel_id=1, source_target_pairs={{0,24},{8,16},{16,8},{24,0},{1,25},{9,17},{17,9},{25,1},{2,26},{10... | collective-permute-start | bytes 393224 | tf_op jit(solution)/shard_map/ppermute | solution.py:1001
  7.6 5.2 %collective-permute-start.2 = (f32[16,256]{1,0:T(8,128)S(1)}, f32[16,256]{1,0:T(8,128)S(1)}, u32[]{:S(2)}, u32[]{:S(2)}) collective-permute-start(f32[16,256]{1,0:T(8,128)S(1)} %get-tuple-element.59), channel_id=1, source_target_pairs={{0,2},{2,0},{4,6},{6,4},{1,3},{3,1},{5,7},{7,5},{8,10},{10,8},{12,... | collective-permute-start | bytes 49160 | tf_op jit(solution)/shard_map/ppermute | solution.py:995
  7.6 5.2 %collective-permute-start.3 = (f32[16,256]{1,0:T(8,128)S(1)}, f32[16,256]{1,0:T(8,128)S(1)}, u32[]{:S(2)}, u32[]{:S(2)}) collective-permute-start(f32[16,256]{1,0:T(8,128)S(1)} %get-tuple-element.60), channel_id=1, source_target_pairs={{0,6},{2,4},{4,2},{6,0},{1,7},{3,5},{5,3},{7,1},{8,14},{10,12},{12... | collective-permute-start | bytes 49160 | tf_op jit(solution)/shard_map/ppermute | solution.py:1001
  9.2 3.6 %collective-permute-start.4 = (f32[8,128]{1,0:T(8,128)S(1)}, f32[8,128]{1,0:T(8,128)S(1)}, u32[]{:S(2)}, u32[]{:S(2)}) collective-permute-start(f32[8,128]{1,0:T(8,128)S(1)} %get-tuple-element.61), channel_id=1, source_target_pairs={{0,1},{1,0},{2,3},{3,2},{4,5},{5,4},{6,7},{7,6},{8,9},{9,8},{10,11... | collective-permute-start | bytes 12296 | tf_op jit(solution)/shard_map/ppermute | solution.py:1010
  13.7 5.7 %copy-start.1 = (s32[1024]{0:T(1024)S(1)}, s32[1024]{0:T(1024)}, u32[]{:S(2)}) copy-start(s32[1024]{0:T(1024)} %param.11) | copy-start | bytes 12292
  13.7 5.7 %copy-start.2 = (s32[1024]{0:T(1024)S(1)}, s32[1024]{0:T(1024)}, u32[]{:S(2)}) copy-start(s32[1024]{0:T(1024)} %param.12) | copy-start | bytes 12292
  13.7 5.7 %copy-start.3 = (s32[1024]{0:T(1024)S(1)}, s32[1024]{0:T(1024)}, u32[]{:S(2)}) copy-start(s32[1024]{0:T(1024)} %param.13) | copy-start | bytes 12292
  14.7 13.7 %collective-permute-start.11 = (f32[8,32,256]{2,1,0:T(8,128)S(1)}, f32[8,32,256]{2,1,0:T(8,128)S(1)}, u32[]{:S(2)}, u32[]{:S(2)}) collective-permute-start(f32[8,32,256]{2,1,0:T(8,128)S(1)} %get-tuple-element.79), channel_id=1, source_target_pairs={{0,24},{8,16},{16,8},{24,0},{1,25},{9,17},{17,9},{25,1},{2,26},{10... | collective-permute-start | bytes 786440 | tf_op jit(solution)/shard_map/ppermute | solution.py:1001
  16.2 5.3 %collective-permute-start.5 = (f32[40,256]{1,0:T(8,128)S(1)}, f32[40,256]{1,0:T(8,128)S(1)}, u32[]{:S(2)}, u32[]{:S(2)}) collective-permute-start(f32[40,256]{1,0:T(8,128)S(1)} %get-tuple-element.67), channel_id=1, source_target_pairs={{0,2},{2,0},{4,6},{6,4},{1,3},{3,1},{5,7},{7,5},{8,10},{10,8},{12,... | collective-permute-start | bytes 122888 | tf_op jit(solution)/shard_map/ppermute | solution.py:995
  16.2 5.3 %collective-permute-start.6 = (f32[40,256]{1,0:T(8,128)S(1)}, f32[40,256]{1,0:T(8,128)S(1)}, u32[]{:S(2)}, u32[]{:S(2)}) collective-permute-start(f32[40,256]{1,0:T(8,128)S(1)} %get-tuple-element.68), channel_id=1, source_target_pairs={{0,6},{2,4},{4,2},{6,0},{1,7},{3,5},{5,3},{7,1},{8,14},{10,12},{12... | collective-permute-start | bytes 122888 | tf_op jit(solution)/shard_map/ppermute | solution.py:1001
  17.8 3.7 %collective-permute-start.7 = (f32[24,128]{1,0:T(8,128)S(1)}, f32[24,128]{1,0:T(8,128)S(1)}, u32[]{:S(2)}, u32[]{:S(2)}) collective-permute-start(f32[24,128]{1,0:T(8,128)S(1)} %get-tuple-element.69), channel_id=1, source_target_pairs={{0,1},{1,0},{2,3},{3,2},{4,5},{5,4},{6,7},{7,6},{8,9},{9,8},{10,11... | collective-permute-start | bytes 36872 | tf_op jit(solution)/shard_map/ppermute | solution.py:1010
  19.7 8.7 %collective-permute-start.10 = (f32[5,32,256]{2,1,0:T(8,128)S(1)}, f32[5,32,256]{2,1,0:T(8,128)S(1)}, u32[]{:S(2)}, u32[]{:S(2)}) collective-permute-start(f32[5,32,256]{2,1,0:T(8,128)S(1)} %get-tuple-element.78), channel_id=1, source_target_pairs={{0,8},{8,0},{16,24},{24,16},{1,9},{9,1},{17,25},{25,17},{2,10},{10... | collective-permute-start | bytes 491528 | tf_op jit(solution)/shard_map/ppermute | solution.py:995
  21.6 2.8 %collective-permute-start.8 = (f32[24,128]{1,0:T(8,128)S(1)}, f32[24,128]{1,0:T(8,128)S(1)}, u32[]{:S(2)}, u32[]{:S(2)}) collective-permute-start(f32[24,128]{1,0:T(8,128)S(1)} %get-tuple-element.71), channel_id=1, source_target_pairs={{0,2},{2,0},{4,6},{6,4},{1,3},{3,1},{5,7},{7,5},{8,10},{10,8},{12,... | collective-permute-start | bytes 36872 | tf_op jit(solution)/shard_map/ppermute | solution.py:995
  21.7 6.6 %collective-permute-start.12 = (f32[32,128]{1,0:T(8,128)S(1)}, f32[32,128]{1,0:T(8,128)S(1)}, u32[]{:S(2)}, u32[]{:S(2)}) collective-permute-start(f32[32,128]{1,0:T(8,128)S(1)} %get-tuple-element.80), channel_id=1, source_target_pairs={{0,8},{8,0},{16,24},{24,16},{1,9},{9,1},{17,25},{25,17},{2,10},{10... | collective-permute-start | bytes 49160 | tf_op jit(solution)/shard_map/ppermute | solution.py:995
  22.6 5.9 %collective-permute-start.13 = (f32[32,128]{1,0:T(8,128)S(1)}, f32[32,128]{1,0:T(8,128)S(1)}, u32[]{:S(2)}, u32[]{:S(2)}) collective-permute-start(f32[32,128]{1,0:T(8,128)S(1)} %get-tuple-element.81), channel_id=1, source_target_pairs={{0,24},{8,16},{16,8},{24,0},{1,25},{9,17},{17,9},{25,1},{2,26},{10... | collective-permute-start | bytes 49160 | tf_op jit(solution)/shard_map/ppermute | solution.py:1001
  24.3 3.2 %collective-permute-start.9 = (f32[24,128]{1,0:T(8,128)S(1)}, f32[24,128]{1,0:T(8,128)S(1)}, u32[]{:S(2)}, u32[]{:S(2)}) collective-permute-start(f32[24,128]{1,0:T(8,128)S(1)} %get-tuple-element.71), channel_id=1, source_target_pairs={{0,6},{2,4},{4,2},{6,0},{1,7},{3,5},{5,3},{7,1},{8,14},{10,12},{12... | collective-permute-start | bytes 36872 | tf_op jit(solution)/shard_map/ppermute | solution.py:1001
  24.4 3.2 %copy-start = (f32[4,32,256]{2,1,0:T(8,128)S(1)}, f32[4,32,256]{2,1,0:T(8,128)}, u32[]{:S(2)}) copy-start(f32[4,32,256]{2,1,0:T(8,128)} %mass.3) | copy-start | bytes 393220
  29.2 3.7 %collective-permute-start.15 = (f32[16,128]{1,0:T(8,128)S(1)}, f32[16,128]{1,0:T(8,128)S(1)}, u32[]{:S(2)}, u32[]{:S(2)}) collective-permute-start(f32[16,128]{1,0:T(8,128)S(1)} %get-tuple-element.97), channel_id=1, source_target_pairs={{0,1},{1,0},{2,3},{3,2},{4,5},{5,4},{6,7},{7,6},{8,9},{9,8},{10,11... | collective-permute-start | bytes 24584 | tf_op jit(solution)/shard_map/ppermute | solution.py:1010
  30.5 2.4 %collective-permute-start.16 = (f32[8,256]{1,0:T(8,128)S(1)}, f32[8,256]{1,0:T(8,128)S(1)}, u32[]{:S(2)}, u32[]{:S(2)}) collective-permute-start(f32[8,256]{1,0:T(8,128)S(1)} %get-tuple-element.98), channel_id=1, source_target_pairs={{0,2},{2,0},{4,6},{6,4},{1,3},{3,1},{5,7},{7,5},{8,10},{10,8},{12,... | collective-permute-start | bytes 24584 | tf_op jit(solution)/shard_map/ppermute | solution.py:995
  30.6 3.1 %collective-permute-start.17 = (f32[8,256]{1,0:T(8,128)S(1)}, f32[8,256]{1,0:T(8,128)S(1)}, u32[]{:S(2)}, u32[]{:S(2)}) collective-permute-start(f32[8,256]{1,0:T(8,128)S(1)} %get-tuple-element.99), channel_id=1, source_target_pairs={{0,6},{2,4},{4,2},{6,0},{1,7},{3,5},{5,3},{7,1},{8,14},{10,12},{12... | collective-permute-start | bytes 24584 | tf_op jit(solution)/shard_map/ppermute | solution.py:1001
  32.1 5.8 %collective-permute-start.14 = (f32[3,32,256]{2,1,0:T(8,128)S(1)}, f32[3,32,256]{2,1,0:T(8,128)S(1)}, u32[]{:S(2)}, u32[]{:S(2)}) collective-permute-start(f32[3,32,256]{2,1,0:T(8,128)S(1)} %get-tuple-element.85), channel_id=1, source_target_pairs={{0,8},{8,0},{16,24},{24,16},{1,9},{9,1},{17,25},{25,17},{2,10},{10... | collective-permute-start | bytes 294920 | tf_op jit(solution)/shard_map/ppermute | solution.py:995
  33.9 6.0 %collective-permute-start.20 = (f32[32,256]{1,0:T(8,128)S(1)}, f32[32,256]{1,0:T(8,128)S(1)}, u32[]{:S(2)}, u32[]{:S(2)}) collective-permute-start(f32[32,256]{1,0:T(8,128)S(1)} %get-tuple-element.100), channel_id=1, source_target_pairs={{0,24},{8,16},{16,8},{24,0},{1,25},{9,17},{17,9},{25,1},{2,26},{10... | collective-permute-start | bytes 98312 | tf_op jit(solution)/shard_map/ppermute | solution.py:1001
  36.2 4.0 %collective-permute-start.21 = (f32[32,256]{1,0:T(8,128)S(1)}, f32[32,256]{1,0:T(8,128)S(1)}, u32[]{:S(2)}, u32[]{:S(2)}) collective-permute-start(f32[32,256]{1,0:T(8,128)S(1)} %get-tuple-element.101), channel_id=1, source_target_pairs={{0,8},{8,0},{16,24},{24,16},{1,9},{9,1},{17,25},{25,17},{2,10},{10... | collective-permute-start | bytes 98312 | tf_op jit(solution)/shard_map/ppermute | solution.py:995
  36.2 3.5 %collective-permute-start.18 = (f32[16,128]{1,0:T(8,128)S(1)}, f32[16,128]{1,0:T(8,128)S(1)}, u32[]{:S(2)}, u32[]{:S(2)}) collective-permute-start(f32[16,128]{1,0:T(8,128)S(1)} %collective-permute-done.15.z_rows), channel_id=1, source_target_pairs={{0,2},{2,0},{4,6},{6,4},{1,3},{3,1},{5,7},{7,5},{8,10},{10,8},{12,... | collective-permute-start | bytes 24584 | tf_op jit(solution)/shard_map/ppermute | solution.py:995
  36.2 3.5 %collective-permute-start.19 = (f32[16,128]{1,0:T(8,128)S(1)}, f32[16,128]{1,0:T(8,128)S(1)}, u32[]{:S(2)}, u32[]{:S(2)}) collective-permute-start(f32[16,128]{1,0:T(8,128)S(1)} %collective-permute-done.15.z_rows), channel_id=1, source_target_pairs={{0,6},{2,4},{4,2},{6,0},{1,7},{3,5},{5,3},{7,1},{8,14},{10,12},{12... | collective-permute-start | bytes 24584 | tf_op jit(solution)/shard_map/ppermute | solution.py:1001
